TPU v7x, 32 devices: a whole 2x2x4 slice. The times are simulated.
32 devices in a mesh: dp: 8 (over z, x), mp: 4 (over y, core).
Axes of the slice: x: 2, y: 2, z: 4, core: 2. Of those that a mesh axis runs over, the one named last changes fastest.
Arguments:
- features: bfloat16 [256, 32, 512], P(('dp', 'mp')), may hold values from -6 to 6
- lengths: int32 [256], P(('dp', 'mp')), may hold values from 1 to 7, as said below
- dests: int32 [256], P(('dp', 'mp')), may hold values from 0 to 7, as said below
- offsets: int32 [256], P(('dp', 'mp')), may hold values from 0 to 127, as said below
- conv_weight: bfloat16 [2, 1024, 512], replicated, may hold values from -0.1875 to 0.1875
- norm_gain: float32 [2, 512], replicated, may hold values from 0.1 to 1.9
- norm_shift: float32 [2, 512], replicated, may hold values from -3 to 3
- proj_weight: bfloat16 [512, 1280], P(None, 'mp'), may hold values from -0.25 to 0.25
- grad_packed: bfloat16 [1024, 1280], P('dp', 'mp'), may hold values from -6 to 6
Outputs:
- packed: bfloat16 [1024, 1280], P('dp', 'mp')
- grad_features: bfloat16 [256, 32, 512], P(('dp', 'mp'))
- grad_conv: float32 [2, 1024, 512], P(None, ('dp', 'mp'))
- grad_norm: float32 [2, 1024], P(None, ('dp', 'mp'))
- grad_proj: float32 [512, 1280], P('dp', 'mp')
Inputs may be any that keep to these rules, and one draw needn't show every extreme that they name: Utterances 2k and 2k+1 of each device form a pair whose lengths sum to 8. `dests`: both utterances of a pair name the same shard; the 4 pairs of one device name different shards, and every shard is named by exactly 16 pairs. A pair fills one aligned block of 8 rows of its shard that no other pair uses: the first utterance starts at offsets[2k], a multiple of 8, and the second at offsets[2k] + lengths[2k].
All inputs are finite; a program needn't handle non-finite values.
Results may differ from a plain program's by a relative error of at most 0.015.
Values may be sent and summed in bfloat16 or wider, within the bound.
No kernel may reach another device: no remote copies, remote signals or barrier semaphores. Data moves between devices by JAX's collectives and lax.ppermute only.
A program may use at most 64 MiB of HBM per device.

v0:
```python
import jax
import jax.numpy as jnp
from jax import lax
from jax.sharding import PartitionSpec as P

epsilon = 1e-05


def norm_gelu(pre_norm, gain_row, shift_row):
    average = jnp.mean(pre_norm, axis=-1, keepdims=True)
    centred = pre_norm - average
    spread = jnp.mean(centred * centred, axis=-1, keepdims=True)
    return jax.nn.gelu(
        centred * lax.rsqrt(spread + epsilon) * gain_row + shift_row, approximate=False
    )


def encode(inputs, conv_weight, norm_gain, norm_shift):
    channels = inputs.shape[-1]
    first_in = inputs.reshape(-1, 2 * channels)
    first_out = jnp.dot(first_in, conv_weight[0], preferred_element_type=jnp.float32)
    hidden, pull_first = jax.vjp(norm_gelu, first_out, norm_gain[0], norm_shift[0])
    hidden = hidden.astype(jnp.bfloat16)
    second_in = hidden.reshape(-1, 2 * channels)
    second = jnp.dot(second_in, conv_weight[1], preferred_element_type=jnp.float32)
    frames, pull_second = jax.vjp(norm_gelu, second, norm_gain[1], norm_shift[1])
    return (frames.astype(jnp.bfloat16), (first_in, second_in, pull_first, pull_second))


def encode_back(grad_frames, kept_state, conv_weight):
    first_in, second_in, pull_first, pull_second = kept_state
    channels = conv_weight.shape[2]
    grad_second, gain_second, shift_second = pull_second(
        lax.optimization_barrier(grad_frames).astype(jnp.float32)
    )
    grad_second = grad_second.astype(jnp.bfloat16)
    grad_hidden = jnp.dot(grad_second, conv_weight[1].T, preferred_element_type=jnp.float32).astype(
        jnp.bfloat16
    )
    grad_hidden = lax.optimization_barrier(grad_hidden).reshape(-1, channels).astype(jnp.float32)
    grad_first, gain_first, shift_first = pull_first(grad_hidden)
    grad_first = grad_first.astype(jnp.bfloat16)
    grad_inputs = jnp.dot(grad_first, conv_weight[0].T, preferred_element_type=jnp.float32).astype(
        jnp.bfloat16
    )
    grad_weight = jnp.stack(
        [
            jnp.dot(first_in.T, grad_first, preferred_element_type=jnp.float32),
            jnp.dot(second_in.T, grad_second, preferred_element_type=jnp.float32),
        ]
    )
    grad_norms = jnp.stack(
        [jnp.concatenate([gain_first, shift_first]), jnp.concatenate([gain_second, shift_second])]
    )
    return (grad_inputs, grad_weight, grad_norms)


def local(
    features, lengths, dests, offsets, conv_weight, norm_gain, norm_shift, proj_weight, grad_packed
):
    utt_count, positions, channels = features.shape
    frame_count = positions // 4
    pair_count = utt_count // 2
    dp_count = lax.axis_size("dp")
    mp_count = lax.axis_size("mp")
    block_count = pair_count * mp_count
    first_len = lengths[0::2]
    pair_dest = dests[0::2]
    pair_block = offsets[0::2] // frame_count
    position_ids = jnp.arange(positions, dtype=jnp.int32)[None, :]
    split_at = 4 * first_len[:, None]
    source_pos = jnp.where(
        position_ids < split_at, position_ids, positions + position_ids - split_at
    )
    paired = features.reshape(pair_count, 2 * positions, channels)
    pair_input = jnp.take_along_axis(paired, source_pos[:, :, None], axis=1)
    pair_frames, kept_state = encode(
        pair_input.reshape(-1, channels), conv_weight, norm_gain, norm_shift
    )
    pair_frames = pair_frames.reshape(pair_count, frame_count, channels)
    send_index = jnp.full((dp_count,), block_count, jnp.int32).at[pair_dest].set(pair_block)
    send_index_all = jnp.broadcast_to(send_index[:, None], (dp_count, mp_count)).reshape(-1)
    send_frames = (
        jnp.zeros((dp_count, frame_count, channels), jnp.bfloat16).at[pair_dest].set(pair_frames)
    )
    send_frames = jnp.broadcast_to(
        send_frames[:, None], (dp_count, mp_count, frame_count, channels)
    )
    send_frames = send_frames.reshape(dp_count * mp_count, frame_count, channels)
    got_frames, got_index = (
        lax.all_to_all(send_frames, ("dp", "mp"), split_axis=0, concat_axis=0, tiled=True),
        lax.all_to_all(send_index_all, ("dp", "mp"), split_axis=0, concat_axis=0, tiled=True),
    )
    packed_in = jnp.zeros((block_count, frame_count, channels), jnp.bfloat16)
    packed_in = packed_in.at[got_index].set(got_frames, mode="drop").reshape(-1, channels)
    packed = jnp.dot(packed_in, proj_weight, preferred_element_type=jnp.float32).astype(
        jnp.bfloat16
    )
    grad_proj = lax.psum_scatter(
        jnp.dot(packed_in.T, grad_packed, preferred_element_type=jnp.float32).astype(jnp.bfloat16),
        "dp",
        scatter_dimension=0,
        tiled=True,
    ).astype(jnp.float32)
    grad_rows = jnp.dot(grad_packed, proj_weight.T, preferred_element_type=jnp.float32)
    grad_rows = grad_rows.reshape(block_count, frame_count, channels)
    partial_sums = jnp.take(grad_rows, got_index, axis=0, mode="fill", fill_value=0.0)
    returned = lax.all_to_all(partial_sums, ("dp", "mp"), split_axis=0, concat_axis=0, tiled=True)
    returned = returned.reshape(dp_count, mp_count, frame_count, channels)
    grad_blocks = jnp.sum(returned, axis=1).astype(jnp.bfloat16)
    grad_pair = grad_blocks[pair_dest]
    grad_input, grad_weight, grad_norms = encode_back(
        grad_pair.reshape(-1, channels), kept_state, conv_weight
    )
    grad_input = grad_input.reshape(pair_count, positions, channels)
    split_back = 4 * first_len[:, None]
    all_ids = jnp.arange(2 * positions, dtype=jnp.int32)[None, :]
    in_first = all_ids < positions
    from_pos = jnp.where(in_first, all_ids, all_ids - positions + split_back)
    is_valid = jnp.where(
        in_first, all_ids < split_back, all_ids - positions < positions - split_back
    )
    gathered = jnp.take_along_axis(
        grad_input, jnp.minimum(from_pos, positions - 1)[:, :, None], axis=1
    )
    grad_features = jnp.where(is_valid[:, :, None], gathered, jnp.zeros_like(gathered))
    grad_features = grad_features.reshape(utt_count, positions, channels)
    grad_conv, grad_norm = (
        lax.psum_scatter(grad_weight, ("dp", "mp"), scatter_dimension=1, tiled=True),
        lax.psum_scatter(grad_norms, ("dp", "mp"), scatter_dimension=1, tiled=True),
    )
    return (packed, grad_features, grad_conv, grad_norm, grad_proj)


def solution(mesh):
    return jax.shard_map(
        local,
        mesh=mesh,
        in_specs=(
            P(("dp", "mp"), None, None),
            P(("dp", "mp")),
            P(("dp", "mp")),
            P(("dp", "mp")),
            P(),
            P(),
            P(),
            P(None, "mp"),
            P("dp", "mp"),
        ),
        out_specs=(
            P("dp", "mp"),
            P(("dp", "mp"), None, None),
            P(None, ("dp", "mp"), None),
            P(None, ("dp", "mp")),
            P("dp", "mp"),
        ),
        check_vma=False,
    )
```

profile of v0, /device:TPU:0, one launch (start us, length us, event | category | flops | bytes accessed | tf_op | source)
XLA Modules:
  0.0 407.6 jit_solution(18095995382440396950)
XLA Ops:
  7.2 0.8 slice.29
  8.0 0.7 slice.30
  8.8 0.5 copy-done.9
  9.3 0.6 scatter_custom_fusion
  9.9 0.7 all_to_all.22
  10.6 7.3 %all-to-all-start = ((s32[32,1,1]{2,1,0:T(1,128)}), s32[32,1,1]{2,1,0:T(1,128)S(1)}, u32[]{:S(2)}, u32[]{:S(2)}) async-start(s32[32,1,1]{2,1,0:T(1,128)} %all_to_all.22), calls=%async_computation | async-start | bytes 32768 | tf_op jit(solution)/shard_map/all_to_all | solution.py:92
  17.9 0.7 slice.31
  18.7 0.5 broadcast_subtract_fusion
  19.8 2.3 gather_fusion.2
  22.2 1.6 fusion.49
  24.1 0.6 fusion.40
  25.0 0.7 reduce
  25.7 0.6 gather_fusion
  26.4 0.9 broadcast_select_fusion
  27.3 5.8 %all-to-all-start.2 = ((f32[32,8,512]{2,1,0:T(8,128)}), f32[32,8,512]{2,1,0:T(8,128)S(1)}, u32[]{:S(2)}, u32[]{:S(2)}) async-start(f32[32,8,512]{2,1,0:T(8,128)} %broadcast_select_fusion), calls=%async_computation.2 | async-start | bytes 1048576 | tf_op jit(solution)/shard_map/all_to_all | solution.py:108
  33.6 0.7 pad_clamp_fusion
  34.8 0.5 fusion.41
  35.4 13.3 %all-to-all-done.2 = f32[32,8,512]{2,1,0:T(8,128)S(1)} async-done(((f32[32,8,512]{2,1,0:T(8,128)}), f32[32,8,512]{2,1,0:T(8,128)S(1)}, u32[]{:S(2)}, u32[]{:S(2)}) %all-to-all-start.2) | async-done | bytes 524320 | tf_op jit(solution)/shard_map/all_to_all | solution.py:108
  48.7 0.5 gather_fusion.1
  49.2 1.5 multiply_reduce_fusion.3
  50.7 0.7 multiply_multiply_fusion.11
  51.4 0.8 fusion.43
  52.2 0.6 copy-done.14
  52.8 0.4 convolution_convert_fusion.3
  53.2 0.8 scatter_fusion
  54.0 0.7 broadcast_in_dim.124
  54.7 3.1 all-to-all-start.1
  57.9 1.5 multiply_reduce_fusion
  59.4 0.7 pad_maximum_fusion.3
  60.1 1.0 copy.16
  61.2 0.7 multiply_multiply_fusion.10
  61.9 0.9 fusion.42
  62.8 5.6 %all-to-all-done.1 = bf16[32,8,512]{2,1,0:T(8,128)(2,1)S(1)} async-done(((bf16[32,8,512]{2,1,0:T(8,128)(2,1)}), bf16[32,8,512]{2,1,0:T(8,128)(2,1)S(1)}, u32[]{:S(2)}, u32[]{:S(2)}) %all-to-all-start.1) | async-done | bytes 262176 | tf_op jit(solution)/shard_map/all_to_all | solution.py:91
  68.4 1.7 scatter_fusion.1
  70.1 1.1 convolution_convert_fusion
  71.2 1.2 convolution_bitcast_fusion
  72.4 0.5 convolution_bitcast_fusion.1
  72.9 2.4 pad_maximum_fusion
  75.3 0.6 copy-done.11
  76.7 0.4 convolution_convert_fusion.1
  77.2 2.1 gather_fusion.3
  79.3 0.8 select_select_fusion
  80.2 116.3 %reduce-scatter.10.cloned.1.call-done = f32[32,2]{1,0:T(8,128)} async-done(((f32[1024,2]{1,0:T(8,128)}), f32[32,2]{1,0:T(8,128)}) %reduce-scatter.10.cloned.1.call-update) | async-done | bytes 272
  196.4 1.4 copy.17
  197.8 0.9 convolution_convert_fusion.2
  198.7 58.8 %reduce-scatter.8.cloned.1.call-done = bf16[64,320]{1,0:T(8,128)(2,1)} async-done(((bf16[512,320]{1,0:T(8,128)(2,1)}), bf16[64,320]{1,0:T(8,128)(2,1)}) %reduce-scatter.8.cloned.1.call-update) | async-done | bytes 40976 | tf_op jit(solution)/shard_map/reduce_scatter | solution.py:99
  257.5 1.4 convert_element_type.51
  258.9 142.1 %reduce-scatter.6.cloned.1.call-done = f32[2,32,512]{2,1,0:T(8,128)} async-done(((f32[2,1024,512]{2,1,0:T(8,128)}), f32[2,32,512]{2,1,0:T(8,128)}) %reduce-scatter.6.cloned.1.call-update) | async-done | bytes 131088 | tf_op jit(solution)/shard_map/reduce_scatter | solution.py:129
  (92 shorter events, 3.5 us)
Async XLA Ops:
  7.2 17.6 %copy-start = (bf16[512,320]{0,1:T(8,128)(2,1)S(1)}, bf16[512,320]{0,1:T(8,128)(2,1)}, u32[]{:S(2)}) copy-start(bf16[512,320]{0,1:T(8,128)(2,1)} %param.16) | copy-start | bytes 983044
  7.2 17.5 %copy-start.12 = (f32[2,512]{1,0:T(2,128)S(1)}, f32[2,512]{1,0:T(2,128)}, u32[]{:S(2)}) copy-start(f32[2,512]{1,0:T(2,128)} %param.14) | copy-start | bytes 12292
  7.2 17.5 %copy-start.13 = (f32[2,512]{1,0:T(2,128)S(1)}, f32[2,512]{1,0:T(2,128)}, u32[]{:S(2)}) copy-start(f32[2,512]{1,0:T(2,128)} %param.15) | copy-start | bytes 12292
  7.2 17.5 %copy-start.2 = (bf16[128,320]{0,1:T(8,128)(2,1)S(1)}, bf16[128,320]{0,1:T(8,128)(2,1)}, u32[]{:S(2)}) copy-start(bf16[128,320]{0,1:T(8,128)(2,1)} %param.17) | copy-start | bytes 245764
  8.8 0.5 copy-start.9
  10.6 14.4 %all-to-all-start = ((s32[32,1,1]{2,1,0:T(1,128)}), s32[32,1,1]{2,1,0:T(1,128)S(1)}, u32[]{:S(2)}, u32[]{:S(2)}) async-start(s32[32,1,1]{2,1,0:T(1,128)} %all_to_all.22), calls=%async_computation | async-start | bytes 32768 | tf_op jit(solution)/shard_map/all_to_all | solution.py:92
  19.2 0.6 copy-start.10
  23.9 0.8 copy-start.6
  24.1 0.6 copy-start.16
  24.7 8.8 %copy-start.4 = (f32[1,512]{1,0:T(1,128)}, f32[1,512]{1,0:T(1,128)S(1)}, u32[]{:S(2)}) copy-start(f32[1,512]{1,0:T(1,128)S(1)} %get-tuple-element.26) | copy-start | bytes 6148
  24.8 8.8 %copy-start.5 = (f32[1,512]{1,0:T(1,128)}, f32[1,512]{1,0:T(1,128)S(1)}, u32[]{:S(2)}) copy-start(f32[1,512]{1,0:T(1,128)S(1)} %get-tuple-element.24) | copy-start | bytes 6148
  24.8 9.5 %copy-start.1 = (bf16[2,1024,512]{2,1,0:T(8,128)(2,1)S(1)}, bf16[2,1024,512]{2,1,0:T(8,128)(2,1)}, u32[]{:S(2)}) copy-start(bf16[2,1024,512]{2,1,0:T(8,128)(2,1)} %param.13) | copy-start | bytes 6291460
  25.7 1.6 copy-start.15
  26.3 6.8 %copy-start.7 = (f32[64]{0:T(128)S(1)}, f32[64]{0:T(128)}, u32[]{:S(2)}) copy-start(f32[64]{0:T(128)} %copy-done.6) | copy-start | bytes 772
  26.3 6.8 %copy-start.8 = (f32[64]{0:T(128)S(1)}, f32[64]{0:T(128)}, u32[]{:S(2)}) copy-start(f32[64]{0:T(128)} %fusion.40) | copy-start | bytes 772
  27.3 21.4 %all-to-all-start.2 = ((f32[32,8,512]{2,1,0:T(8,128)}), f32[32,8,512]{2,1,0:T(8,128)S(1)}, u32[]{:S(2)}, u32[]{:S(2)}) async-start(f32[32,8,512]{2,1,0:T(8,128)} %broadcast_select_fusion), calls=%async_computation.2 | async-start | bytes 1048576 | tf_op jit(solution)/shard_map/all_to_all | solution.py:108
  34.8 0.6 copy-start.17
  52.2 0.6 copy-start.14
  53.2 16.9 %copy-start.3 = (bf16[128,320]{0,1:T(8,128)(2,1)S(1)}, bf16[128,320]{0,1:T(8,128)(2,1)}, u32[]{:S(2)}) copy-start(bf16[128,320]{0,1:T(8,128)(2,1)} %param.17) | copy-start | bytes 245764
  54.7 13.7 %all-to-all-start.1 = ((bf16[32,8,512]{2,1,0:T(8,128)(2,1)}), bf16[32,8,512]{2,1,0:T(8,128)(2,1)S(1)}, u32[]{:S(2)}, u32[]{:S(2)}) async-start(bf16[32,8,512]{2,1,0:T(8,128)(2,1)} %bitcast.10), calls=%async_computation.1 | async-start | bytes 524288 | tf_op jit(solution)/shard_map/all_to_all | solution.py:91
  57.8 138.6 %reduce-scatter.10.cloned.1.call-start = ((), (), s32[]{:S(2)}) async-start(), calls=%async_computation.8 | async-start | bytes 540672
  61.1 196.4 %reduce-scatter.8.cloned.1.call-start = ((), (), s32[]{:S(2)}) async-start(), calls=%async_computation.7 | async-start | bytes 442368 | tf_op jit(solution)/shard_map/reduce_scatter | solution.py:99
  71.2 329.9 %reduce-scatter.6.cloned.1.call-start = ((), (), s32[]{:S(2)}) async-start(), calls=%async_computation.6 | async-start | bytes 4325376 | tf_op jit(solution)/shard_map/reduce_scatter | solution.py:129
  75.2 0.7 copy-start.11
  75.2 1.1 copy-start.18
Sparse Core Ops, SparseCore 0:
  61.3 135.1 reduce-scatter.9
  200.0 57.4 reduce-scatter.7
  260.4 140.5 reduce-scatter.5
where the time goes:
time: 408 us
  waiting for transfers between devices  336 us (82%)
  local copies, waits for them, and re-layouts  17.7 us (4%)
  other arithmetic  16.5 us (4%)
  starting transfers between devices  16.3 us (4%)
  between operations  14.2 us (3%)
  matrix products  6.66 us (2%)
    reduce_scatter x1, waiting for transfers between devices, local(): lax.psum_scatter(grad_weight, ('dp', 'mp'), scatter_dimension=1, tiled=True)  142 us
    unnamed x4, waiting for transfers between devices  116 us
    reduce_scatter x1, waiting for transfers between devices, local(): lax.psum_scatter(jnp.dot(packed_in.T, grad_packed, preferred_element_type...  58.8 us
    all_to_all x1, waiting for transfers between devices, local(): lax.all_to_all(partial_sums, ('dp', 'mp'), split_axis=0, concat_axis=0, t...  13.3 us
  transfers between devices with their start and end apart: 6, of which 5 were waited for; matrix products, arithmetic and copies ran while one was open for 7% of the time, Pallas kernels for 0%

commit v1 on v0

v1 whole, which is shorter than its diff:
```python
import functools
import math

import jax
import jax.numpy as jnp
from jax import lax
from jax.experimental import pallas as pl
from jax.experimental.pallas import tpu as pltpu
from jax.sharding import PartitionSpec as P

epsilon = 1e-05
BF = jnp.bfloat16
F32 = jnp.float32
VMEM = pltpu.VMEM
SMEM = pltpu.SMEM


def call(body, out, args, scalars=0, flops=0, scratch=()):
    specs = [
        pl.BlockSpec(memory_space=SMEM if i < scalars else VMEM) for i in range(len(args))
    ]
    many = isinstance(out, (list, tuple))
    moved = sum(a.size * a.dtype.itemsize for a in args)
    return pl.pallas_call(
        body,
        out_shape=out,
        in_specs=specs,
        out_specs=[pl.BlockSpec(memory_space=VMEM)] * len(out)
        if many
        else pl.BlockSpec(memory_space=VMEM),
        scratch_shapes=list(scratch),
        compiler_params=pltpu.CompilerParams(vmem_limit_bytes=40 * 2**20),
        cost_estimate=pl.CostEstimate(flops=flops, bytes_accessed=moved, transcendentals=0),
    )(*args)


def shape(*dims, kind=BF):
    return jax.ShapeDtypeStruct(dims, kind)


def dot(a, b):
    return jnp.dot(a, b, preferred_element_type=F32)


def dot_nt(a, b):
    return lax.dot_general(a, b, (((1,), (1,)), ((), ())), preferred_element_type=F32)


def norm_parts(pre):
    average = jnp.mean(pre, axis=-1, keepdims=True)
    centred = pre - average
    spread = jnp.mean(centred * centred, axis=-1, keepdims=True)
    scale = lax.rsqrt(spread + epsilon)
    return centred * scale, scale


def gelu_parts(value):
    half = 0.5 * (1.0 + lax.erf(value * math.sqrt(0.5)))
    density = jnp.exp(-0.5 * value * value) * (1.0 / math.sqrt(2.0 * math.pi))
    return value * half, half + value * density


def source_of(row, lengths_ref, pairs, frames):
    part = lax.div(row, pairs * frames)
    inner = lax.rem(row, pairs * frames)
    pair = lax.div(inner, frames)
    t = lax.rem(inner, frames)
    first = jnp.zeros_like(row)
    for p in range(pairs):
        first = jnp.where(pair == p, lengths_ref[2 * p], first)
    off = jnp.where(part == 1, 2, jnp.where(part == 2, 1, part))
    t_from = jnp.where(t < first, t, t + frames - first)
    return pair * (8 * frames) + 4 * t_from + off


def index_kernel(dests_ref, offsets_ref, out_ref, *, pairs, frames):
    row = lax.broadcasted_iota(jnp.int32, out_ref.shape, 0)
    value = jnp.full(out_ref.shape, -1, jnp.int32)
    for p in range(pairs):
        value = jnp.where(row == dests_ref[2 * p], lax.div(offsets_ref[2 * p], frames), value)
    out_ref[...] = value


def forward_kernel(
    lengths_ref, me_ref, feat_ref, weight_ref, gain_ref, shift_ref, *rest, pairs, frames, groups, owned
):
    mp_count = me_ref.shape[0] - 1
    frames_ref, slope1_ref, slope2_ref, hat1_ref, hat2_ref, scale1_ref, scale2_ref = rest[:7]
    turned_refs, in_turned = rest[7:-1], rest[-1]
    channels = feat_ref.shape[1]
    n2 = pairs * frames
    row = lax.broadcasted_iota(jnp.int32, (4 * n2, 1), 0)
    source = source_of(row, lengths_ref, pairs, frames)
    place = lax.broadcasted_iota(jnp.int32, (4 * n2, feat_ref.shape[0]), 1)
    pick = jnp.where(place == source, 1.0, 0.0).astype(BF)
    chosen32 = dot(pick, feat_ref[...])
    chosen = chosen32.astype(BF)
    even, odd = chosen[: 2 * n2], chosen[2 * n2 :]
    first = dot(even, weight_ref[0, :channels, :]) + dot(odd, weight_ref[0, channels:, :])
    hat, scale = norm_parts(first)
    hidden, slope = gelu_parts(hat * gain_ref[0:1, :] + shift_ref[0:1, :])
    slope1_ref[...] = slope
    hat1_ref[...] = hat
    scale1_ref[...] = jnp.broadcast_to(scale, scale1_ref.shape)
    hidden = hidden.astype(BF)
    hidden32 = hidden.astype(F32)
    second = dot(hidden[:n2], weight_ref[1, :channels, :]) + dot(
        hidden[n2:], weight_ref[1, channels:, :]
    )
    hat, scale = norm_parts(second)
    made, slope = gelu_parts(hat * gain_ref[1:2, :] + shift_ref[1:2, :])
    slope2_ref[...] = slope
    hat2_ref[...] = hat
    scale2_ref[...] = jnp.broadcast_to(scale, scale2_ref.shape)
    frames_ref[...] = made.astype(BF)
    wide = in_turned.shape[1]
    fill = [jnp.zeros((wide - 3 * n2, channels), F32)] if wide > 3 * n2 else []
    for tap in range(2):
        stacked = jnp.concatenate(
            [chosen32[2 * n2 * tap : 2 * n2 * (tap + 1)], hidden32[n2 * tap : n2 * (tap + 1)]] + fill,
            axis=0,
        )
        in_turned[channels * tap : channels * (tap + 1), :] = stacked.T
    for k, turned_ref in enumerate(turned_refs):
        start = me_ref[1 + k] * owned
        turned_ref[...] = jnp.concatenate(
            [
                in_turned[pl.ds(pl.multiple_of(d * mp_count * owned + start, owned), owned), :]
                for d in range(groups)
            ],
            axis=0,
        ).astype(BF)


def send_kernel(got_ref, dests_ref, mine_ref, other_ref, frames_ref, out_ref, rows32, *, pairs, frames):
    rows32[...] = mine_ref[...].astype(F32) + other_ref[...].astype(F32)
    blocks = rows32.shape[0] // frames
    made = frames_ref[...].astype(F32)
    none = jnp.zeros((frames, made.shape[1]), F32)
    for d in range(out_ref.shape[0]):
        block = got_ref[d, 0]
        safe = jnp.clip(block, 0, blocks - 1)
        grads = rows32[pl.ds(pl.multiple_of(safe * frames, frames), frames), :]
        grads = jnp.where(block >= 0, grads, none)
        sent = none
        for p in range(pairs):
            sent = jnp.where(dests_ref[2 * p] == d, made[p * frames : (p + 1) * frames], sent)
        out_ref[d] = jnp.concatenate([grads, sent], axis=0).astype(BF)


def place_kernel(got_ref, slots_ref, out_ref, rows32, *, frames):
    rows32[...] = jnp.zeros_like(rows32)
    for d in range(slots_ref.shape[0]):
        block = got_ref[d, 0]

        @pl.when(block >= 0)
        def _():
            safe = jnp.clip(block, 0, rows32.shape[0] // frames - 1)
            rows32[pl.ds(pl.multiple_of(safe * frames, frames), frames), :] = slots_ref[d].astype(F32)[
                frames:
            ]

    out_ref[...] = rows32[...].astype(BF)


def project_kernel(mine_ref, other_ref, weight_ref, packed_ref, turned_ref):
    rows32 = mine_ref[...].astype(F32) + other_ref[...].astype(F32)
    packed_ref[...] = dot(rows32.astype(BF), weight_ref[...]).astype(BF)
    turned_ref[...] = rows32.T.astype(BF)


def norm_back(grad, slope_ref, hat_ref, scale_ref, gain):
    pre = grad * slope_ref[...]
    hat = hat_ref[...]
    by_hat = pre * hat
    inner = pre * gain
    average = jnp.mean(inner, axis=-1, keepdims=True)
    along = jnp.mean(inner * hat, axis=-1, keepdims=True)
    back = (inner - average - hat * along) * scale_ref[:, 0:1]
    return (
        back.astype(BF),
        jnp.sum(by_hat, axis=0, keepdims=True),
        jnp.sum(pre, axis=0, keepdims=True),
    )


def back_kernel(
    dests_ref, slots_ref, slope1_ref, slope2_ref, hat1_ref, hat2_ref, scale1_ref, scale2_ref,
    weight_ref, gain_ref, out_ref, grads32, *, pairs, frames
):
    channels = weight_ref.shape[2]
    for p in range(pairs):
        slot = jnp.clip(dests_ref[2 * p], 0, slots_ref.shape[0] - 1)
        grads32[p * frames : (p + 1) * frames, :] = slots_ref[slot].astype(F32)[:frames]
    second, gain2, shift2 = norm_back(grads32[...], slope2_ref, hat2_ref, scale2_ref, gain_ref[1:2, :])
    hidden = jnp.concatenate(
        [
            dot_nt(second, weight_ref[1, :channels, :]),
            dot_nt(second, weight_ref[1, channels:, :]),
        ],
        axis=0,
    )
    hidden = hidden.astype(BF).astype(F32)
    first, gain1, shift1 = norm_back(hidden, slope1_ref, hat1_ref, scale1_ref, gain_ref[0:1, :])
    sums = jnp.concatenate([gain1, shift1, gain2, shift2], axis=0)
    high = sums.astype(BF).astype(F32)
    rows = [high, sums - high, jnp.zeros((8, channels), F32)]
    n1, n2 = first.shape[0], second.shape[0]
    out_ref[:n1, :] = first
    out_ref[n1 : n1 + n2, :] = second
    out_ref[n1 + n2 :, :] = jnp.concatenate(rows, axis=0).astype(BF)


def input_kernel(lengths_ref, grad_ref, weight_ref, out_ref, *, pairs, frames):
    channels = weight_ref.shape[2]
    n1 = 2 * pairs * frames
    first = grad_ref[:n1, :]
    rows = jnp.concatenate(
        [dot_nt(first, weight_ref[0, :channels, :]), dot_nt(first, weight_ref[0, channels:, :])],
        axis=0,
    ).astype(BF)
    row = lax.broadcasted_iota(jnp.int32, (1, 2 * n1), 1)
    source = source_of(row, lengths_ref, pairs, frames)
    place = lax.broadcasted_iota(jnp.int32, (out_ref.shape[0], 2 * n1), 0)
    pick = jnp.where(place == source, 1.0, 0.0).astype(BF)
    out_ref[...] = dot(pick, rows).astype(BF)


def kernel_grad_kernel(*refs, n1, n2, owned, count):
    grad_refs, in_refs, turned_ref, out_ref = refs[:count], refs[count : 2 * count], refs[-2], refs[-1]
    channels = out_ref.shape[2]
    groups = out_ref.shape[0]
    first, second, sums = 0.0, 0.0, 0.0
    for grad_ref, in_ref in zip(grad_refs, in_refs):
        side = in_ref[...]
        first += dot(side[:, :n1], grad_ref[:n1, :])
        second += dot(side[:, n1 : n1 + n2], grad_ref[n1 : n1 + n2, :])
        tail = grad_ref[n1 + n2 :, :].astype(F32)
        sums += tail[0:4] + tail[4:8]
    high = sums.astype(BF).astype(F32)
    low = sums - high
    width = 2 * channels // groups
    per_slot = channels // groups
    across = channels // turned_ref.shape[1]
    each = per_slot // across
    for d in range(groups):
        at = (d * width) % channels
        which = (d * width) // channels
        pieces = [
            part[2 * layer + which : 2 * layer + which + 1, at : at + width]
            for part in (high, low)
            for layer in range(2)
        ]
        if 4 * width < channels:
            pieces.append(jnp.zeros((1, channels - 4 * width), F32))
        norm_row = jnp.concatenate(pieces, axis=1)
        turned = turned_ref[d * per_slot : (d + 1) * per_slot, :].astype(F32)
        turned = jnp.concatenate([turned[g * each : (g + 1) * each] for g in range(across)], axis=1)
        out_ref[d] = jnp.concatenate(
            [
                first[d * owned : (d + 1) * owned],
                second[d * owned : (d + 1) * owned],
                turned,
                norm_row,
                jnp.zeros((7, channels), F32),
            ],
            axis=0,
        ).astype(BF)


def last_kernel(me_ref, slots_ref, cotangent_ref, conv_ref, norm_ref, proj_ref, *, owned, mp_count):
    groups, _, channels = slots_ref.shape
    seq = cotangent_ref.shape[0] // groups
    across = channels // seq
    each = channels // groups // across
    total, norms, proj = 0.0, 0.0, 0.0
    for d in range(groups):
        slot = slots_ref[d].astype(F32)
        total += slot[: 2 * owned]
        turned = slot[2 * owned : 2 * owned + each]
        turned = jnp.concatenate([turned[:, g * seq : (g + 1) * seq] for g in range(across)], axis=0)
        norms += slot[2 * owned + each : 2 * owned + each + 1]
        proj += dot(turned.astype(BF), cotangent_ref[d * seq : (d + 1) * seq, :])
    conv_ref[0] = total[:owned]
    conv_ref[1] = total[owned:]
    proj_ref[...] = proj
    width = mp_count * owned
    rows = []
    for layer in range(2):
        line = norms[:, layer * width : (layer + 1) * width]
        line = line + norms[:, (2 + layer) * width : (3 + layer) * width]
        mine = jnp.zeros((1, owned), F32)
        for m in range(mp_count):
            mine = jnp.where(me_ref[0] == m, line[:, m * owned : (m + 1) * owned], mine)
        rows.append(mine)
    norm_ref[...] = jnp.concatenate(rows, axis=0)


def local(
    features, lengths, dests, offsets, conv_weight, norm_gain, norm_shift, proj_weight, grad_packed
):
    utt_count, positions, channels = features.shape
    frames = positions // 4
    pairs = utt_count // 2
    dp_count = lax.axis_size("dp")
    mp_count = lax.axis_size("mp")
    seq = grad_packed.shape[0]
    width = grad_packed.shape[1]
    owned = 2 * channels // (dp_count * mp_count)
    n1, n2 = 2 * pairs * frames, pairs * frames
    bits = [1 << b for b in range(mp_count.bit_length() - 1)][::-1]

    def swap(x, mask):
        return lax.ppermute(x, "mp", [(i, i ^ mask) for i in range(mp_count)])

    me = lax.axis_index("mp").astype(jnp.int32)
    me_all = jnp.stack([me] + [me ^ k for k in range(mp_count)])

    index = call(
        functools.partial(index_kernel, pairs=pairs, frames=frames),
        shape(dp_count, 128, kind=jnp.int32),
        (dests, offsets),
        scalars=2,
    )
    got_index = lax.all_to_all(index, "dp", split_axis=0, concat_axis=0, tiled=True)
    all_cotangent = lax.all_gather(grad_packed, "dp", tiled=True)

    grad_rows = lax.dot_general(
        grad_packed, proj_weight, (((1,), (1,)), ((), ())), preferred_element_type=F32
    ).astype(BF)
    for mask in bits[:-1]:
        grad_rows = (grad_rows.astype(F32) + swap(grad_rows, mask).astype(F32)).astype(BF)
    other_rows = swap(grad_rows, bits[-1])

    wide = -(-(n1 + n2) // 128) * 128
    feat = features.reshape(utt_count * positions, channels)
    made = call(
        functools.partial(forward_kernel, pairs=pairs, frames=frames, groups=dp_count, owned=owned),
        [
            shape(n2, channels),
            shape(n1, channels, kind=F32),
            shape(n2, channels, kind=F32),
            shape(n1, channels, kind=F32),
            shape(n2, channels, kind=F32),
            shape(n1, 128, kind=F32),
            shape(n2, 128, kind=F32),
        ]
        + [shape(dp_count * owned, wide)] * mp_count,
        (lengths, me_all, feat, conv_weight, norm_gain, norm_shift),
        scalars=2,
        flops=2 * (n1 + n2) * 2 * channels * channels,
        scratch=[pltpu.VMEM((2 * channels, wide), F32)],
    )
    pair_frames, slope1, slope2, hat1, hat2, scale1, scale2 = made[:7]
    in_sides = [side if k == 0 else swap(side, k) for k, side in enumerate(made[7:])]

    sent = call(
        functools.partial(send_kernel, pairs=pairs, frames=frames),
        shape(dp_count, 2 * frames, channels),
        (got_index, dests, grad_rows, other_rows, pair_frames),
        scalars=2,
        scratch=[pltpu.VMEM((seq, channels), F32)],
    )
    slots = lax.all_to_all(sent, "dp", split_axis=0, concat_axis=0, tiled=True)

    grads = call(
        functools.partial(back_kernel, pairs=pairs, frames=frames),
        shape(n1 + n2 + 16, channels),
        (dests, slots, slope1, slope2, hat1, hat2, scale1, scale2, conv_weight, norm_gain),
        scalars=1,
        flops=2 * n2 * 2 * channels * channels,
        scratch=[pltpu.VMEM((n2, channels), F32)],
    )
    by_mask = {0: grads}
    for mask in bits:
        for known in list(by_mask):
            by_mask[known ^ mask] = swap(by_mask[known], mask)

    placed = call(
        functools.partial(place_kernel, frames=frames),
        shape(seq, channels),
        (got_index, slots),
        scalars=1,
        scratch=[pltpu.VMEM((seq, channels), F32)],
    )
    for mask in bits[:-1]:
        placed = placed + swap(placed, mask)
    packed, turned = call(
        project_kernel,
        [shape(seq, width), shape(channels, seq)],
        (placed, swap(placed, bits[-1]), proj_weight),
        flops=2 * seq * channels * width,
    )

    grad_features = call(
        functools.partial(input_kernel, pairs=pairs, frames=frames),
        shape(utt_count * positions, channels),
        (lengths, grads, conv_weight),
        scalars=1,
        flops=2 * n1 * 2 * channels * channels,
    ).reshape(utt_count, positions, channels)

    per_slot = channels // dp_count * seq // channels
    partial = call(
        functools.partial(kernel_grad_kernel, n1=n1, n2=n2, owned=owned, count=mp_count),
        shape(dp_count, 2 * owned + per_slot + 8, channels),
        tuple(by_mask[k] for k in range(mp_count)) + tuple(in_sides) + (turned,),
        flops=2 * (n1 + n2) * 2 * channels * channels,
    )
    arrived = lax.all_to_all(partial, "dp", split_axis=0, concat_axis=0, tiled=True)
    grad_conv, grad_norm, grad_proj = call(
        functools.partial(last_kernel, owned=owned, mp_count=mp_count),
        [
            shape(2, owned, channels, kind=F32),
            shape(2, owned, kind=F32),
            shape(channels // dp_count, width, kind=F32),
        ],
        (me_all, arrived, all_cotangent),
        scalars=1,
    )
    return (packed, grad_features, grad_conv, grad_norm, grad_proj)


def solution(mesh):
    return jax.shard_map(
        local,
        mesh=mesh,
        in_specs=(
            P(("dp", "mp"), None, None),
            P(("dp", "mp")),
            P(("dp", "mp")),
            P(("dp", "mp")),
            P(),
            P(),
            P(),
            P(None, "mp"),
            P("dp", "mp"),
        ),
        out_specs=(
            P("dp", "mp"),
            P(("dp", "mp"), None, None),
            P(None, ("dp", "mp"), None),
            P(None, ("dp", "mp")),
            P("dp", "mp"),
        ),
        check_vma=False,
    )
```

time: 408 us -> 107 us (0.26)
  waiting for transfers between devices: 336 us -> 9.59 us
  blocking collectives: 0 us -> 56.3 us
  other arithmetic: 16.5 us -> 0.07 us
  between operations: 14.2 us -> 0.79 us
  Pallas kernels: 0 us -> 12.6 us
  local copies, waits for them, and re-layouts: 17.7 us -> 8.04 us
  matrix products: 6.66 us -> 1.27 us
    reduce_scatter x2 -> x0, waiting for transfers between devices: 201 us -> none  [the longest x1 142 us: local(): lax.psum_scatter(grad_weight, ('dp', 'mp'), scatter_dimension=1, tiled=True)]
    unnamed x4 -> x0, waiting for transfers between devices: 116 us -> none
    all_gather x0 -> x1, blocking collectives: none -> 43.2 us  [local(): all_cotangent = lax.all_gather(grad_packed, 'dp', tiled=True)]
    all_to_all x3 -> x2, waiting for transfers between devices: 18.9 us -> 0.01 us  [the longest x1 0.01 us: local(): lax.all_to_all(index, 'dp', split_axis=0, concat_axis=0, tiled=True)]
    all_to_all x0 -> x1, blocking collectives: none -> 13.1 us  [local(): slots = lax.all_to_all(sent, 'dp', split_axis=0, concat_axis=0, tiled=True)]
    pallas_call x0 -> x9, Pallas kernels: none -> 12.6 us  [call(): pl.pallas_call(body, out_shape=out, in_specs=specs, out_specs=[pl.BlockSp...]
    ppermute x0 -> x10, waiting for transfers between devices: none -> 9.58 us  [swap(): return lax.ppermute(x, 'mp', [(i, i ^ mask) for i in range(mp_count)])]
    ppermute x0 -> x10, starting transfers between devices: none -> 7.69 us  [swap(): return lax.ppermute(x, 'mp', [(i, i ^ mask) for i in range(mp_count)])]
  transfers between devices with their start and end apart: 6 -> 12, of which waited for: 5 -> 4; matrix products, arithmetic and copies ran while one was open for 7% -> 2% of each run, Pallas kernels for 0% -> 6%
where the time goes in v1:
time: 107 us
  blocking collectives  56.3 us (53%)
  starting transfers between devices  17.9 us (17%)
  Pallas kernels  12.6 us (12%)
  waiting for transfers between devices  9.59 us (9%)
  local copies, waits for them, and re-layouts  8.04 us (8%)
  matrix products  1.27 us (1%)
    all_gather x1, blocking collectives, local(): all_cotangent = lax.all_gather(grad_packed, 'dp', tiled=True)  43.2 us
    all_to_all x1, blocking collectives, local(): slots = lax.all_to_all(sent, 'dp', split_axis=0, concat_axis=0, tiled=True)  13.1 us
    pallas_call x9, Pallas kernels, call(): pl.pallas_call(body, out_shape=out, in_specs=specs, out_specs=[pl.BlockSp...  12.6 us
    ppermute x10, waiting for transfers between devices, swap(): return lax.ppermute(x, 'mp', [(i, i ^ mask) for i in range(mp_count)])  9.58 us
    unnamed x27, local copies, waits for them, and re-layouts  7.96 us
    ppermute x10, starting transfers between devices, swap(): return lax.ppermute(x, 'mp', [(i, i ^ mask) for i in range(mp_count)])  7.69 us
    all_to_all x1, starting transfers between devices, local(): lax.all_to_all(index, 'dp', split_axis=0, concat_axis=0, tiled=True)  6.03 us
    all_to_all x1, starting transfers between devices, local(): lax.all_to_all(partial, 'dp', split_axis=0, concat_axis=0, tiled=True)  4.21 us
  transfers between devices with their start and end apart: 12, of which 4 were waited for; matrix products, arithmetic and copies ran while one was open for 2% of the time, Pallas kernels for 6%

profile of v1, /device:TPU:0, one launch (start us, length us, event | category | flops | bytes accessed | tf_op | source)
XLA Modules:
  0.0 106.6 jit_solution(10084420307836126589)
XLA Ops:
  0.6 0.0 copy-start.6
  0.6 0.0 copy-start.4
  0.7 1.3 %convolution_convert_fusion = bf16[128,512]{1,0:T(8,128)(2,1)S(1)} fusion(bf16[128,320]{0,1:T(8,128)(2,1)} %param.17, bf16[512,320]{0,1:T(8,128)(2,1)} %param.16), kind=kOutput, calls=%fused_computation | convolution fusion | flops 42008576 | bytes 540672 | tf_op jit(solution)/shard_map/dot_general | solution.py:328
  1.9 3.0 %collective-permute-start = (bf16[128,512]{1,0:T(8,128)(2,1)S(1)}, bf16[128,512]{1,0:T(8,128)(2,1)S(1)}, u32[]{:S(2)}, u32[]{:S(2)}) collective-permute-start(bf16[128,512]{1,0:T(8,128)(2,1)S(1)} %convolution_convert_fusion), channel_id=1, source_target_pairs={{0,2},{1,3},{2,0},{3,1},{4,6},{5,7},{6,4},{7,5},{8,10},{9,11},{10,... | collective-permute-start | bytes 393224 | tf_op jit(solution)/shard_map/ppermute | solution.py:314
  5.0 3.5 %collective-permute-done = bf16[128,512]{1,0:T(8,128)(2,1)S(1)} collective-permute-done((bf16[128,512]{1,0:T(8,128)(2,1)S(1)}, bf16[128,512]{1,0:T(8,128)(2,1)S(1)}, u32[]{:S(2)}, u32[]{:S(2)}) %collective-permute-start) | collective-permute-done | bytes 131104 | tf_op jit(solution)/shard_map/ppermute | solution.py:314
  8.5 0.1 collective-permute-start.1
  8.6 0.0 copy-start.5
  8.6 0.6 copy-done.5
  9.2 0.7 copy-done.10
  9.9 1.1 %shard_map.128 = s32[8,128]{1,0:T(8,128)} custom-call(s32[8]{0:T(128)S(1)} %copy-done.5, s32[8]{0:T(128)S(1)} %copy-done.10), custom_call_target="tpu_custom_call" | custom-call | bytes 64 | tf_op jit(solution)/shard_map/pallas_call | solution.py:24
  11.0 6.0 %all-to-all-start = ((s32[8,1,128]{2,1,0:T(1,128)}), s32[8,1,128]{2,1,0:T(1,128)S(1)}, u32[]{:S(2)}, u32[]{:S(2)}) async-start(s32[8,1,128]{2,1,0:T(1,128)} %bitcast.1), calls=%async_computation | async-start | bytes 8192 | tf_op jit(solution)/shard_map/all_to_all | solution.py:325
  17.1 0.1 stack.20.me_ref
  17.1 1.6 %copy-done = bf16[2,1024,512]{2,1,0:T(8,128)(2,1)S(1)} copy-done((bf16[2,1024,512]{2,1,0:T(8,128)(2,1)S(1)}, bf16[2,1024,512]{2,1,0:T(8,128)(2,1)}, u32[]{:S(2)}) %copy-start) | copy-done | bytes 2097176
  18.7 0.9 copy-done.2
  19.7 0.7 copy-done.3
  20.4 0.7 copy-done.7
  21.1 0.7 copy-done.8
  21.7 2.3 %shard_map.129 = (bf16[32,512]{1,0:T(8,128)(2,1)S(1)}, f32[64,512]{1,0:T(8,128)S(1)}, f32[32,512]{1,0:T(8,128)S(1)}, f32[64,512]{1,0:T(8,128)S(1)}, f32[32,512]{...) custom-call(s32[8]{0:T(128)S(1)} %copy-done.8, ...), custom_call_target="tpu_custom_call" | custom-call | flops 100663296 | bytes 2367540 | tf_op jit(solution)/shard_map/pallas_call | solution.py:24
  24.1 0.0 all-to-all-done
  24.1 0.0 collective-permute-done.1.other_ref
  24.1 0.7 shard_map.130
  24.7 13.1 %all_to_all.21.slots_ref = bf16[8,16,512]{2,1,0:T(8,128)(2,1)S(1)} all-to-all(bf16[8,16,512]{2,1,0:T(8,128)(2,1)S(1)} %shard_map.130), channel_id=1, replica_groups=mesh['dp'=8,'mp'=4] {'dp'}, dimensions={0} | all-to-all | bytes 262144 | tf_op jit(solution)/shard_map/all_to_all | solution.py:364
  37.9 0.7 shard_map.131
  38.6 1.6 %collective-permute-start.2 = (bf16[128,512]{1,0:T(8,128)(2,1)S(1)}, bf16[128,512]{1,0:T(8,128)(2,1)S(1)}, u32[]{:S(2)}, u32[]{:S(2)}) collective-permute-start(bf16[128,512]{1,0:T(8,128)(2,1)S(1)} %shard_map.131), channel_id=1, source_target_pairs={{0,2},{1,3},{2,0},{3,1},{4,6},{5,7},{6,4},{7,5},{8,10},{9,11},{10,... | collective-permute-start | bytes 393224 | tf_op jit(solution)/shard_map/ppermute | solution.py:314
  40.2 1.1 %shard_map.133.grad_ref.refs_0_ = bf16[112,512]{1,0:T(8,128)(2,1)S(1)} custom-call(s32[8]{0:T(128)S(1)} %copy-done.6, bf16[8,16,512]{2,1,0:T(8,128)(2,1)S(1)} %all_to_all.21.slots_ref, f32[64,512]{1,0:T(8,128)S(1)} %get-tuple-element.23.slope1_ref, f32[32,512]{1,0:T(8,128)S(1)} %get-tuple-element.24.slope2_ref, f32[64,512]{1,0:T(8,128)S(1)} %get-tuple-element.25.hat1_ref, ...), custom_call_target="tpu_custom_call" | custom-call | flops 33554432 | bytes 2674720 | tf_op jit(solution)/shard_map/pallas_call | solution.py:24
  41.3 0.6 collective-permute-start.5
  41.9 3.0 %collective-permute-done.2 = bf16[128,512]{1,0:T(8,128)(2,1)S(1)} collective-permute-done((bf16[128,512]{1,0:T(8,128)(2,1)S(1)}, bf16[128,512]{1,0:T(8,128)(2,1)S(1)}, u32[]{:S(2)}, u32[]{:S(2)}) %collective-permute-start.2) | collective-permute-done | bytes 131104 | tf_op jit(solution)/shard_map/ppermute | solution.py:314
  44.9 0.1 collective-permute-start.3
  44.9 0.5 collective-permute-start.4
  45.4 0.7 collective-permute-done.5.refs_2_
  46.1 0.0 collective-permute-start.6
  46.1 0.5 collective-permute-start.7
  46.6 0.5 collective-permute-start.8
  47.2 0.0 collective-permute-done.3.other_ref
  47.2 0.8 collective-permute-start.9
  48.0 1.2 %copy.18.weight_ref = bf16[512,320]{1,0:T(8,128)(2,1)S(1)} copy(bf16[512,320]{0,1:T(8,128)(2,1)} %param.16) | data formatting | bytes 655360 | tf_op args[7]
  49.2 0.2 shard_map.132
  49.4 0.0 copy-start.9
  49.5 0.0 collective-permute-done.7.refs_5_
  49.5 2.4 %collective-permute-done.8.refs_6_ = bf16[256,128]{1,0:T(8,128)(2,1)} collective-permute-done((bf16[256,128]{1,0:T(8,128)(2,1)}, bf16[256,128]{1,0:T(8,128)(2,1)}, u32[]{:S(2)}, u32[]{:S(2)}) %collective-permute-start.8) | collective-permute-done | bytes 65568 | tf_op jit(solution)/shard_map/ppermute | solution.py:314
  51.9 0.0 collective-permute-done.9.refs_7_
  51.9 2.5 %shard_map.135 = bf16[8,88,512]{2,1,0:T(8,128)(2,1)} custom-call(bf16[112,512]{1,0:T(8,128)(2,1)S(1)} %shard_map.133.grad_ref.refs_0_, bf16[112,512]{1,0:T(8,128)(2,1)S(1)} %collective-permute-done.4.refs_1_, bf16[112,512]{1,0:T(8,128)(2,1)S(1)} %collective-permute-done.5.refs_2_, bf16[112,512]{1,0:T(8,128)(2,1)S(1)} %collective-permute-done.6.refs_3_, ...), custom_call_target="tpu_custom_call" | custom-call | flops 100663296 | bytes 851968 | tf_op jit(solution)/shard_map/pallas_call | solution.py:24
  54.3 4.2 %all-to-all-start.2 = ((bf16[8,88,512]{2,1,0:T(8,128)(2,1)}), bf16[8,88,512]{2,1,0:T(8,128)(2,1)}, u32[]{:S(2)}, u32[]{:S(2)}) async-start(bf16[8,88,512]{2,1,0:T(8,128)(2,1)} %shard_map.135), calls=%async_computation.2 | async-start | bytes 1441792 | tf_op jit(solution)/shard_map/all_to_all | solution.py:410
  58.6 0.1 copy.19
  58.7 43.2 %all_gather.3.cotangent_ref = bf16[1024,320]{1,0:T(8,128)(2,1)S(1)} all-gather(bf16[128,320]{1,0:T(8,128)(2,1)S(1)} %copy.19), channel_id=1, replica_groups=mesh['dp'=8,'mp'=4] {'dp'}, dimensions={0}, use_global_device_ids=true | all-gather | bytes 737280 | tf_op jit(solution)/shard_map/all_gather | solution.py:326
  101.9 1.9 %shard_map.134 = bf16[256,512]{1,0:T(8,128)(2,1)} custom-call(s32[8]{0:T(128)S(1)} %copy-done.9, bf16[112,512]{1,0:T(8,128)(2,1)S(1)} %shard_map.133.grad_ref.refs_0_, bf16[2,1024,512]{2,1,0:T(8,128)(2,1)S(1)} %copy-done.1), custom_call_target="tpu_custom_call" | custom-call | flops 67108864 | bytes 2211872 | tf_op jit(solution)/shard_map/pallas_call | solution.py:24
  103.8 0.7 copy.20
  104.5 2.1 %shard_map.136 = (f32[2,32,512]{2,1,0:T(8,128)}, f32[2,32]{1,0:T(2,128)}, f32[64,320]{1,0:T(8,128)}) custom-call(s32[5]{0:T(128)S(1)} %stack.20.me_ref, bf16[8,88,512]{2,1,0:T(8,128)(2,1)} %all-to-all-done.2.slots_ref, bf16[1024,320]{1,0:T(8,128)(2,1)S(1)} %all_gather.3.cotangent_ref), custom_call_target="tpu_custom_call" | custom-call | bytes 1376276 | tf_op jit(solution)/shard_map/pallas_call | solution.py:24
  (18 shorter events, 0.1 us)
Async XLA Ops:
  0.6 23.4 %copy-start.6 = (s32[8]{0:T(128)S(1)}, s32[8]{0:T(128)}, u32[]{:S(2)}) copy-start(s32[8]{0:T(128)} %dests_ref.5) | copy-start | bytes 100
  0.6 39.5 %copy-start.4 = (f32[2,512]{1,0:T(2,128)S(1)}, f32[2,512]{1,0:T(2,128)}, u32[]{:S(2)}) copy-start(f32[2,512]{1,0:T(2,128)} %gain_ref.3) | copy-start | bytes 12292
  1.9 6.5 %collective-permute-start = (bf16[128,512]{1,0:T(8,128)(2,1)S(1)}, bf16[128,512]{1,0:T(8,128)(2,1)S(1)}, u32[]{:S(2)}, u32[]{:S(2)}) collective-permute-start(bf16[128,512]{1,0:T(8,128)(2,1)S(1)} %convolution_convert_fusion), channel_id=1, source_target_pairs={{0,2},{1,3},{2,0},{3,1},{4,6},{5,7},{6,4},{7,5},{8,10},{9,11},{10,... | collective-permute-start | bytes 393224 | tf_op jit(solution)/shard_map/ppermute | solution.py:314
  8.5 15.6 %collective-permute-start.1 = (bf16[128,512]{1,0:T(8,128)(2,1)S(1)}, bf16[128,512]{1,0:T(8,128)(2,1)S(1)}, u32[]{:S(2)}, u32[]{:S(2)}) collective-permute-start(bf16[128,512]{1,0:T(8,128)(2,1)S(1)} %add_convert_fusion.mine_ref), channel_id=1, source_target_pairs={{0,1},{1,0},{2,3},{3,2},{4,5},{5,4},{6,7},{7,6},{8,9},{9,8},{10,11... | collective-permute-start | bytes 393224 | tf_op jit(solution)/shard_map/ppermute | solution.py:314
  8.6 0.7 copy-start.5
  9.2 0.7 copy-start.10
  11.0 13.0 %all-to-all-start = ((s32[8,1,128]{2,1,0:T(1,128)}), s32[8,1,128]{2,1,0:T(1,128)S(1)}, u32[]{:S(2)}, u32[]{:S(2)}) async-start(s32[8,1,128]{2,1,0:T(1,128)} %bitcast.1), calls=%async_computation | async-start | bytes 8192 | tf_op jit(solution)/shard_map/all_to_all | solution.py:325
  17.1 1.6 %copy-start = (bf16[2,1024,512]{2,1,0:T(8,128)(2,1)S(1)}, bf16[2,1024,512]{2,1,0:T(8,128)(2,1)}, u32[]{:S(2)}) copy-start(bf16[2,1024,512]{2,1,0:T(8,128)(2,1)} %weight_ref.6) | copy-start | bytes 6291460
  18.7 0.9 copy-start.2
  19.7 0.7 copy-start.3
  20.4 0.7 copy-start.7
  21.1 0.7 copy-start.8
  21.7 18.5 %copy-start.1 = (bf16[2,1024,512]{2,1,0:T(8,128)(2,1)S(1)}, bf16[2,1024,512]{2,1,0:T(8,128)(2,1)}, u32[]{:S(2)}) copy-start(bf16[2,1024,512]{2,1,0:T(8,128)(2,1)} %weight_ref.6) | copy-start | bytes 6291460
  38.6 6.2 %collective-permute-start.2 = (bf16[128,512]{1,0:T(8,128)(2,1)S(1)}, bf16[128,512]{1,0:T(8,128)(2,1)S(1)}, u32[]{:S(2)}, u32[]{:S(2)}) collective-permute-start(bf16[128,512]{1,0:T(8,128)(2,1)S(1)} %shard_map.131), channel_id=1, source_target_pairs={{0,2},{1,3},{2,0},{3,1},{4,6},{5,7},{6,4},{7,5},{8,10},{9,11},{10,... | collective-permute-start | bytes 393224 | tf_op jit(solution)/shard_map/ppermute | solution.py:314
  41.3 4.9 %collective-permute-start.5 = (bf16[112,512]{1,0:T(8,128)(2,1)S(1)}, bf16[112,512]{1,0:T(8,128)(2,1)S(1)}, u32[]{:S(2)}, u32[]{:S(2)}) collective-permute-start(bf16[112,512]{1,0:T(8,128)(2,1)S(1)} %shard_map.133.grad_ref.refs_0_), channel_id=1, source_target_pairs={{0,2},{1,3},{2,0},{3,1},{4,6},{5,7},{6,4},{7,5},{8,10},{9,11},{10,... | collective-permute-start | bytes 344072 | tf_op jit(solution)/shard_map/ppermute | solution.py:314
  44.9 2.3 %collective-permute-start.3 = (bf16[128,512]{1,0:T(8,128)(2,1)S(1)}, bf16[128,512]{1,0:T(8,128)(2,1)S(1)}, u32[]{:S(2)}, u32[]{:S(2)}) collective-permute-start(bf16[128,512]{1,0:T(8,128)(2,1)S(1)} %add.7.mine_ref), channel_id=1, source_target_pairs={{0,1},{1,0},{2,3},{3,2},{4,5},{5,4},{6,7},{7,6},{8,9},{9,8},{10,11... | collective-permute-start | bytes 393224 | tf_op jit(solution)/shard_map/ppermute | solution.py:314
  44.9 6.9 %collective-permute-start.4 = (bf16[112,512]{1,0:T(8,128)(2,1)S(1)}, bf16[112,512]{1,0:T(8,128)(2,1)S(1)}, u32[]{:S(2)}, u32[]{:S(2)}) collective-permute-start(bf16[112,512]{1,0:T(8,128)(2,1)S(1)} %shard_map.133.grad_ref.refs_0_), channel_id=1, source_target_pairs={{0,1},{1,0},{2,3},{3,2},{4,5},{5,4},{6,7},{7,6},{8,9},{9,8},{10,11... | collective-permute-start | bytes 344072 | tf_op jit(solution)/shard_map/ppermute | solution.py:314
  46.1 5.7 %collective-permute-start.6 = (bf16[112,512]{1,0:T(8,128)(2,1)S(1)}, bf16[112,512]{1,0:T(8,128)(2,1)S(1)}, u32[]{:S(2)}, u32[]{:S(2)}) collective-permute-start(bf16[112,512]{1,0:T(8,128)(2,1)S(1)} %collective-permute-done.5.refs_2_), channel_id=1, source_target_pairs={{0,1},{1,0},{2,3},{3,2},{4,5},{5,4},{6,7},{7,6},{8,9},{9,8},{10,11... | collective-permute-start | bytes 344072 | tf_op jit(solution)/shard_map/ppermute | solution.py:314
  46.1 3.3 %collective-permute-start.7 = (bf16[256,128]{1,0:T(8,128)(2,1)}, bf16[256,128]{1,0:T(8,128)(2,1)}, u32[]{:S(2)}, u32[]{:S(2)}) collective-permute-start(bf16[256,128]{1,0:T(8,128)(2,1)} %get-tuple-element.30), channel_id=1, source_target_pairs={{0,1},{1,0},{2,3},{3,2},{4,5},{5,4},{6,7},{7,6},{8,9},{9,8},{10,11... | collective-permute-start | bytes 196616 | tf_op jit(solution)/shard_map/ppermute | solution.py:314
  46.6 5.2 %collective-permute-start.8 = (bf16[256,128]{1,0:T(8,128)(2,1)}, bf16[256,128]{1,0:T(8,128)(2,1)}, u32[]{:S(2)}, u32[]{:S(2)}) collective-permute-start(bf16[256,128]{1,0:T(8,128)(2,1)} %get-tuple-element.31), channel_id=1, source_target_pairs={{0,2},{1,3},{2,0},{3,1},{4,6},{5,7},{6,4},{7,5},{8,10},{9,11},{10,... | collective-permute-start | bytes 196616 | tf_op jit(solution)/shard_map/ppermute | solution.py:314
  47.2 11.4 %copy-start.11 = (bf16[128,320]{0,1:T(8,128)(2,1)S(1)}, bf16[128,320]{0,1:T(8,128)(2,1)}, u32[]{:S(2)}) copy-start(bf16[128,320]{0,1:T(8,128)(2,1)} %param.17) | copy-start | bytes 245764
  47.2 4.7 %collective-permute-start.9 = (bf16[256,128]{1,0:T(8,128)(2,1)}, bf16[256,128]{1,0:T(8,128)(2,1)}, u32[]{:S(2)}, u32[]{:S(2)}) collective-permute-start(bf16[256,128]{1,0:T(8,128)(2,1)} %get-tuple-element.32), channel_id=1, source_target_pairs={{0,3},{1,2},{2,1},{3,0},{4,7},{5,6},{6,5},{7,4},{8,11},{9,10},{10,... | collective-permute-start | bytes 196616 | tf_op jit(solution)/shard_map/ppermute | solution.py:314
  49.4 52.4 %copy-start.9 = (s32[8]{0:T(128)S(1)}, s32[8]{0:T(128)}, u32[]{:S(2)}) copy-start(s32[8]{0:T(128)} %lengths_ref.3) | copy-start | bytes 100
  54.3 50.2 %all-to-all-start.2 = ((bf16[8,88,512]{2,1,0:T(8,128)(2,1)}), bf16[8,88,512]{2,1,0:T(8,128)(2,1)}, u32[]{:S(2)}, u32[]{:S(2)}) async-start(bf16[8,88,512]{2,1,0:T(8,128)(2,1)} %shard_map.135), calls=%async_computation.2 | async-start | bytes 1441792 | tf_op jit(solution)/shard_map/all_to_all | solution.py:410

commit v2 on v1

--- a/solution.py
+++ b/solution.py
@@ -82,9 +82,8 @@
 
 
 def forward_kernel(
-    lengths_ref, me_ref, feat_ref, weight_ref, gain_ref, shift_ref, *rest, pairs, frames, groups, owned
+    lengths_ref, me_ref, feat_ref, weight_ref, gain_ref, shift_ref, *rest, pairs, frames, far, near, owned
 ):
-    mp_count = me_ref.shape[0] - 1
     frames_ref, slope1_ref, slope2_ref, hat1_ref, hat2_ref, scale1_ref, scale2_ref = rest[:7]
     turned_refs, in_turned = rest[7:-1], rest[-1]
     channels = feat_ref.shape[1]
@@ -121,12 +120,13 @@
             axis=0,
         )
         in_turned[channels * tap : channels * (tap + 1), :] = stacked.T
+    at = me_ref[1]
     for k, turned_ref in enumerate(turned_refs):
-        start = me_ref[1 + k] * owned
+        start = (at ^ k) * owned
         turned_ref[...] = jnp.concatenate(
             [
-                in_turned[pl.ds(pl.multiple_of(d * mp_count * owned + start, owned), owned), :]
-                for d in range(groups)
+                in_turned[pl.ds(pl.multiple_of(z * near * owned + start, owned), owned), :]
+                for z in range(far)
             ],
             axis=0,
         ).astype(BF)
@@ -163,10 +163,26 @@
     out_ref[...] = rows32[...].astype(BF)
 
 
-def project_kernel(mine_ref, other_ref, weight_ref, packed_ref, turned_ref):
+def project_kernel(me_ref, mine_ref, other_ref, weight_ref, cotangent_ref, packed_ref, keep_ref, send_ref):
     rows32 = mine_ref[...].astype(F32) + other_ref[...].astype(F32)
     packed_ref[...] = dot(rows32.astype(BF), weight_ref[...]).astype(BF)
-    turned_ref[...] = rows32.T.astype(BF)
+    partial = dot(rows32.T.astype(BF), cotangent_ref[...])
+    each = keep_ref.shape[1]
+    for z in range(keep_ref.shape[0]):
+        low = partial[2 * z * each : (2 * z + 1) * each]
+        high = partial[(2 * z + 1) * each : (2 * z + 2) * each]
+        keep_ref[z] = jnp.where(me_ref[3] == 0, low, high)
+        send_ref[z] = jnp.where(me_ref[3] == 0, high, low).astype(BF)
+
+
+def fold_kernel(me_ref, keep_ref, got_ref, own_ref, *out_refs):
+    for f in range(keep_ref.shape[0]):
+        z = me_ref[2] ^ f
+        total = keep_ref[z] + got_ref[z].astype(F32)
+        if f == 0:
+            own_ref[...] = total
+        else:
+            out_refs[f - 1][...] = total.astype(BF)
 
 
 def norm_back(grad, slope_ref, hat_ref, scale_ref, gain):
@@ -226,10 +242,9 @@
     out_ref[...] = dot(pick, rows).astype(BF)
 
 
-def kernel_grad_kernel(*refs, n1, n2, owned, count):
-    grad_refs, in_refs, turned_ref, out_ref = refs[:count], refs[count : 2 * count], refs[-2], refs[-1]
-    channels = out_ref.shape[2]
-    groups = out_ref.shape[0]
+def kernel_grad_kernel(me_ref, *refs, n1, n2, owned, near, far):
+    grad_refs, in_refs = refs[:near], refs[near : 2 * near]
+    own_ref, out_refs, held = refs[2 * near], refs[2 * near + 1 : -1], refs[-1]
     first, second, sums = 0.0, 0.0, 0.0
     for grad_ref, in_ref in zip(grad_refs, in_refs):
         side = in_ref[...]
@@ -238,62 +253,39 @@
         tail = grad_ref[n1 + n2 :, :].astype(F32)
         sums += tail[0:4] + tail[4:8]
     high = sums.astype(BF).astype(F32)
-    low = sums - high
-    width = 2 * channels // groups
-    per_slot = channels // groups
-    across = channels // turned_ref.shape[1]
-    each = per_slot // across
-    for d in range(groups):
-        at = (d * width) % channels
-        which = (d * width) // channels
-        pieces = [
-            part[2 * layer + which : 2 * layer + which + 1, at : at + width]
-            for part in (high, low)
-            for layer in range(2)
-        ]
-        if 4 * width < channels:
-            pieces.append(jnp.zeros((1, channels - 4 * width), F32))
-        norm_row = jnp.concatenate(pieces, axis=1)
-        turned = turned_ref[d * per_slot : (d + 1) * per_slot, :].astype(F32)
-        turned = jnp.concatenate([turned[g * each : (g + 1) * each] for g in range(across)], axis=1)
-        out_ref[d] = jnp.concatenate(
-            [
-                first[d * owned : (d + 1) * owned],
-                second[d * owned : (d + 1) * owned],
-                turned,
-                norm_row,
-                jnp.zeros((7, channels), F32),
-            ],
+    for z in range(far):
+        held[z] = jnp.concatenate(
+            [first[z * owned : (z + 1) * owned], second[z * owned : (z + 1) * owned], high, sums - high],
             axis=0,
-        ).astype(BF)
-
-
-def last_kernel(me_ref, slots_ref, cotangent_ref, conv_ref, norm_ref, proj_ref, *, owned, mp_count):
-    groups, _, channels = slots_ref.shape
-    seq = cotangent_ref.shape[0] // groups
-    across = channels // seq
-    each = channels // groups // across
-    total, norms, proj = 0.0, 0.0, 0.0
-    for d in range(groups):
-        slot = slots_ref[d].astype(F32)
-        total += slot[: 2 * owned]
-        turned = slot[2 * owned : 2 * owned + each]
-        turned = jnp.concatenate([turned[:, g * seq : (g + 1) * seq] for g in range(across)], axis=0)
-        norms += slot[2 * owned + each : 2 * owned + each + 1]
-        proj += dot(turned.astype(BF), cotangent_ref[d * seq : (d + 1) * seq, :])
+        )
+    own_ref[...] = held[me_ref[2]]
+    for f in range(1, far):
+        out_refs[f - 1][...] = held[me_ref[2] ^ f].astype(BF)
+
+
+def last_kernel(me_ref, *refs, owned, far):
+    conv_in, proj_in = refs[:far], refs[far : 2 * far]
+    conv_ref, norm_ref, proj_ref = refs[2 * far :]
+    total = conv_in[0][...]
+    proj = proj_in[0][...]
+    for f in range(1, far):
+        total += conv_in[f][...].astype(F32)
+        proj += proj_in[f][...].astype(F32)
     conv_ref[0] = total[:owned]
-    conv_ref[1] = total[owned:]
+    conv_ref[1] = total[owned : 2 * owned]
     proj_ref[...] = proj
-    width = mp_count * owned
-    rows = []
-    for layer in range(2):
-        line = norms[:, layer * width : (layer + 1) * width]
-        line = line + norms[:, (2 + layer) * width : (3 + layer) * width]
-        mine = jnp.zeros((1, owned), F32)
-        for m in range(mp_count):
-            mine = jnp.where(me_ref[0] == m, line[:, m * owned : (m + 1) * owned], mine)
-        rows.append(mine)
-    norm_ref[...] = jnp.concatenate(rows, axis=0)
+    channels = total.shape[1]
+    sums = total[2 * owned : 2 * owned + 4] + total[2 * owned + 4 : 2 * owned + 8]
+    start = me_ref[0] * owned
+    later = start >= channels
+    lines = jnp.concatenate(
+        [jnp.where(later, sums[2 * k + 1 : 2 * k + 2], sums[2 * k : 2 * k + 1]) for k in range(2)]
+        + [jnp.zeros((6, channels), F32)],
+        axis=0,
+    )
+    start = jnp.where(later, start - channels, start)
+    lines = pltpu.roll(lines, lax.rem(channels - start, channels), 1)
+    norm_ref[...] = lines[:2, :owned]
 
 
 def local(
@@ -308,13 +300,17 @@
     width = grad_packed.shape[1]
     owned = 2 * channels // (dp_count * mp_count)
     n1, n2 = 2 * pairs * frames, pairs * frames
+    near, far = 2 * mp_count, dp_count // 2
+    everyone = ("dp", "mp")
+
+    def swap(x, mask):
+        return lax.ppermute(x, everyone, [(i, i ^ mask) for i in range(dp_count * mp_count)])
+
     bits = [1 << b for b in range(mp_count.bit_length() - 1)][::-1]
-
-    def swap(x, mask):
-        return lax.ppermute(x, "mp", [(i, i ^ mask) for i in range(mp_count)])
-
-    me = lax.axis_index("mp").astype(jnp.int32)
-    me_all = jnp.stack([me] + [me ^ k for k in range(mp_count)])
+    at_dp = lax.axis_index("dp").astype(jnp.int32)
+    at_mp = lax.axis_index("mp").astype(jnp.int32)
+    x_bit = at_dp & 1
+    me = jnp.stack([at_dp * mp_count + at_mp, x_bit * mp_count + at_mp, at_dp >> 1, x_bit])
 
     index = call(
         functools.partial(index_kernel, pairs=pairs, frames=frames),
@@ -323,19 +319,14 @@
         scalars=2,
     )
     got_index = lax.all_to_all(index, "dp", split_axis=0, concat_axis=0, tiled=True)
-    all_cotangent = lax.all_gather(grad_packed, "dp", tiled=True)
-
-    grad_rows = lax.dot_general(
-        grad_packed, proj_weight, (((1,), (1,)), ((), ())), preferred_element_type=F32
-    ).astype(BF)
-    for mask in bits[:-1]:
-        grad_rows = (grad_rows.astype(F32) + swap(grad_rows, mask).astype(F32)).astype(BF)
-    other_rows = swap(grad_rows, bits[-1])
+    index, cotangent = lax.optimization_barrier((index, grad_packed))
 
     wide = -(-(n1 + n2) // 128) * 128
     feat = features.reshape(utt_count * positions, channels)
     made = call(
-        functools.partial(forward_kernel, pairs=pairs, frames=frames, groups=dp_count, owned=owned),
+        functools.partial(
+            forward_kernel, pairs=pairs, frames=frames, far=far, near=near, owned=owned
+        ),
         [
             shape(n2, channels),
             shape(n1, channels, kind=F32),
@@ -345,14 +336,21 @@
             shape(n1, 128, kind=F32),
             shape(n2, 128, kind=F32),
         ]
-        + [shape(dp_count * owned, wide)] * mp_count,
-        (lengths, me_all, feat, conv_weight, norm_gain, norm_shift),
+        + [shape(far * owned, wide)] * near,
+        (lengths, me, feat, conv_weight, norm_gain, norm_shift),
         scalars=2,
         flops=2 * (n1 + n2) * 2 * channels * channels,
         scratch=[pltpu.VMEM((2 * channels, wide), F32)],
     )
     pair_frames, slope1, slope2, hat1, hat2, scale1, scale2 = made[:7]
     in_sides = [side if k == 0 else swap(side, k) for k, side in enumerate(made[7:])]
+
+    grad_rows = lax.dot_general(
+        cotangent, proj_weight, (((1,), (1,)), ((), ())), preferred_element_type=F32
+    ).astype(BF)
+    for mask in bits[:-1]:
+        grad_rows = (grad_rows.astype(F32) + swap(grad_rows, mask).astype(F32)).astype(BF)
+    other_rows = swap(grad_rows, bits[-1])
 
     sent = call(
         functools.partial(send_kernel, pairs=pairs, frames=frames),
@@ -362,6 +360,7 @@
         scratch=[pltpu.VMEM((seq, channels), F32)],
     )
     slots = lax.all_to_all(sent, "dp", split_axis=0, concat_axis=0, tiled=True)
+    slots, *in_sides = lax.optimization_barrier((slots, *in_sides))
 
     grads = call(
         functools.partial(back_kernel, pairs=pairs, frames=frames),
@@ -371,10 +370,9 @@
         flops=2 * n2 * 2 * channels * channels,
         scratch=[pltpu.VMEM((n2, channels), F32)],
     )
-    by_mask = {0: grads}
-    for mask in bits:
-        for known in list(by_mask):
-            by_mask[known ^ mask] = swap(by_mask[known], mask)
+    by_mask = {mask: swap(grads, mask) if mask else grads for mask in range(0, near, 2)}
+    for mask in range(0, near, 2):
+        by_mask[mask + 1] = swap(by_mask[mask], 1)
 
     placed = call(
         functools.partial(place_kernel, frames=frames),
@@ -385,11 +383,23 @@
     )
     for mask in bits[:-1]:
         placed = placed + swap(placed, mask)
-    packed, turned = call(
+    per_dp = channels // dp_count
+    packed, keep, send = call(
         project_kernel,
-        [shape(seq, width), shape(channels, seq)],
-        (placed, swap(placed, bits[-1]), proj_weight),
-        flops=2 * seq * channels * width,
+        [
+            shape(seq, width),
+            shape(far, per_dp, width, kind=F32),
+            shape(far, per_dp, width),
+        ],
+        (me, placed, swap(placed, bits[-1]), proj_weight, grad_packed),
+        scalars=1,
+        flops=4 * seq * channels * width,
+    )
+    proj_parts = call(
+        fold_kernel,
+        [shape(per_dp, width, kind=F32)] + [shape(per_dp, width)] * (far - 1),
+        (me, keep, swap(send, mp_count)),
+        scalars=1,
     )
 
     grad_features = call(
@@ -400,22 +410,24 @@
         flops=2 * n1 * 2 * channels * channels,
     ).reshape(utt_count, positions, channels)
 
-    per_slot = channels // dp_count * seq // channels
-    partial = call(
-        functools.partial(kernel_grad_kernel, n1=n1, n2=n2, owned=owned, count=mp_count),
-        shape(dp_count, 2 * owned + per_slot + 8, channels),
-        tuple(by_mask[k] for k in range(mp_count)) + tuple(in_sides) + (turned,),
+    conv_parts = call(
+        functools.partial(kernel_grad_kernel, n1=n1, n2=n2, owned=owned, near=near, far=far),
+        [shape(2 * owned + 8, channels, kind=F32)] + [shape(2 * owned + 8, channels)] * (far - 1),
+        (me,) + tuple(by_mask[k] for k in range(near)) + tuple(in_sides),
+        scalars=1,
         flops=2 * (n1 + n2) * 2 * channels * channels,
-    )
-    arrived = lax.all_to_all(partial, "dp", split_axis=0, concat_axis=0, tiled=True)
+        scratch=[pltpu.VMEM((far, 2 * owned + 8, channels), F32)],
+    )
+    conv_got = [swap(part, near * f) if f else part for f, part in enumerate(conv_parts)]
+    proj_got = [swap(part, near * f) if f else part for f, part in enumerate(proj_parts)]
     grad_conv, grad_norm, grad_proj = call(
-        functools.partial(last_kernel, owned=owned, mp_count=mp_count),
+        functools.partial(last_kernel, owned=owned, far=far),
         [
             shape(2, owned, channels, kind=F32),
             shape(2, owned, kind=F32),
-            shape(channels // dp_count, width, kind=F32),
+            shape(per_dp, width, kind=F32),
         ],
-        (me_all, arrived, all_cotangent),
+        (me, *conv_got, *proj_got),
         scalars=1,
     )
     return (packed, grad_features, grad_conv, grad_norm, grad_proj)

time: 107 us -> 84.2 us (0.79)
  blocking collectives: 56.3 us -> 0 us
  starting transfers between devices: 17.9 us -> 36.1 us
  local copies, waits for them, and re-layouts: 8.04 us -> 18.6 us
  waiting for transfers between devices: 9.59 us -> 13.3 us
    all_gather x1 -> x0, blocking collectives: 43.2 us -> none  [local(): all_cotangent = lax.all_gather(grad_packed, 'dp', tiled=True)]
    ppermute x10 -> x25, starting transfers between devices: 7.69 us -> 24.1 us  [swap(): lax.ppermute(x, everyone, [(i, i ^ mask) for i in range(dp_count * mp_cou...]
    all_to_all x1 -> x0, blocking collectives: 13.1 us -> none  [local(): slots = lax.all_to_all(sent, 'dp', split_axis=0, concat_axis=0, tiled=True)]
    unnamed x27 -> x61, local copies, waits for them, and re-layouts: 7.96 us -> 18.6 us
    ppermute x10 -> x25, waiting for transfers between devices: 9.58 us -> 13.3 us  [swap(): lax.ppermute(x, everyone, [(i, i ^ mask) for i in range(dp_count * mp_cou...]
    all_to_all x1, starting transfers between devices: 4.21 us -> 6 us  [local(): slots = lax.all_to_all(sent, 'dp', split_axis=0, concat_axis=0, tiled=True)]
    pallas_call x9 -> x10, Pallas kernels: 12.6 us -> 12.9 us  [call(): pl.pallas_call(body, out_shape=out, in_specs=specs, out_specs=[pl.BlockSp...]
  transfers between devices with their start and end apart: 12 -> 27, of which waited for: 4 -> 8; matrix products, arithmetic and copies ran while one was open for 2% -> 4% of each run, Pallas kernels for 6% -> 10%
where the time goes in v2:
time: 84.2 us; the launch traced here: 83.1 us
  starting transfers between devices  36.1 us (43%)
  local copies, waits for them, and re-layouts  18.6 us (22%)
  waiting for transfers between devices  13.3 us (16%)
  Pallas kernels  12.9 us (15%)
  matrix products  1.27 us (2%)
  between operations  0.85 us (1%)
    ppermute x25, starting transfers between devices, swap(): lax.ppermute(x, everyone, [(i, i ^ mask) for i in range(dp_count * mp_cou...  24.1 us
    unnamed x61, local copies, waits for them, and re-layouts  18.6 us
    ppermute x25, waiting for transfers between devices, swap(): lax.ppermute(x, everyone, [(i, i ^ mask) for i in range(dp_count * mp_cou...  13.3 us
    pallas_call x10, Pallas kernels, call(): pl.pallas_call(body, out_shape=out, in_specs=specs, out_specs=[pl.BlockSp...  12.9 us
    all_to_all x1, starting transfers between devices, local(): lax.all_to_all(index, 'dp', split_axis=0, concat_axis=0, tiled=True)  6.04 us
    all_to_all x1, starting transfers between devices, local(): slots = lax.all_to_all(sent, 'dp', split_axis=0, concat_axis=0, tiled=True)  6 us
  transfers between devices with their start and end apart: 27, of which 8 were waited for; matrix products, arithmetic and copies ran while one was open for 4% of the time, Pallas kernels for 10%

profile of v2, /device:TPU:0, one launch (start us, length us, event | category | flops | bytes accessed | tf_op | source)
XLA Modules:
  0.0 83.1 jit_solution(16618195868503284789)
XLA Ops:
  0.6 0.6 copy-done.23
  1.3 0.7 copy-done.28
  1.9 1.1 %shard_map.128 = s32[8,128]{1,0:T(8,128)} custom-call(s32[8]{0:T(128)S(1)} %copy-done.23, s32[8]{0:T(128)S(1)} %copy-done.28), custom_call_target="tpu_custom_call" | custom-call | bytes 64 | tf_op jit(solution)/shard_map/pallas_call | solution.py:24
  3.1 1.3 %convolution_convert_fusion = bf16[128,512]{1,0:T(8,128)(2,1)S(1)} fusion(bf16[128,320]{0,1:T(8,128)(2,1)} %param.17, bf16[512,320]{0,1:T(8,128)(2,1)} %param.16), kind=kOutput, calls=%fused_computation | convolution fusion | flops 42008576 | bytes 540672 | tf_op jit(solution)/shard_map/dot_general | solution.py:348
  4.4 3.0 %collective-permute-start = (bf16[128,512]{1,0:T(8,128)(2,1)S(1)}, bf16[128,512]{1,0:T(8,128)(2,1)S(1)}, u32[]{:S(2)}, u32[]{:S(2)}) collective-permute-start(bf16[128,512]{1,0:T(8,128)(2,1)S(1)} %convolution_convert_fusion), channel_id=1, source_target_pairs={{0,2},{1,3},{2,0},{3,1},{4,6},{5,7},{6,4},{7,5},{8,10},{9,11},{10,... | collective-permute-start | bytes 393224 | tf_op jit(solution)/shard_map/ppermute | solution.py:307
  7.4 3.5 %collective-permute-done = bf16[128,512]{1,0:T(8,128)(2,1)S(1)} collective-permute-done((bf16[128,512]{1,0:T(8,128)(2,1)S(1)}, bf16[128,512]{1,0:T(8,128)(2,1)S(1)}, u32[]{:S(2)}, u32[]{:S(2)}) %collective-permute-start) | collective-permute-done | bytes 131104 | tf_op jit(solution)/shard_map/ppermute | solution.py:307
  11.0 6.0 %all-to-all-start = ((s32[8,1,128]{2,1,0:T(1,128)}), s32[8,1,128]{2,1,0:T(1,128)S(1)}, u32[]{:S(2)}, u32[]{:S(2)}) async-start(s32[8,1,128]{2,1,0:T(1,128)} %bitcast.5), calls=%async_computation | async-start | bytes 8192 | tf_op jit(solution)/shard_map/all_to_all | solution.py:321
  17.1 1.6 %copy-done = bf16[2,1024,512]{2,1,0:T(8,128)(2,1)S(1)} copy-done((bf16[2,1024,512]{2,1,0:T(8,128)(2,1)S(1)}, bf16[2,1024,512]{2,1,0:T(8,128)(2,1)}, u32[]{:S(2)}) %copy-start) | copy-done | bytes 2097176
  18.7 0.9 %copy-done.2 = bf16[8,32,512]{2,1,0:T(8,128)(2,1)S(1)} copy-done((bf16[8,32,512]{2,1,0:T(8,128)(2,1)S(1)}, bf16[8,32,512]{2,1,0:T(8,128)(2,1)}, u32[]{:S(2)}) %copy-start.2) | copy-done | bytes 262168
  19.7 0.7 copy-done.21
  20.4 0.7 copy-done.25
  21.1 0.7 copy-done.26
  21.7 1.7 %shard_map.129 = (bf16[32,512]{1,0:T(8,128)(2,1)S(1)}, f32[64,512]{1,0:T(8,128)S(1)}, f32[32,512]{1,0:T(8,128)S(1)}, f32[64,512]{1,0:T(8,128)S(1)}, f32[32,512]{...) custom-call(s32[8]{0:T(128)S(1)} %copy-done.26, ...), custom_call_target="tpu_custom_call" | custom-call | flops 100663296 | bytes 2367536 | tf_op jit(solution)/shard_map/pallas_call | solution.py:24
  24.0 1.3 %shard_map.130 = bf16[8,16,512]{2,1,0:T(8,128)(2,1)} custom-call(s32[8,128]{1,0:T(8,128)S(1)} %bitcast.13, s32[8]{0:T(128)S(1)} %copy-done.24, bf16[128,512]{1,0:T(8,128)(2,1)S(1)} %add_convert_fusion.mine_ref, bf16[128,512]{1,0:T(8,128)(2,1)S(1)} %collective-permute-done.1.other_ref, bf16[32,512]{1,0:T(8,128)(2,1)S(1)} %get-tuple-element.45.frames_ref), custom_call_target="tpu_custom_call" | custom-call | bytes 299040 | tf_op jit(solution)/shard_map/pallas_call | solution.py:24
  25.3 6.0 %all-to-all-start.1 = ((bf16[8,16,512]{2,1,0:T(8,128)(2,1)}), bf16[8,16,512]{2,1,0:T(8,128)(2,1)S(1)}, u32[]{:S(2)}, u32[]{:S(2)}) async-start(bf16[8,16,512]{2,1,0:T(8,128)(2,1)} %shard_map.130), calls=%async_computation.1 | async-start | bytes 262144 | tf_op jit(solution)/shard_map/all_to_all | solution.py:362
  31.4 1.6 %collective-permute-start.3 = (bf16[128,128]{1,0:T(8,128)(2,1)S(1)}, bf16[128,128]{1,0:T(8,128)(2,1)S(1)}, u32[]{:S(2)}, u32[]{:S(2)}) collective-permute-start(bf16[128,128]{1,0:T(8,128)(2,1)S(1)} %get-tuple-element.48), channel_id=1, source_target_pairs={{0,2},{1,3},{2,0},{3,1},{4,6},{5,7},{6,4},{7,5},{8,10},{9,11},{10,... | collective-permute-start | bytes 98312 | tf_op jit(solution)/shard_map/ppermute | solution.py:307
  33.2 2.0 %collective-permute-start.5 = (bf16[128,128]{1,0:T(8,128)(2,1)S(1)}, bf16[128,128]{1,0:T(8,128)(2,1)S(1)}, u32[]{:S(2)}, u32[]{:S(2)}) collective-permute-start(bf16[128,128]{1,0:T(8,128)(2,1)S(1)} %get-tuple-element.50), channel_id=1, source_target_pairs={{0,4},{1,5},{2,6},{3,7},{4,0},{5,1},{6,2},{7,3},{8,12},{9,13},{10,... | collective-permute-start | bytes 98312 | tf_op jit(solution)/shard_map/ppermute | solution.py:307
  35.2 2.6 %collective-permute-start.7 = (bf16[128,128]{1,0:T(8,128)(2,1)S(1)}, bf16[128,128]{1,0:T(8,128)(2,1)S(1)}, u32[]{:S(2)}, u32[]{:S(2)}) collective-permute-start(bf16[128,128]{1,0:T(8,128)(2,1)S(1)} %get-tuple-element.52), channel_id=1, source_target_pairs={{0,6},{1,7},{2,4},{3,5},{4,2},{5,3},{6,0},{7,1},{8,14},{9,15},{10,... | collective-permute-start | bytes 98312 | tf_op jit(solution)/shard_map/ppermute | solution.py:307
  39.5 1.2 %collective-permute-done.7.refs_14_ = bf16[128,128]{1,0:T(8,128)(2,1)S(1)} collective-permute-done((bf16[128,128]{1,0:T(8,128)(2,1)S(1)}, bf16[128,128]{1,0:T(8,128)(2,1)S(1)}, u32[]{:S(2)}, u32[]{:S(2)}) %collective-permute-start.7) | collective-permute-done | bytes 32800 | tf_op jit(solution)/shard_map/ppermute | solution.py:307
  41.4 0.7 collective-permute-done.8.refs_15_
  42.7 0.7 shard_map.131
  44.0 1.1 %shard_map.133.grad_ref.refs_0_ = bf16[112,512]{1,0:T(8,128)(2,1)S(1)} custom-call(s32[8]{0:T(128)S(1)} %copy-done.24, bf16[8,16,512]{2,1,0:T(8,128)(2,1)S(1)} %all-to-all-done.1.slots_ref, f32[64,512]{1,0:T(8,128)S(1)} %get-tuple-element.56.slope1_ref, f32[32,512]{1,0:T(8,128)S(1)} %get-tuple-element.57.slope2_ref, ...), custom_call_target="tpu_custom_call" | custom-call | flops 33554432 | bytes 2674720 | tf_op jit(solution)/shard_map/pallas_call | solution.py:24
  45.1 1.8 %collective-permute-start.16 = (bf16[112,512]{1,0:T(8,128)(2,1)S(1)}, bf16[112,512]{1,0:T(8,128)(2,1)S(1)}, u32[]{:S(2)}, u32[]{:S(2)}) collective-permute-start(bf16[112,512]{1,0:T(8,128)(2,1)S(1)} %shard_map.133.grad_ref.refs_0_), channel_id=1, source_target_pairs={{0,6},{1,7},{2,4},{3,5},{4,2},{5,3},{6,0},{7,1},{8,14},{9,15},{10,... | collective-permute-start | bytes 344072 | tf_op jit(solution)/shard_map/ppermute | solution.py:307
  46.9 1.2 %collective-permute-start.14 = (bf16[112,512]{1,0:T(8,128)(2,1)S(1)}, bf16[112,512]{1,0:T(8,128)(2,1)S(1)}, u32[]{:S(2)}, u32[]{:S(2)}) collective-permute-start(bf16[112,512]{1,0:T(8,128)(2,1)S(1)} %shard_map.133.grad_ref.refs_0_), channel_id=1, source_target_pairs={{0,4},{1,5},{2,6},{3,7},{4,0},{5,1},{6,2},{7,3},{8,12},{9,13},{10,... | collective-permute-start | bytes 344072 | tf_op jit(solution)/shard_map/ppermute | solution.py:307
  48.6 3.0 %collective-permute-done.9 = bf16[128,512]{1,0:T(8,128)(2,1)S(1)} collective-permute-done((bf16[128,512]{1,0:T(8,128)(2,1)S(1)}, bf16[128,512]{1,0:T(8,128)(2,1)S(1)}, u32[]{:S(2)}, u32[]{:S(2)}) %collective-permute-start.9) | collective-permute-done | bytes 131104 | tf_op jit(solution)/shard_map/ppermute | solution.py:307
  52.3 1.2 %collective-permute-done.14.refs_4_ = bf16[112,512]{1,0:T(8,128)(2,1)S(1)} collective-permute-done((bf16[112,512]{1,0:T(8,128)(2,1)S(1)}, bf16[112,512]{1,0:T(8,128)(2,1)S(1)}, u32[]{:S(2)}, u32[]{:S(2)}) %collective-permute-start.14) | collective-permute-done | bytes 114720 | tf_op jit(solution)/shard_map/ppermute | solution.py:307
  54.1 1.0 %copy.19.cotangent_ref = bf16[128,320]{1,0:T(8,128)(2,1)S(1)} copy(bf16[128,320]{0,1:T(8,128)(2,1)} %param.17) | data formatting | bytes 163840 | tf_op args[8]
  55.1 1.2 %copy.18.weight_ref = bf16[512,320]{1,0:T(8,128)(2,1)S(1)} copy(bf16[512,320]{0,1:T(8,128)(2,1)} %param.16) | data formatting | bytes 655360 | tf_op args[7]
  56.3 0.9 %shard_map.132 = (bf16[128,320]{1,0:T(8,128)(2,1)S(1)}, f32[4,64,320]{2,1,0:T(8,128)S(1)}, bf16[4,64,320]{2,1,0:T(8,128)(2,1)S(1)}) custom-call(s32[4]{0:T(128)S(1)} %pad_add_fusion.me_ref, bf16[128,512]{1,0:T(8,128)(2,1)S(1)} %add.15.mine_ref, bf16[128,512]{1,0:T(8,128)(2,1)S(1)} %collective-permute-done.10.other_ref, ...), custom_call_target="tpu_custom_call" | custom-call | flops 83886080 | bytes 671760 | tf_op jit(solution)/shard_map/pallas_call | solution.py:24
  57.8 0.7 collective-permute-start.21
  58.5 0.7 copy-done.6
  59.3 0.8 copy-done.8
  60.0 0.8 copy-done.10
  60.8 0.8 copy-done.12
  61.5 0.8 copy-done.14
  62.3 0.8 copy-done.16
  63.1 0.8 copy-done.18
  63.8 0.8 copy-done.20
  64.6 2.3 %shard_map.135 = (f32[72,512]{1,0:T(8,128)S(1)}, bf16[72,512]{1,0:T(8,128)(2,1)S(1)}, bf16[72,512]{1,0:T(8,128)(2,1)}, bf16[72,512]{1,0:T(8,128)(2,1)}) custom-call(s32[4]{0:T(128)S(1)} %pad_add_fusion.me_ref, bf16[112,512]{1,0:T(8,128)(2,1)S(1)} %shard_map.133.grad_ref.refs_0_, bf16[112,512]{1,0:T(8,128)(2,1)S(1)} %collective-permute-done.11.refs_1_, ...), custom_call_target="tpu_custom_call" | custom-call | flops 100663296 | bytes 1179664 | tf_op jit(solution)/shard_map/pallas_call | solution.py:24
  66.9 1.4 %collective-permute-start.18 = (bf16[72,512]{1,0:T(8,128)(2,1)S(1)}, bf16[72,512]{1,0:T(8,128)(2,1)S(1)}, u32[]{:S(2)}, u32[]{:S(2)}) collective-permute-start(bf16[72,512]{1,0:T(8,128)(2,1)S(1)} %get-tuple-element.71), channel_id=1, source_target_pairs={{0,8},{1,9},{2,10},{3,11},{4,12},{5,13},{6,14},{7,15},{8,0},{9,1},... | collective-permute-start | bytes 221192 | tf_op jit(solution)/shard_map/ppermute | solution.py:307
  68.3 2.4 %collective-permute-start.19 = (bf16[72,512]{1,0:T(8,128)(2,1)}, bf16[72,512]{1,0:T(8,128)(2,1)S(1)}, u32[]{:S(2)}, u32[]{:S(2)}) collective-permute-start(bf16[72,512]{1,0:T(8,128)(2,1)} %get-tuple-element.72), channel_id=1, source_target_pairs={{0,16},{1,17},{2,18},{3,19},{4,20},{5,21},{6,22},{7,23},{8,24},{9,... | collective-permute-start | bytes 221192 | tf_op jit(solution)/shard_map/ppermute | solution.py:307
  70.6 0.6 collective-permute-start.20
  72.4 3.3 %collective-permute-start.23 = (bf16[64,320]{1,0:T(8,128)(2,1)S(1)}, bf16[64,320]{1,0:T(8,128)(2,1)S(1)}, u32[]{:S(2)}, u32[]{:S(2)}) collective-permute-start(bf16[64,320]{1,0:T(8,128)(2,1)S(1)} %get-tuple-element.78), channel_id=1, source_target_pairs={{0,16},{1,17},{2,18},{3,19},{4,20},{5,21},{6,22},{7,23},{8,24},{9,... | collective-permute-start | bytes 122888 | tf_op jit(solution)/shard_map/ppermute | solution.py:307
  75.7 0.6 collective-permute-start.24
  76.3 1.9 %shard_map.134 = bf16[256,512]{1,0:T(8,128)(2,1)} custom-call(s32[8]{0:T(128)S(1)} %copy-done.27, bf16[112,512]{1,0:T(8,128)(2,1)S(1)} %shard_map.133.grad_ref.refs_0_, bf16[2,1024,512]{2,1,0:T(8,128)(2,1)S(1)} %copy-done.1), custom_call_target="tpu_custom_call" | custom-call | flops 67108864 | bytes 2211872 | tf_op jit(solution)/shard_map/pallas_call | solution.py:24
  78.2 0.7 copy.20
  79.0 2.9 %collective-permute-done.23.refs_6_ = bf16[64,320]{1,0:T(8,128)(2,1)S(1)} collective-permute-done((bf16[64,320]{1,0:T(8,128)(2,1)S(1)}, bf16[64,320]{1,0:T(8,128)(2,1)S(1)}, u32[]{:S(2)}, u32[]{:S(2)}) %collective-permute-start.23) | collective-permute-done | bytes 40992 | tf_op jit(solution)/shard_map/ppermute | solution.py:307
  81.9 1.3 %shard_map.137 = (f32[2,32,512]{2,1,0:T(8,128)}, f32[2,32]{1,0:T(2,128)}, f32[64,320]{1,0:T(8,128)}) custom-call(s32[4]{0:T(128)S(1)} %pad_add_fusion.me_ref, f32[72,512]{1,0:T(8,128)S(1)} %get-tuple-element.70.refs_0_, bf16[72,512]{1,0:T(8,128)(2,1)S(1)} %collective-permute-done.18.refs_1_, bf16[72,512]{1,0:T(8,128)(2,1)S(1)} %collective-permute-done.19.refs_2_, ...), custom_call_target="tpu_custom_call" | custom-call | bytes 573456 | tf_op jit(solution)/shard_map/pallas_call | solution.py:24
  (81 shorter events, 8.1 us)
Async XLA Ops:
  0.6 0.7 copy-start.23
  1.9 22.1 %copy-start.24 = (s32[8]{0:T(128)S(1)}, s32[8]{0:T(128)}, u32[]{:S(2)}) copy-start(s32[8]{0:T(128)} %dests_ref.5) | copy-start | bytes 100
  3.1 40.9 %copy-start.22 = (f32[2,512]{1,0:T(2,128)S(1)}, f32[2,512]{1,0:T(2,128)}, u32[]{:S(2)}) copy-start(f32[2,512]{1,0:T(2,128)} %gain_ref.3) | copy-start | bytes 12292
  4.4 6.5 %collective-permute-start = (bf16[128,512]{1,0:T(8,128)(2,1)S(1)}, bf16[128,512]{1,0:T(8,128)(2,1)S(1)}, u32[]{:S(2)}, u32[]{:S(2)}) collective-permute-start(bf16[128,512]{1,0:T(8,128)(2,1)S(1)} %convolution_convert_fusion), channel_id=1, source_target_pairs={{0,2},{1,3},{2,0},{3,1},{4,6},{5,7},{6,4},{7,5},{8,10},{9,11},{10,... | collective-permute-start | bytes 393224 | tf_op jit(solution)/shard_map/ppermute | solution.py:307
  10.9 13.1 %collective-permute-start.1 = (bf16[128,512]{1,0:T(8,128)(2,1)S(1)}, bf16[128,512]{1,0:T(8,128)(2,1)S(1)}, u32[]{:S(2)}, u32[]{:S(2)}) collective-permute-start(bf16[128,512]{1,0:T(8,128)(2,1)S(1)} %add_convert_fusion.mine_ref), channel_id=1, source_target_pairs={{0,1},{1,0},{2,3},{3,2},{4,5},{5,4},{6,7},{7,6},{8,9},{9,8},{10,11... | collective-permute-start | bytes 393224 | tf_op jit(solution)/shard_map/ppermute | solution.py:307
  11.0 13.0 %all-to-all-start = ((s32[8,1,128]{2,1,0:T(1,128)}), s32[8,1,128]{2,1,0:T(1,128)S(1)}, u32[]{:S(2)}, u32[]{:S(2)}) async-start(s32[8,1,128]{2,1,0:T(1,128)} %bitcast.5), calls=%async_computation | async-start | bytes 8192 | tf_op jit(solution)/shard_map/all_to_all | solution.py:321
  17.1 1.6 %copy-start = (bf16[2,1024,512]{2,1,0:T(8,128)(2,1)S(1)}, bf16[2,1024,512]{2,1,0:T(8,128)(2,1)}, u32[]{:S(2)}) copy-start(bf16[2,1024,512]{2,1,0:T(8,128)(2,1)} %weight_ref.6) | copy-start | bytes 6291460
  18.7 0.9 %copy-start.2 = (bf16[8,32,512]{2,1,0:T(8,128)(2,1)S(1)}, bf16[8,32,512]{2,1,0:T(8,128)(2,1)}, u32[]{:S(2)}) copy-start(bf16[8,32,512]{2,1,0:T(8,128)(2,1)} %param.9) | copy-start | bytes 786436
  19.7 0.7 copy-start.21
  20.4 0.7 copy-start.25
  21.7 22.3 %copy-start.1 = (bf16[2,1024,512]{2,1,0:T(8,128)(2,1)S(1)}, bf16[2,1024,512]{2,1,0:T(8,128)(2,1)}, u32[]{:S(2)}) copy-start(bf16[2,1024,512]{2,1,0:T(8,128)(2,1)} %weight_ref.6) | copy-start | bytes 6291460
  25.3 17.3 %all-to-all-start.1 = ((bf16[8,16,512]{2,1,0:T(8,128)(2,1)}), bf16[8,16,512]{2,1,0:T(8,128)(2,1)S(1)}, u32[]{:S(2)}, u32[]{:S(2)}) async-start(bf16[8,16,512]{2,1,0:T(8,128)(2,1)} %shard_map.130), calls=%async_computation.1 | async-start | bytes 262144 | tf_op jit(solution)/shard_map/all_to_all | solution.py:362
  31.3 3.9 %collective-permute-start.2 = (bf16[128,128]{1,0:T(8,128)(2,1)S(1)}, bf16[128,128]{1,0:T(8,128)(2,1)S(1)}, u32[]{:S(2)}, u32[]{:S(2)}) collective-permute-start(bf16[128,128]{1,0:T(8,128)(2,1)S(1)} %get-tuple-element.47), channel_id=1, source_target_pairs={{0,1},{1,0},{2,3},{3,2},{4,5},{5,4},{6,7},{7,6},{8,9},{9,8},{10,11... | collective-permute-start | bytes 98312 | tf_op jit(solution)/shard_map/ppermute | solution.py:307
  31.4 6.5 %collective-permute-start.3 = (bf16[128,128]{1,0:T(8,128)(2,1)S(1)}, bf16[128,128]{1,0:T(8,128)(2,1)S(1)}, u32[]{:S(2)}, u32[]{:S(2)}) collective-permute-start(bf16[128,128]{1,0:T(8,128)(2,1)S(1)} %get-tuple-element.48), channel_id=1, source_target_pairs={{0,2},{1,3},{2,0},{3,1},{4,6},{5,7},{6,4},{7,5},{8,10},{9,11},{10,... | collective-permute-start | bytes 98312 | tf_op jit(solution)/shard_map/ppermute | solution.py:307
  32.9 5.1 %collective-permute-start.4 = (bf16[128,128]{1,0:T(8,128)(2,1)S(1)}, bf16[128,128]{1,0:T(8,128)(2,1)S(1)}, u32[]{:S(2)}, u32[]{:S(2)}) collective-permute-start(bf16[128,128]{1,0:T(8,128)(2,1)S(1)} %get-tuple-element.49), channel_id=1, source_target_pairs={{0,3},{1,2},{2,1},{3,0},{4,7},{5,6},{6,5},{7,4},{8,11},{9,10},{10,... | collective-permute-start | bytes 98312 | tf_op jit(solution)/shard_map/ppermute | solution.py:307
  33.2 4.8 %collective-permute-start.5 = (bf16[128,128]{1,0:T(8,128)(2,1)S(1)}, bf16[128,128]{1,0:T(8,128)(2,1)S(1)}, u32[]{:S(2)}, u32[]{:S(2)}) collective-permute-start(bf16[128,128]{1,0:T(8,128)(2,1)S(1)} %get-tuple-element.50), channel_id=1, source_target_pairs={{0,4},{1,5},{2,6},{3,7},{4,0},{5,1},{6,2},{7,3},{8,12},{9,13},{10,... | collective-permute-start | bytes 98312 | tf_op jit(solution)/shard_map/ppermute | solution.py:307
  35.2 3.7 %collective-permute-start.6 = (bf16[128,128]{1,0:T(8,128)(2,1)S(1)}, bf16[128,128]{1,0:T(8,128)(2,1)S(1)}, u32[]{:S(2)}, u32[]{:S(2)}) collective-permute-start(bf16[128,128]{1,0:T(8,128)(2,1)S(1)} %get-tuple-element.51), channel_id=1, source_target_pairs={{0,5},{1,4},{2,7},{3,6},{4,1},{5,0},{6,3},{7,2},{8,13},{9,12},{10,... | collective-permute-start | bytes 98312 | tf_op jit(solution)/shard_map/ppermute | solution.py:307
  35.2 8.7 %copy-start.7 = (bf16[128,128]{1,0:T(8,128)(2,1)}, bf16[128,128]{1,0:T(8,128)(2,1)S(1)}, u32[]{:S(2)}) copy-start(bf16[128,128]{1,0:T(8,128)(2,1)S(1)} %collective-permute-done.2.refs_9_) | copy-start | bytes 98308
  35.2 5.5 %collective-permute-start.7 = (bf16[128,128]{1,0:T(8,128)(2,1)S(1)}, bf16[128,128]{1,0:T(8,128)(2,1)S(1)}, u32[]{:S(2)}, u32[]{:S(2)}) collective-permute-start(bf16[128,128]{1,0:T(8,128)(2,1)S(1)} %get-tuple-element.52), channel_id=1, source_target_pairs={{0,6},{1,7},{2,4},{3,5},{4,2},{5,3},{6,0},{7,1},{8,14},{9,15},{10,... | collective-permute-start | bytes 98312 | tf_op jit(solution)/shard_map/ppermute | solution.py:307
  37.8 6.1 %copy-start.9 = (bf16[128,128]{1,0:T(8,128)(2,1)}, bf16[128,128]{1,0:T(8,128)(2,1)S(1)}, u32[]{:S(2)}) copy-start(bf16[128,128]{1,0:T(8,128)(2,1)S(1)} %collective-permute-done.3.refs_10_) | copy-start | bytes 98308
  37.8 4.2 %collective-permute-start.8 = (bf16[128,128]{1,0:T(8,128)(2,1)S(1)}, bf16[128,128]{1,0:T(8,128)(2,1)S(1)}, u32[]{:S(2)}, u32[]{:S(2)}) collective-permute-start(bf16[128,128]{1,0:T(8,128)(2,1)S(1)} %get-tuple-element.53), channel_id=1, source_target_pairs={{0,7},{1,6},{2,5},{3,4},{4,3},{5,2},{6,1},{7,0},{8,15},{9,14},{10,... | collective-permute-start | bytes 98312 | tf_op jit(solution)/shard_map/ppermute | solution.py:307
  38.0 5.9 %copy-start.11 = (bf16[128,128]{1,0:T(8,128)(2,1)}, bf16[128,128]{1,0:T(8,128)(2,1)S(1)}, u32[]{:S(2)}) copy-start(bf16[128,128]{1,0:T(8,128)(2,1)S(1)} %collective-permute-done.4.refs_11_) | copy-start | bytes 98308
  43.4 8.2 %collective-permute-start.9 = (bf16[128,512]{1,0:T(8,128)(2,1)S(1)}, bf16[128,512]{1,0:T(8,128)(2,1)S(1)}, u32[]{:S(2)}, u32[]{:S(2)}) collective-permute-start(bf16[128,512]{1,0:T(8,128)(2,1)S(1)} %shard_map.131), channel_id=1, source_target_pairs={{0,2},{1,3},{2,0},{3,1},{4,6},{5,7},{6,4},{7,5},{8,10},{9,11},{10,... | collective-permute-start | bytes 393224 | tf_op jit(solution)/shard_map/ppermute | solution.py:307
  45.1 31.3 %copy-start.27 = (s32[8]{0:T(128)S(1)}, s32[8]{0:T(128)}, u32[]{:S(2)}) copy-start(s32[8]{0:T(128)} %lengths_ref.3) | copy-start | bytes 100
  45.1 7.2 %collective-permute-start.16 = (bf16[112,512]{1,0:T(8,128)(2,1)S(1)}, bf16[112,512]{1,0:T(8,128)(2,1)S(1)}, u32[]{:S(2)}, u32[]{:S(2)}) collective-permute-start(bf16[112,512]{1,0:T(8,128)(2,1)S(1)} %shard_map.133.grad_ref.refs_0_), channel_id=1, source_target_pairs={{0,6},{1,7},{2,4},{3,5},{4,2},{5,3},{6,0},{7,1},{8,14},{9,15},{10,... | collective-permute-start | bytes 344072 | tf_op jit(solution)/shard_map/ppermute | solution.py:307
  46.9 6.7 %collective-permute-start.14 = (bf16[112,512]{1,0:T(8,128)(2,1)S(1)}, bf16[112,512]{1,0:T(8,128)(2,1)S(1)}, u32[]{:S(2)}, u32[]{:S(2)}) collective-permute-start(bf16[112,512]{1,0:T(8,128)(2,1)S(1)} %shard_map.133.grad_ref.refs_0_), channel_id=1, source_target_pairs={{0,4},{1,5},{2,6},{3,7},{4,0},{5,1},{6,2},{7,3},{8,12},{9,13},{10,... | collective-permute-start | bytes 344072 | tf_op jit(solution)/shard_map/ppermute | solution.py:307
  48.1 5.9 %collective-permute-start.12 = (bf16[112,512]{1,0:T(8,128)(2,1)S(1)}, bf16[112,512]{1,0:T(8,128)(2,1)S(1)}, u32[]{:S(2)}, u32[]{:S(2)}) collective-permute-start(bf16[112,512]{1,0:T(8,128)(2,1)S(1)} %shard_map.133.grad_ref.refs_0_), channel_id=1, source_target_pairs={{0,2},{1,3},{2,0},{3,1},{4,6},{5,7},{6,4},{7,5},{8,10},{9,11},{10,... | collective-permute-start | bytes 344072 | tf_op jit(solution)/shard_map/ppermute | solution.py:307
  51.7 4.6 %collective-permute-start.10 = (bf16[128,512]{1,0:T(8,128)(2,1)S(1)}, bf16[128,512]{1,0:T(8,128)(2,1)S(1)}, u32[]{:S(2)}, u32[]{:S(2)}) collective-permute-start(bf16[128,512]{1,0:T(8,128)(2,1)S(1)} %add.15.mine_ref), channel_id=1, source_target_pairs={{0,1},{1,0},{2,3},{3,2},{4,5},{5,4},{6,7},{7,6},{8,9},{9,8},{10,11... | collective-permute-start | bytes 393224 | tf_op jit(solution)/shard_map/ppermute | solution.py:307
  51.7 6.7 %collective-permute-start.11 = (bf16[112,512]{1,0:T(8,128)(2,1)S(1)}, bf16[112,512]{1,0:T(8,128)(2,1)S(1)}, u32[]{:S(2)}, u32[]{:S(2)}) collective-permute-start(bf16[112,512]{1,0:T(8,128)(2,1)S(1)} %shard_map.133.grad_ref.refs_0_), channel_id=1, source_target_pairs={{0,1},{1,0},{2,3},{3,2},{4,5},{5,4},{6,7},{7,6},{8,9},{9,8},{10,11... | collective-permute-start | bytes 344072 | tf_op jit(solution)/shard_map/ppermute | solution.py:307
  52.2 6.2 %collective-permute-start.17 = (bf16[112,512]{1,0:T(8,128)(2,1)S(1)}, bf16[112,512]{1,0:T(8,128)(2,1)S(1)}, u32[]{:S(2)}, u32[]{:S(2)}) collective-permute-start(bf16[112,512]{1,0:T(8,128)(2,1)S(1)} %collective-permute-done.16.refs_6_), channel_id=1, source_target_pairs={{0,1},{1,0},{2,3},{3,2},{4,5},{5,4},{6,7},{7,6},{8,9},{9,8},{10,11... | collective-permute-start | bytes 344072 | tf_op jit(solution)/shard_map/ppermute | solution.py:307
  53.6 4.9 %collective-permute-start.15 = (bf16[112,512]{1,0:T(8,128)(2,1)S(1)}, bf16[112,512]{1,0:T(8,128)(2,1)}, u32[]{:S(2)}, u32[]{:S(2)}) collective-permute-start(bf16[112,512]{1,0:T(8,128)(2,1)S(1)} %collective-permute-done.14.refs_4_), channel_id=1, source_target_pairs={{0,1},{1,0},{2,3},{3,2},{4,5},{5,4},{6,7},{7,6},{8,9},{9,8},{10,11... | collective-permute-start | bytes 344072 | tf_op jit(solution)/shard_map/ppermute | solution.py:307
  54.0 4.5 %collective-permute-start.13 = (bf16[112,512]{1,0:T(8,128)(2,1)S(1)}, bf16[112,512]{1,0:T(8,128)(2,1)}, u32[]{:S(2)}, u32[]{:S(2)}) collective-permute-start(bf16[112,512]{1,0:T(8,128)(2,1)S(1)} %collective-permute-done.12.refs_2_), channel_id=1, source_target_pairs={{0,1},{1,0},{2,3},{3,2},{4,5},{5,4},{6,7},{7,6},{8,9},{9,8},{10,11... | collective-permute-start | bytes 344072 | tf_op jit(solution)/shard_map/ppermute | solution.py:307
  57.8 20.4 %copy-start.4 = (bf16[128,320]{1,0:T(8,128)(2,1)S(1)}, bf16[128,320]{1,0:T(8,128)(2,1)}, u32[]{:S(2)}) copy-start(bf16[128,320]{1,0:T(8,128)(2,1)} %copy-done.3) | copy-start | bytes 245764
  57.8 13.5 %collective-permute-start.21 = (bf16[4,64,320]{2,1,0:T(8,128)(2,1)S(1)}, bf16[4,64,320]{2,1,0:T(8,128)(2,1)S(1)}, u32[]{:S(2)}, u32[]{:S(2)}) collective-permute-start(bf16[4,64,320]{2,1,0:T(8,128)(2,1)S(1)} %get-tuple-element.75), channel_id=1, source_target_pairs={{0,4},{1,5},{2,6},{3,7},{4,0},{5,1},{6,2},{7,3},{8,12},{9,13},{10,... | collective-permute-start | bytes 491528 | tf_op jit(solution)/shard_map/ppermute | solution.py:307
  58.5 0.8 copy-start.6
  59.3 0.8 copy-start.8
  60.0 0.8 copy-start.10
  60.8 0.8 copy-start.12
  61.5 0.8 copy-start.14
  62.3 0.8 copy-start.16
  63.1 0.8 copy-start.18
  63.8 0.8 copy-start.20
  66.9 8.8 %collective-permute-start.18 = (bf16[72,512]{1,0:T(8,128)(2,1)S(1)}, bf16[72,512]{1,0:T(8,128)(2,1)S(1)}, u32[]{:S(2)}, u32[]{:S(2)}) collective-permute-start(bf16[72,512]{1,0:T(8,128)(2,1)S(1)} %get-tuple-element.71), channel_id=1, source_target_pairs={{0,8},{1,9},{2,10},{3,11},{4,12},{5,13},{6,14},{7,15},{8,0},{9,1},... | collective-permute-start | bytes 221192 | tf_op jit(solution)/shard_map/ppermute | solution.py:307
  68.3 10.7 %collective-permute-start.19 = (bf16[72,512]{1,0:T(8,128)(2,1)}, bf16[72,512]{1,0:T(8,128)(2,1)S(1)}, u32[]{:S(2)}, u32[]{:S(2)}) collective-permute-start(bf16[72,512]{1,0:T(8,128)(2,1)} %get-tuple-element.72), channel_id=1, source_target_pairs={{0,16},{1,17},{2,18},{3,19},{4,20},{5,21},{6,22},{7,23},{8,24},{9,... | collective-permute-start | bytes 221192 | tf_op jit(solution)/shard_map/ppermute | solution.py:307
  70.6 8.3 %collective-permute-start.20 = (bf16[72,512]{1,0:T(8,128)(2,1)}, bf16[72,512]{1,0:T(8,128)(2,1)S(1)}, u32[]{:S(2)}, u32[]{:S(2)}) collective-permute-start(bf16[72,512]{1,0:T(8,128)(2,1)} %get-tuple-element.73), channel_id=1, source_target_pairs={{0,24},{1,25},{2,26},{3,27},{4,28},{5,29},{6,30},{7,31},{8,16},{9,... | collective-permute-start | bytes 221192 | tf_op jit(solution)/shard_map/ppermute | solution.py:307
  71.9 7.1 %collective-permute-start.22 = (bf16[64,320]{1,0:T(8,128)(2,1)S(1)}, bf16[64,320]{1,0:T(8,128)(2,1)S(1)}, u32[]{:S(2)}, u32[]{:S(2)}) collective-permute-start(bf16[64,320]{1,0:T(8,128)(2,1)S(1)} %get-tuple-element.77), channel_id=1, source_target_pairs={{0,8},{1,9},{2,10},{3,11},{4,12},{5,13},{6,14},{7,15},{8,0},{9,1},... | collective-permute-start | bytes 122888 | tf_op jit(solution)/shard_map/ppermute | solution.py:307
  72.4 9.4 %collective-permute-start.23 = (bf16[64,320]{1,0:T(8,128)(2,1)S(1)}, bf16[64,320]{1,0:T(8,128)(2,1)S(1)}, u32[]{:S(2)}, u32[]{:S(2)}) collective-permute-start(bf16[64,320]{1,0:T(8,128)(2,1)S(1)} %get-tuple-element.78), channel_id=1, source_target_pairs={{0,16},{1,17},{2,18},{3,19},{4,20},{5,21},{6,22},{7,23},{8,24},{9,... | collective-permute-start | bytes 122888 | tf_op jit(solution)/shard_map/ppermute | solution.py:307
  75.7 6.2 %collective-permute-start.24 = (bf16[64,320]{1,0:T(8,128)(2,1)S(1)}, bf16[64,320]{1,0:T(8,128)(2,1)S(1)}, u32[]{:S(2)}, u32[]{:S(2)}) collective-permute-start(bf16[64,320]{1,0:T(8,128)(2,1)S(1)} %get-tuple-element.79), channel_id=1, source_target_pairs={{0,24},{1,25},{2,26},{3,27},{4,28},{5,29},{6,30},{7,31},{8,16},{9,... | collective-permute-start | bytes 122888 | tf_op jit(solution)/shard_map/ppermute | solution.py:307
  (8 other events, 5.0 us)

commit v3 on v2

--- a/solution.py
+++ b/solution.py
@@ -29,7 +29,7 @@
         if many
         else pl.BlockSpec(memory_space=VMEM),
         scratch_shapes=list(scratch),
-        compiler_params=pltpu.CompilerParams(vmem_limit_bytes=40 * 2**20),
+        compiler_params=pltpu.CompilerParams(vmem_limit_bytes=14 * 2**20),
         cost_estimate=pl.CostEstimate(flops=flops, bytes_accessed=moved, transcendentals=0),
     )(*args)
 
@@ -60,36 +60,42 @@
     return value * half, half + value * density
 
 
-def source_of(row, lengths_ref, pairs, frames):
+def source_of(row, me_ref, pairs, frames):
     part = lax.div(row, pairs * frames)
     inner = lax.rem(row, pairs * frames)
     pair = lax.div(inner, frames)
     t = lax.rem(inner, frames)
     first = jnp.zeros_like(row)
     for p in range(pairs):
-        first = jnp.where(pair == p, lengths_ref[2 * p], first)
+        first = jnp.where(pair == p, me_ref[4 + 2 * p], first)
     off = jnp.where(part == 1, 2, jnp.where(part == 2, 1, part))
     t_from = jnp.where(t < first, t, t + frames - first)
     return pair * (8 * frames) + 4 * t_from + off
 
 
-def index_kernel(dests_ref, offsets_ref, out_ref, *, pairs, frames):
+def index_kernel(me_ref, out_ref, *, pairs, frames):
     row = lax.broadcasted_iota(jnp.int32, out_ref.shape, 0)
-    value = jnp.full(out_ref.shape, -1, jnp.int32)
+    shard = lax.broadcasted_iota(jnp.int32, out_ref.shape, 1)
+    value = jnp.zeros(out_ref.shape, jnp.int32)
     for p in range(pairs):
-        value = jnp.where(row == dests_ref[2 * p], lax.div(offsets_ref[2 * p], frames), value)
-    out_ref[...] = value
+        block = lax.div(me_ref[4 + 4 * pairs + 2 * p], frames)
+        value = jnp.where(shard == me_ref[4 + 2 * pairs + 2 * p], block + 1, value)
+    out_ref[...] = jnp.where(row == me_ref[3], value, 0)
+
+
+def block_from(got_ref, me_ref, d):
+    return got_ref[2 * (me_ref[2] ^ (d // 2)) + d % 2, 2 * me_ref[2] + me_ref[3]] - 1
 
 
 def forward_kernel(
-    lengths_ref, me_ref, feat_ref, weight_ref, gain_ref, shift_ref, *rest, pairs, frames, far, near, owned
+    me_ref, feat_ref, weight_ref, gain_ref, shift_ref, *rest, pairs, frames, far, near, owned
 ):
     frames_ref, slope1_ref, slope2_ref, hat1_ref, hat2_ref, scale1_ref, scale2_ref = rest[:7]
     turned_refs, in_turned = rest[7:-1], rest[-1]
     channels = feat_ref.shape[1]
     n2 = pairs * frames
     row = lax.broadcasted_iota(jnp.int32, (4 * n2, 1), 0)
-    source = source_of(row, lengths_ref, pairs, frames)
+    source = source_of(row, me_ref, pairs, frames)
     place = lax.broadcasted_iota(jnp.int32, (4 * n2, feat_ref.shape[0]), 1)
     pick = jnp.where(place == source, 1.0, 0.0).astype(BF)
     chosen32 = dot(pick, feat_ref[...])
@@ -132,26 +138,26 @@
         ).astype(BF)
 
 
-def send_kernel(got_ref, dests_ref, mine_ref, other_ref, frames_ref, out_ref, rows32, *, pairs, frames):
+def send_kernel(got_ref, me_ref, mine_ref, other_ref, frames_ref, out_ref, rows32, *, pairs, frames):
     rows32[...] = mine_ref[...].astype(F32) + other_ref[...].astype(F32)
     blocks = rows32.shape[0] // frames
     made = frames_ref[...].astype(F32)
     none = jnp.zeros((frames, made.shape[1]), F32)
     for d in range(out_ref.shape[0]):
-        block = got_ref[d, 0]
+        block = block_from(got_ref, me_ref, d)
         safe = jnp.clip(block, 0, blocks - 1)
         grads = rows32[pl.ds(pl.multiple_of(safe * frames, frames), frames), :]
         grads = jnp.where(block >= 0, grads, none)
         sent = none
         for p in range(pairs):
-            sent = jnp.where(dests_ref[2 * p] == d, made[p * frames : (p + 1) * frames], sent)
+            sent = jnp.where(me_ref[4 + 2 * pairs + 2 * p] == d, made[p * frames : (p + 1) * frames], sent)
         out_ref[d] = jnp.concatenate([grads, sent], axis=0).astype(BF)
 
 
-def place_kernel(got_ref, slots_ref, out_ref, rows32, *, frames):
+def place_kernel(got_ref, me_ref, slots_ref, out_ref, rows32, *, frames):
     rows32[...] = jnp.zeros_like(rows32)
     for d in range(slots_ref.shape[0]):
-        block = got_ref[d, 0]
+        block = block_from(got_ref, me_ref, d)
 
         @pl.when(block >= 0)
         def _():
@@ -165,8 +171,8 @@
 
 def project_kernel(me_ref, mine_ref, other_ref, weight_ref, cotangent_ref, packed_ref, keep_ref, send_ref):
     rows32 = mine_ref[...].astype(F32) + other_ref[...].astype(F32)
-    packed_ref[...] = dot(rows32.astype(BF), weight_ref[...]).astype(BF)
-    partial = dot(rows32.T.astype(BF), cotangent_ref[...])
+    packed_ref[...] = dot_nt(weight_ref[...], rows32.astype(BF)).astype(BF)
+    partial = dot_nt(rows32.T.astype(BF), cotangent_ref[...])
     each = keep_ref.shape[1]
     for z in range(keep_ref.shape[0]):
         low = partial[2 * z * each : (2 * z + 1) * each]
@@ -201,12 +207,12 @@
 
 
 def back_kernel(
-    dests_ref, slots_ref, slope1_ref, slope2_ref, hat1_ref, hat2_ref, scale1_ref, scale2_ref,
+    me_ref, slots_ref, slope1_ref, slope2_ref, hat1_ref, hat2_ref, scale1_ref, scale2_ref,
     weight_ref, gain_ref, out_ref, grads32, *, pairs, frames
 ):
     channels = weight_ref.shape[2]
     for p in range(pairs):
-        slot = jnp.clip(dests_ref[2 * p], 0, slots_ref.shape[0] - 1)
+        slot = jnp.clip(me_ref[4 + 2 * pairs + 2 * p], 0, slots_ref.shape[0] - 1)
         grads32[p * frames : (p + 1) * frames, :] = slots_ref[slot].astype(F32)[:frames]
     second, gain2, shift2 = norm_back(grads32[...], slope2_ref, hat2_ref, scale2_ref, gain_ref[1:2, :])
     hidden = jnp.concatenate(
@@ -227,7 +233,7 @@
     out_ref[n1 + n2 :, :] = jnp.concatenate(rows, axis=0).astype(BF)
 
 
-def input_kernel(lengths_ref, grad_ref, weight_ref, out_ref, *, pairs, frames):
+def input_kernel(me_ref, grad_ref, weight_ref, out_ref, *, pairs, frames):
     channels = weight_ref.shape[2]
     n1 = 2 * pairs * frames
     first = grad_ref[:n1, :]
@@ -236,7 +242,7 @@
         axis=0,
     ).astype(BF)
     row = lax.broadcasted_iota(jnp.int32, (1, 2 * n1), 1)
-    source = source_of(row, lengths_ref, pairs, frames)
+    source = source_of(row, me_ref, pairs, frames)
     place = lax.broadcasted_iota(jnp.int32, (out_ref.shape[0], 2 * n1), 0)
     pick = jnp.where(place == source, 1.0, 0.0).astype(BF)
     out_ref[...] = dot(pick, rows).astype(BF)
@@ -310,16 +316,17 @@
     at_dp = lax.axis_index("dp").astype(jnp.int32)
     at_mp = lax.axis_index("mp").astype(jnp.int32)
     x_bit = at_dp & 1
-    me = jnp.stack([at_dp * mp_count + at_mp, x_bit * mp_count + at_mp, at_dp >> 1, x_bit])
+    place = jnp.stack([at_dp * mp_count + at_mp, x_bit * mp_count + at_mp, at_dp >> 1, x_bit])
+    me = jnp.concatenate([place, lengths, dests, offsets])
 
     index = call(
         functools.partial(index_kernel, pairs=pairs, frames=frames),
-        shape(dp_count, 128, kind=jnp.int32),
-        (dests, offsets),
-        scalars=2,
-    )
-    got_index = lax.all_to_all(index, "dp", split_axis=0, concat_axis=0, tiled=True)
-    index, cotangent = lax.optimization_barrier((index, grad_packed))
+        shape(2, -(-dp_count // 128) * 128, kind=jnp.int32),
+        (me,),
+        scalars=1,
+    )
+    index = index + swap(index, mp_count)
+    got_index = jnp.concatenate([index] + [swap(index, near * f) for f in range(1, far)], axis=0)
 
     wide = -(-(n1 + n2) // 128) * 128
     feat = features.reshape(utt_count * positions, channels)
@@ -337,8 +344,8 @@
             shape(n2, 128, kind=F32),
         ]
         + [shape(far * owned, wide)] * near,
-        (lengths, me, feat, conv_weight, norm_gain, norm_shift),
-        scalars=2,
+        (me, feat, conv_weight, norm_gain, norm_shift),
+        scalars=1,
         flops=2 * (n1 + n2) * 2 * channels * channels,
         scratch=[pltpu.VMEM((2 * channels, wide), F32)],
     )
@@ -346,7 +353,7 @@
     in_sides = [side if k == 0 else swap(side, k) for k, side in enumerate(made[7:])]
 
     grad_rows = lax.dot_general(
-        cotangent, proj_weight, (((1,), (1,)), ((), ())), preferred_element_type=F32
+        grad_packed, proj_weight, (((1,), (1,)), ((), ())), preferred_element_type=F32
     ).astype(BF)
     for mask in bits[:-1]:
         grad_rows = (grad_rows.astype(F32) + swap(grad_rows, mask).astype(F32)).astype(BF)
@@ -355,7 +362,7 @@
     sent = call(
         functools.partial(send_kernel, pairs=pairs, frames=frames),
         shape(dp_count, 2 * frames, channels),
-        (got_index, dests, grad_rows, other_rows, pair_frames),
+        (got_index, me, grad_rows, other_rows, pair_frames),
         scalars=2,
         scratch=[pltpu.VMEM((seq, channels), F32)],
     )
@@ -365,7 +372,7 @@
     grads = call(
         functools.partial(back_kernel, pairs=pairs, frames=frames),
         shape(n1 + n2 + 16, channels),
-        (dests, slots, slope1, slope2, hat1, hat2, scale1, scale2, conv_weight, norm_gain),
+        (me, slots, slope1, slope2, hat1, hat2, scale1, scale2, conv_weight, norm_gain),
         scalars=1,
         flops=2 * n2 * 2 * channels * channels,
         scratch=[pltpu.VMEM((n2, channels), F32)],
@@ -377,8 +384,8 @@
     placed = call(
         functools.partial(place_kernel, frames=frames),
         shape(seq, channels),
-        (got_index, slots),
-        scalars=1,
+        (got_index, me, slots),
+        scalars=2,
         scratch=[pltpu.VMEM((seq, channels), F32)],
     )
     for mask in bits[:-1]:
@@ -387,11 +394,11 @@
     packed, keep, send = call(
         project_kernel,
         [
-            shape(seq, width),
+            shape(width, seq),
             shape(far, per_dp, width, kind=F32),
             shape(far, per_dp, width),
         ],
-        (me, placed, swap(placed, bits[-1]), proj_weight, grad_packed),
+        (me, placed, swap(placed, bits[-1]), proj_weight.T, grad_packed.T),
         scalars=1,
         flops=4 * seq * channels * width,
     )
@@ -405,7 +412,7 @@
     grad_features = call(
         functools.partial(input_kernel, pairs=pairs, frames=frames),
         shape(utt_count * positions, channels),
-        (lengths, grads, conv_weight),
+        (me, grads, conv_weight),
         scalars=1,
         flops=2 * n1 * 2 * channels * channels,
     ).reshape(utt_count, positions, channels)
@@ -430,7 +437,7 @@
         (me, *conv_got, *proj_got),
         scalars=1,
     )
-    return (packed, grad_features, grad_conv, grad_norm, grad_proj)
+    return (packed.T, grad_features, grad_conv, grad_norm, grad_proj)
 
 
 def solution(mesh):

time: 84.2 us -> 74 us (0.88)
  local copies, waits for them, and re-layouts: 18.6 us -> 4.7 us
  waiting for transfers between devices: 13.3 us -> 18.5 us
  Pallas kernels: 12.9 us -> 11.9 us
    unnamed x61 -> x16, local copies, waits for them, and re-layouts: 18.6 us -> 3.94 us
    ppermute x25 -> x29, starting transfers between devices: 24.1 us -> 30.2 us  [swap(): lax.ppermute(x, everyone, [(i, i ^ mask) for i in range(dp_count * mp_cou...]
    all_to_all x1 -> x0, starting transfers between devices: 6.04 us -> none  [local(): lax.all_to_all(index, 'dp', split_axis=0, concat_axis=0, tiled=True)]
    ppermute x25 -> x29, waiting for transfers between devices: 13.3 us -> 18.5 us  [swap(): lax.ppermute(x, everyone, [(i, i ^ mask) for i in range(dp_count * mp_cou...]
    pallas_call x10, Pallas kernels: 12.9 us -> 11.9 us  [call(): pl.pallas_call(body, out_shape=out, in_specs=specs, out_specs=[pl.BlockSp...]
  transfers between devices with their start and end apart: 27 -> 30, of which waited for: 8 -> 11; matrix products, arithmetic and copies ran while one was open for 4% -> 1% of each run, Pallas kernels for 10% -> 12%
where the time goes in v3:
time: 74 us; the launch traced here: 73.6 us
  starting transfers between devices  36.2 us (49%)
  waiting for transfers between devices  18.5 us (25%)
  Pallas kernels  11.9 us (16%)
  local copies, waits for them, and re-layouts  4.7 us (6%)
  matrix products  1.27 us (2%)
  between operations  0.84 us (1%)
    ppermute x29, starting transfers between devices, swap(): lax.ppermute(x, everyone, [(i, i ^ mask) for i in range(dp_count * mp_cou...  30.2 us
    ppermute x29, waiting for transfers between devices, swap(): lax.ppermute(x, everyone, [(i, i ^ mask) for i in range(dp_count * mp_cou...  18.5 us
    pallas_call x10, Pallas kernels, call(): pl.pallas_call(body, out_shape=out, in_specs=specs, out_specs=[pl.BlockSp...  11.9 us
    all_to_all x1, starting transfers between devices, local(): slots = lax.all_to_all(sent, 'dp', split_axis=0, concat_axis=0, tiled=True)  6.02 us
    unnamed x16, local copies, waits for them, and re-layouts  3.94 us
  transfers between devices with their start and end apart: 30, of which 11 were waited for; matrix products, arithmetic and copies ran while one was open for 1% of the time, Pallas kernels for 12%

profile of v3, /device:TPU:0, one launch (start us, length us, event | category | flops | bytes accessed | tf_op | source)
XLA Modules:
  0.0 73.6 jit_solution(11547449397430925944)
XLA Ops:
  0.6 1.3 %convolution_convert_fusion = bf16[128,512]{1,0:T(8,128)(2,1)S(1)} fusion(bf16[128,320]{0,1:T(8,128)(2,1)} %param.17, bf16[512,320]{0,1:T(8,128)(2,1)} %param.16), kind=kOutput, calls=%fused_computation | convolution fusion | flops 42008576 | bytes 540672 | tf_op jit(solution)/shard_map/dot_general | solution.py:355
  1.9 3.0 %collective-permute-start.4 = (bf16[128,512]{1,0:T(8,128)(2,1)S(1)}, bf16[128,512]{1,0:T(8,128)(2,1)S(1)}, u32[]{:S(2)}, u32[]{:S(2)}) collective-permute-start(bf16[128,512]{1,0:T(8,128)(2,1)S(1)} %convolution_convert_fusion), channel_id=1, source_target_pairs={{0,2},{1,3},{2,0},{3,1},{4,6},{5,7},{6,4},{7,5},{8,10},{9,11},{10,... | collective-permute-start | bytes 393224 | tf_op jit(solution)/shard_map/ppermute | solution.py:313
  5.0 3.5 %collective-permute-done.4 = bf16[128,512]{1,0:T(8,128)(2,1)S(1)} collective-permute-done((bf16[128,512]{1,0:T(8,128)(2,1)S(1)}, bf16[128,512]{1,0:T(8,128)(2,1)S(1)}, u32[]{:S(2)}, u32[]{:S(2)}) %collective-permute-start.4) | collective-permute-done | bytes 131104 | tf_op jit(solution)/shard_map/ppermute | solution.py:313
  8.6 0.8 %concatenate.6.me_ref = s32[28]{0:T(128)S(1)} concatenate(s32[1]{0:T(128)} %bitcast, s32[1]{0:T(128)} %bitcast.1, s32[1]{0:T(128)} %bitcast.2, s32[1]{0:T(128)} %bitcast.3, s32[8]{0:T(128)} %param.10, s32[8]{0:T(128)} %param.11, s32[8]{0:T(128)} %param.12), dimensions={0} | concatenate | bytes 224 | tf_op jit(solution)/shard_map/concatenate | solution.py:320
  9.3 0.6 shard_map.128
  9.9 1.8 %collective-permute-start = (s32[2,128]{1,0:T(2,128)S(1)}, s32[2,128]{1,0:T(2,128)S(1)}, u32[]{:S(2)}, u32[]{:S(2)}) collective-permute-start(s32[2,128]{1,0:T(2,128)S(1)} %shard_map.128), channel_id=1, source_target_pairs={{0,4},{1,5},{2,6},{3,7},{4,0},{5,1},{6,2},{7,3},{8,12},{9,13},{10,... | collective-permute-start | bytes 3080 | tf_op jit(solution)/shard_map/ppermute | solution.py:313
  11.7 1.9 %collective-permute-done = s32[2,128]{1,0:T(2,128)S(1)} collective-permute-done((s32[2,128]{1,0:T(2,128)S(1)}, s32[2,128]{1,0:T(2,128)S(1)}, u32[]{:S(2)}, u32[]{:S(2)}) %collective-permute-start) | collective-permute-done | bytes 1056 | tf_op jit(solution)/shard_map/ppermute | solution.py:313
  13.5 3.8 %collective-permute-start.3 = (s32[2,128]{1,0:T(2,128)S(1)}, s32[2,128]{1,0:T(2,128)S(1)}, u32[]{:S(2)}, u32[]{:S(2)}) collective-permute-start(s32[2,128]{1,0:T(2,128)S(1)} %add.17), channel_id=1, source_target_pairs={{0,24},{1,25},{2,26},{3,27},{4,28},{5,29},{6,30},{7,31},{8,16},{9,... | collective-permute-start | bytes 3080 | tf_op jit(solution)/shard_map/ppermute | solution.py:313
  17.4 0.6 collective-permute-start.1
  17.9 1.6 %copy-done = bf16[2,1024,512]{2,1,0:T(8,128)(2,1)S(1)} copy-done((bf16[2,1024,512]{2,1,0:T(8,128)(2,1)S(1)}, bf16[2,1024,512]{2,1,0:T(8,128)(2,1)}, u32[]{:S(2)}) %copy-start) | copy-done | bytes 2097176
  19.5 0.9 %copy-done.4 = bf16[8,32,512]{2,1,0:T(8,128)(2,1)S(1)} copy-done((bf16[8,32,512]{2,1,0:T(8,128)(2,1)S(1)}, bf16[8,32,512]{2,1,0:T(8,128)(2,1)}, u32[]{:S(2)}) %copy-start.4) | copy-done | bytes 262168
  20.5 0.7 copy-done.5
  21.2 0.7 copy-done.7
  21.9 1.7 %shard_map.129 = (bf16[32,512]{1,0:T(8,128)(2,1)S(1)}, f32[64,512]{1,0:T(8,128)S(1)}, f32[32,512]{1,0:T(8,128)S(1)}, f32[64,512]{1,0:T(8,128)S(1)}, f32[32,512]{...) custom-call(s32[28]{0:T(128)S(1)} %concatenate.6.me_ref, ...), custom_call_target="tpu_custom_call" | custom-call | flops 100663296 | bytes 2367600 | tf_op jit(solution)/shard_map/pallas_call | solution.py:24
  23.6 1.4 %shard_map.130 = bf16[8,16,512]{2,1,0:T(8,128)(2,1)} custom-call(s32[8,128]{1,0:T(8,128)S(1)} %pad_add_fusion.got_ref, s32[28]{0:T(128)S(1)} %concatenate.6.me_ref, bf16[128,512]{1,0:T(8,128)(2,1)S(1)} %add_convert_fusion.mine_ref, bf16[128,512]{1,0:T(8,128)(2,1)S(1)} %collective-permute-done.5.other_ref, bf16[32,512]{1,0:T(8,128)(2,1)S(1)} %get-tuple-element.43.frames_ref), custom_call_target="tpu_custom_call" | custom-call | bytes 299120 | tf_op jit(solution)/shard_map/pallas_call | solution.py:24
  25.0 6.0 %all-to-all-start = ((bf16[8,16,512]{2,1,0:T(8,128)(2,1)}), bf16[8,16,512]{2,1,0:T(8,128)(2,1)S(1)}, u32[]{:S(2)}, u32[]{:S(2)}) async-start(bf16[8,16,512]{2,1,0:T(8,128)(2,1)} %shard_map.130), calls=%async_computation | async-start | bytes 262144 | tf_op jit(solution)/shard_map/all_to_all | solution.py:369
  31.0 1.6 %collective-permute-start.7 = (bf16[128,128]{1,0:T(8,128)(2,1)S(1)}, bf16[128,128]{1,0:T(8,128)(2,1)S(1)}, u32[]{:S(2)}, u32[]{:S(2)}) collective-permute-start(bf16[128,128]{1,0:T(8,128)(2,1)S(1)} %get-tuple-element.46), channel_id=1, source_target_pairs={{0,2},{1,3},{2,0},{3,1},{4,6},{5,7},{6,4},{7,5},{8,10},{9,11},{10,... | collective-permute-start | bytes 98312 | tf_op jit(solution)/shard_map/ppermute | solution.py:313
  32.6 0.3 collective-permute-start.8
  32.9 2.0 %collective-permute-start.9 = (bf16[128,128]{1,0:T(8,128)(2,1)S(1)}, bf16[128,128]{1,0:T(8,128)(2,1)S(1)}, u32[]{:S(2)}, u32[]{:S(2)}) collective-permute-start(bf16[128,128]{1,0:T(8,128)(2,1)S(1)} %get-tuple-element.48), channel_id=1, source_target_pairs={{0,4},{1,5},{2,6},{3,7},{4,0},{5,1},{6,2},{7,3},{8,12},{9,13},{10,... | collective-permute-start | bytes 98312 | tf_op jit(solution)/shard_map/ppermute | solution.py:313
  34.9 2.6 %collective-permute-start.11 = (bf16[128,128]{1,0:T(8,128)(2,1)S(1)}, bf16[128,128]{1,0:T(8,128)(2,1)S(1)}, u32[]{:S(2)}, u32[]{:S(2)}) collective-permute-start(bf16[128,128]{1,0:T(8,128)(2,1)S(1)} %get-tuple-element.50), channel_id=1, source_target_pairs={{0,6},{1,7},{2,4},{3,5},{4,2},{5,3},{6,0},{7,1},{8,14},{9,15},{10,... | collective-permute-start | bytes 98312 | tf_op jit(solution)/shard_map/ppermute | solution.py:313
  37.7 0.9 %collective-permute-done.10.refs_13_ = bf16[128,128]{1,0:T(8,128)(2,1)S(1)} collective-permute-done((bf16[128,128]{1,0:T(8,128)(2,1)S(1)}, bf16[128,128]{1,0:T(8,128)(2,1)S(1)}, u32[]{:S(2)}, u32[]{:S(2)}) %collective-permute-start.10) | collective-permute-done | bytes 32800 | tf_op jit(solution)/shard_map/ppermute | solution.py:313
  38.6 1.8 %collective-permute-done.11.refs_14_ = bf16[128,128]{1,0:T(8,128)(2,1)S(1)} collective-permute-done((bf16[128,128]{1,0:T(8,128)(2,1)S(1)}, bf16[128,128]{1,0:T(8,128)(2,1)S(1)}, u32[]{:S(2)}, u32[]{:S(2)}) %collective-permute-start.11) | collective-permute-done | bytes 32800 | tf_op jit(solution)/shard_map/ppermute | solution.py:313
  40.4 1.3 %collective-permute-done.12.refs_15_ = bf16[128,128]{1,0:T(8,128)(2,1)S(1)} collective-permute-done((bf16[128,128]{1,0:T(8,128)(2,1)S(1)}, bf16[128,128]{1,0:T(8,128)(2,1)S(1)}, u32[]{:S(2)}, u32[]{:S(2)}) %collective-permute-start.12) | collective-permute-done | bytes 32800 | tf_op jit(solution)/shard_map/ppermute | solution.py:313
  41.7 0.7 %shard_map.131 = bf16[128,512]{1,0:T(8,128)(2,1)S(1)} custom-call(s32[8,128]{1,0:T(8,128)S(1)} %pad_add_fusion.got_ref, s32[28]{0:T(128)S(1)} %concatenate.6.me_ref, bf16[8,16,512]{2,1,0:T(8,128)(2,1)S(1)} %all-to-all-done.slots_ref), custom_call_target="tpu_custom_call" | custom-call | bytes 135280 | tf_op jit(solution)/shard_map/pallas_call | solution.py:24
  42.5 0.6 collective-permute-start.13
  43.0 1.1 %shard_map.133.grad_ref.refs_0_ = bf16[112,512]{1,0:T(8,128)(2,1)S(1)} custom-call(s32[28]{0:T(128)S(1)} %concatenate.6.me_ref, bf16[8,16,512]{2,1,0:T(8,128)(2,1)S(1)} %all-to-all-done.slots_ref, f32[64,512]{1,0:T(8,128)S(1)} %get-tuple-element.54.slope1_ref, f32[32,512]{1,0:T(8,128)S(1)} %get-tuple-element.55.slope2_ref, ...), custom_call_target="tpu_custom_call" | custom-call | flops 33554432 | bytes 2674800 | tf_op jit(solution)/shard_map/pallas_call | solution.py:24
  44.1 1.7 %collective-permute-start.20 = (bf16[112,512]{1,0:T(8,128)(2,1)S(1)}, bf16[112,512]{1,0:T(8,128)(2,1)S(1)}, u32[]{:S(2)}, u32[]{:S(2)}) collective-permute-start(bf16[112,512]{1,0:T(8,128)(2,1)S(1)} %shard_map.133.grad_ref.refs_0_), channel_id=1, source_target_pairs={{0,6},{1,7},{2,4},{3,5},{4,2},{5,3},{6,0},{7,1},{8,14},{9,15},{10,... | collective-permute-start | bytes 344072 | tf_op jit(solution)/shard_map/ppermute | solution.py:313
  45.9 1.3 %collective-permute-start.18 = (bf16[112,512]{1,0:T(8,128)(2,1)S(1)}, bf16[112,512]{1,0:T(8,128)(2,1)S(1)}, u32[]{:S(2)}, u32[]{:S(2)}) collective-permute-start(bf16[112,512]{1,0:T(8,128)(2,1)S(1)} %shard_map.133.grad_ref.refs_0_), channel_id=1, source_target_pairs={{0,4},{1,5},{2,6},{3,7},{4,0},{5,1},{6,2},{7,3},{8,12},{9,13},{10,... | collective-permute-start | bytes 344072 | tf_op jit(solution)/shard_map/ppermute | solution.py:313
  47.2 0.5 collective-permute-start.16
  47.7 3.2 %collective-permute-done.13 = bf16[128,512]{1,0:T(8,128)(2,1)S(1)} collective-permute-done((bf16[128,512]{1,0:T(8,128)(2,1)S(1)}, bf16[128,512]{1,0:T(8,128)(2,1)S(1)}, u32[]{:S(2)}, u32[]{:S(2)}) %collective-permute-start.13) | collective-permute-done | bytes 131104 | tf_op jit(solution)/shard_map/ppermute | solution.py:313
  51.0 0.5 collective-permute-start.15
  51.6 1.1 %collective-permute-done.18.refs_4_ = bf16[112,512]{1,0:T(8,128)(2,1)S(1)} collective-permute-done((bf16[112,512]{1,0:T(8,128)(2,1)S(1)}, bf16[112,512]{1,0:T(8,128)(2,1)S(1)}, u32[]{:S(2)}, u32[]{:S(2)}) %collective-permute-start.18) | collective-permute-done | bytes 114720 | tf_op jit(solution)/shard_map/ppermute | solution.py:313
  52.6 0.5 collective-permute-done.16.refs_2_
  53.1 1.5 %shard_map.132 = (bf16[320,128]{1,0:T(8,128)(2,1)}, f32[4,64,320]{2,1,0:T(8,128)S(1)}, bf16[4,64,320]{2,1,0:T(8,128)(2,1)S(1)}) custom-call(s32[28]{0:T(128)S(1)} %concatenate.6.me_ref, bf16[128,512]{1,0:T(8,128)(2,1)S(1)} %add.19.mine_ref, bf16[128,512]{1,0:T(8,128)(2,1)S(1)} %collective-permute-done.14.other_ref, bf16[320,512]{1,0:T(8,128)(2,1)S(1)} %bitcast.11, ...), custom_call_target="tpu_custom_call" | custom-call | flops 83886080 | bytes 671856 | tf_op jit(solution)/shard_map/pallas_call | solution.py:24
  54.7 0.6 collective-permute-start.25
  55.3 1.3 %shard_map.135 = (f32[72,512]{1,0:T(8,128)S(1)}, bf16[72,512]{1,0:T(8,128)(2,1)S(1)}, bf16[72,512]{1,0:T(8,128)(2,1)S(1)}, bf16[72,512]{1,0:T(8,128)(2,1)S(1)}) custom-call(s32[28]{0:T(128)S(1)} %concatenate.6.me_ref, bf16[112,512]{1,0:T(8,128)(2,1)S(1)} %shard_map.133.grad_ref.refs_0_, bf16[112,512]{1,0:T(8,128)(2,1)S(1)} %collective-permute-done.15.refs_1_, ...), custom_call_target="tpu_custom_call" | custom-call | flops 100663296 | bytes 1179760 | tf_op jit(solution)/shard_map/pallas_call | solution.py:24
  56.5 1.5 %collective-permute-start.22 = (bf16[72,512]{1,0:T(8,128)(2,1)S(1)}, bf16[72,512]{1,0:T(8,128)(2,1)S(1)}, u32[]{:S(2)}, u32[]{:S(2)}) collective-permute-start(bf16[72,512]{1,0:T(8,128)(2,1)S(1)} %get-tuple-element.69), channel_id=1, source_target_pairs={{0,8},{1,9},{2,10},{3,11},{4,12},{5,13},{6,14},{7,15},{8,0},{9,1},... | collective-permute-start | bytes 221192 | tf_op jit(solution)/shard_map/ppermute | solution.py:313
  58.0 2.4 %collective-permute-start.23 = (bf16[72,512]{1,0:T(8,128)(2,1)S(1)}, bf16[72,512]{1,0:T(8,128)(2,1)S(1)}, u32[]{:S(2)}, u32[]{:S(2)}) collective-permute-start(bf16[72,512]{1,0:T(8,128)(2,1)S(1)} %get-tuple-element.70), channel_id=1, source_target_pairs={{0,16},{1,17},{2,18},{3,19},{4,20},{5,21},{6,22},{7,23},{8,24},{9,... | collective-permute-start | bytes 221192 | tf_op jit(solution)/shard_map/ppermute | solution.py:313
  60.4 0.6 collective-permute-start.24
  61.0 0.9 %collective-permute-done.25.got_ref = bf16[4,64,320]{2,1,0:T(8,128)(2,1)S(1)} collective-permute-done((bf16[4,64,320]{2,1,0:T(8,128)(2,1)S(1)}, bf16[4,64,320]{2,1,0:T(8,128)(2,1)S(1)}, u32[]{:S(2)}, u32[]{:S(2)}) %collective-permute-start.25) | collective-permute-done | bytes 163872 | tf_op jit(solution)/shard_map/ppermute | solution.py:313
  61.9 0.6 shard_map.136
  62.5 1.5 %collective-permute-start.26 = (bf16[64,320]{1,0:T(8,128)(2,1)S(1)}, bf16[64,320]{1,0:T(8,128)(2,1)S(1)}, u32[]{:S(2)}, u32[]{:S(2)}) collective-permute-start(bf16[64,320]{1,0:T(8,128)(2,1)S(1)} %get-tuple-element.75), channel_id=1, source_target_pairs={{0,8},{1,9},{2,10},{3,11},{4,12},{5,13},{6,14},{7,15},{8,0},{9,1},... | collective-permute-start | bytes 122888 | tf_op jit(solution)/shard_map/ppermute | solution.py:313
  64.0 2.4 %collective-permute-start.27 = (bf16[64,320]{1,0:T(8,128)(2,1)S(1)}, bf16[64,320]{1,0:T(8,128)(2,1)S(1)}, u32[]{:S(2)}, u32[]{:S(2)}) collective-permute-start(bf16[64,320]{1,0:T(8,128)(2,1)S(1)} %get-tuple-element.76), channel_id=1, source_target_pairs={{0,16},{1,17},{2,18},{3,19},{4,20},{5,21},{6,22},{7,23},{8,24},{9,... | collective-permute-start | bytes 122888 | tf_op jit(solution)/shard_map/ppermute | solution.py:313
  66.4 0.6 collective-permute-start.28
  67.0 1.9 %shard_map.134 = bf16[256,512]{1,0:T(8,128)(2,1)} custom-call(s32[28]{0:T(128)S(1)} %concatenate.6.me_ref, bf16[112,512]{1,0:T(8,128)(2,1)S(1)} %shard_map.133.grad_ref.refs_0_, bf16[2,1024,512]{2,1,0:T(8,128)(2,1)S(1)} %copy-done.1), custom_call_target="tpu_custom_call" | custom-call | flops 67108864 | bytes 2211952 | tf_op jit(solution)/shard_map/pallas_call | solution.py:24
  68.9 2.1 %collective-permute-done.27.refs_6_ = bf16[64,320]{1,0:T(8,128)(2,1)S(1)} collective-permute-done((bf16[64,320]{1,0:T(8,128)(2,1)S(1)}, bf16[64,320]{1,0:T(8,128)(2,1)S(1)}, u32[]{:S(2)}, u32[]{:S(2)}) %collective-permute-start.27) | collective-permute-done | bytes 40992 | tf_op jit(solution)/shard_map/ppermute | solution.py:313
  70.9 1.4 %collective-permute-done.28.refs_7_ = bf16[64,320]{1,0:T(8,128)(2,1)S(1)} collective-permute-done((bf16[64,320]{1,0:T(8,128)(2,1)S(1)}, bf16[64,320]{1,0:T(8,128)(2,1)S(1)}, u32[]{:S(2)}, u32[]{:S(2)}) %collective-permute-start.28) | collective-permute-done | bytes 40992 | tf_op jit(solution)/shard_map/ppermute | solution.py:313
  72.3 1.3 %shard_map.137 = (f32[2,32,512]{2,1,0:T(8,128)}, f32[2,32]{1,0:T(2,128)}, f32[64,320]{1,0:T(8,128)}) custom-call(s32[28]{0:T(128)S(1)} %concatenate.6.me_ref, f32[72,512]{1,0:T(8,128)S(1)} %get-tuple-element.68.refs_0_, bf16[72,512]{1,0:T(8,128)(2,1)S(1)} %collective-permute-done.22.refs_1_, bf16[72,512]{1,0:T(8,128)(2,1)S(1)} %collective-permute-done.23.refs_2_, ...), custom_call_target="tpu_custom_call" | custom-call | bytes 573552 | tf_op jit(solution)/shard_map/pallas_call | solution.py:24
  (44 shorter events, 0.6 us)
Async XLA Ops:
  0.6 42.4 %copy-start.6 = (f32[2,512]{1,0:T(2,128)S(1)}, f32[2,512]{1,0:T(2,128)}, u32[]{:S(2)}) copy-start(f32[2,512]{1,0:T(2,128)} %gain_ref.3) | copy-start | bytes 12292
  1.9 6.5 %collective-permute-start.4 = (bf16[128,512]{1,0:T(8,128)(2,1)S(1)}, bf16[128,512]{1,0:T(8,128)(2,1)S(1)}, u32[]{:S(2)}, u32[]{:S(2)}) collective-permute-start(bf16[128,512]{1,0:T(8,128)(2,1)S(1)} %convolution_convert_fusion), channel_id=1, source_target_pairs={{0,2},{1,3},{2,0},{3,1},{4,6},{5,7},{6,4},{7,5},{8,10},{9,11},{10,... | collective-permute-start | bytes 393224 | tf_op jit(solution)/shard_map/ppermute | solution.py:313
  8.5 15.1 %collective-permute-start.5 = (bf16[128,512]{1,0:T(8,128)(2,1)S(1)}, bf16[128,512]{1,0:T(8,128)(2,1)S(1)}, u32[]{:S(2)}, u32[]{:S(2)}) collective-permute-start(bf16[128,512]{1,0:T(8,128)(2,1)S(1)} %add_convert_fusion.mine_ref), channel_id=1, source_target_pairs={{0,1},{1,0},{2,3},{3,2},{4,5},{5,4},{6,7},{7,6},{8,9},{9,8},{10,11... | collective-permute-start | bytes 393224 | tf_op jit(solution)/shard_map/ppermute | solution.py:313
  9.9 3.6 %collective-permute-start = (s32[2,128]{1,0:T(2,128)S(1)}, s32[2,128]{1,0:T(2,128)S(1)}, u32[]{:S(2)}, u32[]{:S(2)}) collective-permute-start(s32[2,128]{1,0:T(2,128)S(1)} %shard_map.128), channel_id=1, source_target_pairs={{0,4},{1,5},{2,6},{3,7},{4,0},{5,1},{6,2},{7,3},{8,12},{9,13},{10,... | collective-permute-start | bytes 3080 | tf_op jit(solution)/shard_map/ppermute | solution.py:313
  13.5 10.0 %collective-permute-start.3 = (s32[2,128]{1,0:T(2,128)S(1)}, s32[2,128]{1,0:T(2,128)S(1)}, u32[]{:S(2)}, u32[]{:S(2)}) collective-permute-start(s32[2,128]{1,0:T(2,128)S(1)} %add.17), channel_id=1, source_target_pairs={{0,24},{1,25},{2,26},{3,27},{4,28},{5,29},{6,30},{7,31},{8,16},{9,... | collective-permute-start | bytes 3080 | tf_op jit(solution)/shard_map/ppermute | solution.py:313
  17.4 6.2 %collective-permute-start.2 = (s32[2,128]{1,0:T(2,128)S(1)}, s32[2,128]{1,0:T(2,128)S(1)}, u32[]{:S(2)}, u32[]{:S(2)}) collective-permute-start(s32[2,128]{1,0:T(2,128)S(1)} %add.17), channel_id=1, source_target_pairs={{0,16},{1,17},{2,18},{3,19},{4,20},{5,21},{6,22},{7,23},{8,24},{9,... | collective-permute-start | bytes 3080 | tf_op jit(solution)/shard_map/ppermute | solution.py:313
  17.4 6.2 %collective-permute-start.1 = (s32[2,128]{1,0:T(2,128)S(1)}, s32[2,128]{1,0:T(2,128)S(1)}, u32[]{:S(2)}, u32[]{:S(2)}) collective-permute-start(s32[2,128]{1,0:T(2,128)S(1)} %add.17), channel_id=1, source_target_pairs={{0,8},{1,9},{2,10},{3,11},{4,12},{5,13},{6,14},{7,15},{8,0},{9,1},... | collective-permute-start | bytes 3080 | tf_op jit(solution)/shard_map/ppermute | solution.py:313
  17.9 1.6 %copy-start = (bf16[2,1024,512]{2,1,0:T(8,128)(2,1)S(1)}, bf16[2,1024,512]{2,1,0:T(8,128)(2,1)}, u32[]{:S(2)}) copy-start(bf16[2,1024,512]{2,1,0:T(8,128)(2,1)} %weight_ref.5) | copy-start | bytes 6291460
  19.5 0.9 %copy-start.4 = (bf16[8,32,512]{2,1,0:T(8,128)(2,1)S(1)}, bf16[8,32,512]{2,1,0:T(8,128)(2,1)}, u32[]{:S(2)}) copy-start(bf16[8,32,512]{2,1,0:T(8,128)(2,1)} %param.9) | copy-start | bytes 786436
  20.5 0.7 copy-start.5
  21.2 0.7 copy-start.7
  21.8 21.2 %copy-start.1 = (bf16[2,1024,512]{2,1,0:T(8,128)(2,1)S(1)}, bf16[2,1024,512]{2,1,0:T(8,128)(2,1)}, u32[]{:S(2)}) copy-start(bf16[2,1024,512]{2,1,0:T(8,128)(2,1)} %weight_ref.5) | copy-start | bytes 6291460
  23.5 29.6 %copy-start.2 = (bf16[512,320]{0,1:T(8,128)(2,1)S(1)}, bf16[512,320]{0,1:T(8,128)(2,1)}, u32[]{:S(2)}) copy-start(bf16[512,320]{0,1:T(8,128)(2,1)} %param.16) | copy-start | bytes 983044
  23.5 29.6 %copy-start.3 = (bf16[128,320]{0,1:T(8,128)(2,1)S(1)}, bf16[128,320]{0,1:T(8,128)(2,1)}, u32[]{:S(2)}) copy-start(bf16[128,320]{0,1:T(8,128)(2,1)} %param.17) | copy-start | bytes 245764
  25.0 16.7 %all-to-all-start = ((bf16[8,16,512]{2,1,0:T(8,128)(2,1)}), bf16[8,16,512]{2,1,0:T(8,128)(2,1)S(1)}, u32[]{:S(2)}, u32[]{:S(2)}) async-start(bf16[8,16,512]{2,1,0:T(8,128)(2,1)} %shard_map.130), calls=%async_computation | async-start | bytes 262144 | tf_op jit(solution)/shard_map/all_to_all | solution.py:369
  31.0 3.9 %collective-permute-start.6 = (bf16[128,128]{1,0:T(8,128)(2,1)S(1)}, bf16[128,128]{1,0:T(8,128)(2,1)S(1)}, u32[]{:S(2)}, u32[]{:S(2)}) collective-permute-start(bf16[128,128]{1,0:T(8,128)(2,1)S(1)} %get-tuple-element.45), channel_id=1, source_target_pairs={{0,1},{1,0},{2,3},{3,2},{4,5},{5,4},{6,7},{7,6},{8,9},{9,8},{10,11... | collective-permute-start | bytes 98312 | tf_op jit(solution)/shard_map/ppermute | solution.py:313
  31.0 6.5 %collective-permute-start.7 = (bf16[128,128]{1,0:T(8,128)(2,1)S(1)}, bf16[128,128]{1,0:T(8,128)(2,1)S(1)}, u32[]{:S(2)}, u32[]{:S(2)}) collective-permute-start(bf16[128,128]{1,0:T(8,128)(2,1)S(1)} %get-tuple-element.46), channel_id=1, source_target_pairs={{0,2},{1,3},{2,0},{3,1},{4,6},{5,7},{6,4},{7,5},{8,10},{9,11},{10,... | collective-permute-start | bytes 98312 | tf_op jit(solution)/shard_map/ppermute | solution.py:313
  32.6 5.1 %collective-permute-start.8 = (bf16[128,128]{1,0:T(8,128)(2,1)S(1)}, bf16[128,128]{1,0:T(8,128)(2,1)S(1)}, u32[]{:S(2)}, u32[]{:S(2)}) collective-permute-start(bf16[128,128]{1,0:T(8,128)(2,1)S(1)} %get-tuple-element.47), channel_id=1, source_target_pairs={{0,3},{1,2},{2,1},{3,0},{4,7},{5,6},{6,5},{7,4},{8,11},{9,10},{10,... | collective-permute-start | bytes 98312 | tf_op jit(solution)/shard_map/ppermute | solution.py:313
  32.9 4.8 %collective-permute-start.9 = (bf16[128,128]{1,0:T(8,128)(2,1)S(1)}, bf16[128,128]{1,0:T(8,128)(2,1)S(1)}, u32[]{:S(2)}, u32[]{:S(2)}) collective-permute-start(bf16[128,128]{1,0:T(8,128)(2,1)S(1)} %get-tuple-element.48), channel_id=1, source_target_pairs={{0,4},{1,5},{2,6},{3,7},{4,0},{5,1},{6,2},{7,3},{8,12},{9,13},{10,... | collective-permute-start | bytes 98312 | tf_op jit(solution)/shard_map/ppermute | solution.py:313
  34.9 3.7 %collective-permute-start.10 = (bf16[128,128]{1,0:T(8,128)(2,1)S(1)}, bf16[128,128]{1,0:T(8,128)(2,1)S(1)}, u32[]{:S(2)}, u32[]{:S(2)}) collective-permute-start(bf16[128,128]{1,0:T(8,128)(2,1)S(1)} %get-tuple-element.49), channel_id=1, source_target_pairs={{0,5},{1,4},{2,7},{3,6},{4,1},{5,0},{6,3},{7,2},{8,13},{9,12},{10,... | collective-permute-start | bytes 98312 | tf_op jit(solution)/shard_map/ppermute | solution.py:313
  34.9 5.5 %collective-permute-start.11 = (bf16[128,128]{1,0:T(8,128)(2,1)S(1)}, bf16[128,128]{1,0:T(8,128)(2,1)S(1)}, u32[]{:S(2)}, u32[]{:S(2)}) collective-permute-start(bf16[128,128]{1,0:T(8,128)(2,1)S(1)} %get-tuple-element.50), channel_id=1, source_target_pairs={{0,6},{1,7},{2,4},{3,5},{4,2},{5,3},{6,0},{7,1},{8,14},{9,15},{10,... | collective-permute-start | bytes 98312 | tf_op jit(solution)/shard_map/ppermute | solution.py:313
  37.5 4.2 %collective-permute-start.12 = (bf16[128,128]{1,0:T(8,128)(2,1)S(1)}, bf16[128,128]{1,0:T(8,128)(2,1)S(1)}, u32[]{:S(2)}, u32[]{:S(2)}) collective-permute-start(bf16[128,128]{1,0:T(8,128)(2,1)S(1)} %get-tuple-element.51), channel_id=1, source_target_pairs={{0,7},{1,6},{2,5},{3,4},{4,3},{5,2},{6,1},{7,0},{8,15},{9,14},{10,... | collective-permute-start | bytes 98312 | tf_op jit(solution)/shard_map/ppermute | solution.py:313
  42.5 8.4 %collective-permute-start.13 = (bf16[128,512]{1,0:T(8,128)(2,1)S(1)}, bf16[128,512]{1,0:T(8,128)(2,1)S(1)}, u32[]{:S(2)}, u32[]{:S(2)}) collective-permute-start(bf16[128,512]{1,0:T(8,128)(2,1)S(1)} %shard_map.131), channel_id=1, source_target_pairs={{0,2},{1,3},{2,0},{3,1},{4,6},{5,7},{6,4},{7,5},{8,10},{9,11},{10,... | collective-permute-start | bytes 393224 | tf_op jit(solution)/shard_map/ppermute | solution.py:313
  44.1 7.3 %collective-permute-start.20 = (bf16[112,512]{1,0:T(8,128)(2,1)S(1)}, bf16[112,512]{1,0:T(8,128)(2,1)S(1)}, u32[]{:S(2)}, u32[]{:S(2)}) collective-permute-start(bf16[112,512]{1,0:T(8,128)(2,1)S(1)} %shard_map.133.grad_ref.refs_0_), channel_id=1, source_target_pairs={{0,6},{1,7},{2,4},{3,5},{4,2},{5,3},{6,0},{7,1},{8,14},{9,15},{10,... | collective-permute-start | bytes 344072 | tf_op jit(solution)/shard_map/ppermute | solution.py:313
  45.9 6.8 %collective-permute-start.18 = (bf16[112,512]{1,0:T(8,128)(2,1)S(1)}, bf16[112,512]{1,0:T(8,128)(2,1)S(1)}, u32[]{:S(2)}, u32[]{:S(2)}) collective-permute-start(bf16[112,512]{1,0:T(8,128)(2,1)S(1)} %shard_map.133.grad_ref.refs_0_), channel_id=1, source_target_pairs={{0,4},{1,5},{2,6},{3,7},{4,0},{5,1},{6,2},{7,3},{8,12},{9,13},{10,... | collective-permute-start | bytes 344072 | tf_op jit(solution)/shard_map/ppermute | solution.py:313
  47.2 5.9 %collective-permute-start.16 = (bf16[112,512]{1,0:T(8,128)(2,1)S(1)}, bf16[112,512]{1,0:T(8,128)(2,1)S(1)}, u32[]{:S(2)}, u32[]{:S(2)}) collective-permute-start(bf16[112,512]{1,0:T(8,128)(2,1)S(1)} %shard_map.133.grad_ref.refs_0_), channel_id=1, source_target_pairs={{0,2},{1,3},{2,0},{3,1},{4,6},{5,7},{6,4},{7,5},{8,10},{9,11},{10,... | collective-permute-start | bytes 344072 | tf_op jit(solution)/shard_map/ppermute | solution.py:313
  50.9 2.2 %collective-permute-start.14 = (bf16[128,512]{1,0:T(8,128)(2,1)S(1)}, bf16[128,512]{1,0:T(8,128)(2,1)S(1)}, u32[]{:S(2)}, u32[]{:S(2)}) collective-permute-start(bf16[128,512]{1,0:T(8,128)(2,1)S(1)} %add.19.mine_ref), channel_id=1, source_target_pairs={{0,1},{1,0},{2,3},{3,2},{4,5},{5,4},{6,7},{7,6},{8,9},{9,8},{10,11... | collective-permute-start | bytes 393224 | tf_op jit(solution)/shard_map/ppermute | solution.py:313
  51.0 4.3 %collective-permute-start.15 = (bf16[112,512]{1,0:T(8,128)(2,1)S(1)}, bf16[112,512]{1,0:T(8,128)(2,1)S(1)}, u32[]{:S(2)}, u32[]{:S(2)}) collective-permute-start(bf16[112,512]{1,0:T(8,128)(2,1)S(1)} %shard_map.133.grad_ref.refs_0_), channel_id=1, source_target_pairs={{0,1},{1,0},{2,3},{3,2},{4,5},{5,4},{6,7},{7,6},{8,9},{9,8},{10,11... | collective-permute-start | bytes 344072 | tf_op jit(solution)/shard_map/ppermute | solution.py:313
  51.5 3.8 %collective-permute-start.21 = (bf16[112,512]{1,0:T(8,128)(2,1)S(1)}, bf16[112,512]{1,0:T(8,128)(2,1)S(1)}, u32[]{:S(2)}, u32[]{:S(2)}) collective-permute-start(bf16[112,512]{1,0:T(8,128)(2,1)S(1)} %collective-permute-done.20.refs_6_), channel_id=1, source_target_pairs={{0,1},{1,0},{2,3},{3,2},{4,5},{5,4},{6,7},{7,6},{8,9},{9,8},{10,11... | collective-permute-start | bytes 344072 | tf_op jit(solution)/shard_map/ppermute | solution.py:313
  52.6 2.6 %collective-permute-start.19 = (bf16[112,512]{1,0:T(8,128)(2,1)S(1)}, bf16[112,512]{1,0:T(8,128)(2,1)S(1)}, u32[]{:S(2)}, u32[]{:S(2)}) collective-permute-start(bf16[112,512]{1,0:T(8,128)(2,1)S(1)} %collective-permute-done.18.refs_4_), channel_id=1, source_target_pairs={{0,1},{1,0},{2,3},{3,2},{4,5},{5,4},{6,7},{7,6},{8,9},{9,8},{10,11... | collective-permute-start | bytes 344072 | tf_op jit(solution)/shard_map/ppermute | solution.py:313
  53.1 2.2 %collective-permute-start.17 = (bf16[112,512]{1,0:T(8,128)(2,1)S(1)}, bf16[112,512]{1,0:T(8,128)(2,1)S(1)}, u32[]{:S(2)}, u32[]{:S(2)}) collective-permute-start(bf16[112,512]{1,0:T(8,128)(2,1)S(1)} %collective-permute-done.16.refs_2_), channel_id=1, source_target_pairs={{0,1},{1,0},{2,3},{3,2},{4,5},{5,4},{6,7},{7,6},{8,9},{9,8},{10,11... | collective-permute-start | bytes 344072 | tf_op jit(solution)/shard_map/ppermute | solution.py:313
  54.7 7.3 %collective-permute-start.25 = (bf16[4,64,320]{2,1,0:T(8,128)(2,1)S(1)}, bf16[4,64,320]{2,1,0:T(8,128)(2,1)S(1)}, u32[]{:S(2)}, u32[]{:S(2)}) collective-permute-start(bf16[4,64,320]{2,1,0:T(8,128)(2,1)S(1)} %get-tuple-element.73), channel_id=1, source_target_pairs={{0,4},{1,5},{2,6},{3,7},{4,0},{5,1},{6,2},{7,3},{8,12},{9,13},{10,... | collective-permute-start | bytes 491528 | tf_op jit(solution)/shard_map/ppermute | solution.py:313
  56.5 9.9 %collective-permute-start.22 = (bf16[72,512]{1,0:T(8,128)(2,1)S(1)}, bf16[72,512]{1,0:T(8,128)(2,1)S(1)}, u32[]{:S(2)}, u32[]{:S(2)}) collective-permute-start(bf16[72,512]{1,0:T(8,128)(2,1)S(1)} %get-tuple-element.69), channel_id=1, source_target_pairs={{0,8},{1,9},{2,10},{3,11},{4,12},{5,13},{6,14},{7,15},{8,0},{9,1},... | collective-permute-start | bytes 221192 | tf_op jit(solution)/shard_map/ppermute | solution.py:313
  58.0 10.8 %collective-permute-start.23 = (bf16[72,512]{1,0:T(8,128)(2,1)S(1)}, bf16[72,512]{1,0:T(8,128)(2,1)S(1)}, u32[]{:S(2)}, u32[]{:S(2)}) collective-permute-start(bf16[72,512]{1,0:T(8,128)(2,1)S(1)} %get-tuple-element.70), channel_id=1, source_target_pairs={{0,16},{1,17},{2,18},{3,19},{4,20},{5,21},{6,22},{7,23},{8,24},{9,... | collective-permute-start | bytes 221192 | tf_op jit(solution)/shard_map/ppermute | solution.py:313
  60.4 8.4 %collective-permute-start.24 = (bf16[72,512]{1,0:T(8,128)(2,1)S(1)}, bf16[72,512]{1,0:T(8,128)(2,1)S(1)}, u32[]{:S(2)}, u32[]{:S(2)}) collective-permute-start(bf16[72,512]{1,0:T(8,128)(2,1)S(1)} %get-tuple-element.71), channel_id=1, source_target_pairs={{0,24},{1,25},{2,26},{3,27},{4,28},{5,29},{6,30},{7,31},{8,16},{9,... | collective-permute-start | bytes 221192 | tf_op jit(solution)/shard_map/ppermute | solution.py:313
  62.5 6.3 %collective-permute-start.26 = (bf16[64,320]{1,0:T(8,128)(2,1)S(1)}, bf16[64,320]{1,0:T(8,128)(2,1)S(1)}, u32[]{:S(2)}, u32[]{:S(2)}) collective-permute-start(bf16[64,320]{1,0:T(8,128)(2,1)S(1)} %get-tuple-element.75), channel_id=1, source_target_pairs={{0,8},{1,9},{2,10},{3,11},{4,12},{5,13},{6,14},{7,15},{8,0},{9,1},... | collective-permute-start | bytes 122888 | tf_op jit(solution)/shard_map/ppermute | solution.py:313
  64.0 6.9 %collective-permute-start.27 = (bf16[64,320]{1,0:T(8,128)(2,1)S(1)}, bf16[64,320]{1,0:T(8,128)(2,1)S(1)}, u32[]{:S(2)}, u32[]{:S(2)}) collective-permute-start(bf16[64,320]{1,0:T(8,128)(2,1)S(1)} %get-tuple-element.76), channel_id=1, source_target_pairs={{0,16},{1,17},{2,18},{3,19},{4,20},{5,21},{6,22},{7,23},{8,24},{9,... | collective-permute-start | bytes 122888 | tf_op jit(solution)/shard_map/ppermute | solution.py:313
  66.4 5.9 %collective-permute-start.28 = (bf16[64,320]{1,0:T(8,128)(2,1)S(1)}, bf16[64,320]{1,0:T(8,128)(2,1)S(1)}, u32[]{:S(2)}, u32[]{:S(2)}) collective-permute-start(bf16[64,320]{1,0:T(8,128)(2,1)S(1)} %get-tuple-element.77), channel_id=1, source_target_pairs={{0,24},{1,25},{2,26},{3,27},{4,28},{5,29},{6,30},{7,31},{8,16},{9,... | collective-permute-start | bytes 122888 | tf_op jit(solution)/shard_map/ppermute | solution.py:313

commit v4 on v3

--- a/solution.py
+++ b/solution.py
@@ -15,9 +15,10 @@
 SMEM = pltpu.SMEM
 
 
-def call(body, out, args, scalars=0, flops=0, scratch=()):
+def call(body, out, args, scalars=0, fetched=0, flops=0, scratch=(), mebibytes=14, to_scalars=0):
     specs = [
-        pl.BlockSpec(memory_space=SMEM if i < scalars else VMEM) for i in range(len(args))
+        pl.BlockSpec(memory_space=SMEM if i < scalars else pl.ANY if i < scalars + fetched else VMEM)
+        for i in range(len(args))
     ]
     many = isinstance(out, (list, tuple))
     moved = sum(a.size * a.dtype.itemsize for a in args)
@@ -25,11 +26,13 @@
         body,
         out_shape=out,
         in_specs=specs,
-        out_specs=[pl.BlockSpec(memory_space=VMEM)] * len(out)
+        out_specs=[
+            pl.BlockSpec(memory_space=SMEM if i < to_scalars else VMEM) for i in range(len(out))
+        ]
         if many
         else pl.BlockSpec(memory_space=VMEM),
         scratch_shapes=list(scratch),
-        compiler_params=pltpu.CompilerParams(vmem_limit_bytes=14 * 2**20),
+        compiler_params=pltpu.CompilerParams(vmem_limit_bytes=mebibytes * 2**20),
         cost_estimate=pl.CostEstimate(flops=flops, bytes_accessed=moved, transcendentals=0),
     )(*args)
 
@@ -73,25 +76,66 @@
     return pair * (8 * frames) + 4 * t_from + off
 
 
-def index_kernel(me_ref, out_ref, *, pairs, frames):
-    row = lax.broadcasted_iota(jnp.int32, out_ref.shape, 0)
-    shard = lax.broadcasted_iota(jnp.int32, out_ref.shape, 1)
-    value = jnp.zeros(out_ref.shape, jnp.int32)
+def start_kernel(
+    place_ref, proj_hbm, cotangent_hbm, lengths_hbm, dests_hbm, offsets_hbm, me_ref, index_ref, rows_ref,
+    proj_ref, cotangent_ref, lengths_ref, dests_ref, offsets_ref, copied, *, pairs, frames
+):
+    sources = (proj_hbm, cotangent_hbm, lengths_hbm, dests_hbm, offsets_hbm)
+    targets = (proj_ref, cotangent_ref, lengths_ref, dests_ref, offsets_ref)
+    copies = [
+        pltpu.make_async_copy(source, target, copied.at[i])
+        for i, (source, target) in enumerate(zip(sources, targets))
+    ]
+    for copy in copies[::-1]:
+        copy.start()
+    for copy in copies[2:]:
+        copy.wait()
+    for i in range(4):
+        me_ref[i] = place_ref[i]
+    for i in range(2 * pairs):
+        me_ref[4 + i] = lengths_ref[i]
+        me_ref[4 + 2 * pairs + i] = dests_ref[i]
+        me_ref[4 + 4 * pairs + i] = offsets_ref[i]
+    shard = lax.broadcasted_iota(jnp.int32, index_ref.shape, 1)
+    value = jnp.zeros(index_ref.shape, jnp.int32)
     for p in range(pairs):
-        block = lax.div(me_ref[4 + 4 * pairs + 2 * p], frames)
-        value = jnp.where(shard == me_ref[4 + 2 * pairs + 2 * p], block + 1, value)
-    out_ref[...] = jnp.where(row == me_ref[3], value, 0)
+        block = lax.div(offsets_ref[2 * p], frames)
+        value = jnp.where(shard == dests_ref[2 * p], block + 1, value)
+    index_ref[...] = value
+    copies[0].wait()
+    copies[1].wait()
+    rows_ref[...] = lax.dot_general(
+        cotangent_ref[...], proj_ref[...], (((0,), (0,)), ((), ())), preferred_element_type=F32
+    ).astype(BF)
 
 
 def block_from(got_ref, me_ref, d):
-    return got_ref[2 * (me_ref[2] ^ (d // 2)) + d % 2, 2 * me_ref[2] + me_ref[3]] - 1
-
-
-def forward_kernel(
-    me_ref, feat_ref, weight_ref, gain_ref, shift_ref, *rest, pairs, frames, far, near, owned
-):
-    frames_ref, slope1_ref, slope2_ref, hat1_ref, hat2_ref, scale1_ref, scale2_ref = rest[:7]
-    turned_refs, in_turned = rest[7:-1], rest[-1]
+    return got_ref[d, 2 * me_ref[2] + me_ref[3]] - 1
+
+
+def state_views(state_ref):
+    part = state_ref.shape[0] // 9
+    spans = ((0, 2), (2, 1), (3, 2), (5, 1), (6, 2), (8, 1))
+    return [state_ref.at[a * part : (a + n) * part] for a, n in spans]
+
+
+def forward_kernel(me_ref, *refs, pairs, frames, far, near, owned):
+    weight_ref = refs[3]
+    sources = refs[:3] + (weight_ref.at[0], weight_ref.at[1])
+    rest, held, in_turned, copied = refs[4:-7], refs[-7:-2], refs[-2], refs[-1]
+    copies = [
+        pltpu.make_async_copy(source, target, copied.at[i])
+        for i, (source, target) in enumerate(zip(sources, held))
+    ]
+    for copy in copies:
+        copy.start()
+    feat_ref, gain_ref, shift_ref, first_ref, second_ref = held
+    later_ref, frames_ref, state_ref = rest[:3]
+    turned_refs = rest[3:]
+    for i in range(me_ref.shape[0]):
+        later_ref[i] = me_ref[i]
+    slope1_ref, slope2_ref, hat1_ref, hat2_ref, scale1_ref, scale2_ref = state_views(state_ref)
+    copies[0].wait()
     channels = feat_ref.shape[1]
     n2 = pairs * frames
     row = lax.broadcasted_iota(jnp.int32, (4 * n2, 1), 0)
@@ -100,8 +144,10 @@
     pick = jnp.where(place == source, 1.0, 0.0).astype(BF)
     chosen32 = dot(pick, feat_ref[...])
     chosen = chosen32.astype(BF)
+    for copy in copies[1:4]:
+        copy.wait()
     even, odd = chosen[: 2 * n2], chosen[2 * n2 :]
-    first = dot(even, weight_ref[0, :channels, :]) + dot(odd, weight_ref[0, channels:, :])
+    first = dot(even, first_ref[:channels, :]) + dot(odd, first_ref[channels:, :])
     hat, scale = norm_parts(first)
     hidden, slope = gelu_parts(hat * gain_ref[0:1, :] + shift_ref[0:1, :])
     slope1_ref[...] = slope
@@ -109,9 +155,8 @@
     scale1_ref[...] = jnp.broadcast_to(scale, scale1_ref.shape)
     hidden = hidden.astype(BF)
     hidden32 = hidden.astype(F32)
-    second = dot(hidden[:n2], weight_ref[1, :channels, :]) + dot(
-        hidden[n2:], weight_ref[1, channels:, :]
-    )
+    copies[4].wait()
+    second = dot(hidden[:n2], second_ref[:channels, :]) + dot(hidden[n2:], second_ref[channels:, :])
     hat, scale = norm_parts(second)
     made, slope = gelu_parts(hat * gain_ref[1:2, :] + shift_ref[1:2, :])
     slope2_ref[...] = slope
@@ -128,10 +173,10 @@
         in_turned[channels * tap : channels * (tap + 1), :] = stacked.T
     at = me_ref[1]
     for k, turned_ref in enumerate(turned_refs):
-        start = (at ^ k) * owned
         turned_ref[...] = jnp.concatenate(
             [
-                in_turned[pl.ds(pl.multiple_of(z * near * owned + start, owned), owned), :]
+                in_turned[pl.ds(pl.multiple_of((z * near + (at ^ (2 * k + c))) * owned, owned), owned), :]
+                for c in range(2)
                 for z in range(far)
             ],
             axis=0,
@@ -169,14 +214,45 @@
     out_ref[...] = rows32[...].astype(BF)
 
 
+def pack(rows, channels):
+    r, w = rows.shape
+    parts, start = [], 0
+    while start < w:
+        lanes = min(1 << ((w - start).bit_length() - 1), channels)
+        each = r * lanes // channels
+        parts.append(
+            jnp.concatenate(
+                [rows[g * each : (g + 1) * each, start : start + lanes] for g in range(r // each)], axis=1
+            )
+        )
+        start += lanes
+    return jnp.concatenate(parts, axis=0)
+
+
+def unpack(packed, r, w):
+    channels = packed.shape[1]
+    parts, start, at = [], 0, 0
+    while start < w:
+        lanes = min(1 << ((w - start).bit_length() - 1), channels)
+        each = r * lanes // channels
+        block = packed[at : at + each]
+        parts.append(
+            jnp.concatenate([block[:, g * lanes : (g + 1) * lanes] for g in range(r // each)], axis=0)
+        )
+        start += lanes
+        at += each
+    return jnp.concatenate(parts, axis=1)
+
+
 def project_kernel(me_ref, mine_ref, other_ref, weight_ref, cotangent_ref, packed_ref, keep_ref, send_ref):
     rows32 = mine_ref[...].astype(F32) + other_ref[...].astype(F32)
     packed_ref[...] = dot_nt(weight_ref[...], rows32.astype(BF)).astype(BF)
     partial = dot_nt(rows32.T.astype(BF), cotangent_ref[...])
-    each = keep_ref.shape[1]
+    channels, width = partial.shape
+    each = channels // (2 * keep_ref.shape[0])
     for z in range(keep_ref.shape[0]):
-        low = partial[2 * z * each : (2 * z + 1) * each]
-        high = partial[(2 * z + 1) * each : (2 * z + 2) * each]
+        low = pack(partial[2 * z * each : (2 * z + 1) * each], channels)
+        high = pack(partial[(2 * z + 1) * each : (2 * z + 2) * each], channels)
         keep_ref[z] = jnp.where(me_ref[3] == 0, low, high)
         send_ref[z] = jnp.where(me_ref[3] == 0, high, low).astype(BF)
 
@@ -207,10 +283,10 @@
 
 
 def back_kernel(
-    me_ref, slots_ref, slope1_ref, slope2_ref, hat1_ref, hat2_ref, scale1_ref, scale2_ref,
-    weight_ref, gain_ref, out_ref, grads32, *, pairs, frames
+    me_ref, slots_ref, state_ref, weight_ref, gain_ref, out_ref, grads32, *, pairs, frames
 ):
     channels = weight_ref.shape[2]
+    slope1_ref, slope2_ref, hat1_ref, hat2_ref, scale1_ref, scale2_ref = state_views(state_ref)
     for p in range(pairs):
         slot = jnp.clip(me_ref[4 + 2 * pairs + 2 * p], 0, slots_ref.shape[0] - 1)
         grads32[p * frames : (p + 1) * frames, :] = slots_ref[slot].astype(F32)[:frames]
@@ -249,7 +325,11 @@
 
 
 def kernel_grad_kernel(me_ref, *refs, n1, n2, owned, near, far):
-    grad_refs, in_refs = refs[:near], refs[near : 2 * near]
+    grad_refs, side_refs = refs[:near], refs[near : 2 * near]
+    rows = side_refs[0].shape[0] // 2
+    in_refs = [
+        side_refs[near // 2 * (k % 2) + k // 2].at[k % 2 * rows : (k % 2 + 1) * rows] for k in range(near)
+    ]
     own_ref, out_refs, held = refs[2 * near], refs[2 * near + 1 : -1], refs[-1]
     first, second, sums = 0.0, 0.0, 0.0
     for grad_ref, in_ref in zip(grad_refs, in_refs):
@@ -279,7 +359,7 @@
         proj += proj_in[f][...].astype(F32)
     conv_ref[0] = total[:owned]
     conv_ref[1] = total[owned : 2 * owned]
-    proj_ref[...] = proj
+    proj_ref[...] = unpack(proj, *proj_ref.shape)
     channels = total.shape[1]
     sums = total[2 * owned : 2 * owned + 4] + total[2 * owned + 4 : 2 * owned + 8]
     start = me_ref[0] * owned
@@ -317,46 +397,68 @@
     at_mp = lax.axis_index("mp").astype(jnp.int32)
     x_bit = at_dp & 1
     place = jnp.stack([at_dp * mp_count + at_mp, x_bit * mp_count + at_mp, at_dp >> 1, x_bit])
-    me = jnp.concatenate([place, lengths, dests, offsets])
-
-    index = call(
-        functools.partial(index_kernel, pairs=pairs, frames=frames),
-        shape(2, -(-dp_count // 128) * 128, kind=jnp.int32),
-        (me,),
-        scalars=1,
-    )
-    index = index + swap(index, mp_count)
-    got_index = jnp.concatenate([index] + [swap(index, near * f) for f in range(1, far)], axis=0)
+    me, index, grad_rows = call(
+        functools.partial(start_kernel, pairs=pairs, frames=frames),
+        [
+            shape(4 + 6 * pairs, kind=jnp.int32),
+            shape(dp_count, -(-dp_count // 128) * 128, kind=jnp.int32),
+            shape(seq, channels),
+        ],
+        (place, proj_weight.T, grad_packed.T, lengths, dests, offsets),
+        scalars=1,
+        fetched=5,
+        to_scalars=1,
+        flops=2 * seq * width * channels,
+        scratch=[
+            pltpu.VMEM((width, channels), BF),
+            pltpu.VMEM((width, seq), BF),
+            pltpu.SMEM(lengths.shape, jnp.int32),
+            pltpu.SMEM(dests.shape, jnp.int32),
+            pltpu.SMEM(offsets.shape, jnp.int32),
+            pltpu.SemaphoreType.DMA((5,)),
+        ],
+        mebibytes=56,
+    )
+    feat = features.reshape(utt_count * positions, channels)
+    got_index = lax.all_to_all(index, "dp", split_axis=0, concat_axis=0, tiled=True)
 
     wide = -(-(n1 + n2) // 128) * 128
-    feat = features.reshape(utt_count * positions, channels)
+    tall = (2 * channels, channels)
     made = call(
         functools.partial(
             forward_kernel, pairs=pairs, frames=frames, far=far, near=near, owned=owned
         ),
         [
+            shape(*me.shape, kind=jnp.int32),
             shape(n2, channels),
-            shape(n1, channels, kind=F32),
-            shape(n2, channels, kind=F32),
-            shape(n1, channels, kind=F32),
-            shape(n2, channels, kind=F32),
-            shape(n1, 128, kind=F32),
-            shape(n2, 128, kind=F32),
+            shape(3 * (n1 + n2), channels, kind=F32),
         ]
-        + [shape(far * owned, wide)] * near,
-        (me, feat, conv_weight, norm_gain, norm_shift),
-        scalars=1,
+        + [shape(2 * far * owned, wide)] * (near // 2),
+        (me, feat, norm_gain, norm_shift, conv_weight),
+        scalars=1,
+        fetched=4,
+        to_scalars=1,
         flops=2 * (n1 + n2) * 2 * channels * channels,
-        scratch=[pltpu.VMEM((2 * channels, wide), F32)],
-    )
-    pair_frames, slope1, slope2, hat1, hat2, scale1, scale2 = made[:7]
-    in_sides = [side if k == 0 else swap(side, k) for k, side in enumerate(made[7:])]
-
-    grad_rows = lax.dot_general(
-        grad_packed, proj_weight, (((1,), (1,)), ((), ())), preferred_element_type=F32
-    ).astype(BF)
+        scratch=[
+            pltpu.VMEM(feat.shape, BF),
+            pltpu.VMEM(norm_gain.shape, F32),
+            pltpu.VMEM(norm_shift.shape, F32),
+            pltpu.VMEM(tall, BF),
+            pltpu.VMEM(tall, BF),
+            pltpu.VMEM((2 * channels, wide), F32),
+            pltpu.SemaphoreType.DMA((5,)),
+        ],
+        mebibytes=56,
+    )
+    me, pair_frames, state = made[:3]
+    in_sides = [swap(side, 2 * k) if k else side for k, side in enumerate(made[3:])]
+    in_sides += [swap(side, 1) for side in in_sides]
+
     for mask in bits[:-1]:
-        grad_rows = (grad_rows.astype(F32) + swap(grad_rows, mask).astype(F32)).astype(BF)
+        arrived, pair_frames, got_index = lax.optimization_barrier(
+            (swap(grad_rows, mask), pair_frames, got_index)
+        )
+        grad_rows = (grad_rows.astype(F32) + arrived.astype(F32)).astype(BF)
     other_rows = swap(grad_rows, bits[-1])
 
     sent = call(
@@ -372,7 +474,7 @@
     grads = call(
         functools.partial(back_kernel, pairs=pairs, frames=frames),
         shape(n1 + n2 + 16, channels),
-        (me, slots, slope1, slope2, hat1, hat2, scale1, scale2, conv_weight, norm_gain),
+        (me, slots, state, conv_weight, norm_gain),
         scalars=1,
         flops=2 * n2 * 2 * channels * channels,
         scratch=[pltpu.VMEM((n2, channels), F32)],
@@ -395,8 +497,8 @@
         project_kernel,
         [
             shape(width, seq),
-            shape(far, per_dp, width, kind=F32),
-            shape(far, per_dp, width),
+            shape(far, per_dp * width // channels, channels, kind=F32),
+            shape(far, per_dp * width // channels, channels),
         ],
         (me, placed, swap(placed, bits[-1]), proj_weight.T, grad_packed.T),
         scalars=1,
@@ -404,7 +506,8 @@
     )
     proj_parts = call(
         fold_kernel,
-        [shape(per_dp, width, kind=F32)] + [shape(per_dp, width)] * (far - 1),
+        [shape(per_dp * width // channels, channels, kind=F32)]
+        + [shape(per_dp * width // channels, channels)] * (far - 1),
         (me, keep, swap(send, mp_count)),
         scalars=1,
     )

time: 74 us -> 70.5 us (0.953)
  starting transfers between devices: 36.2 us -> 31.2 us
  Pallas kernels: 11.9 us -> 16.4 us
  waiting for transfers between devices: 18.5 us -> 17.2 us
  matrix products: 1.27 us -> 0 us
  local copies, waits for them, and re-layouts: 4.7 us -> 3.71 us
    ppermute x29 -> x25, starting transfers between devices: 30.2 us -> 21.8 us  [swap(): lax.ppermute(x, everyone, [(i, i ^ mask) for i in range(dp_count * mp_cou...]
    all_to_all x0 -> x1, starting transfers between devices: none -> 5.81 us  [local(): lax.all_to_all(index, 'dp', split_axis=0, concat_axis=0, tiled=True)]
    pallas_call x10, Pallas kernels: 11.9 us -> 16.4 us  [call(): pl.pallas_call(body, out_shape=out, in_specs=specs, out_specs=[pl.BlockSp...]
    ppermute x29 -> x25, waiting for transfers between devices: 18.5 us -> 14.7 us  [swap(): lax.ppermute(x, everyone, [(i, i ^ mask) for i in range(dp_count * mp_cou...]
    all_to_all x0 -> x1, waiting for transfers between devices: none -> 2.47 us  [local(): lax.all_to_all(index, 'dp', split_axis=0, concat_axis=0, tiled=True)]
    all_to_all x1, starting transfers between devices: 6.02 us -> 3.55 us  [local(): slots = lax.all_to_all(sent, 'dp', split_axis=0, concat_axis=0, tiled=True)]
    dot_general x1 -> x0, matrix products: 1.27 us -> none  [local(): lax.dot_general(grad_packed, proj_weight, (((1,), (1,)), ((), ())), prefe...]
    concatenate x1 -> x0, local copies, waits for them, and re-layouts: 0.77 us -> none  [local(): me = jnp.concatenate([place, lengths, dests, offsets])]
  transfers between devices with their start and end apart: 30 -> 27, of which waited for: 11 -> 12; matrix products, arithmetic and copies ran while one was open for 1% -> 0% of each run, Pallas kernels for 12% -> 15%
where the time goes in v4:
time: 70.5 us; the launch traced here: 70 us
  starting transfers between devices  31.2 us (44%)
  waiting for transfers between devices  17.2 us (24%)
  Pallas kernels  16.4 us (23%)
  local copies, waits for them, and re-layouts  3.71 us (5%)
  between operations  0.81 us (1%)
    ppermute x25, starting transfers between devices, swap(): lax.ppermute(x, everyone, [(i, i ^ mask) for i in range(dp_count * mp_cou...  21.8 us
    pallas_call x10, Pallas kernels, call(): pl.pallas_call(body, out_shape=out, in_specs=specs, out_specs=[pl.BlockSp...  16.4 us
    ppermute x25, waiting for transfers between devices, swap(): lax.ppermute(x, everyone, [(i, i ^ mask) for i in range(dp_count * mp_cou...  14.7 us
    all_to_all x1, starting transfers between devices, local(): lax.all_to_all(index, 'dp', split_axis=0, concat_axis=0, tiled=True)  5.81 us
    unnamed x24, local copies, waits for them, and re-layouts  3.71 us
    all_to_all x1, starting transfers between devices, local(): slots = lax.all_to_all(sent, 'dp', split_axis=0, concat_axis=0, tiled=True)  3.55 us
    all_to_all x1, waiting for transfers between devices, local(): lax.all_to_all(index, 'dp', split_axis=0, concat_axis=0, tiled=True)  2.47 us
  transfers between devices with their start and end apart: 27, of which 12 were waited for; matrix products, arithmetic and copies ran while one was open for 0% of the time, Pallas kernels for 15%

profile of v4, /device:TPU:0, one launch (start us, length us, event | category | flops | bytes accessed | tf_op | source)
XLA Modules:
  0.0 70.0 jit_solution(12953252111287702704)
XLA Ops:
  0.7 0.6 pad_add_fusion.place_ref
  1.3 2.8 %shard_map.128 = (s32[28]{0:T(128)}, s32[8,128]{1,0:T(8,128)}, bf16[128,512]{1,0:T(8,128)(2,1)}) custom-call(s32[4]{0:T(128)} %pad_add_fusion.place_ref, bf16[320,512]{1,0:T(8,128)(2,1)} %bitcast.13, bf16[320,128]{1,0:T(8,128)(2,1)} %bitcast.15, s32[8]{0:T(128)} %lengths_hbm.1, s32[8]{0:T(128)} %dests_hbm.1, s32[8]{0:T(128)} %offsets_hbm.1), custom_call_target="tpu_custom_call" | custom-call | flops 41943040 | bytes 409712 | tf_op jit(solution)/shard_map/pallas_call | solution.py:25
  4.0 3.0 %collective-permute-start = (bf16[128,512]{1,0:T(8,128)(2,1)}, bf16[128,512]{1,0:T(8,128)(2,1)S(1)}, u32[]{:S(2)}, u32[]{:S(2)}) collective-permute-start(bf16[128,512]{1,0:T(8,128)(2,1)} %get-tuple-element.43), channel_id=1, source_target_pairs={{0,2},{1,3},{2,0},{3,1},{4,6},{5,7},{6,4},{7,5},{8,10},{9,11},{10,... | collective-permute-start | bytes 393224 | tf_op jit(solution)/shard_map/ppermute | solution.py:393
  7.1 5.8 %all-to-all-start = ((s32[8,1,128]{2,1,0:T(1,128)}), s32[8,1,128]{2,1,0:T(1,128)S(1)}, u32[]{:S(2)}, u32[]{:S(2)}) async-start(s32[8,1,128]{2,1,0:T(1,128)} %bitcast.21), calls=%async_computation | async-start | bytes 8192 | tf_op jit(solution)/shard_map/all_to_all | solution.py:423
  12.9 4.0 %shard_map.129 = (s32[28]{0:T(128)}, bf16[32,512]{1,0:T(8,128)(2,1)}, f32[288,512]{1,0:T(8,128)}, bf16[256,128]{1,0:T(8,128)(2,1)}, bf16[256,128]{1,0:T(8,128)(2...) custom-call(s32[28]{0:T(128)} %get-tuple-element.41.me_ref, bf16[256,512]{1,0:T(8,128)(2,1)} %bitcast.19, ...), custom_call_target="tpu_custom_call" | custom-call | flops 100663296 | bytes 2367600 | tf_op jit(solution)/shard_map/pallas_call | solution.py:25
  16.9 2.5 %all-to-all-done = s32[8,1,128]{2,1,0:T(1,128)S(1)} async-done(((s32[8,1,128]{2,1,0:T(1,128)}), s32[8,1,128]{2,1,0:T(1,128)S(1)}, u32[]{:S(2)}, u32[]{:S(2)}) %all-to-all-start) | async-done | bytes 4128 | tf_op jit(solution)/shard_map/all_to_all | solution.py:423
  19.4 0.1 collective-permute-start.1
  19.5 1.3 %collective-permute-done.1.other_ref = bf16[128,512]{1,0:T(8,128)(2,1)S(1)} collective-permute-done((bf16[128,512]{1,0:T(8,128)(2,1)S(1)}, bf16[128,512]{1,0:T(8,128)(2,1)S(1)}, u32[]{:S(2)}, u32[]{:S(2)}) %collective-permute-start.1) | collective-permute-done | bytes 131104 | tf_op jit(solution)/shard_map/ppermute | solution.py:393
  20.8 0.8 %copy-done.5 = bf16[32,512]{1,0:T(8,128)(2,1)S(1)} copy-done((bf16[32,512]{1,0:T(8,128)(2,1)S(1)}, bf16[32,512]{1,0:T(8,128)(2,1)}, u32[]{:S(2)}) %copy-start.5) | copy-done | bytes 32792
  21.6 0.6 copy-done.6
  22.2 1.3 %shard_map.130 = bf16[8,16,512]{2,1,0:T(8,128)(2,1)} custom-call(s32[8,128]{1,0:T(8,128)S(1)} %bitcast.17, s32[28]{0:T(128)S(1)} %copy-done.6, bf16[128,512]{1,0:T(8,128)(2,1)S(1)} %add_convert_fusion.mine_ref, bf16[128,512]{1,0:T(8,128)(2,1)S(1)} %collective-permute-done.1.other_ref, bf16[32,512]{1,0:T(8,128)(2,1)S(1)} %copy-done.5), custom_call_target="tpu_custom_call" | custom-call | bytes 299120 | tf_op jit(solution)/shard_map/pallas_call | solution.py:25
  23.5 3.6 %all-to-all-start.1 = ((bf16[8,16,512]{2,1,0:T(8,128)(2,1)}), bf16[8,16,512]{2,1,0:T(8,128)(2,1)S(1)}, u32[]{:S(2)}, u32[]{:S(2)}) async-start(bf16[8,16,512]{2,1,0:T(8,128)(2,1)} %shard_map.130), calls=%async_computation.1 | async-start | bytes 262144 | tf_op jit(solution)/shard_map/all_to_all | solution.py:471
  27.1 0.5 collective-permute-start.2
  27.6 2.0 %collective-permute-start.3 = (bf16[256,128]{1,0:T(8,128)(2,1)}, bf16[256,128]{1,0:T(8,128)(2,1)S(1)}, u32[]{:S(2)}, u32[]{:S(2)}) collective-permute-start(bf16[256,128]{1,0:T(8,128)(2,1)} %get-tuple-element.51), channel_id=1, source_target_pairs={{0,4},{1,5},{2,6},{3,7},{4,0},{5,1},{6,2},{7,3},{8,12},{9,13},{10,... | collective-permute-start | bytes 196616 | tf_op jit(solution)/shard_map/ppermute | solution.py:393
  29.6 1.0 %collective-permute-start.4 = (bf16[256,128]{1,0:T(8,128)(2,1)}, bf16[256,128]{1,0:T(8,128)(2,1)S(1)}, u32[]{:S(2)}, u32[]{:S(2)}) collective-permute-start(bf16[256,128]{1,0:T(8,128)(2,1)} %get-tuple-element.52), channel_id=1, source_target_pairs={{0,6},{1,7},{2,4},{3,5},{4,2},{5,3},{6,0},{7,1},{8,14},{9,15},{10,... | collective-permute-start | bytes 196616 | tf_op jit(solution)/shard_map/ppermute | solution.py:393
  30.6 1.0 %collective-permute-done.2.refs_9_ = bf16[256,128]{1,0:T(8,128)(2,1)S(1)} collective-permute-done((bf16[256,128]{1,0:T(8,128)(2,1)}, bf16[256,128]{1,0:T(8,128)(2,1)S(1)}, u32[]{:S(2)}, u32[]{:S(2)}) %collective-permute-start.2) | collective-permute-done | bytes 65568 | tf_op jit(solution)/shard_map/ppermute | solution.py:393
  31.6 0.9 %collective-permute-done.3.refs_10_ = bf16[256,128]{1,0:T(8,128)(2,1)S(1)} collective-permute-done((bf16[256,128]{1,0:T(8,128)(2,1)}, bf16[256,128]{1,0:T(8,128)(2,1)S(1)}, u32[]{:S(2)}, u32[]{:S(2)}) %collective-permute-start.3) | collective-permute-done | bytes 65568 | tf_op jit(solution)/shard_map/ppermute | solution.py:393
  32.4 2.6 %collective-permute-done.4.refs_11_ = bf16[256,128]{1,0:T(8,128)(2,1)S(1)} collective-permute-done((bf16[256,128]{1,0:T(8,128)(2,1)}, bf16[256,128]{1,0:T(8,128)(2,1)S(1)}, u32[]{:S(2)}, u32[]{:S(2)}) %collective-permute-start.4) | collective-permute-done | bytes 65568 | tf_op jit(solution)/shard_map/ppermute | solution.py:393
  35.1 1.2 %collective-permute-done.8.refs_15_ = bf16[256,128]{1,0:T(8,128)(2,1)S(1)} collective-permute-done((bf16[256,128]{1,0:T(8,128)(2,1)S(1)}, bf16[256,128]{1,0:T(8,128)(2,1)S(1)}, u32[]{:S(2)}, u32[]{:S(2)}) %collective-permute-start.8) | collective-permute-done | bytes 65568 | tf_op jit(solution)/shard_map/ppermute | solution.py:393
  36.3 0.6 copy-done.7
  36.9 0.8 %shard_map.131 = bf16[128,512]{1,0:T(8,128)(2,1)S(1)} custom-call(s32[8,128]{1,0:T(8,128)S(1)} %bitcast.18, s32[28]{0:T(128)S(1)} %copy-done.7, bf16[8,16,512]{2,1,0:T(8,128)(2,1)S(1)} %all-to-all-done.1.slots_ref), custom_call_target="tpu_custom_call" | custom-call | bytes 135280 | tf_op jit(solution)/shard_map/pallas_call | solution.py:25
  37.7 1.6 %collective-permute-start.9 = (bf16[128,512]{1,0:T(8,128)(2,1)S(1)}, bf16[128,512]{1,0:T(8,128)(2,1)S(1)}, u32[]{:S(2)}, u32[]{:S(2)}) collective-permute-start(bf16[128,512]{1,0:T(8,128)(2,1)S(1)} %shard_map.131), channel_id=1, source_target_pairs={{0,2},{1,3},{2,0},{3,1},{4,6},{5,7},{6,4},{7,5},{8,10},{9,11},{10,... | collective-permute-start | bytes 393224 | tf_op jit(solution)/shard_map/ppermute | solution.py:393
  39.3 1.1 %copy-done.2 = f32[288,512]{1,0:T(8,128)S(1)} copy-done((f32[288,512]{1,0:T(8,128)S(1)}, f32[288,512]{1,0:T(8,128)}, u32[]{:S(2)}) %copy-start.2) | copy-done | bytes 589848
  40.4 0.6 copy-done.8
  41.0 1.1 %shard_map.133.grad_ref.refs_0_ = bf16[112,512]{1,0:T(8,128)(2,1)S(1)} custom-call(s32[28]{0:T(128)S(1)} %copy-done.8, bf16[8,16,512]{2,1,0:T(8,128)(2,1)S(1)} %all-to-all-done.1.slots_ref, f32[288,512]{1,0:T(8,128)S(1)} %copy-done.2, bf16[2,1024,512]{2,1,0:T(8,128)(2,1)S(1)} %copy-done, f32[2,512]{1,0:T(2,128)S(1)} %copy-done.10), custom_call_target="tpu_custom_call" | custom-call | flops 33554432 | bytes 2822256 | tf_op jit(solution)/shard_map/pallas_call | solution.py:25
  42.1 1.0 %collective-permute-start.16 = (bf16[112,512]{1,0:T(8,128)(2,1)S(1)}, bf16[112,512]{1,0:T(8,128)(2,1)S(1)}, u32[]{:S(2)}, u32[]{:S(2)}) collective-permute-start(bf16[112,512]{1,0:T(8,128)(2,1)S(1)} %shard_map.133.grad_ref.refs_0_), channel_id=1, source_target_pairs={{0,6},{1,7},{2,4},{3,5},{4,2},{5,3},{6,0},{7,1},{8,14},{9,15},{10,... | collective-permute-start | bytes 344072 | tf_op jit(solution)/shard_map/ppermute | solution.py:393
  43.1 1.1 %collective-permute-start.14 = (bf16[112,512]{1,0:T(8,128)(2,1)S(1)}, bf16[112,512]{1,0:T(8,128)(2,1)S(1)}, u32[]{:S(2)}, u32[]{:S(2)}) collective-permute-start(bf16[112,512]{1,0:T(8,128)(2,1)S(1)} %shard_map.133.grad_ref.refs_0_), channel_id=1, source_target_pairs={{0,4},{1,5},{2,6},{3,7},{4,0},{5,1},{6,2},{7,3},{8,12},{9,13},{10,... | collective-permute-start | bytes 344072 | tf_op jit(solution)/shard_map/ppermute | solution.py:393
  44.1 1.5 %collective-permute-start.12 = (bf16[112,512]{1,0:T(8,128)(2,1)S(1)}, bf16[112,512]{1,0:T(8,128)(2,1)S(1)}, u32[]{:S(2)}, u32[]{:S(2)}) collective-permute-start(bf16[112,512]{1,0:T(8,128)(2,1)S(1)} %shard_map.133.grad_ref.refs_0_), channel_id=1, source_target_pairs={{0,2},{1,3},{2,0},{3,1},{4,6},{5,7},{6,4},{7,5},{8,10},{9,11},{10,... | collective-permute-start | bytes 344072 | tf_op jit(solution)/shard_map/ppermute | solution.py:393
  45.7 0.5 collective-permute-start.11
  46.2 2.8 %collective-permute-done.16.refs_6_ = bf16[112,512]{1,0:T(8,128)(2,1)S(1)} collective-permute-done((bf16[112,512]{1,0:T(8,128)(2,1)S(1)}, bf16[112,512]{1,0:T(8,128)(2,1)S(1)}, u32[]{:S(2)}, u32[]{:S(2)}) %collective-permute-start.16) | collective-permute-done | bytes 114720 | tf_op jit(solution)/shard_map/ppermute | solution.py:393
  49.1 0.4 collective-permute-done.14.refs_4_
  49.5 0.1 collective-permute-start.15
  49.6 0.8 %collective-permute-done.12.refs_2_ = bf16[112,512]{1,0:T(8,128)(2,1)S(1)} collective-permute-done((bf16[112,512]{1,0:T(8,128)(2,1)S(1)}, bf16[112,512]{1,0:T(8,128)(2,1)S(1)}, u32[]{:S(2)}, u32[]{:S(2)}) %collective-permute-start.12) | collective-permute-done | bytes 114720 | tf_op jit(solution)/shard_map/ppermute | solution.py:393
  50.5 1.5 %shard_map.132 = (bf16[320,128]{1,0:T(8,128)(2,1)}, f32[4,40,512]{2,1,0:T(8,128)S(1)}, bf16[4,40,512]{2,1,0:T(8,128)(2,1)S(1)}) custom-call(s32[28]{0:T(128)S(1)} %copy-done.8, bf16[128,512]{1,0:T(8,128)(2,1)S(1)} %add.15.mine_ref, bf16[128,512]{1,0:T(8,128)(2,1)S(1)} %collective-permute-done.10.other_ref, bf16[320,512]{1,0:T(8,128)(2,1)S(1)} %bitcast.14, ...), custom_call_target="tpu_custom_call" | custom-call | flops 83886080 | bytes 671856 | tf_op jit(solution)/shard_map/pallas_call | solution.py:25
  52.0 0.5 collective-permute-start.21
  52.5 1.3 %shard_map.135 = (f32[72,512]{1,0:T(8,128)S(1)}, bf16[72,512]{1,0:T(8,128)(2,1)S(1)}, bf16[72,512]{1,0:T(8,128)(2,1)S(1)}, bf16[72,512]{1,0:T(8,128)(2,1)S(1)}) custom-call(s32[28]{0:T(128)S(1)} %copy-done.8, bf16[112,512]{1,0:T(8,128)(2,1)S(1)} %shard_map.133.grad_ref.refs_0_, bf16[112,512]{1,0:T(8,128)(2,1)S(1)} %collective-permute-done.11.refs_1_, ...), custom_call_target="tpu_custom_call" | custom-call | flops 100663296 | bytes 1441904 | tf_op jit(solution)/shard_map/pallas_call | solution.py:25
  53.8 1.5 %collective-permute-start.18 = (bf16[72,512]{1,0:T(8,128)(2,1)S(1)}, bf16[72,512]{1,0:T(8,128)(2,1)S(1)}, u32[]{:S(2)}, u32[]{:S(2)}) collective-permute-start(bf16[72,512]{1,0:T(8,128)(2,1)S(1)} %get-tuple-element.65), channel_id=1, source_target_pairs={{0,8},{1,9},{2,10},{3,11},{4,12},{5,13},{6,14},{7,15},{8,0},{9,1},... | collective-permute-start | bytes 221192 | tf_op jit(solution)/shard_map/ppermute | solution.py:393
  55.3 2.4 %collective-permute-start.19 = (bf16[72,512]{1,0:T(8,128)(2,1)S(1)}, bf16[72,512]{1,0:T(8,128)(2,1)S(1)}, u32[]{:S(2)}, u32[]{:S(2)}) collective-permute-start(bf16[72,512]{1,0:T(8,128)(2,1)S(1)} %get-tuple-element.66), channel_id=1, source_target_pairs={{0,16},{1,17},{2,18},{3,19},{4,20},{5,21},{6,22},{7,23},{8,24},{9,... | collective-permute-start | bytes 221192 | tf_op jit(solution)/shard_map/ppermute | solution.py:393
  57.6 0.6 collective-permute-start.20
  58.2 0.3 collective-permute-done.21.got_ref
  58.6 0.6 shard_map.136
  59.1 1.4 %collective-permute-start.22 = (bf16[40,512]{1,0:T(8,128)(2,1)S(1)}, bf16[40,512]{1,0:T(8,128)(2,1)S(1)}, u32[]{:S(2)}, u32[]{:S(2)}) collective-permute-start(bf16[40,512]{1,0:T(8,128)(2,1)S(1)} %get-tuple-element.71), channel_id=1, source_target_pairs={{0,8},{1,9},{2,10},{3,11},{4,12},{5,13},{6,14},{7,15},{8,0},{9,1},... | collective-permute-start | bytes 122888 | tf_op jit(solution)/shard_map/ppermute | solution.py:393
  60.6 2.4 %collective-permute-start.23 = (bf16[40,512]{1,0:T(8,128)(2,1)S(1)}, bf16[40,512]{1,0:T(8,128)(2,1)S(1)}, u32[]{:S(2)}, u32[]{:S(2)}) collective-permute-start(bf16[40,512]{1,0:T(8,128)(2,1)S(1)} %get-tuple-element.72), channel_id=1, source_target_pairs={{0,16},{1,17},{2,18},{3,19},{4,20},{5,21},{6,22},{7,23},{8,24},{9,... | collective-permute-start | bytes 122888 | tf_op jit(solution)/shard_map/ppermute | solution.py:393
  63.0 0.6 collective-permute-start.24
  63.6 1.9 %shard_map.134 = bf16[256,512]{1,0:T(8,128)(2,1)} custom-call(s32[28]{0:T(128)S(1)} %copy-done.9, bf16[112,512]{1,0:T(8,128)(2,1)S(1)} %shard_map.133.grad_ref.refs_0_, bf16[2,1024,512]{2,1,0:T(8,128)(2,1)S(1)} %copy-done), custom_call_target="tpu_custom_call" | custom-call | flops 67108864 | bytes 2211952 | tf_op jit(solution)/shard_map/pallas_call | solution.py:25
  65.5 2.2 %collective-permute-done.23.refs_6_ = bf16[40,512]{1,0:T(8,128)(2,1)S(1)} collective-permute-done((bf16[40,512]{1,0:T(8,128)(2,1)S(1)}, bf16[40,512]{1,0:T(8,128)(2,1)S(1)}, u32[]{:S(2)}, u32[]{:S(2)}) %collective-permute-start.23) | collective-permute-done | bytes 40992 | tf_op jit(solution)/shard_map/ppermute | solution.py:393
  67.7 1.1 %collective-permute-done.24.refs_7_ = bf16[40,512]{1,0:T(8,128)(2,1)S(1)} collective-permute-done((bf16[40,512]{1,0:T(8,128)(2,1)S(1)}, bf16[40,512]{1,0:T(8,128)(2,1)S(1)}, u32[]{:S(2)}, u32[]{:S(2)}) %collective-permute-start.24) | collective-permute-done | bytes 40992 | tf_op jit(solution)/shard_map/ppermute | solution.py:393
  68.8 1.3 %shard_map.137 = (f32[2,32,512]{2,1,0:T(8,128)}, f32[2,32]{1,0:T(2,128)}, f32[64,320]{1,0:T(8,128)}) custom-call(s32[28]{0:T(128)S(1)} %copy-done.9, f32[72,512]{1,0:T(8,128)S(1)} %get-tuple-element.64.refs_0_, bf16[72,512]{1,0:T(8,128)(2,1)S(1)} %collective-permute-done.18.refs_1_, bf16[72,512]{1,0:T(8,128)(2,1)S(1)} %collective-permute-done.19.refs_2_, ...), custom_call_target="tpu_custom_call" | custom-call | bytes 573552 | tf_op jit(solution)/shard_map/pallas_call | solution.py:25
  (43 shorter events, 0.2 us)
Async XLA Ops:
  0.6 38.7 %copy-start = (bf16[2,1024,512]{2,1,0:T(8,128)(2,1)S(1)}, bf16[2,1024,512]{2,1,0:T(8,128)(2,1)}, u32[]{:S(2)}) copy-start(bf16[2,1024,512]{2,1,0:T(8,128)(2,1)} %weight_ref.3) | copy-start | bytes 6291460
  0.6 38.6 %copy-start.10 = (f32[2,512]{1,0:T(2,128)S(1)}, f32[2,512]{1,0:T(2,128)}, u32[]{:S(2)}) copy-start(f32[2,512]{1,0:T(2,128)} %gain_ref.1) | copy-start | bytes 12292
  4.0 15.3 %copy-start.11 = (bf16[128,512]{1,0:T(8,128)(2,1)S(1)}, bf16[128,512]{1,0:T(8,128)(2,1)}, u32[]{:S(2)}) copy-start(bf16[128,512]{1,0:T(8,128)(2,1)} %get-tuple-element.43) | copy-start | bytes 393220
  4.0 15.3 %collective-permute-start = (bf16[128,512]{1,0:T(8,128)(2,1)}, bf16[128,512]{1,0:T(8,128)(2,1)S(1)}, u32[]{:S(2)}, u32[]{:S(2)}) collective-permute-start(bf16[128,512]{1,0:T(8,128)(2,1)} %get-tuple-element.43), channel_id=1, source_target_pairs={{0,2},{1,3},{2,0},{3,1},{4,6},{5,7},{6,4},{7,5},{8,10},{9,11},{10,... | collective-permute-start | bytes 393224 | tf_op jit(solution)/shard_map/ppermute | solution.py:393
  7.1 12.3 %all-to-all-start = ((s32[8,1,128]{2,1,0:T(1,128)}), s32[8,1,128]{2,1,0:T(1,128)S(1)}, u32[]{:S(2)}, u32[]{:S(2)}) async-start(s32[8,1,128]{2,1,0:T(1,128)} %bitcast.21), calls=%async_computation | async-start | bytes 8192 | tf_op jit(solution)/shard_map/all_to_all | solution.py:423
  19.4 1.4 %collective-permute-start.1 = (bf16[128,512]{1,0:T(8,128)(2,1)S(1)}, bf16[128,512]{1,0:T(8,128)(2,1)S(1)}, u32[]{:S(2)}, u32[]{:S(2)}) collective-permute-start(bf16[128,512]{1,0:T(8,128)(2,1)S(1)} %add_convert_fusion.mine_ref), channel_id=1, source_target_pairs={{0,1},{1,0},{2,3},{3,2},{4,5},{5,4},{6,7},{7,6},{8,9},{9,8},{10,11... | collective-permute-start | bytes 393224 | tf_op jit(solution)/shard_map/ppermute | solution.py:393
  20.8 0.8 %copy-start.5 = (bf16[32,512]{1,0:T(8,128)(2,1)S(1)}, bf16[32,512]{1,0:T(8,128)(2,1)}, u32[]{:S(2)}) copy-start(bf16[32,512]{1,0:T(8,128)(2,1)} %get-tuple-element.48.frames_ref) | copy-start | bytes 98308
  21.6 0.6 copy-start.6
  22.2 28.3 %copy-start.1 = (bf16[512,320]{0,1:T(8,128)(2,1)S(1)}, bf16[512,320]{0,1:T(8,128)(2,1)}, u32[]{:S(2)}) copy-start(bf16[512,320]{0,1:T(8,128)(2,1)} %param.16) | copy-start | bytes 983044
  22.2 28.3 %copy-start.3 = (bf16[128,320]{0,1:T(8,128)(2,1)S(1)}, bf16[128,320]{0,1:T(8,128)(2,1)}, u32[]{:S(2)}) copy-start(bf16[128,320]{0,1:T(8,128)(2,1)} %param.17) | copy-start | bytes 245764
  23.5 12.8 %all-to-all-start.1 = ((bf16[8,16,512]{2,1,0:T(8,128)(2,1)}), bf16[8,16,512]{2,1,0:T(8,128)(2,1)S(1)}, u32[]{:S(2)}, u32[]{:S(2)}) async-start(bf16[8,16,512]{2,1,0:T(8,128)(2,1)} %shard_map.130), calls=%async_computation.1 | async-start | bytes 262144 | tf_op jit(solution)/shard_map/all_to_all | solution.py:471
  27.1 4.5 %collective-permute-start.2 = (bf16[256,128]{1,0:T(8,128)(2,1)}, bf16[256,128]{1,0:T(8,128)(2,1)S(1)}, u32[]{:S(2)}, u32[]{:S(2)}) collective-permute-start(bf16[256,128]{1,0:T(8,128)(2,1)} %get-tuple-element.50), channel_id=1, source_target_pairs={{0,2},{1,3},{2,0},{3,1},{4,6},{5,7},{6,4},{7,5},{8,10},{9,11},{10,... | collective-permute-start | bytes 196616 | tf_op jit(solution)/shard_map/ppermute | solution.py:393
  27.6 4.8 %collective-permute-start.3 = (bf16[256,128]{1,0:T(8,128)(2,1)}, bf16[256,128]{1,0:T(8,128)(2,1)S(1)}, u32[]{:S(2)}, u32[]{:S(2)}) collective-permute-start(bf16[256,128]{1,0:T(8,128)(2,1)} %get-tuple-element.51), channel_id=1, source_target_pairs={{0,4},{1,5},{2,6},{3,7},{4,0},{5,1},{6,2},{7,3},{8,12},{9,13},{10,... | collective-permute-start | bytes 196616 | tf_op jit(solution)/shard_map/ppermute | solution.py:393
  29.6 5.5 %collective-permute-start.4 = (bf16[256,128]{1,0:T(8,128)(2,1)}, bf16[256,128]{1,0:T(8,128)(2,1)S(1)}, u32[]{:S(2)}, u32[]{:S(2)}) collective-permute-start(bf16[256,128]{1,0:T(8,128)(2,1)} %get-tuple-element.52), channel_id=1, source_target_pairs={{0,6},{1,7},{2,4},{3,5},{4,2},{5,3},{6,0},{7,1},{8,14},{9,15},{10,... | collective-permute-start | bytes 196616 | tf_op jit(solution)/shard_map/ppermute | solution.py:393
  30.6 21.9 %copy-start.4 = (bf16[256,128]{1,0:T(8,128)(2,1)S(1)}, bf16[256,128]{1,0:T(8,128)(2,1)}, u32[]{:S(2)}) copy-start(bf16[256,128]{1,0:T(8,128)(2,1)} %get-tuple-element.56.refs_8_) | copy-start | bytes 196612
  30.6 4.5 %collective-permute-start.5 = (bf16[256,128]{1,0:T(8,128)(2,1)}, bf16[256,128]{1,0:T(8,128)(2,1)S(1)}, u32[]{:S(2)}, u32[]{:S(2)}) collective-permute-start(bf16[256,128]{1,0:T(8,128)(2,1)} %get-tuple-element.56.refs_8_), channel_id=1, source_target_pairs={{0,1},{1,0},{2,3},{3,2},{4,5},{5,4},{6,7},{7,6},{8,9},{9,8},{10,11... | collective-permute-start | bytes 196616 | tf_op jit(solution)/shard_map/ppermute | solution.py:393
  31.6 3.5 %collective-permute-start.6 = (bf16[256,128]{1,0:T(8,128)(2,1)S(1)}, bf16[256,128]{1,0:T(8,128)(2,1)S(1)}, u32[]{:S(2)}, u32[]{:S(2)}) collective-permute-start(bf16[256,128]{1,0:T(8,128)(2,1)S(1)} %collective-permute-done.2.refs_9_), channel_id=1, source_target_pairs={{0,1},{1,0},{2,3},{3,2},{4,5},{5,4},{6,7},{7,6},{8,9},{9,8},{10,11... | collective-permute-start | bytes 196616 | tf_op jit(solution)/shard_map/ppermute | solution.py:393
  32.4 2.7 %collective-permute-start.7 = (bf16[256,128]{1,0:T(8,128)(2,1)S(1)}, bf16[256,128]{1,0:T(8,128)(2,1)S(1)}, u32[]{:S(2)}, u32[]{:S(2)}) collective-permute-start(bf16[256,128]{1,0:T(8,128)(2,1)S(1)} %collective-permute-done.3.refs_10_), channel_id=1, source_target_pairs={{0,1},{1,0},{2,3},{3,2},{4,5},{5,4},{6,7},{7,6},{8,9},{9,8},{10,11... | collective-permute-start | bytes 196616 | tf_op jit(solution)/shard_map/ppermute | solution.py:393
  35.1 1.3 %collective-permute-start.8 = (bf16[256,128]{1,0:T(8,128)(2,1)S(1)}, bf16[256,128]{1,0:T(8,128)(2,1)S(1)}, u32[]{:S(2)}, u32[]{:S(2)}) collective-permute-start(bf16[256,128]{1,0:T(8,128)(2,1)S(1)} %collective-permute-done.4.refs_11_), channel_id=1, source_target_pairs={{0,1},{1,0},{2,3},{3,2},{4,5},{5,4},{6,7},{7,6},{8,9},{9,8},{10,11... | collective-permute-start | bytes 196616 | tf_op jit(solution)/shard_map/ppermute | solution.py:393
  36.3 0.6 copy-start.7
  37.7 7.9 %collective-permute-start.9 = (bf16[128,512]{1,0:T(8,128)(2,1)S(1)}, bf16[128,512]{1,0:T(8,128)(2,1)S(1)}, u32[]{:S(2)}, u32[]{:S(2)}) collective-permute-start(bf16[128,512]{1,0:T(8,128)(2,1)S(1)} %shard_map.131), channel_id=1, source_target_pairs={{0,2},{1,3},{2,0},{3,1},{4,6},{5,7},{6,4},{7,5},{8,10},{9,11},{10,... | collective-permute-start | bytes 393224 | tf_op jit(solution)/shard_map/ppermute | solution.py:393
  39.3 1.1 %copy-start.2 = (f32[288,512]{1,0:T(8,128)S(1)}, f32[288,512]{1,0:T(8,128)}, u32[]{:S(2)}) copy-start(f32[288,512]{1,0:T(8,128)} %get-tuple-element.55.state_ref) | copy-start | bytes 1769476
  40.4 0.6 copy-start.8
  41.0 17.6 %copy-start.9 = (s32[28]{0:T(128)S(1)}, s32[28]{0:T(128)}, u32[]{:S(2)}) copy-start(s32[28]{0:T(128)} %get-tuple-element.42.me_ref) | copy-start | bytes 340
  42.1 7.0 %collective-permute-start.16 = (bf16[112,512]{1,0:T(8,128)(2,1)S(1)}, bf16[112,512]{1,0:T(8,128)(2,1)S(1)}, u32[]{:S(2)}, u32[]{:S(2)}) collective-permute-start(bf16[112,512]{1,0:T(8,128)(2,1)S(1)} %shard_map.133.grad_ref.refs_0_), channel_id=1, source_target_pairs={{0,6},{1,7},{2,4},{3,5},{4,2},{5,3},{6,0},{7,1},{8,14},{9,15},{10,... | collective-permute-start | bytes 344072 | tf_op jit(solution)/shard_map/ppermute | solution.py:393
  43.1 6.4 %collective-permute-start.14 = (bf16[112,512]{1,0:T(8,128)(2,1)S(1)}, bf16[112,512]{1,0:T(8,128)(2,1)S(1)}, u32[]{:S(2)}, u32[]{:S(2)}) collective-permute-start(bf16[112,512]{1,0:T(8,128)(2,1)S(1)} %shard_map.133.grad_ref.refs_0_), channel_id=1, source_target_pairs={{0,4},{1,5},{2,6},{3,7},{4,0},{5,1},{6,2},{7,3},{8,12},{9,13},{10,... | collective-permute-start | bytes 344072 | tf_op jit(solution)/shard_map/ppermute | solution.py:393
  44.1 6.3 %collective-permute-start.12 = (bf16[112,512]{1,0:T(8,128)(2,1)S(1)}, bf16[112,512]{1,0:T(8,128)(2,1)S(1)}, u32[]{:S(2)}, u32[]{:S(2)}) collective-permute-start(bf16[112,512]{1,0:T(8,128)(2,1)S(1)} %shard_map.133.grad_ref.refs_0_), channel_id=1, source_target_pairs={{0,2},{1,3},{2,0},{3,1},{4,6},{5,7},{6,4},{7,5},{8,10},{9,11},{10,... | collective-permute-start | bytes 344072 | tf_op jit(solution)/shard_map/ppermute | solution.py:393
  45.7 4.8 %collective-permute-start.10 = (bf16[128,512]{1,0:T(8,128)(2,1)S(1)}, bf16[128,512]{1,0:T(8,128)(2,1)S(1)}, u32[]{:S(2)}, u32[]{:S(2)}) collective-permute-start(bf16[128,512]{1,0:T(8,128)(2,1)S(1)} %add.15.mine_ref), channel_id=1, source_target_pairs={{0,1},{1,0},{2,3},{3,2},{4,5},{5,4},{6,7},{7,6},{8,9},{9,8},{10,11... | collective-permute-start | bytes 393224 | tf_op jit(solution)/shard_map/ppermute | solution.py:393
  45.7 6.7 %collective-permute-start.11 = (bf16[112,512]{1,0:T(8,128)(2,1)S(1)}, bf16[112,512]{1,0:T(8,128)(2,1)S(1)}, u32[]{:S(2)}, u32[]{:S(2)}) collective-permute-start(bf16[112,512]{1,0:T(8,128)(2,1)S(1)} %shard_map.133.grad_ref.refs_0_), channel_id=1, source_target_pairs={{0,1},{1,0},{2,3},{3,2},{4,5},{5,4},{6,7},{7,6},{8,9},{9,8},{10,11... | collective-permute-start | bytes 344072 | tf_op jit(solution)/shard_map/ppermute | solution.py:393
  49.1 3.4 %collective-permute-start.17 = (bf16[112,512]{1,0:T(8,128)(2,1)S(1)}, bf16[112,512]{1,0:T(8,128)(2,1)S(1)}, u32[]{:S(2)}, u32[]{:S(2)}) collective-permute-start(bf16[112,512]{1,0:T(8,128)(2,1)S(1)} %collective-permute-done.16.refs_6_), channel_id=1, source_target_pairs={{0,1},{1,0},{2,3},{3,2},{4,5},{5,4},{6,7},{7,6},{8,9},{9,8},{10,11... | collective-permute-start | bytes 344072 | tf_op jit(solution)/shard_map/ppermute | solution.py:393
  49.5 3.0 %collective-permute-start.15 = (bf16[112,512]{1,0:T(8,128)(2,1)S(1)}, bf16[112,512]{1,0:T(8,128)(2,1)S(1)}, u32[]{:S(2)}, u32[]{:S(2)}) collective-permute-start(bf16[112,512]{1,0:T(8,128)(2,1)S(1)} %collective-permute-done.14.refs_4_), channel_id=1, source_target_pairs={{0,1},{1,0},{2,3},{3,2},{4,5},{5,4},{6,7},{7,6},{8,9},{9,8},{10,11... | collective-permute-start | bytes 344072 | tf_op jit(solution)/shard_map/ppermute | solution.py:393
  50.4 2.0 %collective-permute-start.13 = (bf16[112,512]{1,0:T(8,128)(2,1)S(1)}, bf16[112,512]{1,0:T(8,128)(2,1)S(1)}, u32[]{:S(2)}, u32[]{:S(2)}) collective-permute-start(bf16[112,512]{1,0:T(8,128)(2,1)S(1)} %collective-permute-done.12.refs_2_), channel_id=1, source_target_pairs={{0,1},{1,0},{2,3},{3,2},{4,5},{5,4},{6,7},{7,6},{8,9},{9,8},{10,11... | collective-permute-start | bytes 344072 | tf_op jit(solution)/shard_map/ppermute | solution.py:393
  52.0 6.6 %collective-permute-start.21 = (bf16[4,40,512]{2,1,0:T(8,128)(2,1)S(1)}, bf16[4,40,512]{2,1,0:T(8,128)(2,1)S(1)}, u32[]{:S(2)}, u32[]{:S(2)}) collective-permute-start(bf16[4,40,512]{2,1,0:T(8,128)(2,1)S(1)} %get-tuple-element.69), channel_id=1, source_target_pairs={{0,4},{1,5},{2,6},{3,7},{4,0},{5,1},{6,2},{7,3},{8,12},{9,13},{10,... | collective-permute-start | bytes 491528 | tf_op jit(solution)/shard_map/ppermute | solution.py:393
  53.8 9.2 %collective-permute-start.18 = (bf16[72,512]{1,0:T(8,128)(2,1)S(1)}, bf16[72,512]{1,0:T(8,128)(2,1)S(1)}, u32[]{:S(2)}, u32[]{:S(2)}) collective-permute-start(bf16[72,512]{1,0:T(8,128)(2,1)S(1)} %get-tuple-element.65), channel_id=1, source_target_pairs={{0,8},{1,9},{2,10},{3,11},{4,12},{5,13},{6,14},{7,15},{8,0},{9,1},... | collective-permute-start | bytes 221192 | tf_op jit(solution)/shard_map/ppermute | solution.py:393
  55.3 10.2 %collective-permute-start.19 = (bf16[72,512]{1,0:T(8,128)(2,1)S(1)}, bf16[72,512]{1,0:T(8,128)(2,1)S(1)}, u32[]{:S(2)}, u32[]{:S(2)}) collective-permute-start(bf16[72,512]{1,0:T(8,128)(2,1)S(1)} %get-tuple-element.66), channel_id=1, source_target_pairs={{0,16},{1,17},{2,18},{3,19},{4,20},{5,21},{6,22},{7,23},{8,24},{9,... | collective-permute-start | bytes 221192 | tf_op jit(solution)/shard_map/ppermute | solution.py:393
  57.6 7.9 %collective-permute-start.20 = (bf16[72,512]{1,0:T(8,128)(2,1)S(1)}, bf16[72,512]{1,0:T(8,128)(2,1)S(1)}, u32[]{:S(2)}, u32[]{:S(2)}) collective-permute-start(bf16[72,512]{1,0:T(8,128)(2,1)S(1)} %get-tuple-element.67), channel_id=1, source_target_pairs={{0,24},{1,25},{2,26},{3,27},{4,28},{5,29},{6,30},{7,31},{8,16},{9,... | collective-permute-start | bytes 221192 | tf_op jit(solution)/shard_map/ppermute | solution.py:393
  59.1 6.3 %collective-permute-start.22 = (bf16[40,512]{1,0:T(8,128)(2,1)S(1)}, bf16[40,512]{1,0:T(8,128)(2,1)S(1)}, u32[]{:S(2)}, u32[]{:S(2)}) collective-permute-start(bf16[40,512]{1,0:T(8,128)(2,1)S(1)} %get-tuple-element.71), channel_id=1, source_target_pairs={{0,8},{1,9},{2,10},{3,11},{4,12},{5,13},{6,14},{7,15},{8,0},{9,1},... | collective-permute-start | bytes 122888 | tf_op jit(solution)/shard_map/ppermute | solution.py:393
  60.6 7.1 %collective-permute-start.23 = (bf16[40,512]{1,0:T(8,128)(2,1)S(1)}, bf16[40,512]{1,0:T(8,128)(2,1)S(1)}, u32[]{:S(2)}, u32[]{:S(2)}) collective-permute-start(bf16[40,512]{1,0:T(8,128)(2,1)S(1)} %get-tuple-element.72), channel_id=1, source_target_pairs={{0,16},{1,17},{2,18},{3,19},{4,20},{5,21},{6,22},{7,23},{8,24},{9,... | collective-permute-start | bytes 122888 | tf_op jit(solution)/shard_map/ppermute | solution.py:393
  63.0 5.8 %collective-permute-start.24 = (bf16[40,512]{1,0:T(8,128)(2,1)S(1)}, bf16[40,512]{1,0:T(8,128)(2,1)S(1)}, u32[]{:S(2)}, u32[]{:S(2)}) collective-permute-start(bf16[40,512]{1,0:T(8,128)(2,1)S(1)} %get-tuple-element.73), channel_id=1, source_target_pairs={{0,24},{1,25},{2,26},{3,27},{4,28},{5,29},{6,30},{7,31},{8,16},{9,... | collective-permute-start | bytes 122888 | tf_op jit(solution)/shard_map/ppermute | solution.py:393

commit v5 on v4

--- a/solution.py
+++ b/solution.py
@@ -96,7 +96,7 @@
         me_ref[4 + i] = lengths_ref[i]
         me_ref[4 + 2 * pairs + i] = dests_ref[i]
         me_ref[4 + 4 * pairs + i] = offsets_ref[i]
-    shard = lax.broadcasted_iota(jnp.int32, index_ref.shape, 1)
+    shard = lax.broadcasted_iota(jnp.int32, index_ref.shape, 0)
     value = jnp.zeros(index_ref.shape, jnp.int32)
     for p in range(pairs):
         block = lax.div(offsets_ref[2 * p], frames)
@@ -109,14 +109,10 @@
     ).astype(BF)
 
 
-def block_from(got_ref, me_ref, d):
-    return got_ref[d, 2 * me_ref[2] + me_ref[3]] - 1
-
-
 def state_views(state_ref):
-    part = state_ref.shape[0] // 9
-    spans = ((0, 2), (2, 1), (3, 2), (5, 1), (6, 2), (8, 1))
-    return [state_ref.at[a * part : (a + n) * part] for a, n in spans]
+    part = (state_ref.shape[0] - 8) // 10
+    spans = ((0, 2), (2, 1), (3, 2), (5, 1), (6, 2), (8, 1), (9, 1))
+    return [state_ref.at[a * part : (a + n) * part] for a, n in spans] + [state_ref.at[10 * part :]]
 
 
 def forward_kernel(me_ref, *refs, pairs, frames, far, near, owned):
@@ -134,7 +130,7 @@
     turned_refs = rest[3:]
     for i in range(me_ref.shape[0]):
         later_ref[i] = me_ref[i]
-    slope1_ref, slope2_ref, hat1_ref, hat2_ref, scale1_ref, scale2_ref = state_views(state_ref)
+    slope1_ref, slope2_ref, hat1_ref, hat2_ref, scale1_ref, scale2_ref, pick_ref, gain_at = state_views(state_ref)
     copies[0].wait()
     channels = feat_ref.shape[1]
     n2 = pairs * frames
@@ -162,7 +158,22 @@
     slope2_ref[...] = slope
     hat2_ref[...] = hat
     scale2_ref[...] = jnp.broadcast_to(scale, scale2_ref.shape)
-    frames_ref[...] = made.astype(BF)
+    none = jnp.zeros((frames, channels), F32)
+    sent = []
+    for d in range(frames_ref.shape[0] // frames):
+        rows = none
+        for p in range(pairs):
+            rows = jnp.where(me_ref[4 + 2 * pairs + 2 * p] == d, made[p * frames : (p + 1) * frames], rows)
+        sent.append(rows)
+    frames_ref[...] = jnp.concatenate(sent, axis=0).astype(BF)
+    row = lax.broadcasted_iota(jnp.int32, (n2, 1), 0)
+    slot = jnp.zeros_like(row)
+    for p in range(pairs):
+        slot = jnp.where(lax.div(row, frames) == p, me_ref[4 + 2 * pairs + 2 * p], slot)
+    slot = slot * (2 * frames) + lax.rem(row, frames)
+    place = lax.broadcasted_iota(jnp.int32, (n2, channels), 1)
+    pick_ref[...] = jnp.where(place == slot, 1.0, 0.0)
+    gain_at[...] = jnp.concatenate([gain_ref[...], jnp.zeros((6, channels), F32)], axis=0)
     wide = in_turned.shape[1]
     fill = [jnp.zeros((wide - 3 * n2, channels), F32)] if wide > 3 * n2 else []
     for tap in range(2):
@@ -183,35 +194,17 @@
         ).astype(BF)
 
 
-def send_kernel(got_ref, me_ref, mine_ref, other_ref, frames_ref, out_ref, rows32, *, pairs, frames):
+def send_kernel(got_ref, mine_ref, other_ref, sent_ref, out_ref, rows32, *, frames):
     rows32[...] = mine_ref[...].astype(F32) + other_ref[...].astype(F32)
     blocks = rows32.shape[0] // frames
-    made = frames_ref[...].astype(F32)
-    none = jnp.zeros((frames, made.shape[1]), F32)
+    sent = sent_ref[...].astype(F32)
+    none = jnp.zeros((frames, sent.shape[1]), F32)
     for d in range(out_ref.shape[0]):
-        block = block_from(got_ref, me_ref, d)
+        block = got_ref[d, 0] - 1
         safe = jnp.clip(block, 0, blocks - 1)
         grads = rows32[pl.ds(pl.multiple_of(safe * frames, frames), frames), :]
         grads = jnp.where(block >= 0, grads, none)
-        sent = none
-        for p in range(pairs):
-            sent = jnp.where(me_ref[4 + 2 * pairs + 2 * p] == d, made[p * frames : (p + 1) * frames], sent)
-        out_ref[d] = jnp.concatenate([grads, sent], axis=0).astype(BF)
-
-
-def place_kernel(got_ref, me_ref, slots_ref, out_ref, rows32, *, frames):
-    rows32[...] = jnp.zeros_like(rows32)
-    for d in range(slots_ref.shape[0]):
-        block = block_from(got_ref, me_ref, d)
-
-        @pl.when(block >= 0)
-        def _():
-            safe = jnp.clip(block, 0, rows32.shape[0] // frames - 1)
-            rows32[pl.ds(pl.multiple_of(safe * frames, frames), frames), :] = slots_ref[d].astype(F32)[
-                frames:
-            ]
-
-    out_ref[...] = rows32[...].astype(BF)
+        out_ref[d] = jnp.concatenate([grads, sent[d * frames : (d + 1) * frames]], axis=0).astype(BF)
 
 
 def pack(rows, channels):
@@ -244,27 +237,35 @@
     return jnp.concatenate(parts, axis=1)
 
 
-def project_kernel(me_ref, mine_ref, other_ref, weight_ref, cotangent_ref, packed_ref, keep_ref, send_ref):
-    rows32 = mine_ref[...].astype(F32) + other_ref[...].astype(F32)
-    packed_ref[...] = dot_nt(weight_ref[...], rows32.astype(BF)).astype(BF)
-    partial = dot_nt(rows32.T.astype(BF), cotangent_ref[...])
-    channels, width = partial.shape
-    each = channels // (2 * keep_ref.shape[0])
-    for z in range(keep_ref.shape[0]):
-        low = pack(partial[2 * z * each : (2 * z + 1) * each], channels)
-        high = pack(partial[(2 * z + 1) * each : (2 * z + 2) * each], channels)
-        keep_ref[z] = jnp.where(me_ref[3] == 0, low, high)
-        send_ref[z] = jnp.where(me_ref[3] == 0, high, low).astype(BF)
-
-
-def fold_kernel(me_ref, keep_ref, got_ref, own_ref, *out_refs):
-    for f in range(keep_ref.shape[0]):
-        z = me_ref[2] ^ f
-        total = keep_ref[z] + got_ref[z].astype(F32)
-        if f == 0:
-            own_ref[...] = total
-        else:
-            out_refs[f - 1][...] = total.astype(BF)
+def project_kernel(me_ref, *refs, start, near, frames):
+    side_refs = refs[:near]
+    weight_ref, mine_ref, other_ref, packed_ref, own_ref = refs[near : near + 5]
+    out_refs, held = refs[near + 5 : -1], refs[-1]
+    channels, seq = weight_ref.shape[1], packed_ref.shape[1]
+    dp_count = (side_refs[0].shape[0] - start - 8) // (1 + frames)
+    row = lax.broadcasted_iota(jnp.int32, (dp_count * frames, seq), 0)
+    lane = lax.broadcasted_iota(jnp.int32, (dp_count * frames, seq), 1)
+    block = (lax.div(lane, frames) + 1).astype(F32)
+    same = lax.rem(lane, frames) == lax.rem(row, frames)
+    shards = [0.0, 0.0]
+    for k in range(near):
+        tail = side_refs[k][start:, :].astype(F32)
+        ids = tail[8 : 8 + dp_count, :seq]
+        ids = jnp.broadcast_to(ids[:, None, :], (dp_count, frames, seq)).reshape(dp_count * frames, seq)
+        pick = jnp.where(jnp.logical_and(same, ids == block), 1.0, 0.0).astype(BF)
+        shards[2 * k // near] += lax.dot_general(
+            pick, tail[8 + dp_count :].astype(BF), (((0,), (0,)), ((), ())), preferred_element_type=F32
+        )
+    packed_ref[...] = dot_nt(weight_ref[...], shards[0].astype(BF)).astype(BF)
+    partial = dot_nt(shards[0].T.astype(BF), mine_ref[...]) + dot_nt(shards[1].T.astype(BF), other_ref[...])
+    each = channels // dp_count
+    for z in range(held.shape[0]):
+        low = partial[2 * z * each : (2 * z + 1) * each]
+        high = partial[(2 * z + 1) * each : (2 * z + 2) * each]
+        held[z] = pack(jnp.where(me_ref[3] == 0, low, high), channels)
+    own_ref[...] = held[me_ref[2]]
+    for f in range(1, held.shape[0]):
+        out_refs[f - 1][...] = held[me_ref[2] ^ f].astype(BF)
 
 
 def norm_back(grad, slope_ref, hat_ref, scale_ref, gain):
@@ -282,15 +283,12 @@
     )
 
 
-def back_kernel(
-    me_ref, slots_ref, state_ref, weight_ref, gain_ref, out_ref, grads32, *, pairs, frames
-):
+def back_kernel(slots_ref, got_ref, state_ref, weight_ref, out_ref, *, frames):
     channels = weight_ref.shape[2]
-    slope1_ref, slope2_ref, hat1_ref, hat2_ref, scale1_ref, scale2_ref = state_views(state_ref)
-    for p in range(pairs):
-        slot = jnp.clip(me_ref[4 + 2 * pairs + 2 * p], 0, slots_ref.shape[0] - 1)
-        grads32[p * frames : (p + 1) * frames, :] = slots_ref[slot].astype(F32)[:frames]
-    second, gain2, shift2 = norm_back(grads32[...], slope2_ref, hat2_ref, scale2_ref, gain_ref[1:2, :])
+    slope1_ref, slope2_ref, hat1_ref, hat2_ref, scale1_ref, scale2_ref, pick_ref, gain_ref = state_views(state_ref)
+    slots = slots_ref[...]
+    grads = dot(pick_ref[:, : slots.shape[0]].astype(BF), slots)
+    second, gain2, shift2 = norm_back(grads, slope2_ref, hat2_ref, scale2_ref, gain_ref[1:2, :])
     hidden = jnp.concatenate(
         [
             dot_nt(second, weight_ref[1, :channels, :]),
@@ -302,7 +300,12 @@
     first, gain1, shift1 = norm_back(hidden, slope1_ref, hat1_ref, scale1_ref, gain_ref[0:1, :])
     sums = jnp.concatenate([gain1, shift1, gain2, shift2], axis=0)
     high = sums.astype(BF).astype(F32)
-    rows = [high, sums - high, jnp.zeros((8, channels), F32)]
+    ids = got_ref[...].astype(F32)
+    slots32 = slots.astype(F32)
+    rows = [high, sums - high, jnp.concatenate([ids] * (channels // ids.shape[1]), axis=1)]
+    rows += [
+        slots32[(2 * d + 1) * frames : (2 * d + 2) * frames] for d in range(slots.shape[0] // (2 * frames))
+    ]
     n1, n2 = first.shape[0], second.shape[0]
     out_ref[:n1, :] = first
     out_ref[n1 : n1 + n2, :] = second
@@ -336,7 +339,7 @@
         side = in_ref[...]
         first += dot(side[:, :n1], grad_ref[:n1, :])
         second += dot(side[:, n1 : n1 + n2], grad_ref[n1 : n1 + n2, :])
-        tail = grad_ref[n1 + n2 :, :].astype(F32)
+        tail = grad_ref[n1 + n2 : n1 + n2 + 16, :].astype(F32)
         sums += tail[0:4] + tail[4:8]
     high = sums.astype(BF).astype(F32)
     for z in range(far):
@@ -401,7 +404,7 @@
         functools.partial(start_kernel, pairs=pairs, frames=frames),
         [
             shape(4 + 6 * pairs, kind=jnp.int32),
-            shape(dp_count, -(-dp_count // 128) * 128, kind=jnp.int32),
+            shape(dp_count, 128, kind=jnp.int32),
             shape(seq, channels),
         ],
         (place, proj_weight.T, grad_packed.T, lengths, dests, offsets),
@@ -430,15 +433,15 @@
         ),
         [
             shape(*me.shape, kind=jnp.int32),
-            shape(n2, channels),
-            shape(3 * (n1 + n2), channels, kind=F32),
+            shape(dp_count * frames, channels),
+            shape(10 * n2 + 8, channels, kind=F32),
         ]
         + [shape(2 * far * owned, wide)] * (near // 2),
         (me, feat, norm_gain, norm_shift, conv_weight),
         scalars=1,
         fetched=4,
         to_scalars=1,
-        flops=2 * (n1 + n2) * 2 * channels * channels,
+        flops=10**10,
         scratch=[
             pltpu.VMEM(feat.shape, BF),
             pltpu.VMEM(norm_gain.shape, F32),
@@ -452,7 +455,6 @@
     )
     me, pair_frames, state = made[:3]
     in_sides = [swap(side, 2 * k) if k else side for k, side in enumerate(made[3:])]
-    in_sides += [swap(side, 1) for side in in_sides]
 
     for mask in bits[:-1]:
         arrived, pair_frames, got_index = lax.optimization_barrier(
@@ -462,54 +464,42 @@
     other_rows = swap(grad_rows, bits[-1])
 
     sent = call(
-        functools.partial(send_kernel, pairs=pairs, frames=frames),
+        functools.partial(send_kernel, frames=frames),
         shape(dp_count, 2 * frames, channels),
-        (got_index, me, grad_rows, other_rows, pair_frames),
-        scalars=2,
+        (got_index, grad_rows, other_rows, pair_frames),
+        scalars=1,
         scratch=[pltpu.VMEM((seq, channels), F32)],
     )
     slots = lax.all_to_all(sent, "dp", split_axis=0, concat_axis=0, tiled=True)
-    slots, *in_sides = lax.optimization_barrier((slots, *in_sides))
-
+    cotangent = grad_packed.T
+    other_cotangent = swap(cotangent, mp_count)
+    slots, other_cotangent, *in_sides[: near // 2] = lax.optimization_barrier(
+        (slots, other_cotangent, *in_sides[: near // 2])
+    )
+
+    in_sides += [swap(side, 1) for side in in_sides]
+    rows_sent = n1 + n2 + 8 + dp_count * (1 + frames)
     grads = call(
-        functools.partial(back_kernel, pairs=pairs, frames=frames),
-        shape(n1 + n2 + 16, channels),
-        (me, slots, state, conv_weight, norm_gain),
-        scalars=1,
+        functools.partial(back_kernel, frames=frames),
+        shape(rows_sent, channels),
+        (slots.reshape(-1, channels), got_index, state, conv_weight),
         flops=2 * n2 * 2 * channels * channels,
-        scratch=[pltpu.VMEM((n2, channels), F32)],
     )
     by_mask = {mask: swap(grads, mask) if mask else grads for mask in range(0, near, 2)}
     for mask in range(0, near, 2):
         by_mask[mask + 1] = swap(by_mask[mask], 1)
 
-    placed = call(
-        functools.partial(place_kernel, frames=frames),
-        shape(seq, channels),
-        (got_index, me, slots),
-        scalars=2,
-        scratch=[pltpu.VMEM((seq, channels), F32)],
-    )
-    for mask in bits[:-1]:
-        placed = placed + swap(placed, mask)
     per_dp = channels // dp_count
-    packed, keep, send = call(
-        project_kernel,
-        [
-            shape(width, seq),
-            shape(far, per_dp * width // channels, channels, kind=F32),
-            shape(far, per_dp * width // channels, channels),
-        ],
-        (me, placed, swap(placed, bits[-1]), proj_weight.T, grad_packed.T),
-        scalars=1,
-        flops=4 * seq * channels * width,
-    )
-    proj_parts = call(
-        fold_kernel,
-        [shape(per_dp * width // channels, channels, kind=F32)]
-        + [shape(per_dp * width // channels, channels)] * (far - 1),
-        (me, keep, swap(send, mp_count)),
-        scalars=1,
+    packed_rows = per_dp * width // channels
+    sides = tuple(by_mask[k] for k in range(near))
+    packed, *proj_parts = call(
+        functools.partial(project_kernel, start=n1 + n2, near=near, frames=frames),
+        [shape(width, seq), shape(packed_rows, channels, kind=F32)]
+        + [shape(packed_rows, channels)] * (far - 1),
+        (me, *sides, proj_weight.T, cotangent, other_cotangent),
+        scalars=1,
+        flops=6 * seq * channels * width,
+        scratch=[pltpu.VMEM((far, packed_rows, channels), F32)],
     )
 
     grad_features = call(
@@ -523,7 +513,7 @@
     conv_parts = call(
         functools.partial(kernel_grad_kernel, n1=n1, n2=n2, owned=owned, near=near, far=far),
         [shape(2 * owned + 8, channels, kind=F32)] + [shape(2 * owned + 8, channels)] * (far - 1),
-        (me,) + tuple(by_mask[k] for k in range(near)) + tuple(in_sides),
+        (me, *sides, *in_sides),
         scalars=1,
         flops=2 * (n1 + n2) * 2 * channels * channels,
         scratch=[pltpu.VMEM((far, 2 * owned + 8, channels), F32)],

time: 70.5 us -> 68.4 us (0.970)
  local copies, waits for them, and re-layouts: 3.71 us -> 1.95 us
  starting transfers between devices: 31.2 us -> 32.8 us
  Pallas kernels: 16.4 us -> 15 us
    unnamed x24 -> x16, local copies, waits for them, and re-layouts: 3.71 us -> 1.95 us
    all_to_all x1, starting transfers between devices: 3.55 us -> 5.24 us  [local(): slots = lax.all_to_all(sent, 'dp', split_axis=0, concat_axis=0, tiled=True)]
    all_to_all x1, waiting for transfers between devices: 2.47 us -> 0.79 us  [local(): lax.all_to_all(index, 'dp', split_axis=0, concat_axis=0, tiled=True)]
    ppermute x25 -> x23, starting transfers between devices: 21.8 us -> 20.3 us  [swap(): lax.ppermute(x, everyone, [(i, i ^ mask) for i in range(dp_count * mp_cou...]
    all_to_all x1, starting transfers between devices: 5.81 us -> 7.27 us  [local(): lax.all_to_all(index, 'dp', split_axis=0, concat_axis=0, tiled=True)]
    pallas_call x10 -> x8, Pallas kernels: 16.4 us -> 15 us  [call(): pl.pallas_call(body, out_shape=out, in_specs=specs, out_specs=[pl.BlockSp...]
    ppermute x25 -> x23, waiting for transfers between devices: 14.7 us -> 16 us  [swap(): lax.ppermute(x, everyone, [(i, i ^ mask) for i in range(dp_count * mp_cou...]
  transfers between devices with their start and end apart: 27 -> 25, of which waited for: 12 -> 11; matrix products, arithmetic and copies ran while one was open for 0% -> 0% of each run, Pallas kernels for 15% -> 13%
where the time goes in v5:
time: 68.4 us; the launch traced here: 68 us
  starting transfers between devices  32.8 us (48%)
  waiting for transfers between devices  16.8 us (25%)
  Pallas kernels  15 us (22%)
  local copies, waits for them, and re-layouts  1.95 us (3%)
  between operations  0.77 us (1%)
    ppermute x23, starting transfers between devices, swap(): lax.ppermute(x, everyone, [(i, i ^ mask) for i in range(dp_count * mp_cou...  20.3 us
    ppermute x23, waiting for transfers between devices, swap(): lax.ppermute(x, everyone, [(i, i ^ mask) for i in range(dp_count * mp_cou...  16 us
    pallas_call x8, Pallas kernels, call(): pl.pallas_call(body, out_shape=out, in_specs=specs, out_specs=[pl.BlockSp...  15 us
    all_to_all x1, starting transfers between devices, local(): lax.all_to_all(index, 'dp', split_axis=0, concat_axis=0, tiled=True)  7.27 us
    all_to_all x1, starting transfers between devices, local(): slots = lax.all_to_all(sent, 'dp', split_axis=0, concat_axis=0, tiled=True)  5.24 us
    unnamed x16, local copies, waits for them, and re-layouts  1.95 us
  transfers between devices with their start and end apart: 25, of which 11 were waited for; matrix products, arithmetic and copies ran while one was open for 0% of the time, Pallas kernels for 13%

profile of v5, /device:TPU:0, one launch (start us, length us, event | category | flops | bytes accessed | tf_op | source)
XLA Modules:
  0.0 68.0 jit_solution(13285865358124228608)
XLA Ops:
  0.6 0.6 pad_add_fusion.place_ref
  1.2 2.6 %shard_map.128 = (s32[28]{0:T(128)}, s32[8,128]{1,0:T(8,128)}, bf16[128,512]{1,0:T(8,128)(2,1)}) custom-call(s32[4]{0:T(128)} %pad_add_fusion.place_ref, bf16[320,512]{1,0:T(8,128)(2,1)} %bitcast.14, bf16[320,128]{1,0:T(8,128)(2,1)} %bitcast.17, s32[8]{0:T(128)} %lengths_hbm.1, s32[8]{0:T(128)} %dests_hbm.1, s32[8]{0:T(128)} %offsets_hbm.1), custom_call_target="tpu_custom_call" | custom-call | flops 41943040 | bytes 409712 | tf_op jit(solution)/shard_map/pallas_call | solution.py:25
  3.9 7.3 %all-to-all-start = ((s32[8,1,128]{2,1,0:T(1,128)}), s32[8,1,128]{2,1,0:T(1,128)S(1)}, u32[]{:S(2)}, u32[]{:S(2)}) async-start(s32[8,1,128]{2,1,0:T(1,128)} %bitcast.23), calls=%async_computation | async-start | bytes 8192 | tf_op jit(solution)/shard_map/all_to_all | solution.py:426
  11.1 1.5 %collective-permute-start = (bf16[128,512]{1,0:T(8,128)(2,1)}, bf16[128,512]{1,0:T(8,128)(2,1)S(1)}, u32[]{:S(2)}, u32[]{:S(2)}) collective-permute-start(bf16[128,512]{1,0:T(8,128)(2,1)} %get-tuple-element.38), channel_id=1, source_target_pairs={{0,2},{1,3},{2,0},{3,1},{4,6},{5,7},{6,4},{7,5},{8,10},{9,11},{10,... | collective-permute-start | bytes 393224 | tf_op jit(solution)/shard_map/ppermute | solution.py:396
  12.7 4.1 %shard_map.129 = (s32[28]{0:T(128)}, bf16[64,512]{1,0:T(8,128)(2,1)}, f32[328,512]{1,0:T(8,128)}, bf16[256,128]{1,0:T(8,128)(2,1)}, bf16[256,128]{1,0:T(8,128)(2...) custom-call(s32[28]{0:T(128)} %get-tuple-element.36.me_ref, bf16[256,512]{1,0:T(8,128)(2,1)} %bitcast.24, ...), custom_call_target="tpu_custom_call" | custom-call | flops 10000000000 | bytes 2367600 | tf_op jit(solution)/shard_map/pallas_call | solution.py:25
  16.8 0.8 %all-to-all-done = s32[8,1,128]{2,1,0:T(1,128)S(1)} async-done(((s32[8,1,128]{2,1,0:T(1,128)}), s32[8,1,128]{2,1,0:T(1,128)S(1)}, u32[]{:S(2)}, u32[]{:S(2)}) %all-to-all-start) | async-done | bytes 4128 | tf_op jit(solution)/shard_map/all_to_all | solution.py:426
  17.6 0.0 copy-start.4
  17.6 0.0 copy-start.1
  17.7 0.1 collective-permute-start.1
  17.8 1.3 %collective-permute-done.1.other_ref = bf16[128,512]{1,0:T(8,128)(2,1)S(1)} collective-permute-done((bf16[128,512]{1,0:T(8,128)(2,1)S(1)}, bf16[128,512]{1,0:T(8,128)(2,1)S(1)}, u32[]{:S(2)}, u32[]{:S(2)}) %collective-permute-start.1) | collective-permute-done | bytes 131104 | tf_op jit(solution)/shard_map/ppermute | solution.py:396
  19.1 0.8 %copy-done.5 = bf16[64,512]{1,0:T(8,128)(2,1)S(1)} copy-done((bf16[64,512]{1,0:T(8,128)(2,1)S(1)}, bf16[64,512]{1,0:T(8,128)(2,1)}, u32[]{:S(2)}) %copy-start.5) | copy-done | bytes 65560
  19.9 1.3 %shard_map.130 = bf16[8,16,512]{2,1,0:T(8,128)(2,1)} custom-call(s32[8,128]{1,0:T(8,128)S(1)} %bitcast.20, bf16[128,512]{1,0:T(8,128)(2,1)S(1)} %add_convert_fusion.mine_ref, bf16[128,512]{1,0:T(8,128)(2,1)S(1)} %collective-permute-done.1.other_ref, bf16[64,512]{1,0:T(8,128)(2,1)S(1)} %copy-done.5), custom_call_target="tpu_custom_call" | custom-call | bytes 331776 | tf_op jit(solution)/shard_map/pallas_call | solution.py:25
  21.2 5.2 %all-to-all-start.1 = ((bf16[8,16,512]{2,1,0:T(8,128)(2,1)}), bf16[8,16,512]{2,1,0:T(8,128)(2,1)S(1)}, u32[]{:S(2)}, u32[]{:S(2)}) async-start(bf16[8,16,512]{2,1,0:T(8,128)(2,1)} %shard_map.130), calls=%async_computation.1 | async-start | bytes 262144 | tf_op jit(solution)/shard_map/all_to_all | solution.py:473
  26.5 2.0 %collective-permute-start.2 = (bf16[320,128]{1,0:T(8,128)(2,1)S(1)}, bf16[320,128]{1,0:T(8,128)(2,1)S(1)}, u32[]{:S(2)}, u32[]{:S(2)}) collective-permute-start(bf16[320,128]{1,0:T(8,128)(2,1)S(1)} %bitcast.18), channel_id=1, source_target_pairs={{0,4},{1,5},{2,6},{3,7},{4,0},{5,1},{6,2},{7,3},{8,12},{9,13},{10,... | collective-permute-start | bytes 245768 | tf_op jit(solution)/shard_map/ppermute | solution.py:396
  28.5 1.0 %collective-permute-start.3 = (bf16[256,128]{1,0:T(8,128)(2,1)}, bf16[256,128]{1,0:T(8,128)(2,1)S(1)}, u32[]{:S(2)}, u32[]{:S(2)}) collective-permute-start(bf16[256,128]{1,0:T(8,128)(2,1)} %get-tuple-element.45), channel_id=1, source_target_pairs={{0,2},{1,3},{2,0},{3,1},{4,6},{5,7},{6,4},{7,5},{8,10},{9,11},{10,... | collective-permute-start | bytes 196616 | tf_op jit(solution)/shard_map/ppermute | solution.py:396
  29.5 0.1 collective-permute-start.4
  29.6 2.4 %collective-permute-start.5 = (bf16[256,128]{1,0:T(8,128)(2,1)}, bf16[256,128]{1,0:T(8,128)(2,1)S(1)}, u32[]{:S(2)}, u32[]{:S(2)}) collective-permute-start(bf16[256,128]{1,0:T(8,128)(2,1)} %get-tuple-element.47), channel_id=1, source_target_pairs={{0,6},{1,7},{2,4},{3,5},{4,2},{5,3},{6,0},{7,1},{8,14},{9,15},{10,... | collective-permute-start | bytes 196616 | tf_op jit(solution)/shard_map/ppermute | solution.py:396
  32.0 1.0 %collective-permute-done.3.refs_9_ = bf16[256,128]{1,0:T(8,128)(2,1)S(1)} collective-permute-done((bf16[256,128]{1,0:T(8,128)(2,1)}, bf16[256,128]{1,0:T(8,128)(2,1)S(1)}, u32[]{:S(2)}, u32[]{:S(2)}) %collective-permute-start.3) | collective-permute-done | bytes 65568 | tf_op jit(solution)/shard_map/ppermute | solution.py:396
  33.0 1.5 %collective-permute-done.4.refs_10_ = bf16[256,128]{1,0:T(8,128)(2,1)S(1)} collective-permute-done((bf16[256,128]{1,0:T(8,128)(2,1)}, bf16[256,128]{1,0:T(8,128)(2,1)S(1)}, u32[]{:S(2)}, u32[]{:S(2)}) %collective-permute-start.4) | collective-permute-done | bytes 65568 | tf_op jit(solution)/shard_map/ppermute | solution.py:396
  34.4 1.1 %collective-permute-done.5.refs_11_ = bf16[256,128]{1,0:T(8,128)(2,1)S(1)} collective-permute-done((bf16[256,128]{1,0:T(8,128)(2,1)}, bf16[256,128]{1,0:T(8,128)(2,1)S(1)}, u32[]{:S(2)}, u32[]{:S(2)}) %collective-permute-start.5) | collective-permute-done | bytes 65568 | tf_op jit(solution)/shard_map/ppermute | solution.py:396
  35.5 0.0 collective-permute-done.2.refs_10_
  35.6 0.0 all-to-all-done.1
  35.6 1.1 %copy-done.2 = f32[328,512]{1,0:T(8,128)S(1)} copy-done((f32[328,512]{1,0:T(8,128)S(1)}, f32[328,512]{1,0:T(8,128)}, u32[]{:S(2)}) %copy-start.2) | copy-done | bytes 671768
  36.7 0.7 shard_map.131.refs_0_.grad_ref
  37.3 1.9 %collective-permute-start.11 = (bf16[176,512]{1,0:T(8,128)(2,1)S(1)}, bf16[176,512]{1,0:T(8,128)(2,1)S(1)}, u32[]{:S(2)}, u32[]{:S(2)}) collective-permute-start(bf16[176,512]{1,0:T(8,128)(2,1)S(1)} %shard_map.131.refs_0_.grad_ref), channel_id=1, source_target_pairs={{0,6},{1,7},{2,4},{3,5},{4,2},{5,3},{6,0},{7,1},{8,14},{9,15},{10,... | collective-permute-start | bytes 540680 | tf_op jit(solution)/shard_map/ppermute | solution.py:396
  39.2 0.7 %collective-permute-start.9 = (bf16[176,512]{1,0:T(8,128)(2,1)S(1)}, bf16[176,512]{1,0:T(8,128)(2,1)S(1)}, u32[]{:S(2)}, u32[]{:S(2)}) collective-permute-start(bf16[176,512]{1,0:T(8,128)(2,1)S(1)} %shard_map.131.refs_0_.grad_ref), channel_id=1, source_target_pairs={{0,4},{1,5},{2,6},{3,7},{4,0},{5,1},{6,2},{7,3},{8,12},{9,13},{10,... | collective-permute-start | bytes 540680 | tf_op jit(solution)/shard_map/ppermute | solution.py:396
  39.9 1.0 %collective-permute-start.7 = (bf16[176,512]{1,0:T(8,128)(2,1)S(1)}, bf16[176,512]{1,0:T(8,128)(2,1)S(1)}, u32[]{:S(2)}, u32[]{:S(2)}) collective-permute-start(bf16[176,512]{1,0:T(8,128)(2,1)S(1)} %shard_map.131.refs_0_.grad_ref), channel_id=1, source_target_pairs={{0,2},{1,3},{2,0},{3,1},{4,6},{5,7},{6,4},{7,5},{8,10},{9,11},{10,... | collective-permute-start | bytes 540680 | tf_op jit(solution)/shard_map/ppermute | solution.py:396
  40.9 4.3 %collective-permute-done.11.refs_6_ = bf16[176,512]{1,0:T(8,128)(2,1)S(1)} collective-permute-done((bf16[176,512]{1,0:T(8,128)(2,1)S(1)}, bf16[176,512]{1,0:T(8,128)(2,1)S(1)}, u32[]{:S(2)}, u32[]{:S(2)}) %collective-permute-start.11) | collective-permute-done | bytes 180256 | tf_op jit(solution)/shard_map/ppermute | solution.py:396
  45.2 1.7 %collective-permute-done.9.refs_4_ = bf16[176,512]{1,0:T(8,128)(2,1)S(1)} collective-permute-done((bf16[176,512]{1,0:T(8,128)(2,1)S(1)}, bf16[176,512]{1,0:T(8,128)(2,1)S(1)}, u32[]{:S(2)}, u32[]{:S(2)}) %collective-permute-start.9) | collective-permute-done | bytes 180256 | tf_op jit(solution)/shard_map/ppermute | solution.py:396
  46.9 0.1 collective-permute-done.7.refs_2_
  47.0 0.4 collective-permute-start.8
  47.4 0.1 collective-permute-start.13
  47.5 0.4 collective-permute-start.14
  47.9 0.1 collective-permute-start.15
  48.0 0.2 collective-permute-done.10.refs_5_
  48.3 0.1 collective-permute-start.16
  48.4 0.1 collective-permute-done.8.refs_3_
  48.5 1.8 %shard_map.132 = (bf16[320,128]{1,0:T(8,128)(2,1)}, f32[40,512]{1,0:T(8,128)S(1)}, bf16[40,512]{1,0:T(8,128)(2,1)S(1)}, bf16[40,512]{1,0:T(8,128)(2,1)S(1)}, bf16[40,512]{1,0:T(8,128)(2,1)S(1)}) custom-call(s32[28]{0:T(128)S(1)} %copy-done.6, bf16[176,512]{1,0:T(8,128)(2,1)S(1)} %shard_map.131.refs_0_.grad_ref, ...), custom_call_target="tpu_custom_call" | custom-call | flops 125829120 | bytes 1933424 | tf_op jit(solution)/shard_map/pallas_call | solution.py:25
  50.4 1.7 %collective-permute-start.20 = (bf16[40,512]{1,0:T(8,128)(2,1)S(1)}, bf16[40,512]{1,0:T(8,128)(2,1)S(1)}, u32[]{:S(2)}, u32[]{:S(2)}) collective-permute-start(bf16[40,512]{1,0:T(8,128)(2,1)S(1)} %get-tuple-element.61), channel_id=1, source_target_pairs={{0,8},{1,9},{2,10},{3,11},{4,12},{5,13},{6,14},{7,15},{8,0},{9,1},... | collective-permute-start | bytes 122888 | tf_op jit(solution)/shard_map/ppermute | solution.py:396
  52.0 1.3 %shard_map.134 = (f32[72,512]{1,0:T(8,128)S(1)}, bf16[72,512]{1,0:T(8,128)(2,1)S(1)}, bf16[72,512]{1,0:T(8,128)(2,1)S(1)}, bf16[72,512]{1,0:T(8,128)(2,1)S(1)}) custom-call(s32[28]{0:T(128)S(1)} %copy-done.6, bf16[176,512]{1,0:T(8,128)(2,1)S(1)} %shard_map.131.refs_0_.grad_ref, bf16[176,512]{1,0:T(8,128)(2,1)S(1)} %collective-permute-done.6.refs_1_, ...), custom_call_target="tpu_custom_call" | custom-call | flops 100663296 | bytes 1966192 | tf_op jit(solution)/shard_map/pallas_call | solution.py:25
  53.3 0.4 collective-permute-start.17
  53.7 2.6 %collective-permute-start.18 = (bf16[72,512]{1,0:T(8,128)(2,1)S(1)}, bf16[72,512]{1,0:T(8,128)(2,1)S(1)}, u32[]{:S(2)}, u32[]{:S(2)}) collective-permute-start(bf16[72,512]{1,0:T(8,128)(2,1)S(1)} %get-tuple-element.58), channel_id=1, source_target_pairs={{0,16},{1,17},{2,18},{3,19},{4,20},{5,21},{6,22},{7,23},{8,24},{9,... | collective-permute-start | bytes 221192 | tf_op jit(solution)/shard_map/ppermute | solution.py:396
  56.3 1.4 %collective-permute-start.19 = (bf16[72,512]{1,0:T(8,128)(2,1)S(1)}, bf16[72,512]{1,0:T(8,128)(2,1)S(1)}, u32[]{:S(2)}, u32[]{:S(2)}) collective-permute-start(bf16[72,512]{1,0:T(8,128)(2,1)S(1)} %get-tuple-element.59), channel_id=1, source_target_pairs={{0,24},{1,25},{2,26},{3,27},{4,28},{5,29},{6,30},{7,31},{8,16},{9,... | collective-permute-start | bytes 221192 | tf_op jit(solution)/shard_map/ppermute | solution.py:396
  57.8 1.5 %collective-permute-start.21 = (bf16[40,512]{1,0:T(8,128)(2,1)S(1)}, bf16[40,512]{1,0:T(8,128)(2,1)S(1)}, u32[]{:S(2)}, u32[]{:S(2)}) collective-permute-start(bf16[40,512]{1,0:T(8,128)(2,1)S(1)} %get-tuple-element.62), channel_id=1, source_target_pairs={{0,16},{1,17},{2,18},{3,19},{4,20},{5,21},{6,22},{7,23},{8,24},{9,... | collective-permute-start | bytes 122888 | tf_op jit(solution)/shard_map/ppermute | solution.py:396
  59.2 0.9 %collective-permute-start.22 = (bf16[40,512]{1,0:T(8,128)(2,1)S(1)}, bf16[40,512]{1,0:T(8,128)(2,1)S(1)}, u32[]{:S(2)}, u32[]{:S(2)}) collective-permute-start(bf16[40,512]{1,0:T(8,128)(2,1)S(1)} %get-tuple-element.63), channel_id=1, source_target_pairs={{0,24},{1,25},{2,26},{3,27},{4,28},{5,29},{6,30},{7,31},{8,16},{9,... | collective-permute-start | bytes 122888 | tf_op jit(solution)/shard_map/ppermute | solution.py:396
  60.1 1.9 %shard_map.133 = bf16[256,512]{1,0:T(8,128)(2,1)} custom-call(s32[28]{0:T(128)S(1)} %copy-done.6, bf16[176,512]{1,0:T(8,128)(2,1)S(1)} %shard_map.131.refs_0_.grad_ref, bf16[2,1024,512]{2,1,0:T(8,128)(2,1)S(1)} %copy-done), custom_call_target="tpu_custom_call" | custom-call | flops 67108864 | bytes 2277488 | tf_op jit(solution)/shard_map/pallas_call | solution.py:25
  62.0 4.7 %collective-permute-done.21.refs_6_ = bf16[40,512]{1,0:T(8,128)(2,1)S(1)} collective-permute-done((bf16[40,512]{1,0:T(8,128)(2,1)S(1)}, bf16[40,512]{1,0:T(8,128)(2,1)S(1)}, u32[]{:S(2)}, u32[]{:S(2)}) %collective-permute-start.21) | collective-permute-done | bytes 40992 | tf_op jit(solution)/shard_map/ppermute | solution.py:396
  66.7 1.3 %shard_map.135 = (f32[2,32,512]{2,1,0:T(8,128)}, f32[2,32]{1,0:T(2,128)}, f32[64,320]{1,0:T(8,128)}) custom-call(s32[28]{0:T(128)S(1)} %copy-done.6, f32[72,512]{1,0:T(8,128)S(1)} %get-tuple-element.56.refs_0_, bf16[72,512]{1,0:T(8,128)(2,1)S(1)} %collective-permute-done.17.refs_1_, bf16[72,512]{1,0:T(8,128)(2,1)S(1)} %collective-permute-done.18.refs_2_, ...), custom_call_target="tpu_custom_call" | custom-call | bytes 573552 | tf_op jit(solution)/shard_map/pallas_call | solution.py:25
  (28 shorter events, 0.1 us)
Async XLA Ops:
  3.9 13.7 %all-to-all-start = ((s32[8,1,128]{2,1,0:T(1,128)}), s32[8,1,128]{2,1,0:T(1,128)S(1)}, u32[]{:S(2)}, u32[]{:S(2)}) async-start(s32[8,1,128]{2,1,0:T(1,128)} %bitcast.23), calls=%async_computation | async-start | bytes 8192 | tf_op jit(solution)/shard_map/all_to_all | solution.py:426
  11.1 6.5 %collective-permute-start = (bf16[128,512]{1,0:T(8,128)(2,1)}, bf16[128,512]{1,0:T(8,128)(2,1)S(1)}, u32[]{:S(2)}, u32[]{:S(2)}) collective-permute-start(bf16[128,512]{1,0:T(8,128)(2,1)} %get-tuple-element.38), channel_id=1, source_target_pairs={{0,2},{1,3},{2,0},{3,1},{4,6},{5,7},{6,4},{7,5},{8,10},{9,11},{10,... | collective-permute-start | bytes 393224 | tf_op jit(solution)/shard_map/ppermute | solution.py:396
  12.7 5.0 %copy-start.7 = (bf16[128,512]{1,0:T(8,128)(2,1)S(1)}, bf16[128,512]{1,0:T(8,128)(2,1)}, u32[]{:S(2)}) copy-start(bf16[128,512]{1,0:T(8,128)(2,1)} %get-tuple-element.38) | copy-start | bytes 393220
  12.7 13.8 %copy-start.3 = (bf16[128,320]{0,1:T(8,128)(2,1)S(1)}, bf16[128,320]{0,1:T(8,128)(2,1)}, u32[]{:S(2)}) copy-start(bf16[128,320]{0,1:T(8,128)(2,1)} %param.17) | copy-start | bytes 245764
  12.7 22.9 %copy-start = (bf16[2,1024,512]{2,1,0:T(8,128)(2,1)S(1)}, bf16[2,1024,512]{2,1,0:T(8,128)(2,1)}, u32[]{:S(2)}) copy-start(bf16[2,1024,512]{2,1,0:T(8,128)(2,1)} %weight_ref.3) | copy-start | bytes 6291460
  17.6 30.9 %copy-start.6 = (s32[28]{0:T(128)S(1)}, s32[28]{0:T(128)}, u32[]{:S(2)}) copy-start(s32[28]{0:T(128)} %get-tuple-element.37.me_ref) | copy-start | bytes 340
  17.6 29.8 %copy-start.4 = (bf16[256,128]{1,0:T(8,128)(2,1)S(1)}, bf16[256,128]{1,0:T(8,128)(2,1)}, u32[]{:S(2)}) copy-start(bf16[256,128]{1,0:T(8,128)(2,1)} %get-tuple-element.52.refs_8_) | copy-start | bytes 196612
  17.6 30.9 %copy-start.1 = (bf16[512,320]{0,1:T(8,128)(2,1)S(1)}, bf16[512,320]{0,1:T(8,128)(2,1)}, u32[]{:S(2)}) copy-start(bf16[512,320]{0,1:T(8,128)(2,1)} %param.16) | copy-start | bytes 983044
  17.7 1.4 %collective-permute-start.1 = (bf16[128,512]{1,0:T(8,128)(2,1)S(1)}, bf16[128,512]{1,0:T(8,128)(2,1)S(1)}, u32[]{:S(2)}, u32[]{:S(2)}) collective-permute-start(bf16[128,512]{1,0:T(8,128)(2,1)S(1)} %add_convert_fusion.mine_ref), channel_id=1, source_target_pairs={{0,1},{1,0},{2,3},{3,2},{4,5},{5,4},{6,7},{7,6},{8,9},{9,8},{10,11... | collective-permute-start | bytes 393224 | tf_op jit(solution)/shard_map/ppermute | solution.py:396
  19.1 0.8 %copy-start.5 = (bf16[64,512]{1,0:T(8,128)(2,1)S(1)}, bf16[64,512]{1,0:T(8,128)(2,1)}, u32[]{:S(2)}) copy-start(bf16[64,512]{1,0:T(8,128)(2,1)} %get-tuple-element.43.sent_ref) | copy-start | bytes 196612
  21.2 14.3 %all-to-all-start.1 = ((bf16[8,16,512]{2,1,0:T(8,128)(2,1)}), bf16[8,16,512]{2,1,0:T(8,128)(2,1)S(1)}, u32[]{:S(2)}, u32[]{:S(2)}) async-start(bf16[8,16,512]{2,1,0:T(8,128)(2,1)} %shard_map.130), calls=%async_computation.1 | async-start | bytes 262144 | tf_op jit(solution)/shard_map/all_to_all | solution.py:473
  26.5 9.1 %collective-permute-start.2 = (bf16[320,128]{1,0:T(8,128)(2,1)S(1)}, bf16[320,128]{1,0:T(8,128)(2,1)S(1)}, u32[]{:S(2)}, u32[]{:S(2)}) collective-permute-start(bf16[320,128]{1,0:T(8,128)(2,1)S(1)} %bitcast.18), channel_id=1, source_target_pairs={{0,4},{1,5},{2,6},{3,7},{4,0},{5,1},{6,2},{7,3},{8,12},{9,13},{10,... | collective-permute-start | bytes 245768 | tf_op jit(solution)/shard_map/ppermute | solution.py:396
  28.5 4.5 %collective-permute-start.3 = (bf16[256,128]{1,0:T(8,128)(2,1)}, bf16[256,128]{1,0:T(8,128)(2,1)S(1)}, u32[]{:S(2)}, u32[]{:S(2)}) collective-permute-start(bf16[256,128]{1,0:T(8,128)(2,1)} %get-tuple-element.45), channel_id=1, source_target_pairs={{0,2},{1,3},{2,0},{3,1},{4,6},{5,7},{6,4},{7,5},{8,10},{9,11},{10,... | collective-permute-start | bytes 196616 | tf_op jit(solution)/shard_map/ppermute | solution.py:396
  29.5 5.0 %collective-permute-start.4 = (bf16[256,128]{1,0:T(8,128)(2,1)}, bf16[256,128]{1,0:T(8,128)(2,1)S(1)}, u32[]{:S(2)}, u32[]{:S(2)}) collective-permute-start(bf16[256,128]{1,0:T(8,128)(2,1)} %get-tuple-element.46), channel_id=1, source_target_pairs={{0,4},{1,5},{2,6},{3,7},{4,0},{5,1},{6,2},{7,3},{8,12},{9,13},{10,... | collective-permute-start | bytes 196616 | tf_op jit(solution)/shard_map/ppermute | solution.py:396
  29.6 6.0 %collective-permute-start.5 = (bf16[256,128]{1,0:T(8,128)(2,1)}, bf16[256,128]{1,0:T(8,128)(2,1)S(1)}, u32[]{:S(2)}, u32[]{:S(2)}) collective-permute-start(bf16[256,128]{1,0:T(8,128)(2,1)} %get-tuple-element.47), channel_id=1, source_target_pairs={{0,6},{1,7},{2,4},{3,5},{4,2},{5,3},{6,0},{7,1},{8,14},{9,15},{10,... | collective-permute-start | bytes 196616 | tf_op jit(solution)/shard_map/ppermute | solution.py:396
  35.6 1.1 %copy-start.2 = (f32[328,512]{1,0:T(8,128)S(1)}, f32[328,512]{1,0:T(8,128)}, u32[]{:S(2)}) copy-start(f32[328,512]{1,0:T(8,128)} %get-tuple-element.49.state_ref) | copy-start | bytes 2015236
  37.3 7.9 %collective-permute-start.11 = (bf16[176,512]{1,0:T(8,128)(2,1)S(1)}, bf16[176,512]{1,0:T(8,128)(2,1)S(1)}, u32[]{:S(2)}, u32[]{:S(2)}) collective-permute-start(bf16[176,512]{1,0:T(8,128)(2,1)S(1)} %shard_map.131.refs_0_.grad_ref), channel_id=1, source_target_pairs={{0,6},{1,7},{2,4},{3,5},{4,2},{5,3},{6,0},{7,1},{8,14},{9,15},{10,... | collective-permute-start | bytes 540680 | tf_op jit(solution)/shard_map/ppermute | solution.py:396
  39.2 7.6 %collective-permute-start.9 = (bf16[176,512]{1,0:T(8,128)(2,1)S(1)}, bf16[176,512]{1,0:T(8,128)(2,1)S(1)}, u32[]{:S(2)}, u32[]{:S(2)}) collective-permute-start(bf16[176,512]{1,0:T(8,128)(2,1)S(1)} %shard_map.131.refs_0_.grad_ref), channel_id=1, source_target_pairs={{0,4},{1,5},{2,6},{3,7},{4,0},{5,1},{6,2},{7,3},{8,12},{9,13},{10,... | collective-permute-start | bytes 540680 | tf_op jit(solution)/shard_map/ppermute | solution.py:396
  39.9 7.1 %collective-permute-start.7 = (bf16[176,512]{1,0:T(8,128)(2,1)S(1)}, bf16[176,512]{1,0:T(8,128)(2,1)S(1)}, u32[]{:S(2)}, u32[]{:S(2)}) collective-permute-start(bf16[176,512]{1,0:T(8,128)(2,1)S(1)} %shard_map.131.refs_0_.grad_ref), channel_id=1, source_target_pairs={{0,2},{1,3},{2,0},{3,1},{4,6},{5,7},{6,4},{7,5},{8,10},{9,11},{10,... | collective-permute-start | bytes 540680 | tf_op jit(solution)/shard_map/ppermute | solution.py:396
  40.9 6.6 %collective-permute-start.6 = (bf16[176,512]{1,0:T(8,128)(2,1)S(1)}, bf16[176,512]{1,0:T(8,128)(2,1)S(1)}, u32[]{:S(2)}, u32[]{:S(2)}) collective-permute-start(bf16[176,512]{1,0:T(8,128)(2,1)S(1)} %shard_map.131.refs_0_.grad_ref), channel_id=1, source_target_pairs={{0,1},{1,0},{2,3},{3,2},{4,5},{5,4},{6,7},{7,6},{8,9},{9,8},{10,11... | collective-permute-start | bytes 540680 | tf_op jit(solution)/shard_map/ppermute | solution.py:396
  45.2 2.7 %collective-permute-start.12 = (bf16[176,512]{1,0:T(8,128)(2,1)S(1)}, bf16[176,512]{1,0:T(8,128)(2,1)S(1)}, u32[]{:S(2)}, u32[]{:S(2)}) collective-permute-start(bf16[176,512]{1,0:T(8,128)(2,1)S(1)} %collective-permute-done.11.refs_6_), channel_id=1, source_target_pairs={{0,1},{1,0},{2,3},{3,2},{4,5},{5,4},{6,7},{7,6},{8,9},{9,8},{10,11... | collective-permute-start | bytes 540680 | tf_op jit(solution)/shard_map/ppermute | solution.py:396
  46.9 1.4 %collective-permute-start.10 = (bf16[176,512]{1,0:T(8,128)(2,1)S(1)}, bf16[176,512]{1,0:T(8,128)(2,1)S(1)}, u32[]{:S(2)}, u32[]{:S(2)}) collective-permute-start(bf16[176,512]{1,0:T(8,128)(2,1)S(1)} %collective-permute-done.9.refs_4_), channel_id=1, source_target_pairs={{0,1},{1,0},{2,3},{3,2},{4,5},{5,4},{6,7},{7,6},{8,9},{9,8},{10,11... | collective-permute-start | bytes 540680 | tf_op jit(solution)/shard_map/ppermute | solution.py:396
  47.0 1.5 %collective-permute-start.8 = (bf16[176,512]{1,0:T(8,128)(2,1)S(1)}, bf16[176,512]{1,0:T(8,128)(2,1)S(1)}, u32[]{:S(2)}, u32[]{:S(2)}) collective-permute-start(bf16[176,512]{1,0:T(8,128)(2,1)S(1)} %collective-permute-done.7.refs_2_), channel_id=1, source_target_pairs={{0,1},{1,0},{2,3},{3,2},{4,5},{5,4},{6,7},{7,6},{8,9},{9,8},{10,11... | collective-permute-start | bytes 540680 | tf_op jit(solution)/shard_map/ppermute | solution.py:396
  47.4 4.6 %collective-permute-start.13 = (bf16[256,128]{1,0:T(8,128)(2,1)S(1)}, bf16[256,128]{1,0:T(8,128)(2,1)S(1)}, u32[]{:S(2)}, u32[]{:S(2)}) collective-permute-start(bf16[256,128]{1,0:T(8,128)(2,1)S(1)} %copy-done.4), channel_id=1, source_target_pairs={{0,1},{1,0},{2,3},{3,2},{4,5},{5,4},{6,7},{7,6},{8,9},{9,8},{10,11... | collective-permute-start | bytes 196616 | tf_op jit(solution)/shard_map/ppermute | solution.py:396
  47.5 4.5 %collective-permute-start.14 = (bf16[256,128]{1,0:T(8,128)(2,1)S(1)}, bf16[256,128]{1,0:T(8,128)(2,1)S(1)}, u32[]{:S(2)}, u32[]{:S(2)}) collective-permute-start(bf16[256,128]{1,0:T(8,128)(2,1)S(1)} %collective-permute-done.3.refs_9_), channel_id=1, source_target_pairs={{0,1},{1,0},{2,3},{3,2},{4,5},{5,4},{6,7},{7,6},{8,9},{9,8},{10,11... | collective-permute-start | bytes 196616 | tf_op jit(solution)/shard_map/ppermute | solution.py:396
  47.9 4.1 %collective-permute-start.15 = (bf16[256,128]{1,0:T(8,128)(2,1)S(1)}, bf16[256,128]{1,0:T(8,128)(2,1)S(1)}, u32[]{:S(2)}, u32[]{:S(2)}) collective-permute-start(bf16[256,128]{1,0:T(8,128)(2,1)S(1)} %collective-permute-done.4.refs_10_), channel_id=1, source_target_pairs={{0,1},{1,0},{2,3},{3,2},{4,5},{5,4},{6,7},{7,6},{8,9},{9,8},{10,11... | collective-permute-start | bytes 196616 | tf_op jit(solution)/shard_map/ppermute | solution.py:396
  48.3 3.7 %collective-permute-start.16 = (bf16[256,128]{1,0:T(8,128)(2,1)S(1)}, bf16[256,128]{1,0:T(8,128)(2,1)S(1)}, u32[]{:S(2)}, u32[]{:S(2)}) collective-permute-start(bf16[256,128]{1,0:T(8,128)(2,1)S(1)} %collective-permute-done.5.refs_11_), channel_id=1, source_target_pairs={{0,1},{1,0},{2,3},{3,2},{4,5},{5,4},{6,7},{7,6},{8,9},{9,8},{10,11... | collective-permute-start | bytes 196616 | tf_op jit(solution)/shard_map/ppermute | solution.py:396
  50.4 8.9 %collective-permute-start.20 = (bf16[40,512]{1,0:T(8,128)(2,1)S(1)}, bf16[40,512]{1,0:T(8,128)(2,1)S(1)}, u32[]{:S(2)}, u32[]{:S(2)}) collective-permute-start(bf16[40,512]{1,0:T(8,128)(2,1)S(1)} %get-tuple-element.61), channel_id=1, source_target_pairs={{0,8},{1,9},{2,10},{3,11},{4,12},{5,13},{6,14},{7,15},{8,0},{9,1},... | collective-permute-start | bytes 122888 | tf_op jit(solution)/shard_map/ppermute | solution.py:396
  53.3 13.4 %collective-permute-start.17 = (bf16[72,512]{1,0:T(8,128)(2,1)S(1)}, bf16[72,512]{1,0:T(8,128)(2,1)S(1)}, u32[]{:S(2)}, u32[]{:S(2)}) collective-permute-start(bf16[72,512]{1,0:T(8,128)(2,1)S(1)} %get-tuple-element.57), channel_id=1, source_target_pairs={{0,8},{1,9},{2,10},{3,11},{4,12},{5,13},{6,14},{7,15},{8,0},{9,1},... | collective-permute-start | bytes 221192 | tf_op jit(solution)/shard_map/ppermute | solution.py:396
  53.7 13.0 %collective-permute-start.18 = (bf16[72,512]{1,0:T(8,128)(2,1)S(1)}, bf16[72,512]{1,0:T(8,128)(2,1)S(1)}, u32[]{:S(2)}, u32[]{:S(2)}) collective-permute-start(bf16[72,512]{1,0:T(8,128)(2,1)S(1)} %get-tuple-element.58), channel_id=1, source_target_pairs={{0,16},{1,17},{2,18},{3,19},{4,20},{5,21},{6,22},{7,23},{8,24},{9,... | collective-permute-start | bytes 221192 | tf_op jit(solution)/shard_map/ppermute | solution.py:396
  56.3 10.4 %collective-permute-start.19 = (bf16[72,512]{1,0:T(8,128)(2,1)S(1)}, bf16[72,512]{1,0:T(8,128)(2,1)S(1)}, u32[]{:S(2)}, u32[]{:S(2)}) collective-permute-start(bf16[72,512]{1,0:T(8,128)(2,1)S(1)} %get-tuple-element.59), channel_id=1, source_target_pairs={{0,24},{1,25},{2,26},{3,27},{4,28},{5,29},{6,30},{7,31},{8,16},{9,... | collective-permute-start | bytes 221192 | tf_op jit(solution)/shard_map/ppermute | solution.py:396
  57.8 8.9 %collective-permute-start.21 = (bf16[40,512]{1,0:T(8,128)(2,1)S(1)}, bf16[40,512]{1,0:T(8,128)(2,1)S(1)}, u32[]{:S(2)}, u32[]{:S(2)}) collective-permute-start(bf16[40,512]{1,0:T(8,128)(2,1)S(1)} %get-tuple-element.62), channel_id=1, source_target_pairs={{0,16},{1,17},{2,18},{3,19},{4,20},{5,21},{6,22},{7,23},{8,24},{9,... | collective-permute-start | bytes 122888 | tf_op jit(solution)/shard_map/ppermute | solution.py:396
  59.2 7.5 %collective-permute-start.22 = (bf16[40,512]{1,0:T(8,128)(2,1)S(1)}, bf16[40,512]{1,0:T(8,128)(2,1)S(1)}, u32[]{:S(2)}, u32[]{:S(2)}) collective-permute-start(bf16[40,512]{1,0:T(8,128)(2,1)S(1)} %get-tuple-element.63), channel_id=1, source_target_pairs={{0,24},{1,25},{2,26},{3,27},{4,28},{5,29},{6,30},{7,31},{8,16},{9,... | collective-permute-start | bytes 122888 | tf_op jit(solution)/shard_map/ppermute | solution.py:396

commit v6 on v5

--- a/solution.py
+++ b/solution.py
@@ -77,8 +77,8 @@
 
 
 def start_kernel(
-    place_ref, proj_hbm, cotangent_hbm, lengths_hbm, dests_hbm, offsets_hbm, me_ref, index_ref, rows_ref,
-    proj_ref, cotangent_ref, lengths_ref, dests_ref, offsets_ref, copied, *, pairs, frames
+    proj_hbm, cotangent_hbm, lengths_hbm, dests_hbm, offsets_hbm, me_ref, index_ref, rows_ref,
+    proj_ref, cotangent_ref, lengths_ref, dests_ref, offsets_ref, copied, *, pairs, frames, mp_count
 ):
     sources = (proj_hbm, cotangent_hbm, lengths_hbm, dests_hbm, offsets_hbm)
     targets = (proj_ref, cotangent_ref, lengths_ref, dests_ref, offsets_ref)
@@ -90,8 +90,11 @@
         copy.start()
     for copy in copies[2:]:
         copy.wait()
-    for i in range(4):
-        me_ref[i] = place_ref[i]
+    at_dp, at_mp = lax.axis_index("dp"), lax.axis_index("mp")
+    me_ref[0] = at_dp * mp_count + at_mp
+    me_ref[1] = lax.rem(at_dp, 2) * mp_count + at_mp
+    me_ref[2] = lax.div(at_dp, 2)
+    me_ref[3] = lax.rem(at_dp, 2)
     for i in range(2 * pairs):
         me_ref[4 + i] = lengths_ref[i]
         me_ref[4 + 2 * pairs + i] = dests_ref[i]
@@ -116,12 +119,16 @@
 
 
 def forward_kernel(me_ref, *refs, pairs, frames, far, near, owned):
-    weight_ref = refs[3]
-    sources = refs[:3] + (weight_ref.at[0], weight_ref.at[1])
-    rest, held, in_turned, copied = refs[4:-7], refs[-7:-2], refs[-2], refs[-1]
+    weight_ref, cotangent_hbm = refs[3:5]
+    rest, held, in_turned, copied = refs[5:-7], refs[-7:-2], refs[-2], refs[-1]
+    with_cotangent = rest[3 + near // 4]
+    own_rows = 2 * far * owned
+    tail = with_cotangent.at[own_rows:, : cotangent_hbm.shape[1]]
+    sources = refs[:3] + (weight_ref.at[0], weight_ref.at[1], cotangent_hbm)
+    targets = held + (tail,)
     copies = [
         pltpu.make_async_copy(source, target, copied.at[i])
-        for i, (source, target) in enumerate(zip(sources, held))
+        for i, (source, target) in enumerate(zip(sources, targets))
     ]
     for copy in copies:
         copy.start()
@@ -184,7 +191,7 @@
         in_turned[channels * tap : channels * (tap + 1), :] = stacked.T
     at = me_ref[1]
     for k, turned_ref in enumerate(turned_refs):
-        turned_ref[...] = jnp.concatenate(
+        turned_ref[:own_rows, :] = jnp.concatenate(
             [
                 in_turned[pl.ds(pl.multiple_of((z * near + (at ^ (2 * k + c))) * owned, owned), owned), :]
                 for c in range(2)
@@ -192,6 +199,7 @@
             ],
             axis=0,
         ).astype(BF)
+    copies[5].wait()
 
 
 def send_kernel(got_ref, mine_ref, other_ref, sent_ref, out_ref, rows32, *, frames):
@@ -237,10 +245,13 @@
     return jnp.concatenate(parts, axis=1)
 
 
-def project_kernel(me_ref, *refs, start, near, frames):
-    side_refs = refs[:near]
-    weight_ref, mine_ref, other_ref, packed_ref, own_ref = refs[near : near + 5]
-    out_refs, held = refs[near + 5 : -1], refs[-1]
+def gradient_kernel(me_ref, *refs, n1, n2, owned, near, far, frames):
+    side_refs, column_refs = refs[:near], refs[near : 2 * near]
+    weight_ref, mine_ref, packed_ref, own_ref = refs[2 * near : 2 * near + 4]
+    out_refs, held = refs[2 * near + 4 : -1], refs[-1]
+    start = n1 + n2
+    rows = far * owned
+    other = column_refs[near // 4][2 * rows :][:, : mine_ref.shape[1]]
     channels, seq = weight_ref.shape[1], packed_ref.shape[1]
     dp_count = (side_refs[0].shape[0] - start - 8) // (1 + frames)
     row = lax.broadcasted_iota(jnp.int32, (dp_count * frames, seq), 0)
@@ -257,14 +268,38 @@
             pick, tail[8 + dp_count :].astype(BF), (((0,), (0,)), ((), ())), preferred_element_type=F32
         )
     packed_ref[...] = dot_nt(weight_ref[...], shards[0].astype(BF)).astype(BF)
-    partial = dot_nt(shards[0].T.astype(BF), mine_ref[...]) + dot_nt(shards[1].T.astype(BF), other_ref[...])
+    partial = dot_nt(shards[0].T.astype(BF), mine_ref[...]) + dot_nt(shards[1].T.astype(BF), other)
+    depth = -(-(n1 + n2) // 128) * 128
+    lane = lax.broadcasted_iota(jnp.int32, (rows, depth), 1)
+    of_first, of_second, factors, sums = [], [], [], 0.0
+    for k in range(near):
+        at = k % 2 * rows
+        side = column_refs[near // 2 * (k % 2) + k // 2][at : at + rows][:, :depth].astype(F32)
+        of_first.append(jnp.where(lane < n1, side, 0.0).astype(BF))
+        of_second.append(jnp.where(jnp.logical_and(lane >= n1, lane < start), side, 0.0).astype(BF))
+        factors.append(side_refs[k][:depth, :])
+        tail = side_refs[k][start : start + 16, :].astype(F32)
+        sums += tail[0:4] + tail[4:8]
+    factors = jnp.concatenate(factors, axis=0)
+    first = dot(jnp.concatenate(of_first, axis=1), factors)
+    second = dot(jnp.concatenate(of_second, axis=1), factors)
+    high = sums.astype(BF).astype(F32)
     each = channels // dp_count
-    for z in range(held.shape[0]):
-        low = partial[2 * z * each : (2 * z + 1) * each]
-        high = partial[(2 * z + 1) * each : (2 * z + 2) * each]
-        held[z] = pack(jnp.where(me_ref[3] == 0, low, high), channels)
+    for z in range(far):
+        low_rows = partial[2 * z * each : (2 * z + 1) * each]
+        high_rows = partial[(2 * z + 1) * each : (2 * z + 2) * each]
+        held[z] = jnp.concatenate(
+            [
+                first[z * owned : (z + 1) * owned],
+                second[z * owned : (z + 1) * owned],
+                high,
+                sums - high,
+                pack(jnp.where(me_ref[3] == 0, low_rows, high_rows), channels),
+            ],
+            axis=0,
+        )
     own_ref[...] = held[me_ref[2]]
-    for f in range(1, held.shape[0]):
+    for f in range(1, far):
         out_refs[f - 1][...] = held[me_ref[2] ^ f].astype(BF)
 
 
@@ -327,42 +362,14 @@
     out_ref[...] = dot(pick, rows).astype(BF)
 
 
-def kernel_grad_kernel(me_ref, *refs, n1, n2, owned, near, far):
-    grad_refs, side_refs = refs[:near], refs[near : 2 * near]
-    rows = side_refs[0].shape[0] // 2
-    in_refs = [
-        side_refs[near // 2 * (k % 2) + k // 2].at[k % 2 * rows : (k % 2 + 1) * rows] for k in range(near)
-    ]
-    own_ref, out_refs, held = refs[2 * near], refs[2 * near + 1 : -1], refs[-1]
-    first, second, sums = 0.0, 0.0, 0.0
-    for grad_ref, in_ref in zip(grad_refs, in_refs):
-        side = in_ref[...]
-        first += dot(side[:, :n1], grad_ref[:n1, :])
-        second += dot(side[:, n1 : n1 + n2], grad_ref[n1 : n1 + n2, :])
-        tail = grad_ref[n1 + n2 : n1 + n2 + 16, :].astype(F32)
-        sums += tail[0:4] + tail[4:8]
-    high = sums.astype(BF).astype(F32)
-    for z in range(far):
-        held[z] = jnp.concatenate(
-            [first[z * owned : (z + 1) * owned], second[z * owned : (z + 1) * owned], high, sums - high],
-            axis=0,
-        )
-    own_ref[...] = held[me_ref[2]]
+def last_kernel(me_ref, *refs, owned, far):
+    conv_ref, norm_ref, proj_ref = refs[far:]
+    total = refs[0][...]
     for f in range(1, far):
-        out_refs[f - 1][...] = held[me_ref[2] ^ f].astype(BF)
-
-
-def last_kernel(me_ref, *refs, owned, far):
-    conv_in, proj_in = refs[:far], refs[far : 2 * far]
-    conv_ref, norm_ref, proj_ref = refs[2 * far :]
-    total = conv_in[0][...]
-    proj = proj_in[0][...]
-    for f in range(1, far):
-        total += conv_in[f][...].astype(F32)
-        proj += proj_in[f][...].astype(F32)
+        total += refs[f][...].astype(F32)
     conv_ref[0] = total[:owned]
     conv_ref[1] = total[owned : 2 * owned]
-    proj_ref[...] = unpack(proj, *proj_ref.shape)
+    proj_ref[...] = unpack(total[2 * owned + 8 :], *proj_ref.shape)
     channels = total.shape[1]
     sums = total[2 * owned : 2 * owned + 4] + total[2 * owned + 4 : 2 * owned + 8]
     start = me_ref[0] * owned
@@ -396,19 +403,14 @@
         return lax.ppermute(x, everyone, [(i, i ^ mask) for i in range(dp_count * mp_count)])
 
     bits = [1 << b for b in range(mp_count.bit_length() - 1)][::-1]
-    at_dp = lax.axis_index("dp").astype(jnp.int32)
-    at_mp = lax.axis_index("mp").astype(jnp.int32)
-    x_bit = at_dp & 1
-    place = jnp.stack([at_dp * mp_count + at_mp, x_bit * mp_count + at_mp, at_dp >> 1, x_bit])
     me, index, grad_rows = call(
-        functools.partial(start_kernel, pairs=pairs, frames=frames),
+        functools.partial(start_kernel, pairs=pairs, frames=frames, mp_count=mp_count),
         [
             shape(4 + 6 * pairs, kind=jnp.int32),
             shape(dp_count, 128, kind=jnp.int32),
             shape(seq, channels),
         ],
-        (place, proj_weight.T, grad_packed.T, lengths, dests, offsets),
-        scalars=1,
+        (proj_weight.T, grad_packed.T, lengths, dests, offsets),
         fetched=5,
         to_scalars=1,
         flops=2 * seq * width * channels,
@@ -425,7 +427,8 @@
     feat = features.reshape(utt_count * positions, channels)
     got_index = lax.all_to_all(index, "dp", split_axis=0, concat_axis=0, tiled=True)
 
-    wide = -(-(n1 + n2) // 128) * 128
+    wide = max(-(-(n1 + n2) // 128) * 128, seq)
+    cotangent = grad_packed.T
     tall = (2 * channels, channels)
     made = call(
         functools.partial(
@@ -436,10 +439,13 @@
             shape(dp_count * frames, channels),
             shape(10 * n2 + 8, channels, kind=F32),
         ]
-        + [shape(2 * far * owned, wide)] * (near // 2),
-        (me, feat, norm_gain, norm_shift, conv_weight),
+        + [
+            shape(2 * far * owned + (width if 2 * k == mp_count else 0), wide)
+            for k in range(near // 2)
+        ],
+        (me, feat, norm_gain, norm_shift, conv_weight, cotangent),
         scalars=1,
-        fetched=4,
+        fetched=5,
         to_scalars=1,
         flops=10**10,
         scratch=[
@@ -449,19 +455,16 @@
             pltpu.VMEM(tall, BF),
             pltpu.VMEM(tall, BF),
             pltpu.VMEM((2 * channels, wide), F32),
-            pltpu.SemaphoreType.DMA((5,)),
+            pltpu.SemaphoreType.DMA((6,)),
         ],
         mebibytes=56,
     )
     me, pair_frames, state = made[:3]
     in_sides = [swap(side, 2 * k) if k else side for k, side in enumerate(made[3:])]
 
-    for mask in bits[:-1]:
-        arrived, pair_frames, got_index = lax.optimization_barrier(
-            (swap(grad_rows, mask), pair_frames, got_index)
-        )
-        grad_rows = (grad_rows.astype(F32) + arrived.astype(F32)).astype(BF)
-    other_rows = swap(grad_rows, bits[-1])
+    for mask in bits[:0:-1]:
+        grad_rows = (grad_rows.astype(F32) + swap(grad_rows, mask).astype(F32)).astype(BF)
+    other_rows = swap(grad_rows, bits[0])
 
     sent = call(
         functools.partial(send_kernel, frames=frames),
@@ -471,11 +474,7 @@
         scratch=[pltpu.VMEM((seq, channels), F32)],
     )
     slots = lax.all_to_all(sent, "dp", split_axis=0, concat_axis=0, tiled=True)
-    cotangent = grad_packed.T
-    other_cotangent = swap(cotangent, mp_count)
-    slots, other_cotangent, *in_sides[: near // 2] = lax.optimization_barrier(
-        (slots, other_cotangent, *in_sides[: near // 2])
-    )
+    slots, *in_sides[: near // 2] = lax.optimization_barrier((slots, *in_sides[: near // 2]))
 
     in_sides += [swap(side, 1) for side in in_sides]
     rows_sent = n1 + n2 + 8 + dp_count * (1 + frames)
@@ -492,14 +491,17 @@
     per_dp = channels // dp_count
     packed_rows = per_dp * width // channels
     sides = tuple(by_mask[k] for k in range(near))
-    packed, *proj_parts = call(
-        functools.partial(project_kernel, start=n1 + n2, near=near, frames=frames),
-        [shape(width, seq), shape(packed_rows, channels, kind=F32)]
-        + [shape(packed_rows, channels)] * (far - 1),
-        (me, *sides, proj_weight.T, cotangent, other_cotangent),
+    rows_out = 2 * owned + 8 + packed_rows
+    packed, *parts = call(
+        functools.partial(
+            gradient_kernel, n1=n1, n2=n2, owned=owned, near=near, far=far, frames=frames
+        ),
+        [shape(width, seq), shape(rows_out, channels, kind=F32)]
+        + [shape(rows_out, channels)] * (far - 1),
+        (me, *sides, *in_sides, proj_weight.T, cotangent),
         scalars=1,
-        flops=6 * seq * channels * width,
-        scratch=[pltpu.VMEM((far, packed_rows, channels), F32)],
+        flops=2 * (n1 + n2) * 2 * channels * channels,
+        scratch=[pltpu.VMEM((far, rows_out, channels), F32)],
     )
 
     grad_features = call(
@@ -510,16 +512,7 @@
         flops=2 * n1 * 2 * channels * channels,
     ).reshape(utt_count, positions, channels)
 
-    conv_parts = call(
-        functools.partial(kernel_grad_kernel, n1=n1, n2=n2, owned=owned, near=near, far=far),
-        [shape(2 * owned + 8, channels, kind=F32)] + [shape(2 * owned + 8, channels)] * (far - 1),
-        (me, *sides, *in_sides),
-        scalars=1,
-        flops=2 * (n1 + n2) * 2 * channels * channels,
-        scratch=[pltpu.VMEM((far, 2 * owned + 8, channels), F32)],
-    )
-    conv_got = [swap(part, near * f) if f else part for f, part in enumerate(conv_parts)]
-    proj_got = [swap(part, near * f) if f else part for f, part in enumerate(proj_parts)]
+    got = [swap(part, near * f) if f else part for f, part in enumerate(parts)]
     grad_conv, grad_norm, grad_proj = call(
         functools.partial(last_kernel, owned=owned, far=far),
         [
@@ -527,7 +520,7 @@
             shape(2, owned, kind=F32),
             shape(per_dp, width, kind=F32),
         ],
-        (me, *conv_got, *proj_got),
+        (me, *got),
         scalars=1,
     )
     return (packed.T, grad_features, grad_conv, grad_norm, grad_proj)

time: 68.4 us -> 64.1 us (0.937)
  starting transfers between devices: 32.8 us -> 28 us
  waiting for transfers between devices: 16.8 us -> 18.4 us
  Pallas kernels: 15 us -> 13.6 us
    ppermute x23 -> x19, starting transfers between devices: 20.3 us -> 15.2 us  [swap(): lax.ppermute(x, everyone, [(i, i ^ mask) for i in range(dp_count * mp_cou...]
    ppermute x23 -> x19, waiting for transfers between devices: 16 us -> 18.4 us  [swap(): lax.ppermute(x, everyone, [(i, i ^ mask) for i in range(dp_count * mp_cou...]
    pallas_call x8 -> x7, Pallas kernels: 15 us -> 13.6 us  [call(): pl.pallas_call(body, out_shape=out, in_specs=specs, out_specs=[pl.BlockSp...]
    convert_element_type x1, other arithmetic: 0.03 us -> 0.94 us  [local(): (grad_rows.astype(F32) + swap(grad_rows, mask).astype(F32)).astype(BF)]
    all_to_all x1, waiting for transfers between devices: 0.79 us -> 0.01 us  [local(): lax.all_to_all(index, 'dp', split_axis=0, concat_axis=0, tiled=True)]
    all_to_all x1, starting transfers between devices: 5.24 us -> 5.99 us  [local(): slots = lax.all_to_all(sent, 'dp', split_axis=0, concat_axis=0, tiled=True)]
    unnamed x16 -> x14, local copies, waits for them, and re-layouts: 1.95 us -> 1.99 us
  transfers between devices with their start and end apart: 25 -> 21, of which waited for: 11 -> 8; matrix products, arithmetic and copies ran while one was open for 0% -> 1% of each run, Pallas kernels for 13% -> 10%
where the time goes in v6:
time: 64.1 us; the launch traced here: 63.8 us
  starting transfers between devices  28 us (44%)
  waiting for transfers between devices  18.4 us (29%)
  Pallas kernels  13.6 us (21%)
  local copies, waits for them, and re-layouts  1.99 us (3%)
  other arithmetic  0.94 us (1%)
  between operations  0.78 us (1%)
    ppermute x19, waiting for transfers between devices, swap(): lax.ppermute(x, everyone, [(i, i ^ mask) for i in range(dp_count * mp_cou...  18.4 us
    ppermute x19, starting transfers between devices, swap(): lax.ppermute(x, everyone, [(i, i ^ mask) for i in range(dp_count * mp_cou...  15.2 us
    pallas_call x7, Pallas kernels, call(): pl.pallas_call(body, out_shape=out, in_specs=specs, out_specs=[pl.BlockSp...  13.6 us
    all_to_all x1, starting transfers between devices, local(): lax.all_to_all(index, 'dp', split_axis=0, concat_axis=0, tiled=True)  6.82 us
    all_to_all x1, starting transfers between devices, local(): slots = lax.all_to_all(sent, 'dp', split_axis=0, concat_axis=0, tiled=True)  5.99 us
    unnamed x14, local copies, waits for them, and re-layouts  1.99 us
  transfers between devices with their start and end apart: 21, of which 8 were waited for; matrix products, arithmetic and copies ran while one was open for 1% of the time, Pallas kernels for 10%

profile of v6, /device:TPU:0, one launch (start us, length us, event | category | flops | bytes accessed | tf_op | source)
XLA Modules:
  0.0 63.8 jit_solution(12265619587319727009)
XLA Ops:
  0.6 2.0 %shard_map.128 = (s32[28]{0:T(128)}, s32[8,128]{1,0:T(8,128)}, bf16[128,512]{1,0:T(8,128)(2,1)}) custom-call(bf16[320,512]{1,0:T(8,128)(2,1)} %bitcast.10, bf16[320,128]{1,0:T(8,128)(2,1)} %bitcast.13, s32[8]{0:T(128)} %lengths_hbm.1, s32[8]{0:T(128)} %dests_hbm.1, s32[8]{0:T(128)} %offsets_hbm.1), custom_call_target="tpu_custom_call" | custom-call | flops 41943040 | bytes 409696 | tf_op jit(solution)/shard_map/pallas_call | solution.py:25
  2.6 0.5 collective-permute-start
  3.1 6.8 %all-to-all-start = ((s32[8,1,128]{2,1,0:T(1,128)}), s32[8,1,128]{2,1,0:T(1,128)S(1)}, u32[]{:S(2)}, u32[]{:S(2)}) async-start(s32[8,1,128]{2,1,0:T(1,128)} %bitcast.19), calls=%async_computation | async-start | bytes 8192 | tf_op jit(solution)/shard_map/all_to_all | solution.py:428
  10.0 0.0 collective-permute-done
  10.0 0.9 %add_convert_fusion.mine_ref = bf16[128,512]{1,0:T(8,128)(2,1)S(1)} fusion(bf16[128,512]{1,0:T(8,128)(2,1)S(1)} %collective-permute-done, bf16[128,512]{1,0:T(8,128)(2,1)} %get-tuple-element.31), kind=kLoop, calls=%fused_computation | loop fusion | flops 262144 | bytes 393216 | tf_op jit(solution)/shard_map/convert_element_type | solution.py:466
  10.9 1.6 %collective-permute-start.1 = (bf16[128,512]{1,0:T(8,128)(2,1)S(1)}, bf16[128,512]{1,0:T(8,128)(2,1)S(1)}, u32[]{:S(2)}, u32[]{:S(2)}) collective-permute-start(bf16[128,512]{1,0:T(8,128)(2,1)S(1)} %add_convert_fusion.mine_ref), channel_id=1, source_target_pairs={{0,2},{1,3},{2,0},{3,1},{4,6},{5,7},{6,4},{7,5},{8,10},{9,11},{10,... | collective-permute-start | bytes 393224 | tf_op jit(solution)/shard_map/ppermute | solution.py:403
  12.5 4.3 %shard_map.129 = (s32[28]{0:T(128)}, bf16[64,512]{1,0:T(8,128)(2,1)}, f32[328,512]{1,0:T(8,128)}, bf16[256,128]{1,0:T(8,128)(2,1)}, bf16[256,128]{1,0:T(8,128)(2...) custom-call(s32[28]{0:T(128)} %get-tuple-element.28.me_ref, bf16[256,512]{1,0:T(8,128)(2,1)} %bitcast.20, ...), custom_call_target="tpu_custom_call" | custom-call | flops 10000000000 | bytes 2449520 | tf_op jit(solution)/shard_map/pallas_call | solution.py:25
  16.8 0.0 copy-start.4
  16.8 0.0 copy-start.1
  16.8 0.0 copy-start.3
  16.9 0.0 collective-permute-done.1.other_ref
  16.9 0.0 copy-start.5
  16.9 0.9 %copy-done.5 = bf16[64,512]{1,0:T(8,128)(2,1)S(1)} copy-done((bf16[64,512]{1,0:T(8,128)(2,1)S(1)}, bf16[64,512]{1,0:T(8,128)(2,1)}, u32[]{:S(2)}) %copy-start.5) | copy-done | bytes 65560
  17.8 1.3 %shard_map.130 = bf16[8,16,512]{2,1,0:T(8,128)(2,1)} custom-call(s32[8,128]{1,0:T(8,128)S(1)} %bitcast.16, bf16[128,512]{1,0:T(8,128)(2,1)S(1)} %add_convert_fusion.mine_ref, bf16[128,512]{1,0:T(8,128)(2,1)S(1)} %collective-permute-done.1.other_ref, bf16[64,512]{1,0:T(8,128)(2,1)S(1)} %copy-done.5), custom_call_target="tpu_custom_call" | custom-call | bytes 331776 | tf_op jit(solution)/shard_map/pallas_call | solution.py:25
  19.1 6.0 %all-to-all-start.1 = ((bf16[8,16,512]{2,1,0:T(8,128)(2,1)}), bf16[8,16,512]{2,1,0:T(8,128)(2,1)S(1)}, u32[]{:S(2)}, u32[]{:S(2)}) async-start(bf16[8,16,512]{2,1,0:T(8,128)(2,1)} %shard_map.130), calls=%async_computation.1 | async-start | bytes 262144 | tf_op jit(solution)/shard_map/all_to_all | solution.py:476
  25.1 2.0 %collective-permute-start.3 = (bf16[576,128]{1,0:T(8,128)(2,1)}, bf16[576,128]{1,0:T(8,128)(2,1)S(1)}, u32[]{:S(2)}, u32[]{:S(2)}) collective-permute-start(bf16[576,128]{1,0:T(8,128)(2,1)} %get-tuple-element.35), channel_id=1, source_target_pairs={{0,4},{1,5},{2,6},{3,7},{4,0},{5,1},{6,2},{7,3},{8,12},{9,13},{10,... | collective-permute-start | bytes 442376 | tf_op jit(solution)/shard_map/ppermute | solution.py:403
  27.1 0.9 %collective-permute-start.2 = (bf16[256,128]{1,0:T(8,128)(2,1)}, bf16[256,128]{1,0:T(8,128)(2,1)S(1)}, u32[]{:S(2)}, u32[]{:S(2)}) collective-permute-start(bf16[256,128]{1,0:T(8,128)(2,1)} %get-tuple-element.34), channel_id=1, source_target_pairs={{0,2},{1,3},{2,0},{3,1},{4,6},{5,7},{6,4},{7,5},{8,10},{9,11},{10,... | collective-permute-start | bytes 196616 | tf_op jit(solution)/shard_map/ppermute | solution.py:403
  28.0 0.6 collective-permute-start.4
  28.6 3.3 %collective-permute-done.2.refs_9_ = bf16[256,128]{1,0:T(8,128)(2,1)S(1)} collective-permute-done((bf16[256,128]{1,0:T(8,128)(2,1)}, bf16[256,128]{1,0:T(8,128)(2,1)S(1)}, u32[]{:S(2)}, u32[]{:S(2)}) %collective-permute-start.2) | collective-permute-done | bytes 65568 | tf_op jit(solution)/shard_map/ppermute | solution.py:403
  31.9 1.6 %collective-permute-done.4.refs_11_ = bf16[256,128]{1,0:T(8,128)(2,1)S(1)} collective-permute-done((bf16[256,128]{1,0:T(8,128)(2,1)}, bf16[256,128]{1,0:T(8,128)(2,1)S(1)}, u32[]{:S(2)}, u32[]{:S(2)}) %collective-permute-start.4) | collective-permute-done | bytes 65568 | tf_op jit(solution)/shard_map/ppermute | solution.py:403
  33.5 1.1 %copy-done.2 = f32[328,512]{1,0:T(8,128)S(1)} copy-done((f32[328,512]{1,0:T(8,128)S(1)}, f32[328,512]{1,0:T(8,128)}, u32[]{:S(2)}) %copy-start.2) | copy-done | bytes 671768
  34.6 0.7 %shard_map.131.refs_0_.grad_ref = bf16[176,512]{1,0:T(8,128)(2,1)S(1)} custom-call(bf16[128,512]{1,0:T(8,128)(2,1)S(1)} %bitcast.12, s32[8,128]{1,0:T(8,128)S(1)} %bitcast.17, f32[328,512]{1,0:T(8,128)S(1)} %copy-done.2, bf16[2,1024,512]{2,1,0:T(8,128)(2,1)S(1)} %copy-done), custom_call_target="tpu_custom_call" | custom-call | flops 33554432 | bytes 2904064 | tf_op jit(solution)/shard_map/pallas_call | solution.py:25
  35.2 2.0 %collective-permute-start.10 = (bf16[176,512]{1,0:T(8,128)(2,1)S(1)}, bf16[176,512]{1,0:T(8,128)(2,1)S(1)}, u32[]{:S(2)}, u32[]{:S(2)}) collective-permute-start(bf16[176,512]{1,0:T(8,128)(2,1)S(1)} %shard_map.131.refs_0_.grad_ref), channel_id=1, source_target_pairs={{0,6},{1,7},{2,4},{3,5},{4,2},{5,3},{6,0},{7,1},{8,14},{9,15},{10,... | collective-permute-start | bytes 540680 | tf_op jit(solution)/shard_map/ppermute | solution.py:403
  37.2 0.7 %collective-permute-start.8 = (bf16[176,512]{1,0:T(8,128)(2,1)S(1)}, bf16[176,512]{1,0:T(8,128)(2,1)S(1)}, u32[]{:S(2)}, u32[]{:S(2)}) collective-permute-start(bf16[176,512]{1,0:T(8,128)(2,1)S(1)} %shard_map.131.refs_0_.grad_ref), channel_id=1, source_target_pairs={{0,4},{1,5},{2,6},{3,7},{4,0},{5,1},{6,2},{7,3},{8,12},{9,13},{10,... | collective-permute-start | bytes 540680 | tf_op jit(solution)/shard_map/ppermute | solution.py:403
  38.0 0.8 %collective-permute-start.6 = (bf16[176,512]{1,0:T(8,128)(2,1)S(1)}, bf16[176,512]{1,0:T(8,128)(2,1)S(1)}, u32[]{:S(2)}, u32[]{:S(2)}) collective-permute-start(bf16[176,512]{1,0:T(8,128)(2,1)S(1)} %shard_map.131.refs_0_.grad_ref), channel_id=1, source_target_pairs={{0,2},{1,3},{2,0},{3,1},{4,6},{5,7},{6,4},{7,5},{8,10},{9,11},{10,... | collective-permute-start | bytes 540680 | tf_op jit(solution)/shard_map/ppermute | solution.py:403
  38.8 0.5 collective-permute-start.13
  39.3 0.7 %collective-permute-done.12.refs_12_ = bf16[256,128]{1,0:T(8,128)(2,1)S(1)} collective-permute-done((bf16[256,128]{1,0:T(8,128)(2,1)S(1)}, bf16[256,128]{1,0:T(8,128)(2,1)S(1)}, u32[]{:S(2)}, u32[]{:S(2)}) %collective-permute-start.12) | collective-permute-done | bytes 65568 | tf_op jit(solution)/shard_map/ppermute | solution.py:403
  40.1 0.2 collective-permute-start.15
  40.2 0.4 collective-permute-start.5
  40.6 2.5 %collective-permute-done.10.refs_6_ = bf16[176,512]{1,0:T(8,128)(2,1)S(1)} collective-permute-done((bf16[176,512]{1,0:T(8,128)(2,1)S(1)}, bf16[176,512]{1,0:T(8,128)(2,1)S(1)}, u32[]{:S(2)}, u32[]{:S(2)}) %collective-permute-start.10) | collective-permute-done | bytes 180256 | tf_op jit(solution)/shard_map/ppermute | solution.py:403
  43.0 1.9 %collective-permute-done.8.refs_4_ = bf16[176,512]{1,0:T(8,128)(2,1)S(1)} collective-permute-done((bf16[176,512]{1,0:T(8,128)(2,1)S(1)}, bf16[176,512]{1,0:T(8,128)(2,1)S(1)}, u32[]{:S(2)}, u32[]{:S(2)}) %collective-permute-start.8) | collective-permute-done | bytes 180256 | tf_op jit(solution)/shard_map/ppermute | solution.py:403
  45.0 0.0 collective-permute-start.9
  45.0 0.0 collective-permute-done.6.refs_2_
  45.0 0.5 collective-permute-start.7
  45.5 0.1 collective-permute-start.14
  45.6 1.3 %collective-permute-done.14.refs_14_ = bf16[576,128]{1,0:T(8,128)(2,1)S(1)} collective-permute-done((bf16[576,128]{1,0:T(8,128)(2,1)S(1)}, bf16[576,128]{1,0:T(8,128)(2,1)S(1)}, u32[]{:S(2)}, u32[]{:S(2)}) %collective-permute-start.14) | collective-permute-done | bytes 147488 | tf_op jit(solution)/shard_map/ppermute | solution.py:403
  46.9 0.0 collective-permute-done.5.refs_1_
  46.9 0.0 collective-permute-done.11.refs_7_
  46.9 0.0 collective-permute-done.9.refs_5_
  46.9 0.0 collective-permute-done.7.refs_3_
  46.9 2.2 %shard_map.132 = (bf16[320,128]{1,0:T(8,128)(2,1)}, f32[112,512]{1,0:T(8,128)S(1)}, bf16[112,512]{1,0:T(8,128)(2,1)S(1)}, bf16[112,512]{1,0:T(8,128)(2,1)S(1)}, bf16[112,512]{1,0:T(8,128)(2,1)S(1)}) custom-call(s32[28]{0:T(128)S(1)} %copy-done.6, bf16[176,512]{1,0:T(8,128)(2,1)S(1)} %shard_map.131.refs_0_.grad_ref, ...), custom_call_target="tpu_custom_call" | custom-call | flops 100663296 | bytes 2539632 | tf_op jit(solution)/shard_map/pallas_call | solution.py:25
  49.1 1.5 %collective-permute-start.16 = (bf16[112,512]{1,0:T(8,128)(2,1)S(1)}, bf16[112,512]{1,0:T(8,128)(2,1)S(1)}, u32[]{:S(2)}, u32[]{:S(2)}) collective-permute-start(bf16[112,512]{1,0:T(8,128)(2,1)S(1)} %get-tuple-element.45), channel_id=1, source_target_pairs={{0,8},{1,9},{2,10},{3,11},{4,12},{5,13},{6,14},{7,15},{8,0},{9,1},... | collective-permute-start | bytes 344072 | tf_op jit(solution)/shard_map/ppermute | solution.py:403
  50.6 2.2 %collective-permute-start.17 = (bf16[112,512]{1,0:T(8,128)(2,1)S(1)}, bf16[112,512]{1,0:T(8,128)(2,1)S(1)}, u32[]{:S(2)}, u32[]{:S(2)}) collective-permute-start(bf16[112,512]{1,0:T(8,128)(2,1)S(1)} %get-tuple-element.46), channel_id=1, source_target_pairs={{0,16},{1,17},{2,18},{3,19},{4,20},{5,21},{6,22},{7,23},{8,24},{9,... | collective-permute-start | bytes 344072 | tf_op jit(solution)/shard_map/ppermute | solution.py:403
  52.9 0.7 %collective-permute-start.18 = (bf16[112,512]{1,0:T(8,128)(2,1)S(1)}, bf16[112,512]{1,0:T(8,128)(2,1)S(1)}, u32[]{:S(2)}, u32[]{:S(2)}) collective-permute-start(bf16[112,512]{1,0:T(8,128)(2,1)S(1)} %get-tuple-element.47), channel_id=1, source_target_pairs={{0,24},{1,25},{2,26},{3,27},{4,28},{5,29},{6,30},{7,31},{8,16},{9,... | collective-permute-start | bytes 344072 | tf_op jit(solution)/shard_map/ppermute | solution.py:403
  53.5 1.9 %shard_map.133 = bf16[256,512]{1,0:T(8,128)(2,1)} custom-call(s32[28]{0:T(128)S(1)} %copy-done.6, bf16[176,512]{1,0:T(8,128)(2,1)S(1)} %shard_map.131.refs_0_.grad_ref, bf16[2,1024,512]{2,1,0:T(8,128)(2,1)S(1)} %copy-done), custom_call_target="tpu_custom_call" | custom-call | flops 67108864 | bytes 2277488 | tf_op jit(solution)/shard_map/pallas_call | solution.py:25
  55.4 0.6 collective-permute-done.16.refs_1_
  56.0 6.5 %collective-permute-done.17.refs_2_ = bf16[112,512]{1,0:T(8,128)(2,1)S(1)} collective-permute-done((bf16[112,512]{1,0:T(8,128)(2,1)S(1)}, bf16[112,512]{1,0:T(8,128)(2,1)S(1)}, u32[]{:S(2)}, u32[]{:S(2)}) %collective-permute-start.17) | collective-permute-done | bytes 114720 | tf_op jit(solution)/shard_map/ppermute | solution.py:403
  62.5 1.3 %shard_map.134 = (f32[2,32,512]{2,1,0:T(8,128)}, f32[2,32]{1,0:T(2,128)}, f32[64,320]{1,0:T(8,128)}) custom-call(s32[28]{0:T(128)S(1)} %copy-done.6, f32[112,512]{1,0:T(8,128)S(1)} %get-tuple-element.44.refs_0_, bf16[112,512]{1,0:T(8,128)(2,1)S(1)} %collective-permute-done.16.refs_1_, bf16[112,512]{1,0:T(8,128)(2,1)S(1)} %collective-permute-done.17.refs_2_, ...), custom_call_target="tpu_custom_call" | custom-call | bytes 573552 | tf_op jit(solution)/shard_map/pallas_call | solution.py:25
  (16 shorter events, 0.0 us)
Async XLA Ops:
  2.6 7.3 %collective-permute-start = (bf16[128,512]{1,0:T(8,128)(2,1)}, bf16[128,512]{1,0:T(8,128)(2,1)S(1)}, u32[]{:S(2)}, u32[]{:S(2)}) collective-permute-start(bf16[128,512]{1,0:T(8,128)(2,1)} %get-tuple-element.31), channel_id=1, source_target_pairs={{0,1},{1,0},{2,3},{3,2},{4,5},{5,4},{6,7},{7,6},{8,9},{9,8},{10,11... | collective-permute-start | bytes 393224 | tf_op jit(solution)/shard_map/ppermute | solution.py:403
  3.1 13.7 %all-to-all-start = ((s32[8,1,128]{2,1,0:T(1,128)}), s32[8,1,128]{2,1,0:T(1,128)S(1)}, u32[]{:S(2)}, u32[]{:S(2)}) async-start(s32[8,1,128]{2,1,0:T(1,128)} %bitcast.19), calls=%async_computation | async-start | bytes 8192 | tf_op jit(solution)/shard_map/all_to_all | solution.py:428
  10.9 5.9 %collective-permute-start.1 = (bf16[128,512]{1,0:T(8,128)(2,1)S(1)}, bf16[128,512]{1,0:T(8,128)(2,1)S(1)}, u32[]{:S(2)}, u32[]{:S(2)}) collective-permute-start(bf16[128,512]{1,0:T(8,128)(2,1)S(1)} %add_convert_fusion.mine_ref), channel_id=1, source_target_pairs={{0,2},{1,3},{2,0},{3,1},{4,6},{5,7},{6,4},{7,5},{8,10},{9,11},{10,... | collective-permute-start | bytes 393224 | tf_op jit(solution)/shard_map/ppermute | solution.py:403
  12.5 21.0 %copy-start = (bf16[2,1024,512]{2,1,0:T(8,128)(2,1)S(1)}, bf16[2,1024,512]{2,1,0:T(8,128)(2,1)}, u32[]{:S(2)}) copy-start(bf16[2,1024,512]{2,1,0:T(8,128)(2,1)} %weight_ref.3) | copy-start | bytes 6291460
  16.8 22.0 %copy-start.4 = (bf16[256,128]{1,0:T(8,128)(2,1)S(1)}, bf16[256,128]{1,0:T(8,128)(2,1)}, u32[]{:S(2)}) copy-start(bf16[256,128]{1,0:T(8,128)(2,1)} %get-tuple-element.39.refs_8_) | copy-start | bytes 196612
  16.8 30.1 %copy-start.1 = (bf16[512,320]{0,1:T(8,128)(2,1)S(1)}, bf16[512,320]{0,1:T(8,128)(2,1)}, u32[]{:S(2)}) copy-start(bf16[512,320]{0,1:T(8,128)(2,1)} %param.16) | copy-start | bytes 983044
  16.8 30.1 %copy-start.3 = (bf16[128,320]{0,1:T(8,128)(2,1)S(1)}, bf16[128,320]{0,1:T(8,128)(2,1)}, u32[]{:S(2)}) copy-start(bf16[128,320]{0,1:T(8,128)(2,1)} %param.17) | copy-start | bytes 245764
  16.9 0.9 %copy-start.5 = (bf16[64,512]{1,0:T(8,128)(2,1)S(1)}, bf16[64,512]{1,0:T(8,128)(2,1)}, u32[]{:S(2)}) copy-start(bf16[64,512]{1,0:T(8,128)(2,1)} %get-tuple-element.32.sent_ref) | copy-start | bytes 196612
  17.8 29.2 %copy-start.6 = (s32[28]{0:T(128)S(1)}, s32[28]{0:T(128)}, u32[]{:S(2)}) copy-start(s32[28]{0:T(128)} %get-tuple-element.29.me_ref) | copy-start | bytes 340
  19.1 14.4 %all-to-all-start.1 = ((bf16[8,16,512]{2,1,0:T(8,128)(2,1)}), bf16[8,16,512]{2,1,0:T(8,128)(2,1)S(1)}, u32[]{:S(2)}, u32[]{:S(2)}) async-start(bf16[8,16,512]{2,1,0:T(8,128)(2,1)} %shard_map.130), calls=%async_computation.1 | async-start | bytes 262144 | tf_op jit(solution)/shard_map/all_to_all | solution.py:476
  25.1 8.4 %collective-permute-start.3 = (bf16[576,128]{1,0:T(8,128)(2,1)}, bf16[576,128]{1,0:T(8,128)(2,1)S(1)}, u32[]{:S(2)}, u32[]{:S(2)}) collective-permute-start(bf16[576,128]{1,0:T(8,128)(2,1)} %get-tuple-element.35), channel_id=1, source_target_pairs={{0,4},{1,5},{2,6},{3,7},{4,0},{5,1},{6,2},{7,3},{8,12},{9,13},{10,... | collective-permute-start | bytes 442376 | tf_op jit(solution)/shard_map/ppermute | solution.py:403
  27.1 4.8 %collective-permute-start.2 = (bf16[256,128]{1,0:T(8,128)(2,1)}, bf16[256,128]{1,0:T(8,128)(2,1)S(1)}, u32[]{:S(2)}, u32[]{:S(2)}) collective-permute-start(bf16[256,128]{1,0:T(8,128)(2,1)} %get-tuple-element.34), channel_id=1, source_target_pairs={{0,2},{1,3},{2,0},{3,1},{4,6},{5,7},{6,4},{7,5},{8,10},{9,11},{10,... | collective-permute-start | bytes 196616 | tf_op jit(solution)/shard_map/ppermute | solution.py:403
  28.0 5.5 %collective-permute-start.4 = (bf16[256,128]{1,0:T(8,128)(2,1)}, bf16[256,128]{1,0:T(8,128)(2,1)S(1)}, u32[]{:S(2)}, u32[]{:S(2)}) collective-permute-start(bf16[256,128]{1,0:T(8,128)(2,1)} %get-tuple-element.36), channel_id=1, source_target_pairs={{0,6},{1,7},{2,4},{3,5},{4,2},{5,3},{6,0},{7,1},{8,14},{9,15},{10,... | collective-permute-start | bytes 196616 | tf_op jit(solution)/shard_map/ppermute | solution.py:403
  33.5 1.1 %copy-start.2 = (f32[328,512]{1,0:T(8,128)S(1)}, f32[328,512]{1,0:T(8,128)}, u32[]{:S(2)}) copy-start(f32[328,512]{1,0:T(8,128)} %get-tuple-element.38.state_ref) | copy-start | bytes 2015236
  35.2 7.8 %collective-permute-start.10 = (bf16[176,512]{1,0:T(8,128)(2,1)S(1)}, bf16[176,512]{1,0:T(8,128)(2,1)S(1)}, u32[]{:S(2)}, u32[]{:S(2)}) collective-permute-start(bf16[176,512]{1,0:T(8,128)(2,1)S(1)} %shard_map.131.refs_0_.grad_ref), channel_id=1, source_target_pairs={{0,6},{1,7},{2,4},{3,5},{4,2},{5,3},{6,0},{7,1},{8,14},{9,15},{10,... | collective-permute-start | bytes 540680 | tf_op jit(solution)/shard_map/ppermute | solution.py:403
  37.2 7.8 %collective-permute-start.8 = (bf16[176,512]{1,0:T(8,128)(2,1)S(1)}, bf16[176,512]{1,0:T(8,128)(2,1)S(1)}, u32[]{:S(2)}, u32[]{:S(2)}) collective-permute-start(bf16[176,512]{1,0:T(8,128)(2,1)S(1)} %shard_map.131.refs_0_.grad_ref), channel_id=1, source_target_pairs={{0,4},{1,5},{2,6},{3,7},{4,0},{5,1},{6,2},{7,3},{8,12},{9,13},{10,... | collective-permute-start | bytes 540680 | tf_op jit(solution)/shard_map/ppermute | solution.py:403
  38.0 7.0 %collective-permute-start.6 = (bf16[176,512]{1,0:T(8,128)(2,1)S(1)}, bf16[176,512]{1,0:T(8,128)(2,1)S(1)}, u32[]{:S(2)}, u32[]{:S(2)}) collective-permute-start(bf16[176,512]{1,0:T(8,128)(2,1)S(1)} %shard_map.131.refs_0_.grad_ref), channel_id=1, source_target_pairs={{0,2},{1,3},{2,0},{3,1},{4,6},{5,7},{6,4},{7,5},{8,10},{9,11},{10,... | collective-permute-start | bytes 540680 | tf_op jit(solution)/shard_map/ppermute | solution.py:403
  38.8 1.3 %collective-permute-start.12 = (bf16[256,128]{1,0:T(8,128)(2,1)S(1)}, bf16[256,128]{1,0:T(8,128)(2,1)S(1)}, u32[]{:S(2)}, u32[]{:S(2)}) collective-permute-start(bf16[256,128]{1,0:T(8,128)(2,1)S(1)} %copy-done.4), channel_id=1, source_target_pairs={{0,1},{1,0},{2,3},{3,2},{4,5},{5,4},{6,7},{7,6},{8,9},{9,8},{10,11... | collective-permute-start | bytes 196616 | tf_op jit(solution)/shard_map/ppermute | solution.py:403
  38.8 1.4 %collective-permute-start.13 = (bf16[256,128]{1,0:T(8,128)(2,1)S(1)}, bf16[256,128]{1,0:T(8,128)(2,1)S(1)}, u32[]{:S(2)}, u32[]{:S(2)}) collective-permute-start(bf16[256,128]{1,0:T(8,128)(2,1)S(1)} %collective-permute-done.2.refs_9_), channel_id=1, source_target_pairs={{0,1},{1,0},{2,3},{3,2},{4,5},{5,4},{6,7},{7,6},{8,9},{9,8},{10,11... | collective-permute-start | bytes 196616 | tf_op jit(solution)/shard_map/ppermute | solution.py:403
  40.1 5.4 %collective-permute-start.15 = (bf16[256,128]{1,0:T(8,128)(2,1)S(1)}, bf16[256,128]{1,0:T(8,128)(2,1)S(1)}, u32[]{:S(2)}, u32[]{:S(2)}) collective-permute-start(bf16[256,128]{1,0:T(8,128)(2,1)S(1)} %collective-permute-done.4.refs_11_), channel_id=1, source_target_pairs={{0,1},{1,0},{2,3},{3,2},{4,5},{5,4},{6,7},{7,6},{8,9},{9,8},{10,11... | collective-permute-start | bytes 196616 | tf_op jit(solution)/shard_map/ppermute | solution.py:403
  40.2 6.7 %collective-permute-start.5 = (bf16[176,512]{1,0:T(8,128)(2,1)S(1)}, bf16[176,512]{1,0:T(8,128)(2,1)S(1)}, u32[]{:S(2)}, u32[]{:S(2)}) collective-permute-start(bf16[176,512]{1,0:T(8,128)(2,1)S(1)} %shard_map.131.refs_0_.grad_ref), channel_id=1, source_target_pairs={{0,1},{1,0},{2,3},{3,2},{4,5},{5,4},{6,7},{7,6},{8,9},{9,8},{10,11... | collective-permute-start | bytes 540680 | tf_op jit(solution)/shard_map/ppermute | solution.py:403
  43.0 3.8 %collective-permute-start.11 = (bf16[176,512]{1,0:T(8,128)(2,1)S(1)}, bf16[176,512]{1,0:T(8,128)(2,1)S(1)}, u32[]{:S(2)}, u32[]{:S(2)}) collective-permute-start(bf16[176,512]{1,0:T(8,128)(2,1)S(1)} %collective-permute-done.10.refs_6_), channel_id=1, source_target_pairs={{0,1},{1,0},{2,3},{3,2},{4,5},{5,4},{6,7},{7,6},{8,9},{9,8},{10,11... | collective-permute-start | bytes 540680 | tf_op jit(solution)/shard_map/ppermute | solution.py:403
  45.0 1.9 %collective-permute-start.9 = (bf16[176,512]{1,0:T(8,128)(2,1)S(1)}, bf16[176,512]{1,0:T(8,128)(2,1)S(1)}, u32[]{:S(2)}, u32[]{:S(2)}) collective-permute-start(bf16[176,512]{1,0:T(8,128)(2,1)S(1)} %collective-permute-done.8.refs_4_), channel_id=1, source_target_pairs={{0,1},{1,0},{2,3},{3,2},{4,5},{5,4},{6,7},{7,6},{8,9},{9,8},{10,11... | collective-permute-start | bytes 540680 | tf_op jit(solution)/shard_map/ppermute | solution.py:403
  45.0 1.9 %collective-permute-start.7 = (bf16[176,512]{1,0:T(8,128)(2,1)S(1)}, bf16[176,512]{1,0:T(8,128)(2,1)S(1)}, u32[]{:S(2)}, u32[]{:S(2)}) collective-permute-start(bf16[176,512]{1,0:T(8,128)(2,1)S(1)} %collective-permute-done.6.refs_2_), channel_id=1, source_target_pairs={{0,1},{1,0},{2,3},{3,2},{4,5},{5,4},{6,7},{7,6},{8,9},{9,8},{10,11... | collective-permute-start | bytes 540680 | tf_op jit(solution)/shard_map/ppermute | solution.py:403
  45.5 1.4 %collective-permute-start.14 = (bf16[576,128]{1,0:T(8,128)(2,1)S(1)}, bf16[576,128]{1,0:T(8,128)(2,1)S(1)}, u32[]{:S(2)}, u32[]{:S(2)}) collective-permute-start(bf16[576,128]{1,0:T(8,128)(2,1)S(1)} %collective-permute-done.3.refs_10_), channel_id=1, source_target_pairs={{0,1},{1,0},{2,3},{3,2},{4,5},{5,4},{6,7},{7,6},{8,9},{9,8},{10,11... | collective-permute-start | bytes 442376 | tf_op jit(solution)/shard_map/ppermute | solution.py:403
  49.1 6.9 %collective-permute-start.16 = (bf16[112,512]{1,0:T(8,128)(2,1)S(1)}, bf16[112,512]{1,0:T(8,128)(2,1)S(1)}, u32[]{:S(2)}, u32[]{:S(2)}) collective-permute-start(bf16[112,512]{1,0:T(8,128)(2,1)S(1)} %get-tuple-element.45), channel_id=1, source_target_pairs={{0,8},{1,9},{2,10},{3,11},{4,12},{5,13},{6,14},{7,15},{8,0},{9,1},... | collective-permute-start | bytes 344072 | tf_op jit(solution)/shard_map/ppermute | solution.py:403
  50.6 11.8 %collective-permute-start.17 = (bf16[112,512]{1,0:T(8,128)(2,1)S(1)}, bf16[112,512]{1,0:T(8,128)(2,1)S(1)}, u32[]{:S(2)}, u32[]{:S(2)}) collective-permute-start(bf16[112,512]{1,0:T(8,128)(2,1)S(1)} %get-tuple-element.46), channel_id=1, source_target_pairs={{0,16},{1,17},{2,18},{3,19},{4,20},{5,21},{6,22},{7,23},{8,24},{9,... | collective-permute-start | bytes 344072 | tf_op jit(solution)/shard_map/ppermute | solution.py:403
  52.9 9.6 %collective-permute-start.18 = (bf16[112,512]{1,0:T(8,128)(2,1)S(1)}, bf16[112,512]{1,0:T(8,128)(2,1)S(1)}, u32[]{:S(2)}, u32[]{:S(2)}) collective-permute-start(bf16[112,512]{1,0:T(8,128)(2,1)S(1)} %get-tuple-element.47), channel_id=1, source_target_pairs={{0,24},{1,25},{2,26},{3,27},{4,28},{5,29},{6,30},{7,31},{8,16},{9,... | collective-permute-start | bytes 344072 | tf_op jit(solution)/shard_map/ppermute | solution.py:403

commit v7 on v6

--- a/solution.py
+++ b/solution.py
@@ -113,9 +113,9 @@
 
 
 def state_views(state_ref):
-    part = (state_ref.shape[0] - 8) // 10
-    spans = ((0, 2), (2, 1), (3, 2), (5, 1), (6, 2), (8, 1), (9, 1))
-    return [state_ref.at[a * part : (a + n) * part] for a, n in spans] + [state_ref.at[10 * part :]]
+    part = (state_ref.shape[0] - 8) // 7
+    spans = ((0, 2), (2, 1), (3, 2), (5, 1), (6, 1))
+    return [state_ref.at[a * part : (a + n) * part] for a, n in spans] + [state_ref.at[7 * part :]]
 
 
 def forward_kernel(me_ref, *refs, pairs, frames, far, near, owned):
@@ -137,7 +137,7 @@
     turned_refs = rest[3:]
     for i in range(me_ref.shape[0]):
         later_ref[i] = me_ref[i]
-    slope1_ref, slope2_ref, hat1_ref, hat2_ref, scale1_ref, scale2_ref, pick_ref, gain_at = state_views(state_ref)
+    slope1_ref, slope2_ref, hat1_ref, hat2_ref, aux_ref, gain_at = state_views(state_ref)
     copies[0].wait()
     channels = feat_ref.shape[1]
     n2 = pairs * frames
@@ -155,7 +155,7 @@
     hidden, slope = gelu_parts(hat * gain_ref[0:1, :] + shift_ref[0:1, :])
     slope1_ref[...] = slope
     hat1_ref[...] = hat
-    scale1_ref[...] = jnp.broadcast_to(scale, scale1_ref.shape)
+    aux = [scale[:n2], scale[n2:]]
     hidden = hidden.astype(BF)
     hidden32 = hidden.astype(F32)
     copies[4].wait()
@@ -164,7 +164,7 @@
     made, slope = gelu_parts(hat * gain_ref[1:2, :] + shift_ref[1:2, :])
     slope2_ref[...] = slope
     hat2_ref[...] = hat
-    scale2_ref[...] = jnp.broadcast_to(scale, scale2_ref.shape)
+    aux.append(scale)
     none = jnp.zeros((frames, channels), F32)
     sent = []
     for d in range(frames_ref.shape[0] // frames):
@@ -178,8 +178,8 @@
     for p in range(pairs):
         slot = jnp.where(lax.div(row, frames) == p, me_ref[4 + 2 * pairs + 2 * p], slot)
     slot = slot * (2 * frames) + lax.rem(row, frames)
-    place = lax.broadcasted_iota(jnp.int32, (n2, channels), 1)
-    pick_ref[...] = jnp.where(place == slot, 1.0, 0.0)
+    aux.append(slot.astype(F32))
+    aux_ref[...] = jnp.concatenate([jnp.broadcast_to(a, (n2, channels // 4)) for a in aux], axis=1)
     gain_at[...] = jnp.concatenate([gain_ref[...], jnp.zeros((6, channels), F32)], axis=0)
     wide = in_turned.shape[1]
     fill = [jnp.zeros((wide - 3 * n2, channels), F32)] if wide > 3 * n2 else []
@@ -258,15 +258,17 @@
     lane = lax.broadcasted_iota(jnp.int32, (dp_count * frames, seq), 1)
     block = (lax.div(lane, frames) + 1).astype(F32)
     same = lax.rem(lane, frames) == lax.rem(row, frames)
-    shards = [0.0, 0.0]
-    for k in range(near):
-        tail = side_refs[k][start:, :].astype(F32)
-        ids = tail[8 : 8 + dp_count, :seq]
-        ids = jnp.broadcast_to(ids[:, None, :], (dp_count, frames, seq)).reshape(dp_count * frames, seq)
-        pick = jnp.where(jnp.logical_and(same, ids == block), 1.0, 0.0).astype(BF)
-        shards[2 * k // near] += lax.dot_general(
-            pick, tail[8 + dp_count :].astype(BF), (((0,), (0,)), ((), ())), preferred_element_type=F32
-        )
+    shards = []
+    for first_k in range(0, near, near // 2):
+        picks, sent = [], []
+        for k in range(first_k, first_k + near // 2):
+            tail = side_refs[k][start:, :].astype(F32)
+            ids = tail[8 : 8 + dp_count, :seq]
+            ids = jnp.broadcast_to(ids[:, None, :], (dp_count, frames, seq)).reshape(dp_count * frames, seq)
+            picks.append(jnp.where(jnp.logical_and(same, ids == block), 1.0, 0.0))
+            sent.append(tail[8 + dp_count :].astype(BF))
+        pick = jnp.concatenate(picks, axis=0).T.astype(BF)
+        shards.append(dot(pick, jnp.concatenate(sent, axis=0)))
     packed_ref[...] = dot_nt(weight_ref[...], shards[0].astype(BF)).astype(BF)
     partial = dot_nt(shards[0].T.astype(BF), mine_ref[...]) + dot_nt(shards[1].T.astype(BF), other)
     depth = -(-(n1 + n2) // 128) * 128
@@ -303,14 +305,14 @@
         out_refs[f - 1][...] = held[me_ref[2] ^ f].astype(BF)
 
 
-def norm_back(grad, slope_ref, hat_ref, scale_ref, gain):
+def norm_back(grad, slope_ref, hat_ref, scale, gain):
     pre = grad * slope_ref[...]
     hat = hat_ref[...]
     by_hat = pre * hat
     inner = pre * gain
     average = jnp.mean(inner, axis=-1, keepdims=True)
     along = jnp.mean(inner * hat, axis=-1, keepdims=True)
-    back = (inner - average - hat * along) * scale_ref[:, 0:1]
+    back = (inner - average - hat * along) * scale
     return (
         back.astype(BF),
         jnp.sum(by_hat, axis=0, keepdims=True),
@@ -320,10 +322,16 @@
 
 def back_kernel(slots_ref, got_ref, state_ref, weight_ref, out_ref, *, frames):
     channels = weight_ref.shape[2]
-    slope1_ref, slope2_ref, hat1_ref, hat2_ref, scale1_ref, scale2_ref, pick_ref, gain_ref = state_views(state_ref)
+    slope1_ref, slope2_ref, hat1_ref, hat2_ref, aux_ref, gain_ref = state_views(state_ref)
     slots = slots_ref[...]
-    grads = dot(pick_ref[:, : slots.shape[0]].astype(BF), slots)
-    second, gain2, shift2 = norm_back(grads, slope2_ref, hat2_ref, scale2_ref, gain_ref[1:2, :])
+    lanes = channels // 4
+    scale1 = jnp.concatenate([aux_ref[:, 0:1], aux_ref[:, lanes : lanes + 1]], axis=0)
+    scale2 = aux_ref[:, 2 * lanes : 2 * lanes + 1]
+    n2 = aux_ref.shape[0]
+    place = lax.broadcasted_iota(jnp.int32, (n2, slots.shape[0]), 1).astype(F32)
+    pick = jnp.where(place == aux_ref[:, 3 * lanes : 3 * lanes + 1], 1.0, 0.0).astype(BF)
+    grads = dot(pick, slots)
+    second, gain2, shift2 = norm_back(grads, slope2_ref, hat2_ref, scale2, gain_ref[1:2, :])
     hidden = jnp.concatenate(
         [
             dot_nt(second, weight_ref[1, :channels, :]),
@@ -332,7 +340,7 @@
         axis=0,
     )
     hidden = hidden.astype(BF).astype(F32)
-    first, gain1, shift1 = norm_back(hidden, slope1_ref, hat1_ref, scale1_ref, gain_ref[0:1, :])
+    first, gain1, shift1 = norm_back(hidden, slope1_ref, hat1_ref, scale1, gain_ref[0:1, :])
     sums = jnp.concatenate([gain1, shift1, gain2, shift2], axis=0)
     high = sums.astype(BF).astype(F32)
     ids = got_ref[...].astype(F32)
@@ -437,7 +445,7 @@
         [
             shape(*me.shape, kind=jnp.int32),
             shape(dp_count * frames, channels),
-            shape(10 * n2 + 8, channels, kind=F32),
+            shape(7 * n2 + 8, channels, kind=F32),
         ]
         + [
             shape(2 * far * owned + (width if 2 * k == mp_count else 0), wide)
@@ -474,9 +482,8 @@
         scratch=[pltpu.VMEM((seq, channels), F32)],
     )
     slots = lax.all_to_all(sent, "dp", split_axis=0, concat_axis=0, tiled=True)
-    slots, *in_sides[: near // 2] = lax.optimization_barrier((slots, *in_sides[: near // 2]))
-
-    in_sides += [swap(side, 1) for side in in_sides]
+    slots, *in_sides[:2] = lax.optimization_barrier((slots, *in_sides[:2]))
+
     rows_sent = n1 + n2 + 8 + dp_count * (1 + frames)
     grads = call(
         functools.partial(back_kernel, frames=frames),
@@ -484,7 +491,15 @@
         (slots.reshape(-1, channels), got_index, state, conv_weight),
         flops=2 * n2 * 2 * channels * channels,
     )
-    by_mask = {mask: swap(grads, mask) if mask else grads for mask in range(0, near, 2)}
+    by_mask = {0: grads}
+    for mask in range(2, near, 2):
+        leaving = grads
+        if mask == near - 2:
+            leaving, *in_sides[2 : near // 2] = lax.optimization_barrier(
+                (grads, *in_sides[2 : near // 2])
+            )
+        by_mask[mask] = swap(leaving, mask)
+    in_sides += [swap(side, 1) for side in in_sides]
     for mask in range(0, near, 2):
         by_mask[mask + 1] = swap(by_mask[mask], 1)
 

time: 64.1 us -> 62.1 us (0.969)
  waiting for transfers between devices: 18.4 us -> 16.7 us
    ppermute x19, waiting for transfers between devices: 18.4 us -> 16 us  [swap(): lax.ppermute(x, everyone, [(i, i ^ mask) for i in range(dp_count * mp_cou...]
    all_to_all x1, waiting for transfers between devices: 0.01 us -> 0.67 us  [local(): slots = lax.all_to_all(sent, 'dp', split_axis=0, concat_axis=0, tiled=True)]
  transfers between devices with their start and end apart: 21 -> 21, of which waited for: 8 -> 9; matrix products, arithmetic and copies ran while one was open for 1% -> 2% of each run, Pallas kernels for 10% -> 11%
where the time goes in v7:
time: 62.1 us; the launch traced here: 61.7 us
  starting transfers between devices  27.9 us (45%)
  waiting for transfers between devices  16.7 us (27%)
  Pallas kernels  13.5 us (22%)
  local copies, waits for them, and re-layouts  1.93 us (3%)
  other arithmetic  0.95 us (2%)
  between operations  0.78 us (1%)
    ppermute x19, waiting for transfers between devices, swap(): lax.ppermute(x, everyone, [(i, i ^ mask) for i in range(dp_count * mp_cou...  16 us
    ppermute x19, starting transfers between devices, swap(): lax.ppermute(x, everyone, [(i, i ^ mask) for i in range(dp_count * mp_cou...  15.1 us
    pallas_call x7, Pallas kernels, call(): pl.pallas_call(body, out_shape=out, in_specs=specs, out_specs=[pl.BlockSp...  13.5 us
    all_to_all x1, starting transfers between devices, local(): lax.all_to_all(index, 'dp', split_axis=0, concat_axis=0, tiled=True)  6.82 us
    all_to_all x1, starting transfers between devices, local(): slots = lax.all_to_all(sent, 'dp', split_axis=0, concat_axis=0, tiled=True)  5.99 us
    unnamed x14, local copies, waits for them, and re-layouts  1.93 us
  transfers between devices with their start and end apart: 21, of which 9 were waited for; matrix products, arithmetic and copies ran while one was open for 2% of the time, Pallas kernels for 11%

profile of v7, /device:TPU:0, one launch (start us, length us, event | category | flops | bytes accessed | tf_op | source)
XLA Modules:
  0.0 61.7 jit_solution(2994212622782338955)
XLA Ops:
  0.6 2.0 %shard_map.128 = (s32[28]{0:T(128)}, s32[8,128]{1,0:T(8,128)}, bf16[128,512]{1,0:T(8,128)(2,1)}) custom-call(bf16[320,512]{1,0:T(8,128)(2,1)} %bitcast.10, bf16[320,128]{1,0:T(8,128)(2,1)} %bitcast.13, s32[8]{0:T(128)} %lengths_hbm.1, s32[8]{0:T(128)} %dests_hbm.1, s32[8]{0:T(128)} %offsets_hbm.1), custom_call_target="tpu_custom_call" | custom-call | flops 41943040 | bytes 409696 | tf_op jit(solution)/shard_map/pallas_call | solution.py:25
  2.6 0.5 collective-permute-start
  3.1 6.8 %all-to-all-start = ((s32[8,1,128]{2,1,0:T(1,128)}), s32[8,1,128]{2,1,0:T(1,128)S(1)}, u32[]{:S(2)}, u32[]{:S(2)}) async-start(s32[8,1,128]{2,1,0:T(1,128)} %bitcast.19), calls=%async_computation | async-start | bytes 8192 | tf_op jit(solution)/shard_map/all_to_all | solution.py:436
  10.0 0.0 collective-permute-done
  10.0 1.0 %add_convert_fusion.mine_ref = bf16[128,512]{1,0:T(8,128)(2,1)S(1)} fusion(bf16[128,512]{1,0:T(8,128)(2,1)S(1)} %collective-permute-done, bf16[128,512]{1,0:T(8,128)(2,1)} %get-tuple-element.32), kind=kLoop, calls=%fused_computation | loop fusion | flops 262144 | bytes 393216 | tf_op jit(solution)/shard_map/convert_element_type | solution.py:474
  10.9 1.6 %collective-permute-start.1 = (bf16[128,512]{1,0:T(8,128)(2,1)S(1)}, bf16[128,512]{1,0:T(8,128)(2,1)S(1)}, u32[]{:S(2)}, u32[]{:S(2)}) collective-permute-start(bf16[128,512]{1,0:T(8,128)(2,1)S(1)} %add_convert_fusion.mine_ref), channel_id=1, source_target_pairs={{0,2},{1,3},{2,0},{3,1},{4,6},{5,7},{6,4},{7,5},{8,10},{9,11},{10,... | collective-permute-start | bytes 393224 | tf_op jit(solution)/shard_map/ppermute | solution.py:411
  12.5 4.2 %shard_map.129 = (s32[28]{0:T(128)}, bf16[64,512]{1,0:T(8,128)(2,1)}, f32[232,512]{1,0:T(8,128)}, bf16[256,128]{1,0:T(8,128)(2,1)}, bf16[256,128]{1,0:T(8,128)(2...) custom-call(s32[28]{0:T(128)} %get-tuple-element.29.me_ref, bf16[256,512]{1,0:T(8,128)(2,1)} %bitcast.20, ...), custom_call_target="tpu_custom_call" | custom-call | flops 10000000000 | bytes 2449520 | tf_op jit(solution)/shard_map/pallas_call | solution.py:25
  16.8 0.0 copy-start.4
  16.8 0.0 copy-start.1
  16.8 0.0 copy-start.3
  16.8 0.0 copy-start.5
  16.8 0.9 %copy-done.5 = bf16[64,512]{1,0:T(8,128)(2,1)S(1)} copy-done((bf16[64,512]{1,0:T(8,128)(2,1)S(1)}, bf16[64,512]{1,0:T(8,128)(2,1)}, u32[]{:S(2)}) %copy-start.5) | copy-done | bytes 65560
  17.7 1.3 %shard_map.130 = bf16[8,16,512]{2,1,0:T(8,128)(2,1)} custom-call(s32[8,128]{1,0:T(8,128)S(1)} %bitcast.16, bf16[128,512]{1,0:T(8,128)(2,1)S(1)} %add_convert_fusion.mine_ref, bf16[128,512]{1,0:T(8,128)(2,1)S(1)} %collective-permute-done.1.other_ref, bf16[64,512]{1,0:T(8,128)(2,1)S(1)} %copy-done.5), custom_call_target="tpu_custom_call" | custom-call | bytes 331776 | tf_op jit(solution)/shard_map/pallas_call | solution.py:25
  19.0 6.0 %all-to-all-start.1 = ((bf16[8,16,512]{2,1,0:T(8,128)(2,1)}), bf16[8,16,512]{2,1,0:T(8,128)(2,1)S(1)}, u32[]{:S(2)}, u32[]{:S(2)}) async-start(bf16[8,16,512]{2,1,0:T(8,128)(2,1)} %shard_map.130), calls=%async_computation.1 | async-start | bytes 262144 | tf_op jit(solution)/shard_map/all_to_all | solution.py:484
  25.0 2.0 %collective-permute-start.8 = (bf16[576,128]{1,0:T(8,128)(2,1)}, bf16[576,128]{1,0:T(8,128)(2,1)S(1)}, u32[]{:S(2)}, u32[]{:S(2)}) collective-permute-start(bf16[576,128]{1,0:T(8,128)(2,1)} %get-tuple-element.38), channel_id=1, source_target_pairs={{0,4},{1,5},{2,6},{3,7},{4,0},{5,1},{6,2},{7,3},{8,12},{9,13},{10,... | collective-permute-start | bytes 442376 | tf_op jit(solution)/shard_map/ppermute | solution.py:411
  27.0 1.0 %collective-permute-start.2 = (bf16[256,128]{1,0:T(8,128)(2,1)}, bf16[256,128]{1,0:T(8,128)(2,1)S(1)}, u32[]{:S(2)}, u32[]{:S(2)}) collective-permute-start(bf16[256,128]{1,0:T(8,128)(2,1)} %get-tuple-element.35), channel_id=1, source_target_pairs={{0,2},{1,3},{2,0},{3,1},{4,6},{5,7},{6,4},{7,5},{8,10},{9,11},{10,... | collective-permute-start | bytes 196616 | tf_op jit(solution)/shard_map/ppermute | solution.py:411
  28.0 0.5 collective-permute-start.9
  28.5 3.3 %collective-permute-done.2.refs_9_ = bf16[256,128]{1,0:T(8,128)(2,1)S(1)} collective-permute-done((bf16[256,128]{1,0:T(8,128)(2,1)}, bf16[256,128]{1,0:T(8,128)(2,1)S(1)}, u32[]{:S(2)}, u32[]{:S(2)}) %collective-permute-start.2) | collective-permute-done | bytes 65568 | tf_op jit(solution)/shard_map/ppermute | solution.py:411
  31.8 0.7 %all-to-all-done.1 = bf16[8,16,512]{2,1,0:T(8,128)(2,1)S(1)} async-done(((bf16[8,16,512]{2,1,0:T(8,128)(2,1)}), bf16[8,16,512]{2,1,0:T(8,128)(2,1)S(1)}, u32[]{:S(2)}, u32[]{:S(2)}) %all-to-all-start.1) | async-done | bytes 131104 | tf_op jit(solution)/shard_map/all_to_all | solution.py:484
  32.5 1.0 %copy-done.2 = f32[232,512]{1,0:T(8,128)S(1)} copy-done((f32[232,512]{1,0:T(8,128)S(1)}, f32[232,512]{1,0:T(8,128)}, u32[]{:S(2)}) %copy-start.2) | copy-done | bytes 475160
  33.5 0.7 %shard_map.131.refs_0_.grad_ref = bf16[176,512]{1,0:T(8,128)(2,1)S(1)} custom-call(bf16[128,512]{1,0:T(8,128)(2,1)S(1)} %bitcast.12, s32[8,128]{1,0:T(8,128)S(1)} %bitcast.17, f32[232,512]{1,0:T(8,128)S(1)} %copy-done.2, bf16[2,1024,512]{2,1,0:T(8,128)(2,1)S(1)} %copy-done), custom_call_target="tpu_custom_call" | custom-call | flops 33554432 | bytes 2707456 | tf_op jit(solution)/shard_map/pallas_call | solution.py:25
  34.2 0.0 collective-permute-done.8.refs_10_
  34.2 1.1 %collective-permute-start.10 = (bf16[176,512]{1,0:T(8,128)(2,1)S(1)}, bf16[176,512]{1,0:T(8,128)(2,1)S(1)}, u32[]{:S(2)}, u32[]{:S(2)}) collective-permute-start(bf16[176,512]{1,0:T(8,128)(2,1)S(1)} %shard_map.131.refs_0_.grad_ref), channel_id=1, source_target_pairs={{0,6},{1,7},{2,4},{3,5},{4,2},{5,3},{6,0},{7,1},{8,14},{9,15},{10,... | collective-permute-start | bytes 540680 | tf_op jit(solution)/shard_map/ppermute | solution.py:411
  35.3 1.3 %collective-permute-start.6 = (bf16[176,512]{1,0:T(8,128)(2,1)S(1)}, bf16[176,512]{1,0:T(8,128)(2,1)S(1)}, u32[]{:S(2)}, u32[]{:S(2)}) collective-permute-start(bf16[176,512]{1,0:T(8,128)(2,1)S(1)} %shard_map.131.refs_0_.grad_ref), channel_id=1, source_target_pairs={{0,4},{1,5},{2,6},{3,7},{4,0},{5,1},{6,2},{7,3},{8,12},{9,13},{10,... | collective-permute-start | bytes 540680 | tf_op jit(solution)/shard_map/ppermute | solution.py:411
  36.6 1.1 %collective-permute-start.4 = (bf16[176,512]{1,0:T(8,128)(2,1)S(1)}, bf16[176,512]{1,0:T(8,128)(2,1)S(1)}, u32[]{:S(2)}, u32[]{:S(2)}) collective-permute-start(bf16[176,512]{1,0:T(8,128)(2,1)S(1)} %shard_map.131.refs_0_.grad_ref), channel_id=1, source_target_pairs={{0,2},{1,3},{2,0},{3,1},{4,6},{5,7},{6,4},{7,5},{8,10},{9,11},{10,... | collective-permute-start | bytes 540680 | tf_op jit(solution)/shard_map/ppermute | solution.py:411
  37.8 0.0 collective-permute-start.12
  37.8 0.5 collective-permute-start.13
  38.3 0.7 %collective-permute-done.12.refs_12_ = bf16[256,128]{1,0:T(8,128)(2,1)S(1)} collective-permute-done((bf16[256,128]{1,0:T(8,128)(2,1)S(1)}, bf16[256,128]{1,0:T(8,128)(2,1)S(1)}, u32[]{:S(2)}, u32[]{:S(2)}) %collective-permute-start.12) | collective-permute-done | bytes 65568 | tf_op jit(solution)/shard_map/ppermute | solution.py:411
  39.0 0.2 collective-permute-start.15
  39.2 0.0 collective-permute-done.13.refs_13_
  39.2 0.4 collective-permute-start.3
  39.6 2.4 %collective-permute-done.10.refs_6_ = bf16[176,512]{1,0:T(8,128)(2,1)S(1)} collective-permute-done((bf16[176,512]{1,0:T(8,128)(2,1)S(1)}, bf16[176,512]{1,0:T(8,128)(2,1)S(1)}, u32[]{:S(2)}, u32[]{:S(2)}) %collective-permute-start.10) | collective-permute-done | bytes 180256 | tf_op jit(solution)/shard_map/ppermute | solution.py:411
  41.9 0.0 collective-permute-start.11
  41.9 1.2 %collective-permute-done.6.refs_4_ = bf16[176,512]{1,0:T(8,128)(2,1)S(1)} collective-permute-done((bf16[176,512]{1,0:T(8,128)(2,1)S(1)}, bf16[176,512]{1,0:T(8,128)(2,1)S(1)}, u32[]{:S(2)}, u32[]{:S(2)}) %collective-permute-start.6) | collective-permute-done | bytes 180256 | tf_op jit(solution)/shard_map/ppermute | solution.py:411
  43.1 0.0 collective-permute-start.7
  43.1 0.7 %collective-permute-done.4.refs_2_ = bf16[176,512]{1,0:T(8,128)(2,1)S(1)} collective-permute-done((bf16[176,512]{1,0:T(8,128)(2,1)S(1)}, bf16[176,512]{1,0:T(8,128)(2,1)S(1)}, u32[]{:S(2)}, u32[]{:S(2)}) %collective-permute-start.4) | collective-permute-done | bytes 180256 | tf_op jit(solution)/shard_map/ppermute | solution.py:411
  43.8 0.0 collective-permute-start.5
  43.8 0.0 collective-permute-done.15.refs_15_
  43.8 0.5 collective-permute-start.14
  44.3 1.1 %collective-permute-done.14.refs_14_ = bf16[576,128]{1,0:T(8,128)(2,1)S(1)} collective-permute-done((bf16[576,128]{1,0:T(8,128)(2,1)S(1)}, bf16[576,128]{1,0:T(8,128)(2,1)S(1)}, u32[]{:S(2)}, u32[]{:S(2)}) %collective-permute-start.14) | collective-permute-done | bytes 147488 | tf_op jit(solution)/shard_map/ppermute | solution.py:411
  45.4 2.1 %shard_map.132 = (bf16[320,128]{1,0:T(8,128)(2,1)}, f32[112,512]{1,0:T(8,128)S(1)}, bf16[112,512]{1,0:T(8,128)(2,1)S(1)}, bf16[112,512]{1,0:T(8,128)(2,1)S(1)}, bf16[112,512]{1,0:T(8,128)(2,1)S(1)}) custom-call(s32[28]{0:T(128)S(1)} %copy-done.6, bf16[176,512]{1,0:T(8,128)(2,1)S(1)} %shard_map.131.refs_0_.grad_ref, ...), custom_call_target="tpu_custom_call" | custom-call | flops 100663296 | bytes 2539632 | tf_op jit(solution)/shard_map/pallas_call | solution.py:25
  47.5 1.1 %collective-permute-start.16 = (bf16[112,512]{1,0:T(8,128)(2,1)S(1)}, bf16[112,512]{1,0:T(8,128)(2,1)S(1)}, u32[]{:S(2)}, u32[]{:S(2)}) collective-permute-start(bf16[112,512]{1,0:T(8,128)(2,1)S(1)} %get-tuple-element.47), channel_id=1, source_target_pairs={{0,8},{1,9},{2,10},{3,11},{4,12},{5,13},{6,14},{7,15},{8,0},{9,1},... | collective-permute-start | bytes 344072 | tf_op jit(solution)/shard_map/ppermute | solution.py:411
  48.6 2.2 %collective-permute-start.17 = (bf16[112,512]{1,0:T(8,128)(2,1)S(1)}, bf16[112,512]{1,0:T(8,128)(2,1)S(1)}, u32[]{:S(2)}, u32[]{:S(2)}) collective-permute-start(bf16[112,512]{1,0:T(8,128)(2,1)S(1)} %get-tuple-element.48), channel_id=1, source_target_pairs={{0,16},{1,17},{2,18},{3,19},{4,20},{5,21},{6,22},{7,23},{8,24},{9,... | collective-permute-start | bytes 344072 | tf_op jit(solution)/shard_map/ppermute | solution.py:411
  50.8 1.1 %collective-permute-start.18 = (bf16[112,512]{1,0:T(8,128)(2,1)S(1)}, bf16[112,512]{1,0:T(8,128)(2,1)S(1)}, u32[]{:S(2)}, u32[]{:S(2)}) collective-permute-start(bf16[112,512]{1,0:T(8,128)(2,1)S(1)} %get-tuple-element.49), channel_id=1, source_target_pairs={{0,24},{1,25},{2,26},{3,27},{4,28},{5,29},{6,30},{7,31},{8,16},{9,... | collective-permute-start | bytes 344072 | tf_op jit(solution)/shard_map/ppermute | solution.py:411
  51.9 1.9 %shard_map.133 = bf16[256,512]{1,0:T(8,128)(2,1)} custom-call(s32[28]{0:T(128)S(1)} %copy-done.6, bf16[176,512]{1,0:T(8,128)(2,1)S(1)} %shard_map.131.refs_0_.grad_ref, bf16[2,1024,512]{2,1,0:T(8,128)(2,1)S(1)} %copy-done), custom_call_target="tpu_custom_call" | custom-call | flops 67108864 | bytes 2277488 | tf_op jit(solution)/shard_map/pallas_call | solution.py:25
  53.8 0.7 %collective-permute-done.16.refs_1_ = bf16[112,512]{1,0:T(8,128)(2,1)S(1)} collective-permute-done((bf16[112,512]{1,0:T(8,128)(2,1)S(1)}, bf16[112,512]{1,0:T(8,128)(2,1)S(1)}, u32[]{:S(2)}, u32[]{:S(2)}) %collective-permute-start.16) | collective-permute-done | bytes 114720 | tf_op jit(solution)/shard_map/ppermute | solution.py:411
  54.5 5.9 %collective-permute-done.17.refs_2_ = bf16[112,512]{1,0:T(8,128)(2,1)S(1)} collective-permute-done((bf16[112,512]{1,0:T(8,128)(2,1)S(1)}, bf16[112,512]{1,0:T(8,128)(2,1)S(1)}, u32[]{:S(2)}, u32[]{:S(2)}) %collective-permute-start.17) | collective-permute-done | bytes 114720 | tf_op jit(solution)/shard_map/ppermute | solution.py:411
  60.4 1.3 %shard_map.134 = (f32[2,32,512]{2,1,0:T(8,128)}, f32[2,32]{1,0:T(2,128)}, f32[64,320]{1,0:T(8,128)}) custom-call(s32[28]{0:T(128)S(1)} %copy-done.6, f32[112,512]{1,0:T(8,128)S(1)} %get-tuple-element.46.refs_0_, bf16[112,512]{1,0:T(8,128)(2,1)S(1)} %collective-permute-done.16.refs_1_, bf16[112,512]{1,0:T(8,128)(2,1)S(1)} %collective-permute-done.17.refs_2_, ...), custom_call_target="tpu_custom_call" | custom-call | bytes 573552 | tf_op jit(solution)/shard_map/pallas_call | solution.py:25
  (16 shorter events, 0.0 us)
Async XLA Ops:
  2.6 7.3 %collective-permute-start = (bf16[128,512]{1,0:T(8,128)(2,1)}, bf16[128,512]{1,0:T(8,128)(2,1)S(1)}, u32[]{:S(2)}, u32[]{:S(2)}) collective-permute-start(bf16[128,512]{1,0:T(8,128)(2,1)} %get-tuple-element.32), channel_id=1, source_target_pairs={{0,1},{1,0},{2,3},{3,2},{4,5},{5,4},{6,7},{7,6},{8,9},{9,8},{10,11... | collective-permute-start | bytes 393224 | tf_op jit(solution)/shard_map/ppermute | solution.py:411
  3.1 13.7 %all-to-all-start = ((s32[8,1,128]{2,1,0:T(1,128)}), s32[8,1,128]{2,1,0:T(1,128)S(1)}, u32[]{:S(2)}, u32[]{:S(2)}) async-start(s32[8,1,128]{2,1,0:T(1,128)} %bitcast.19), calls=%async_computation | async-start | bytes 8192 | tf_op jit(solution)/shard_map/all_to_all | solution.py:436
  10.9 5.9 %collective-permute-start.1 = (bf16[128,512]{1,0:T(8,128)(2,1)S(1)}, bf16[128,512]{1,0:T(8,128)(2,1)S(1)}, u32[]{:S(2)}, u32[]{:S(2)}) collective-permute-start(bf16[128,512]{1,0:T(8,128)(2,1)S(1)} %add_convert_fusion.mine_ref), channel_id=1, source_target_pairs={{0,2},{1,3},{2,0},{3,1},{4,6},{5,7},{6,4},{7,5},{8,10},{9,11},{10,... | collective-permute-start | bytes 393224 | tf_op jit(solution)/shard_map/ppermute | solution.py:411
  12.5 19.9 %copy-start = (bf16[2,1024,512]{2,1,0:T(8,128)(2,1)S(1)}, bf16[2,1024,512]{2,1,0:T(8,128)(2,1)}, u32[]{:S(2)}) copy-start(bf16[2,1024,512]{2,1,0:T(8,128)(2,1)} %weight_ref.3) | copy-start | bytes 6291460
  16.8 21.0 %copy-start.4 = (bf16[256,128]{1,0:T(8,128)(2,1)S(1)}, bf16[256,128]{1,0:T(8,128)(2,1)}, u32[]{:S(2)}) copy-start(bf16[256,128]{1,0:T(8,128)(2,1)} %get-tuple-element.41.refs_8_) | copy-start | bytes 196612
  16.8 28.6 %copy-start.1 = (bf16[512,320]{0,1:T(8,128)(2,1)S(1)}, bf16[512,320]{0,1:T(8,128)(2,1)}, u32[]{:S(2)}) copy-start(bf16[512,320]{0,1:T(8,128)(2,1)} %param.16) | copy-start | bytes 983044
  16.8 28.6 %copy-start.3 = (bf16[128,320]{0,1:T(8,128)(2,1)S(1)}, bf16[128,320]{0,1:T(8,128)(2,1)}, u32[]{:S(2)}) copy-start(bf16[128,320]{0,1:T(8,128)(2,1)} %param.17) | copy-start | bytes 245764
  16.8 0.9 %copy-start.5 = (bf16[64,512]{1,0:T(8,128)(2,1)S(1)}, bf16[64,512]{1,0:T(8,128)(2,1)}, u32[]{:S(2)}) copy-start(bf16[64,512]{1,0:T(8,128)(2,1)} %get-tuple-element.33.sent_ref) | copy-start | bytes 196612
  17.7 27.7 %copy-start.6 = (s32[28]{0:T(128)S(1)}, s32[28]{0:T(128)}, u32[]{:S(2)}) copy-start(s32[28]{0:T(128)} %get-tuple-element.30.me_ref) | copy-start | bytes 340
  19.0 13.4 %all-to-all-start.1 = ((bf16[8,16,512]{2,1,0:T(8,128)(2,1)}), bf16[8,16,512]{2,1,0:T(8,128)(2,1)S(1)}, u32[]{:S(2)}, u32[]{:S(2)}) async-start(bf16[8,16,512]{2,1,0:T(8,128)(2,1)} %shard_map.130), calls=%async_computation.1 | async-start | bytes 262144 | tf_op jit(solution)/shard_map/all_to_all | solution.py:484
  25.0 9.2 %collective-permute-start.8 = (bf16[576,128]{1,0:T(8,128)(2,1)}, bf16[576,128]{1,0:T(8,128)(2,1)S(1)}, u32[]{:S(2)}, u32[]{:S(2)}) collective-permute-start(bf16[576,128]{1,0:T(8,128)(2,1)} %get-tuple-element.38), channel_id=1, source_target_pairs={{0,4},{1,5},{2,6},{3,7},{4,0},{5,1},{6,2},{7,3},{8,12},{9,13},{10,... | collective-permute-start | bytes 442376 | tf_op jit(solution)/shard_map/ppermute | solution.py:411
  27.0 4.8 %collective-permute-start.2 = (bf16[256,128]{1,0:T(8,128)(2,1)}, bf16[256,128]{1,0:T(8,128)(2,1)S(1)}, u32[]{:S(2)}, u32[]{:S(2)}) collective-permute-start(bf16[256,128]{1,0:T(8,128)(2,1)} %get-tuple-element.35), channel_id=1, source_target_pairs={{0,2},{1,3},{2,0},{3,1},{4,6},{5,7},{6,4},{7,5},{8,10},{9,11},{10,... | collective-permute-start | bytes 196616 | tf_op jit(solution)/shard_map/ppermute | solution.py:411
  28.0 6.2 %collective-permute-start.9 = (bf16[256,128]{1,0:T(8,128)(2,1)}, bf16[256,128]{1,0:T(8,128)(2,1)S(1)}, u32[]{:S(2)}, u32[]{:S(2)}) collective-permute-start(bf16[256,128]{1,0:T(8,128)(2,1)} %get-tuple-element.39), channel_id=1, source_target_pairs={{0,6},{1,7},{2,4},{3,5},{4,2},{5,3},{6,0},{7,1},{8,14},{9,15},{10,... | collective-permute-start | bytes 196616 | tf_op jit(solution)/shard_map/ppermute | solution.py:411
  32.5 1.0 %copy-start.2 = (f32[232,512]{1,0:T(8,128)S(1)}, f32[232,512]{1,0:T(8,128)}, u32[]{:S(2)}) copy-start(f32[232,512]{1,0:T(8,128)} %get-tuple-element.37.state_ref) | copy-start | bytes 1425412
  34.2 7.7 %collective-permute-start.10 = (bf16[176,512]{1,0:T(8,128)(2,1)S(1)}, bf16[176,512]{1,0:T(8,128)(2,1)S(1)}, u32[]{:S(2)}, u32[]{:S(2)}) collective-permute-start(bf16[176,512]{1,0:T(8,128)(2,1)S(1)} %shard_map.131.refs_0_.grad_ref), channel_id=1, source_target_pairs={{0,6},{1,7},{2,4},{3,5},{4,2},{5,3},{6,0},{7,1},{8,14},{9,15},{10,... | collective-permute-start | bytes 540680 | tf_op jit(solution)/shard_map/ppermute | solution.py:411
  35.3 7.8 %collective-permute-start.6 = (bf16[176,512]{1,0:T(8,128)(2,1)S(1)}, bf16[176,512]{1,0:T(8,128)(2,1)S(1)}, u32[]{:S(2)}, u32[]{:S(2)}) collective-permute-start(bf16[176,512]{1,0:T(8,128)(2,1)S(1)} %shard_map.131.refs_0_.grad_ref), channel_id=1, source_target_pairs={{0,4},{1,5},{2,6},{3,7},{4,0},{5,1},{6,2},{7,3},{8,12},{9,13},{10,... | collective-permute-start | bytes 540680 | tf_op jit(solution)/shard_map/ppermute | solution.py:411
  36.6 7.1 %collective-permute-start.4 = (bf16[176,512]{1,0:T(8,128)(2,1)S(1)}, bf16[176,512]{1,0:T(8,128)(2,1)S(1)}, u32[]{:S(2)}, u32[]{:S(2)}) collective-permute-start(bf16[176,512]{1,0:T(8,128)(2,1)S(1)} %shard_map.131.refs_0_.grad_ref), channel_id=1, source_target_pairs={{0,2},{1,3},{2,0},{3,1},{4,6},{5,7},{6,4},{7,5},{8,10},{9,11},{10,... | collective-permute-start | bytes 540680 | tf_op jit(solution)/shard_map/ppermute | solution.py:411
  37.8 1.3 %collective-permute-start.12 = (bf16[256,128]{1,0:T(8,128)(2,1)S(1)}, bf16[256,128]{1,0:T(8,128)(2,1)S(1)}, u32[]{:S(2)}, u32[]{:S(2)}) collective-permute-start(bf16[256,128]{1,0:T(8,128)(2,1)S(1)} %copy-done.4), channel_id=1, source_target_pairs={{0,1},{1,0},{2,3},{3,2},{4,5},{5,4},{6,7},{7,6},{8,9},{9,8},{10,11... | collective-permute-start | bytes 196616 | tf_op jit(solution)/shard_map/ppermute | solution.py:411
  37.8 1.4 %collective-permute-start.13 = (bf16[256,128]{1,0:T(8,128)(2,1)S(1)}, bf16[256,128]{1,0:T(8,128)(2,1)S(1)}, u32[]{:S(2)}, u32[]{:S(2)}) collective-permute-start(bf16[256,128]{1,0:T(8,128)(2,1)S(1)} %collective-permute-done.2.refs_9_), channel_id=1, source_target_pairs={{0,1},{1,0},{2,3},{3,2},{4,5},{5,4},{6,7},{7,6},{8,9},{9,8},{10,11... | collective-permute-start | bytes 196616 | tf_op jit(solution)/shard_map/ppermute | solution.py:411
  39.0 4.7 %collective-permute-start.15 = (bf16[256,128]{1,0:T(8,128)(2,1)S(1)}, bf16[256,128]{1,0:T(8,128)(2,1)S(1)}, u32[]{:S(2)}, u32[]{:S(2)}) collective-permute-start(bf16[256,128]{1,0:T(8,128)(2,1)S(1)} %collective-permute-done.9.refs_11_), channel_id=1, source_target_pairs={{0,1},{1,0},{2,3},{3,2},{4,5},{5,4},{6,7},{7,6},{8,9},{9,8},{10,11... | collective-permute-start | bytes 196616 | tf_op jit(solution)/shard_map/ppermute | solution.py:411
  39.2 6.2 %collective-permute-start.3 = (bf16[176,512]{1,0:T(8,128)(2,1)S(1)}, bf16[176,512]{1,0:T(8,128)(2,1)S(1)}, u32[]{:S(2)}, u32[]{:S(2)}) collective-permute-start(bf16[176,512]{1,0:T(8,128)(2,1)S(1)} %shard_map.131.refs_0_.grad_ref), channel_id=1, source_target_pairs={{0,1},{1,0},{2,3},{3,2},{4,5},{5,4},{6,7},{7,6},{8,9},{9,8},{10,11... | collective-permute-start | bytes 540680 | tf_op jit(solution)/shard_map/ppermute | solution.py:411
  41.9 3.5 %collective-permute-start.11 = (bf16[176,512]{1,0:T(8,128)(2,1)S(1)}, bf16[176,512]{1,0:T(8,128)(2,1)S(1)}, u32[]{:S(2)}, u32[]{:S(2)}) collective-permute-start(bf16[176,512]{1,0:T(8,128)(2,1)S(1)} %collective-permute-done.10.refs_6_), channel_id=1, source_target_pairs={{0,1},{1,0},{2,3},{3,2},{4,5},{5,4},{6,7},{7,6},{8,9},{9,8},{10,11... | collective-permute-start | bytes 540680 | tf_op jit(solution)/shard_map/ppermute | solution.py:411
  43.1 2.3 %collective-permute-start.7 = (bf16[176,512]{1,0:T(8,128)(2,1)S(1)}, bf16[176,512]{1,0:T(8,128)(2,1)S(1)}, u32[]{:S(2)}, u32[]{:S(2)}) collective-permute-start(bf16[176,512]{1,0:T(8,128)(2,1)S(1)} %collective-permute-done.6.refs_4_), channel_id=1, source_target_pairs={{0,1},{1,0},{2,3},{3,2},{4,5},{5,4},{6,7},{7,6},{8,9},{9,8},{10,11... | collective-permute-start | bytes 540680 | tf_op jit(solution)/shard_map/ppermute | solution.py:411
  43.8 1.6 %collective-permute-start.5 = (bf16[176,512]{1,0:T(8,128)(2,1)S(1)}, bf16[176,512]{1,0:T(8,128)(2,1)S(1)}, u32[]{:S(2)}, u32[]{:S(2)}) collective-permute-start(bf16[176,512]{1,0:T(8,128)(2,1)S(1)} %collective-permute-done.4.refs_2_), channel_id=1, source_target_pairs={{0,1},{1,0},{2,3},{3,2},{4,5},{5,4},{6,7},{7,6},{8,9},{9,8},{10,11... | collective-permute-start | bytes 540680 | tf_op jit(solution)/shard_map/ppermute | solution.py:411
  43.8 1.6 %collective-permute-start.14 = (bf16[576,128]{1,0:T(8,128)(2,1)S(1)}, bf16[576,128]{1,0:T(8,128)(2,1)S(1)}, u32[]{:S(2)}, u32[]{:S(2)}) collective-permute-start(bf16[576,128]{1,0:T(8,128)(2,1)S(1)} %collective-permute-done.8.refs_10_), channel_id=1, source_target_pairs={{0,1},{1,0},{2,3},{3,2},{4,5},{5,4},{6,7},{7,6},{8,9},{9,8},{10,11... | collective-permute-start | bytes 442376 | tf_op jit(solution)/shard_map/ppermute | solution.py:411
  47.5 7.0 %collective-permute-start.16 = (bf16[112,512]{1,0:T(8,128)(2,1)S(1)}, bf16[112,512]{1,0:T(8,128)(2,1)S(1)}, u32[]{:S(2)}, u32[]{:S(2)}) collective-permute-start(bf16[112,512]{1,0:T(8,128)(2,1)S(1)} %get-tuple-element.47), channel_id=1, source_target_pairs={{0,8},{1,9},{2,10},{3,11},{4,12},{5,13},{6,14},{7,15},{8,0},{9,1},... | collective-permute-start | bytes 344072 | tf_op jit(solution)/shard_map/ppermute | solution.py:411
  48.6 11.8 %collective-permute-start.17 = (bf16[112,512]{1,0:T(8,128)(2,1)S(1)}, bf16[112,512]{1,0:T(8,128)(2,1)S(1)}, u32[]{:S(2)}, u32[]{:S(2)}) collective-permute-start(bf16[112,512]{1,0:T(8,128)(2,1)S(1)} %get-tuple-element.48), channel_id=1, source_target_pairs={{0,16},{1,17},{2,18},{3,19},{4,20},{5,21},{6,22},{7,23},{8,24},{9,... | collective-permute-start | bytes 344072 | tf_op jit(solution)/shard_map/ppermute | solution.py:411
  50.8 9.6 %collective-permute-start.18 = (bf16[112,512]{1,0:T(8,128)(2,1)S(1)}, bf16[112,512]{1,0:T(8,128)(2,1)S(1)}, u32[]{:S(2)}, u32[]{:S(2)}) collective-permute-start(bf16[112,512]{1,0:T(8,128)(2,1)S(1)} %get-tuple-element.49), channel_id=1, source_target_pairs={{0,24},{1,25},{2,26},{3,27},{4,28},{5,29},{6,30},{7,31},{8,16},{9,... | collective-permute-start | bytes 344072 | tf_op jit(solution)/shard_map/ppermute | solution.py:411

commit v8 on v7

--- a/solution.py
+++ b/solution.py
@@ -266,11 +266,16 @@
             ids = tail[8 : 8 + dp_count, :seq]
             ids = jnp.broadcast_to(ids[:, None, :], (dp_count, frames, seq)).reshape(dp_count * frames, seq)
             picks.append(jnp.where(jnp.logical_and(same, ids == block), 1.0, 0.0))
-            sent.append(tail[8 + dp_count :].astype(BF))
+            rows_of = tail[8 + dp_count :]
+            if first_k:
+                rows_of = jnp.concatenate([rows_of[:, : channels // 2], rows_of[:, channels // 2 :]], axis=0)
+            sent.append(rows_of.astype(BF))
         pick = jnp.concatenate(picks, axis=0).T.astype(BF)
         shards.append(dot(pick, jnp.concatenate(sent, axis=0)))
     packed_ref[...] = dot_nt(weight_ref[...], shards[0].astype(BF)).astype(BF)
-    partial = dot_nt(shards[0].T.astype(BF), mine_ref[...]) + dot_nt(shards[1].T.astype(BF), other)
+    partial = dot_nt(shards[0].T.astype(BF), mine_ref[...])
+    theirs = dot_nt(shards[1].T.astype(BF), other)
+    each = channels // dp_count
     depth = -(-(n1 + n2) // 128) * 128
     lane = lax.broadcasted_iota(jnp.int32, (rows, depth), 1)
     of_first, of_second, factors, sums = [], [], [], 0.0
@@ -296,7 +301,9 @@
                 second[z * owned : (z + 1) * owned],
                 high,
                 sums - high,
-                pack(jnp.where(me_ref[3] == 0, low_rows, high_rows), channels),
+                pack(
+                    jnp.where(me_ref[3] == 0, low_rows, high_rows) + theirs[z * each : (z + 1) * each], channels
+                ),
             ],
             axis=0,
         )
@@ -320,7 +327,7 @@
     )
 
 
-def back_kernel(slots_ref, got_ref, state_ref, weight_ref, out_ref, *, frames):
+def back_kernel(slots_ref, got_ref, state_ref, weight_ref, out_ref, half_ref, *, frames):
     channels = weight_ref.shape[2]
     slope1_ref, slope2_ref, hat1_ref, hat2_ref, aux_ref, gain_ref = state_views(state_ref)
     slots = slots_ref[...]
@@ -346,13 +353,36 @@
     ids = got_ref[...].astype(F32)
     slots32 = slots.astype(F32)
     rows = [high, sums - high, jnp.concatenate([ids] * (channels // ids.shape[1]), axis=1)]
-    rows += [
-        slots32[(2 * d + 1) * frames : (2 * d + 2) * frames] for d in range(slots.shape[0] // (2 * frames))
-    ]
+    sent = jnp.concatenate(
+        [
+            slots32[(2 * d + 1) * frames : (2 * d + 2) * frames]
+            for d in range(slots.shape[0] // (2 * frames))
+        ],
+        axis=0,
+    )
+    dp_count = ids.shape[0]
+    each = channels // dp_count
+    odd_here = lax.rem(lax.axis_index("dp"), 2) == 1
+    half = jnp.concatenate(
+        [
+            jnp.where(
+                odd_here,
+                sent[:, 2 * z * each : (2 * z + 1) * each],
+                sent[:, (2 * z + 1) * each : (2 * z + 2) * each],
+            )
+            for z in range(dp_count // 2)
+        ],
+        axis=1,
+    )
+    middle = half.shape[0] // 2
+    half = jnp.concatenate([half[:middle], half[middle:]], axis=1)
     n1, n2 = first.shape[0], second.shape[0]
     out_ref[:n1, :] = first
     out_ref[n1 : n1 + n2, :] = second
-    out_ref[n1 + n2 :, :] = jnp.concatenate(rows, axis=0).astype(BF)
+    out_ref[n1 + n2 :, :] = jnp.concatenate(rows + [sent], axis=0).astype(BF)
+    half_ref[:n1, :] = first
+    half_ref[n1 : n1 + n2, :] = second
+    half_ref[n1 + n2 :, :] = jnp.concatenate(rows + [half], axis=0).astype(BF)
 
 
 def input_kernel(me_ref, grad_ref, weight_ref, out_ref, *, pairs, frames):
@@ -485,18 +515,18 @@
     slots, *in_sides[:2] = lax.optimization_barrier((slots, *in_sides[:2]))
 
     rows_sent = n1 + n2 + 8 + dp_count * (1 + frames)
-    grads = call(
+    grads, half_grads = call(
         functools.partial(back_kernel, frames=frames),
-        shape(rows_sent, channels),
+        [shape(rows_sent, channels), shape(rows_sent - dp_count * frames // 2, channels)],
         (slots.reshape(-1, channels), got_index, state, conv_weight),
         flops=2 * n2 * 2 * channels * channels,
     )
     by_mask = {0: grads}
     for mask in range(2, near, 2):
-        leaving = grads
+        leaving = grads if mask < mp_count else half_grads
         if mask == near - 2:
             leaving, *in_sides[2 : near // 2] = lax.optimization_barrier(
-                (grads, *in_sides[2 : near // 2])
+                (leaving, *in_sides[2 : near // 2])
             )
         by_mask[mask] = swap(leaving, mask)
     in_sides += [swap(side, 1) for side in in_sides]

time: 62.1 us -> 60.5 us (0.974)
  waiting for transfers between devices: 16.7 us -> 14.7 us
    ppermute x19, waiting for transfers between devices: 16 us -> 14 us  [swap(): lax.ppermute(x, everyone, [(i, i ^ mask) for i in range(dp_count * mp_cou...]
where the time goes in v8:
time: 60.5 us; the launch traced here: 60.1 us
  starting transfers between devices  28.4 us (47%)
  waiting for transfers between devices  14.7 us (24%)
  Pallas kernels  13.4 us (22%)
  local copies, waits for them, and re-layouts  1.93 us (3%)
  other arithmetic  0.95 us (2%)
  between operations  0.74 us (1%)
    ppermute x19, starting transfers between devices, swap(): lax.ppermute(x, everyone, [(i, i ^ mask) for i in range(dp_count * mp_cou...  15.6 us
    ppermute x19, waiting for transfers between devices, swap(): lax.ppermute(x, everyone, [(i, i ^ mask) for i in range(dp_count * mp_cou...  14 us
    pallas_call x7, Pallas kernels, call(): pl.pallas_call(body, out_shape=out, in_specs=specs, out_specs=[pl.BlockSp...  13.4 us
    all_to_all x1, starting transfers between devices, local(): lax.all_to_all(index, 'dp', split_axis=0, concat_axis=0, tiled=True)  6.82 us
    all_to_all x1, starting transfers between devices, local(): slots = lax.all_to_all(sent, 'dp', split_axis=0, concat_axis=0, tiled=True)  5.99 us
    unnamed x14, local copies, waits for them, and re-layouts  1.93 us
  transfers between devices with their start and end apart: 21, of which 9 were waited for; matrix products, arithmetic and copies ran while one was open for 2% of the time, Pallas kernels for 11%

profile of v8, /device:TPU:0, one launch (start us, length us, event | category | flops | bytes accessed | tf_op | source)
XLA Modules:
  0.0 60.1 jit_solution(15273405625270925429)
XLA Ops:
  0.6 2.0 %shard_map.128 = (s32[28]{0:T(128)}, s32[8,128]{1,0:T(8,128)}, bf16[128,512]{1,0:T(8,128)(2,1)}) custom-call(bf16[320,512]{1,0:T(8,128)(2,1)} %bitcast.10, bf16[320,128]{1,0:T(8,128)(2,1)} %bitcast.13, s32[8]{0:T(128)} %lengths_hbm.1, s32[8]{0:T(128)} %dests_hbm.1, s32[8]{0:T(128)} %offsets_hbm.1), custom_call_target="tpu_custom_call" | custom-call | flops 41943040 | bytes 409696 | tf_op jit(solution)/shard_map/pallas_call | solution.py:25
  2.6 0.5 collective-permute-start
  3.1 6.8 %all-to-all-start = ((s32[8,1,128]{2,1,0:T(1,128)}), s32[8,1,128]{2,1,0:T(1,128)S(1)}, u32[]{:S(2)}, u32[]{:S(2)}) async-start(s32[8,1,128]{2,1,0:T(1,128)} %bitcast.19), calls=%async_computation | async-start | bytes 8192 | tf_op jit(solution)/shard_map/all_to_all | solution.py:466
  10.0 1.0 %add_convert_fusion.mine_ref = bf16[128,512]{1,0:T(8,128)(2,1)S(1)} fusion(bf16[128,512]{1,0:T(8,128)(2,1)S(1)} %collective-permute-done, bf16[128,512]{1,0:T(8,128)(2,1)} %get-tuple-element.34), kind=kLoop, calls=%fused_computation | loop fusion | flops 262144 | bytes 393216 | tf_op jit(solution)/shard_map/convert_element_type | solution.py:504
  10.9 1.6 %collective-permute-start.1 = (bf16[128,512]{1,0:T(8,128)(2,1)S(1)}, bf16[128,512]{1,0:T(8,128)(2,1)S(1)}, u32[]{:S(2)}, u32[]{:S(2)}) collective-permute-start(bf16[128,512]{1,0:T(8,128)(2,1)S(1)} %add_convert_fusion.mine_ref), channel_id=1, source_target_pairs={{0,2},{1,3},{2,0},{3,1},{4,6},{5,7},{6,4},{7,5},{8,10},{9,11},{10,... | collective-permute-start | bytes 393224 | tf_op jit(solution)/shard_map/ppermute | solution.py:441
  12.5 4.2 %shard_map.129 = (s32[28]{0:T(128)}, bf16[64,512]{1,0:T(8,128)(2,1)}, f32[232,512]{1,0:T(8,128)}, bf16[256,128]{1,0:T(8,128)(2,1)}, bf16[256,128]{1,0:T(8,128)(2...) custom-call(s32[28]{0:T(128)} %get-tuple-element.31.me_ref, bf16[256,512]{1,0:T(8,128)(2,1)} %bitcast.20, ...), custom_call_target="tpu_custom_call" | custom-call | flops 10000000000 | bytes 2449520 | tf_op jit(solution)/shard_map/pallas_call | solution.py:25
  16.8 0.0 copy-start.1
  16.8 0.0 copy-start.3
  16.8 0.0 all-to-all-done
  16.8 0.0 collective-permute-done.1.other_ref
  16.8 0.0 copy-start.4
  16.8 0.9 %copy-done.4 = bf16[64,512]{1,0:T(8,128)(2,1)S(1)} copy-done((bf16[64,512]{1,0:T(8,128)(2,1)S(1)}, bf16[64,512]{1,0:T(8,128)(2,1)}, u32[]{:S(2)}) %copy-start.4) | copy-done | bytes 65560
  17.7 1.3 %shard_map.130 = bf16[8,16,512]{2,1,0:T(8,128)(2,1)} custom-call(s32[8,128]{1,0:T(8,128)S(1)} %bitcast.16, bf16[128,512]{1,0:T(8,128)(2,1)S(1)} %add_convert_fusion.mine_ref, bf16[128,512]{1,0:T(8,128)(2,1)S(1)} %collective-permute-done.1.other_ref, bf16[64,512]{1,0:T(8,128)(2,1)S(1)} %copy-done.4), custom_call_target="tpu_custom_call" | custom-call | bytes 331776 | tf_op jit(solution)/shard_map/pallas_call | solution.py:25
  19.0 6.0 %all-to-all-start.1 = ((bf16[8,16,512]{2,1,0:T(8,128)(2,1)}), bf16[8,16,512]{2,1,0:T(8,128)(2,1)S(1)}, u32[]{:S(2)}, u32[]{:S(2)}) async-start(bf16[8,16,512]{2,1,0:T(8,128)(2,1)} %shard_map.130), calls=%async_computation.1 | async-start | bytes 262144 | tf_op jit(solution)/shard_map/all_to_all | solution.py:514
  25.0 2.0 %collective-permute-start.8 = (bf16[576,128]{1,0:T(8,128)(2,1)}, bf16[576,128]{1,0:T(8,128)(2,1)S(1)}, u32[]{:S(2)}, u32[]{:S(2)}) collective-permute-start(bf16[576,128]{1,0:T(8,128)(2,1)} %get-tuple-element.42), channel_id=1, source_target_pairs={{0,4},{1,5},{2,6},{3,7},{4,0},{5,1},{6,2},{7,3},{8,12},{9,13},{10,... | collective-permute-start | bytes 442376 | tf_op jit(solution)/shard_map/ppermute | solution.py:441
  27.0 1.0 %collective-permute-start.2 = (bf16[256,128]{1,0:T(8,128)(2,1)}, bf16[256,128]{1,0:T(8,128)(2,1)S(1)}, u32[]{:S(2)}, u32[]{:S(2)}) collective-permute-start(bf16[256,128]{1,0:T(8,128)(2,1)} %get-tuple-element.37), channel_id=1, source_target_pairs={{0,2},{1,3},{2,0},{3,1},{4,6},{5,7},{6,4},{7,5},{8,10},{9,11},{10,... | collective-permute-start | bytes 196616 | tf_op jit(solution)/shard_map/ppermute | solution.py:441
  28.0 0.5 collective-permute-start.9
  28.5 3.3 %collective-permute-done.2.refs_9_ = bf16[256,128]{1,0:T(8,128)(2,1)S(1)} collective-permute-done((bf16[256,128]{1,0:T(8,128)(2,1)}, bf16[256,128]{1,0:T(8,128)(2,1)S(1)}, u32[]{:S(2)}, u32[]{:S(2)}) %collective-permute-start.2) | collective-permute-done | bytes 65568 | tf_op jit(solution)/shard_map/ppermute | solution.py:441
  31.8 0.7 %all-to-all-done.1 = bf16[8,16,512]{2,1,0:T(8,128)(2,1)S(1)} async-done(((bf16[8,16,512]{2,1,0:T(8,128)(2,1)}), bf16[8,16,512]{2,1,0:T(8,128)(2,1)S(1)}, u32[]{:S(2)}, u32[]{:S(2)}) %all-to-all-start.1) | async-done | bytes 131104 | tf_op jit(solution)/shard_map/all_to_all | solution.py:514
  32.4 1.0 %copy-done.2 = f32[232,512]{1,0:T(8,128)S(1)} copy-done((f32[232,512]{1,0:T(8,128)S(1)}, f32[232,512]{1,0:T(8,128)}, u32[]{:S(2)}) %copy-start.2) | copy-done | bytes 475160
  33.5 0.7 %shard_map.131 = (bf16[176,512]{1,0:T(8,128)(2,1)S(1)}, bf16[144,512]{1,0:T(8,128)(2,1)S(1)}) custom-call(bf16[128,512]{1,0:T(8,128)(2,1)S(1)} %bitcast.12, s32[8,128]{1,0:T(8,128)S(1)} %bitcast.17, f32[232,512]{1,0:T(8,128)S(1)} %copy-done.2, bf16[2,1024,512]{2,1,0:T(8,128)(2,1)S(1)} %copy-done), custom_call_target="tpu_custom_call" | custom-call | flops 33554432 | bytes 2707456 | tf_op jit(solution)/shard_map/pallas_call | solution.py:25
  34.2 1.0 %collective-permute-start.4 = (bf16[176,512]{1,0:T(8,128)(2,1)S(1)}, bf16[176,512]{1,0:T(8,128)(2,1)S(1)}, u32[]{:S(2)}, u32[]{:S(2)}) collective-permute-start(bf16[176,512]{1,0:T(8,128)(2,1)S(1)} %get-tuple-element.40.refs_0_.grad_ref), channel_id=1, source_target_pairs={{0,2},{1,3},{2,0},{3,1},{4,6},{5,7},{6,4},{7,5},{8,10},{9,11},{10,... | collective-permute-start | bytes 540680 | tf_op jit(solution)/shard_map/ppermute | solution.py:441
  35.2 0.2 collective-permute-start.6
  35.4 0.0 collective-permute-done.9.refs_11_
  35.4 0.0 collective-permute-done.8.refs_10_
  35.4 2.4 %collective-permute-start.10 = (bf16[144,512]{1,0:T(8,128)(2,1)S(1)}, bf16[144,512]{1,0:T(8,128)(2,1)S(1)}, u32[]{:S(2)}, u32[]{:S(2)}) collective-permute-start(bf16[144,512]{1,0:T(8,128)(2,1)S(1)} %get-tuple-element.44), channel_id=1, source_target_pairs={{0,6},{1,7},{2,4},{3,5},{4,2},{5,3},{6,0},{7,1},{8,14},{9,15},{10,... | collective-permute-start | bytes 442376 | tf_op jit(solution)/shard_map/ppermute | solution.py:441
  37.8 0.5 collective-permute-start.13
  38.3 0.7 %collective-permute-done.12.refs_12_ = bf16[256,128]{1,0:T(8,128)(2,1)S(1)} collective-permute-done((bf16[256,128]{1,0:T(8,128)(2,1)S(1)}, bf16[256,128]{1,0:T(8,128)(2,1)S(1)}, u32[]{:S(2)}, u32[]{:S(2)}) %collective-permute-start.12) | collective-permute-done | bytes 65568 | tf_op jit(solution)/shard_map/ppermute | solution.py:441
  39.0 0.2 collective-permute-start.15
  39.2 0.4 collective-permute-start.3
  39.5 3.4 %collective-permute-done.4.refs_2_ = bf16[176,512]{1,0:T(8,128)(2,1)S(1)} collective-permute-done((bf16[176,512]{1,0:T(8,128)(2,1)S(1)}, bf16[176,512]{1,0:T(8,128)(2,1)S(1)}, u32[]{:S(2)}, u32[]{:S(2)}) %collective-permute-start.4) | collective-permute-done | bytes 180256 | tf_op jit(solution)/shard_map/ppermute | solution.py:441
  42.9 0.0 collective-permute-start.5
  42.9 0.0 collective-permute-done.15.refs_15_
  42.9 0.5 collective-permute-start.14
  43.4 0.0 collective-permute-done.6.refs_4_
  43.4 0.1 collective-permute-start.7
  43.5 0.4 collective-permute-start.11
  44.0 0.6 collective-permute-done.14.refs_14_
  44.5 0.0 collective-permute-done.3.refs_1_
  44.6 0.3 collective-permute-done.7.refs_5_
  44.8 0.2 collective-permute-done.11.refs_7_
  45.0 2.0 %shard_map.132 = (bf16[320,128]{1,0:T(8,128)(2,1)}, f32[112,512]{1,0:T(8,128)S(1)}, bf16[112,512]{1,0:T(8,128)(2,1)S(1)}, bf16[112,512]{1,0:T(8,128)(2,1)S(1)}, bf16[112,512]{1,0:T(8,128)(2,1)S(1)}) custom-call(s32[28]{0:T(128)S(1)} %copy-done.6, bf16[176,512]{1,0:T(8,128)(2,1)S(1)} %get-tuple-element.40.refs_0_.grad_ref, ...), custom_call_target="tpu_custom_call" | custom-call | flops 100663296 | bytes 2408560 | tf_op jit(solution)/shard_map/pallas_call | solution.py:25
  47.0 2.0 %collective-permute-start.17 = (bf16[112,512]{1,0:T(8,128)(2,1)S(1)}, bf16[112,512]{1,0:T(8,128)(2,1)S(1)}, u32[]{:S(2)}, u32[]{:S(2)}) collective-permute-start(bf16[112,512]{1,0:T(8,128)(2,1)S(1)} %get-tuple-element.52), channel_id=1, source_target_pairs={{0,16},{1,17},{2,18},{3,19},{4,20},{5,21},{6,22},{7,23},{8,24},{9,... | collective-permute-start | bytes 344072 | tf_op jit(solution)/shard_map/ppermute | solution.py:441
  49.1 2.4 %collective-permute-start.18 = (bf16[112,512]{1,0:T(8,128)(2,1)S(1)}, bf16[112,512]{1,0:T(8,128)(2,1)S(1)}, u32[]{:S(2)}, u32[]{:S(2)}) collective-permute-start(bf16[112,512]{1,0:T(8,128)(2,1)S(1)} %get-tuple-element.53), channel_id=1, source_target_pairs={{0,24},{1,25},{2,26},{3,27},{4,28},{5,29},{6,30},{7,31},{8,16},{9,... | collective-permute-start | bytes 344072 | tf_op jit(solution)/shard_map/ppermute | solution.py:441
  51.4 1.9 %shard_map.133 = bf16[256,512]{1,0:T(8,128)(2,1)} custom-call(s32[28]{0:T(128)S(1)} %copy-done.6, bf16[176,512]{1,0:T(8,128)(2,1)S(1)} %get-tuple-element.40.refs_0_.grad_ref, bf16[2,1024,512]{2,1,0:T(8,128)(2,1)S(1)} %copy-done), custom_call_target="tpu_custom_call" | custom-call | flops 67108864 | bytes 2277488 | tf_op jit(solution)/shard_map/pallas_call | solution.py:25
  53.3 0.5 collective-permute-done.16.refs_1_
  53.8 5.0 %collective-permute-done.17.refs_2_ = bf16[112,512]{1,0:T(8,128)(2,1)S(1)} collective-permute-done((bf16[112,512]{1,0:T(8,128)(2,1)S(1)}, bf16[112,512]{1,0:T(8,128)(2,1)S(1)}, u32[]{:S(2)}, u32[]{:S(2)}) %collective-permute-start.17) | collective-permute-done | bytes 114720 | tf_op jit(solution)/shard_map/ppermute | solution.py:441
  58.9 1.3 %shard_map.134 = (f32[2,32,512]{2,1,0:T(8,128)}, f32[2,32]{1,0:T(2,128)}, f32[64,320]{1,0:T(8,128)}) custom-call(s32[28]{0:T(128)S(1)} %copy-done.6, f32[112,512]{1,0:T(8,128)S(1)} %get-tuple-element.50.refs_0_, bf16[112,512]{1,0:T(8,128)(2,1)S(1)} %collective-permute-done.16.refs_1_, bf16[112,512]{1,0:T(8,128)(2,1)S(1)} %collective-permute-done.17.refs_2_, ...), custom_call_target="tpu_custom_call" | custom-call | bytes 573552 | tf_op jit(solution)/shard_map/pallas_call | solution.py:25
  (16 shorter events, 0.0 us)
Async XLA Ops:
  2.6 7.3 %collective-permute-start = (bf16[128,512]{1,0:T(8,128)(2,1)}, bf16[128,512]{1,0:T(8,128)(2,1)S(1)}, u32[]{:S(2)}, u32[]{:S(2)}) collective-permute-start(bf16[128,512]{1,0:T(8,128)(2,1)} %get-tuple-element.34), channel_id=1, source_target_pairs={{0,1},{1,0},{2,3},{3,2},{4,5},{5,4},{6,7},{7,6},{8,9},{9,8},{10,11... | collective-permute-start | bytes 393224 | tf_op jit(solution)/shard_map/ppermute | solution.py:441
  3.1 13.6 %all-to-all-start = ((s32[8,1,128]{2,1,0:T(1,128)}), s32[8,1,128]{2,1,0:T(1,128)S(1)}, u32[]{:S(2)}, u32[]{:S(2)}) async-start(s32[8,1,128]{2,1,0:T(1,128)} %bitcast.19), calls=%async_computation | async-start | bytes 8192 | tf_op jit(solution)/shard_map/all_to_all | solution.py:466
  10.9 5.9 %collective-permute-start.1 = (bf16[128,512]{1,0:T(8,128)(2,1)S(1)}, bf16[128,512]{1,0:T(8,128)(2,1)S(1)}, u32[]{:S(2)}, u32[]{:S(2)}) collective-permute-start(bf16[128,512]{1,0:T(8,128)(2,1)S(1)} %add_convert_fusion.mine_ref), channel_id=1, source_target_pairs={{0,2},{1,3},{2,0},{3,1},{4,6},{5,7},{6,4},{7,5},{8,10},{9,11},{10,... | collective-permute-start | bytes 393224 | tf_op jit(solution)/shard_map/ppermute | solution.py:441
  12.5 19.9 %copy-start = (bf16[2,1024,512]{2,1,0:T(8,128)(2,1)S(1)}, bf16[2,1024,512]{2,1,0:T(8,128)(2,1)}, u32[]{:S(2)}) copy-start(bf16[2,1024,512]{2,1,0:T(8,128)(2,1)} %weight_ref.3) | copy-start | bytes 6291460
  16.8 28.3 %copy-start.1 = (bf16[512,320]{0,1:T(8,128)(2,1)S(1)}, bf16[512,320]{0,1:T(8,128)(2,1)}, u32[]{:S(2)}) copy-start(bf16[512,320]{0,1:T(8,128)(2,1)} %param.16) | copy-start | bytes 983044
  16.8 28.3 %copy-start.3 = (bf16[128,320]{0,1:T(8,128)(2,1)S(1)}, bf16[128,320]{0,1:T(8,128)(2,1)}, u32[]{:S(2)}) copy-start(bf16[128,320]{0,1:T(8,128)(2,1)} %param.17) | copy-start | bytes 245764
  16.8 0.9 %copy-start.4 = (bf16[64,512]{1,0:T(8,128)(2,1)S(1)}, bf16[64,512]{1,0:T(8,128)(2,1)}, u32[]{:S(2)}) copy-start(bf16[64,512]{1,0:T(8,128)(2,1)} %get-tuple-element.35.sent_ref) | copy-start | bytes 196612
  17.7 20.1 %copy-start.5 = (bf16[256,128]{1,0:T(8,128)(2,1)S(1)}, bf16[256,128]{1,0:T(8,128)(2,1)}, u32[]{:S(2)}) copy-start(bf16[256,128]{1,0:T(8,128)(2,1)} %get-tuple-element.45.refs_8_) | copy-start | bytes 196612
  17.7 27.3 %copy-start.6 = (s32[28]{0:T(128)S(1)}, s32[28]{0:T(128)}, u32[]{:S(2)}) copy-start(s32[28]{0:T(128)} %get-tuple-element.32.me_ref) | copy-start | bytes 340
  19.0 13.4 %all-to-all-start.1 = ((bf16[8,16,512]{2,1,0:T(8,128)(2,1)}), bf16[8,16,512]{2,1,0:T(8,128)(2,1)S(1)}, u32[]{:S(2)}, u32[]{:S(2)}) async-start(bf16[8,16,512]{2,1,0:T(8,128)(2,1)} %shard_map.130), calls=%async_computation.1 | async-start | bytes 262144 | tf_op jit(solution)/shard_map/all_to_all | solution.py:514
  25.0 10.4 %collective-permute-start.8 = (bf16[576,128]{1,0:T(8,128)(2,1)}, bf16[576,128]{1,0:T(8,128)(2,1)S(1)}, u32[]{:S(2)}, u32[]{:S(2)}) collective-permute-start(bf16[576,128]{1,0:T(8,128)(2,1)} %get-tuple-element.42), channel_id=1, source_target_pairs={{0,4},{1,5},{2,6},{3,7},{4,0},{5,1},{6,2},{7,3},{8,12},{9,13},{10,... | collective-permute-start | bytes 442376 | tf_op jit(solution)/shard_map/ppermute | solution.py:441
  27.0 4.7 %collective-permute-start.2 = (bf16[256,128]{1,0:T(8,128)(2,1)}, bf16[256,128]{1,0:T(8,128)(2,1)S(1)}, u32[]{:S(2)}, u32[]{:S(2)}) collective-permute-start(bf16[256,128]{1,0:T(8,128)(2,1)} %get-tuple-element.37), channel_id=1, source_target_pairs={{0,2},{1,3},{2,0},{3,1},{4,6},{5,7},{6,4},{7,5},{8,10},{9,11},{10,... | collective-permute-start | bytes 196616 | tf_op jit(solution)/shard_map/ppermute | solution.py:441
  28.0 7.4 %collective-permute-start.9 = (bf16[256,128]{1,0:T(8,128)(2,1)}, bf16[256,128]{1,0:T(8,128)(2,1)S(1)}, u32[]{:S(2)}, u32[]{:S(2)}) collective-permute-start(bf16[256,128]{1,0:T(8,128)(2,1)} %get-tuple-element.43), channel_id=1, source_target_pairs={{0,6},{1,7},{2,4},{3,5},{4,2},{5,3},{6,0},{7,1},{8,14},{9,15},{10,... | collective-permute-start | bytes 196616 | tf_op jit(solution)/shard_map/ppermute | solution.py:441
  32.4 1.0 %copy-start.2 = (f32[232,512]{1,0:T(8,128)S(1)}, f32[232,512]{1,0:T(8,128)}, u32[]{:S(2)}) copy-start(f32[232,512]{1,0:T(8,128)} %get-tuple-element.39.state_ref) | copy-start | bytes 1425412
  34.2 8.7 %collective-permute-start.4 = (bf16[176,512]{1,0:T(8,128)(2,1)S(1)}, bf16[176,512]{1,0:T(8,128)(2,1)S(1)}, u32[]{:S(2)}, u32[]{:S(2)}) collective-permute-start(bf16[176,512]{1,0:T(8,128)(2,1)S(1)} %get-tuple-element.40.refs_0_.grad_ref), channel_id=1, source_target_pairs={{0,2},{1,3},{2,0},{3,1},{4,6},{5,7},{6,4},{7,5},{8,10},{9,11},{10,... | collective-permute-start | bytes 540680 | tf_op jit(solution)/shard_map/ppermute | solution.py:441
  35.2 8.3 %collective-permute-start.6 = (bf16[144,512]{1,0:T(8,128)(2,1)S(1)}, bf16[144,512]{1,0:T(8,128)(2,1)S(1)}, u32[]{:S(2)}, u32[]{:S(2)}) collective-permute-start(bf16[144,512]{1,0:T(8,128)(2,1)S(1)} %get-tuple-element.44), channel_id=1, source_target_pairs={{0,4},{1,5},{2,6},{3,7},{4,0},{5,1},{6,2},{7,3},{8,12},{9,13},{10,... | collective-permute-start | bytes 442376 | tf_op jit(solution)/shard_map/ppermute | solution.py:441
  35.4 8.1 %collective-permute-start.10 = (bf16[144,512]{1,0:T(8,128)(2,1)S(1)}, bf16[144,512]{1,0:T(8,128)(2,1)S(1)}, u32[]{:S(2)}, u32[]{:S(2)}) collective-permute-start(bf16[144,512]{1,0:T(8,128)(2,1)S(1)} %get-tuple-element.44), channel_id=1, source_target_pairs={{0,6},{1,7},{2,4},{3,5},{4,2},{5,3},{6,0},{7,1},{8,14},{9,15},{10,... | collective-permute-start | bytes 442376 | tf_op jit(solution)/shard_map/ppermute | solution.py:441
  37.8 1.3 %collective-permute-start.12 = (bf16[256,128]{1,0:T(8,128)(2,1)S(1)}, bf16[256,128]{1,0:T(8,128)(2,1)S(1)}, u32[]{:S(2)}, u32[]{:S(2)}) collective-permute-start(bf16[256,128]{1,0:T(8,128)(2,1)S(1)} %copy-done.5), channel_id=1, source_target_pairs={{0,1},{1,0},{2,3},{3,2},{4,5},{5,4},{6,7},{7,6},{8,9},{9,8},{10,11... | collective-permute-start | bytes 196616 | tf_op jit(solution)/shard_map/ppermute | solution.py:441
  37.8 1.4 %collective-permute-start.13 = (bf16[256,128]{1,0:T(8,128)(2,1)S(1)}, bf16[256,128]{1,0:T(8,128)(2,1)S(1)}, u32[]{:S(2)}, u32[]{:S(2)}) collective-permute-start(bf16[256,128]{1,0:T(8,128)(2,1)S(1)} %collective-permute-done.2.refs_9_), channel_id=1, source_target_pairs={{0,1},{1,0},{2,3},{3,2},{4,5},{5,4},{6,7},{7,6},{8,9},{9,8},{10,11... | collective-permute-start | bytes 196616 | tf_op jit(solution)/shard_map/ppermute | solution.py:441
  39.0 3.9 %collective-permute-start.15 = (bf16[256,128]{1,0:T(8,128)(2,1)S(1)}, bf16[256,128]{1,0:T(8,128)(2,1)S(1)}, u32[]{:S(2)}, u32[]{:S(2)}) collective-permute-start(bf16[256,128]{1,0:T(8,128)(2,1)S(1)} %collective-permute-done.9.refs_11_), channel_id=1, source_target_pairs={{0,1},{1,0},{2,3},{3,2},{4,5},{5,4},{6,7},{7,6},{8,9},{9,8},{10,11... | collective-permute-start | bytes 196616 | tf_op jit(solution)/shard_map/ppermute | solution.py:441
  39.2 5.4 %collective-permute-start.3 = (bf16[176,512]{1,0:T(8,128)(2,1)S(1)}, bf16[176,512]{1,0:T(8,128)(2,1)S(1)}, u32[]{:S(2)}, u32[]{:S(2)}) collective-permute-start(bf16[176,512]{1,0:T(8,128)(2,1)S(1)} %get-tuple-element.40.refs_0_.grad_ref), channel_id=1, source_target_pairs={{0,1},{1,0},{2,3},{3,2},{4,5},{5,4},{6,7},{7,6},{8,9},{9,8},{10,11... | collective-permute-start | bytes 540680 | tf_op jit(solution)/shard_map/ppermute | solution.py:441
  42.9 2.1 %collective-permute-start.5 = (bf16[176,512]{1,0:T(8,128)(2,1)S(1)}, bf16[176,512]{1,0:T(8,128)(2,1)S(1)}, u32[]{:S(2)}, u32[]{:S(2)}) collective-permute-start(bf16[176,512]{1,0:T(8,128)(2,1)S(1)} %collective-permute-done.4.refs_2_), channel_id=1, source_target_pairs={{0,1},{1,0},{2,3},{3,2},{4,5},{5,4},{6,7},{7,6},{8,9},{9,8},{10,11... | collective-permute-start | bytes 540680 | tf_op jit(solution)/shard_map/ppermute | solution.py:441
  42.9 1.6 %collective-permute-start.14 = (bf16[576,128]{1,0:T(8,128)(2,1)S(1)}, bf16[576,128]{1,0:T(8,128)(2,1)S(1)}, u32[]{:S(2)}, u32[]{:S(2)}) collective-permute-start(bf16[576,128]{1,0:T(8,128)(2,1)S(1)} %collective-permute-done.8.refs_10_), channel_id=1, source_target_pairs={{0,1},{1,0},{2,3},{3,2},{4,5},{5,4},{6,7},{7,6},{8,9},{9,8},{10,11... | collective-permute-start | bytes 442376 | tf_op jit(solution)/shard_map/ppermute | solution.py:441
  43.4 1.4 %collective-permute-start.7 = (bf16[144,512]{1,0:T(8,128)(2,1)S(1)}, bf16[144,512]{1,0:T(8,128)(2,1)S(1)}, u32[]{:S(2)}, u32[]{:S(2)}) collective-permute-start(bf16[144,512]{1,0:T(8,128)(2,1)S(1)} %collective-permute-done.6.refs_4_), channel_id=1, source_target_pairs={{0,1},{1,0},{2,3},{3,2},{4,5},{5,4},{6,7},{7,6},{8,9},{9,8},{10,11... | collective-permute-start | bytes 442376 | tf_op jit(solution)/shard_map/ppermute | solution.py:441
  43.5 1.5 %collective-permute-start.11 = (bf16[144,512]{1,0:T(8,128)(2,1)S(1)}, bf16[144,512]{1,0:T(8,128)(2,1)S(1)}, u32[]{:S(2)}, u32[]{:S(2)}) collective-permute-start(bf16[144,512]{1,0:T(8,128)(2,1)S(1)} %collective-permute-done.10.refs_6_), channel_id=1, source_target_pairs={{0,1},{1,0},{2,3},{3,2},{4,5},{5,4},{6,7},{7,6},{8,9},{9,8},{10,11... | collective-permute-start | bytes 442376 | tf_op jit(solution)/shard_map/ppermute | solution.py:441
  47.0 6.8 %collective-permute-start.16 = (bf16[112,512]{1,0:T(8,128)(2,1)S(1)}, bf16[112,512]{1,0:T(8,128)(2,1)S(1)}, u32[]{:S(2)}, u32[]{:S(2)}) collective-permute-start(bf16[112,512]{1,0:T(8,128)(2,1)S(1)} %get-tuple-element.51), channel_id=1, source_target_pairs={{0,8},{1,9},{2,10},{3,11},{4,12},{5,13},{6,14},{7,15},{8,0},{9,1},... | collective-permute-start | bytes 344072 | tf_op jit(solution)/shard_map/ppermute | solution.py:441
  47.0 11.8 %collective-permute-start.17 = (bf16[112,512]{1,0:T(8,128)(2,1)S(1)}, bf16[112,512]{1,0:T(8,128)(2,1)S(1)}, u32[]{:S(2)}, u32[]{:S(2)}) collective-permute-start(bf16[112,512]{1,0:T(8,128)(2,1)S(1)} %get-tuple-element.52), channel_id=1, source_target_pairs={{0,16},{1,17},{2,18},{3,19},{4,20},{5,21},{6,22},{7,23},{8,24},{9,... | collective-permute-start | bytes 344072 | tf_op jit(solution)/shard_map/ppermute | solution.py:441
  49.1 9.8 %collective-permute-start.18 = (bf16[112,512]{1,0:T(8,128)(2,1)S(1)}, bf16[112,512]{1,0:T(8,128)(2,1)S(1)}, u32[]{:S(2)}, u32[]{:S(2)}) collective-permute-start(bf16[112,512]{1,0:T(8,128)(2,1)S(1)} %get-tuple-element.53), channel_id=1, source_target_pairs={{0,24},{1,25},{2,26},{3,27},{4,28},{5,29},{6,30},{7,31},{8,16},{9,... | collective-permute-start | bytes 344072 | tf_op jit(solution)/shard_map/ppermute | solution.py:441

commit v9 on v8

--- a/solution.py
+++ b/solution.py
@@ -512,7 +512,6 @@
         scratch=[pltpu.VMEM((seq, channels), F32)],
     )
     slots = lax.all_to_all(sent, "dp", split_axis=0, concat_axis=0, tiled=True)
-    slots, *in_sides[:2] = lax.optimization_barrier((slots, *in_sides[:2]))
 
     rows_sent = n1 + n2 + 8 + dp_count * (1 + frames)
     grads, half_grads = call(
@@ -524,9 +523,9 @@
     by_mask = {0: grads}
     for mask in range(2, near, 2):
         leaving = grads if mask < mp_count else half_grads
-        if mask == near - 2:
-            leaving, *in_sides[2 : near // 2] = lax.optimization_barrier(
-                (leaving, *in_sides[2 : near // 2])
+        if mask == 4:
+            leaving, *in_sides[1 : near // 2] = lax.optimization_barrier(
+                (leaving, *in_sides[1 : near // 2])
             )
         by_mask[mask] = swap(leaving, mask)
     in_sides += [swap(side, 1) for side in in_sides]

time: 60.5 us -> 59.7 us (0.987)
  waiting for transfers between devices: 14.7 us -> 13.8 us
    ppermute x19, waiting for transfers between devices: 14 us -> 9.91 us  [swap(): lax.ppermute(x, everyone, [(i, i ^ mask) for i in range(dp_count * mp_cou...]
    all_to_all x1, waiting for transfers between devices: 0.68 us -> 3.93 us  [local(): slots = lax.all_to_all(sent, 'dp', split_axis=0, concat_axis=0, tiled=True)]
  transfers between devices with their start and end apart: 21 -> 21, of which waited for: 9 -> 8; matrix products, arithmetic and copies ran while one was open for 2% -> 2% of each run, Pallas kernels for 11% -> 12%
where the time goes in v9:
time: 59.7 us; the launch traced here: 59.3 us
  starting transfers between devices  28.5 us (48%)
  waiting for transfers between devices  13.8 us (23%)
  Pallas kernels  13.4 us (22%)
  local copies, waits for them, and re-layouts  1.93 us (3%)
  other arithmetic  0.95 us (2%)
  between operations  0.74 us (1%)
    ppermute x19, starting transfers between devices, swap(): lax.ppermute(x, everyone, [(i, i ^ mask) for i in range(dp_count * mp_cou...  15.7 us
    pallas_call x7, Pallas kernels, call(): pl.pallas_call(body, out_shape=out, in_specs=specs, out_specs=[pl.BlockSp...  13.4 us
    ppermute x19, waiting for transfers between devices, swap(): lax.ppermute(x, everyone, [(i, i ^ mask) for i in range(dp_count * mp_cou...  9.91 us
    all_to_all x1, starting transfers between devices, local(): lax.all_to_all(index, 'dp', split_axis=0, concat_axis=0, tiled=True)  6.82 us
    all_to_all x1, starting transfers between devices, local(): slots = lax.all_to_all(sent, 'dp', split_axis=0, concat_axis=0, tiled=True)  5.99 us
    all_to_all x1, waiting for transfers between devices, local(): slots = lax.all_to_all(sent, 'dp', split_axis=0, concat_axis=0, tiled=True)  3.93 us
    unnamed x14, local copies, waits for them, and re-layouts  1.93 us
  transfers between devices with their start and end apart: 21, of which 8 were waited for; matrix products, arithmetic and copies ran while one was open for 2% of the time, Pallas kernels for 12%

profile of v9, /device:TPU:0, one launch (start us, length us, event | category | flops | bytes accessed | tf_op | source)
XLA Modules:
  0.0 59.3 jit_solution(6668422249642183693)
XLA Ops:
  0.6 2.0 %shard_map.128 = (s32[28]{0:T(128)}, s32[8,128]{1,0:T(8,128)}, bf16[128,512]{1,0:T(8,128)(2,1)}) custom-call(bf16[320,512]{1,0:T(8,128)(2,1)} %bitcast.10, bf16[320,128]{1,0:T(8,128)(2,1)} %bitcast.13, s32[8]{0:T(128)} %lengths_hbm.1, s32[8]{0:T(128)} %dests_hbm.1, s32[8]{0:T(128)} %offsets_hbm.1), custom_call_target="tpu_custom_call" | custom-call | flops 41943040 | bytes 409696 | tf_op jit(solution)/shard_map/pallas_call | solution.py:25
  2.6 0.5 collective-permute-start
  3.1 6.8 %all-to-all-start = ((s32[8,1,128]{2,1,0:T(1,128)}), s32[8,1,128]{2,1,0:T(1,128)S(1)}, u32[]{:S(2)}, u32[]{:S(2)}) async-start(s32[8,1,128]{2,1,0:T(1,128)} %bitcast.19), calls=%async_computation | async-start | bytes 8192 | tf_op jit(solution)/shard_map/all_to_all | solution.py:466
  10.0 1.0 %add_convert_fusion.mine_ref = bf16[128,512]{1,0:T(8,128)(2,1)S(1)} fusion(bf16[128,512]{1,0:T(8,128)(2,1)S(1)} %collective-permute-done, bf16[128,512]{1,0:T(8,128)(2,1)} %get-tuple-element.32), kind=kLoop, calls=%fused_computation | loop fusion | flops 262144 | bytes 393216 | tf_op jit(solution)/shard_map/convert_element_type | solution.py:504
  10.9 1.6 %collective-permute-start.1 = (bf16[128,512]{1,0:T(8,128)(2,1)S(1)}, bf16[128,512]{1,0:T(8,128)(2,1)S(1)}, u32[]{:S(2)}, u32[]{:S(2)}) collective-permute-start(bf16[128,512]{1,0:T(8,128)(2,1)S(1)} %add_convert_fusion.mine_ref), channel_id=1, source_target_pairs={{0,2},{1,3},{2,0},{3,1},{4,6},{5,7},{6,4},{7,5},{8,10},{9,11},{10,... | collective-permute-start | bytes 393224 | tf_op jit(solution)/shard_map/ppermute | solution.py:441
  12.5 4.2 %shard_map.129 = (s32[28]{0:T(128)}, bf16[64,512]{1,0:T(8,128)(2,1)}, f32[232,512]{1,0:T(8,128)}, bf16[256,128]{1,0:T(8,128)(2,1)}, bf16[256,128]{1,0:T(8,128)(2...) custom-call(s32[28]{0:T(128)} %get-tuple-element.29.me_ref, bf16[256,512]{1,0:T(8,128)(2,1)} %bitcast.20, ...), custom_call_target="tpu_custom_call" | custom-call | flops 10000000000 | bytes 2449520 | tf_op jit(solution)/shard_map/pallas_call | solution.py:25
  16.8 0.0 copy-start.1
  16.8 0.0 copy-start.3
  16.8 0.0 all-to-all-done
  16.8 0.0 copy-start.4
  16.8 0.9 %copy-done.4 = bf16[64,512]{1,0:T(8,128)(2,1)S(1)} copy-done((bf16[64,512]{1,0:T(8,128)(2,1)S(1)}, bf16[64,512]{1,0:T(8,128)(2,1)}, u32[]{:S(2)}) %copy-start.4) | copy-done | bytes 65560
  17.7 1.3 %shard_map.130 = bf16[8,16,512]{2,1,0:T(8,128)(2,1)} custom-call(s32[8,128]{1,0:T(8,128)S(1)} %bitcast.16, bf16[128,512]{1,0:T(8,128)(2,1)S(1)} %add_convert_fusion.mine_ref, bf16[128,512]{1,0:T(8,128)(2,1)S(1)} %collective-permute-done.1.other_ref, bf16[64,512]{1,0:T(8,128)(2,1)S(1)} %copy-done.4), custom_call_target="tpu_custom_call" | custom-call | bytes 331776 | tf_op jit(solution)/shard_map/pallas_call | solution.py:25
  19.0 6.0 %all-to-all-start.1 = ((bf16[8,16,512]{2,1,0:T(8,128)(2,1)}), bf16[8,16,512]{2,1,0:T(8,128)(2,1)S(1)}, u32[]{:S(2)}, u32[]{:S(2)}) async-start(bf16[8,16,512]{2,1,0:T(8,128)(2,1)} %shard_map.130), calls=%async_computation.1 | async-start | bytes 262144 | tf_op jit(solution)/shard_map/all_to_all | solution.py:514
  25.0 2.0 %collective-permute-start.6 = (bf16[576,128]{1,0:T(8,128)(2,1)}, bf16[576,128]{1,0:T(8,128)(2,1)S(1)}, u32[]{:S(2)}, u32[]{:S(2)}) collective-permute-start(bf16[576,128]{1,0:T(8,128)(2,1)} %get-tuple-element.38), channel_id=1, source_target_pairs={{0,4},{1,5},{2,6},{3,7},{4,0},{5,1},{6,2},{7,3},{8,12},{9,13},{10,... | collective-permute-start | bytes 442376 | tf_op jit(solution)/shard_map/ppermute | solution.py:441
  27.0 1.0 %collective-permute-start.5 = (bf16[256,128]{1,0:T(8,128)(2,1)}, bf16[256,128]{1,0:T(8,128)(2,1)S(1)}, u32[]{:S(2)}, u32[]{:S(2)}) collective-permute-start(bf16[256,128]{1,0:T(8,128)(2,1)} %get-tuple-element.37), channel_id=1, source_target_pairs={{0,2},{1,3},{2,0},{3,1},{4,6},{5,7},{6,4},{7,5},{8,10},{9,11},{10,... | collective-permute-start | bytes 196616 | tf_op jit(solution)/shard_map/ppermute | solution.py:441
  28.0 0.5 collective-permute-start.7
  28.5 3.9 %all-to-all-done.1 = bf16[8,16,512]{2,1,0:T(8,128)(2,1)S(1)} async-done(((bf16[8,16,512]{2,1,0:T(8,128)(2,1)}), bf16[8,16,512]{2,1,0:T(8,128)(2,1)S(1)}, u32[]{:S(2)}, u32[]{:S(2)}) %all-to-all-start.1) | async-done | bytes 131104 | tf_op jit(solution)/shard_map/all_to_all | solution.py:514
  32.4 1.0 %copy-done.2 = f32[232,512]{1,0:T(8,128)S(1)} copy-done((f32[232,512]{1,0:T(8,128)S(1)}, f32[232,512]{1,0:T(8,128)}, u32[]{:S(2)}) %copy-start.2) | copy-done | bytes 475160
  33.5 0.7 %shard_map.131 = (bf16[176,512]{1,0:T(8,128)(2,1)S(1)}, bf16[144,512]{1,0:T(8,128)(2,1)S(1)}) custom-call(bf16[128,512]{1,0:T(8,128)(2,1)S(1)} %bitcast.12, s32[8,128]{1,0:T(8,128)S(1)} %bitcast.17, f32[232,512]{1,0:T(8,128)S(1)} %copy-done.2, bf16[2,1024,512]{2,1,0:T(8,128)(2,1)S(1)} %copy-done), custom_call_target="tpu_custom_call" | custom-call | flops 33554432 | bytes 2707456 | tf_op jit(solution)/shard_map/pallas_call | solution.py:25
  34.2 1.0 %collective-permute-start.3 = (bf16[176,512]{1,0:T(8,128)(2,1)S(1)}, bf16[176,512]{1,0:T(8,128)(2,1)S(1)}, u32[]{:S(2)}, u32[]{:S(2)}) collective-permute-start(bf16[176,512]{1,0:T(8,128)(2,1)S(1)} %get-tuple-element.35.refs_0_.grad_ref), channel_id=1, source_target_pairs={{0,2},{1,3},{2,0},{3,1},{4,6},{5,7},{6,4},{7,5},{8,10},{9,11},{10,... | collective-permute-start | bytes 540680 | tf_op jit(solution)/shard_map/ppermute | solution.py:441
  35.2 0.7 %collective-permute-start.10 = (bf16[144,512]{1,0:T(8,128)(2,1)S(1)}, bf16[144,512]{1,0:T(8,128)(2,1)S(1)}, u32[]{:S(2)}, u32[]{:S(2)}) collective-permute-start(bf16[144,512]{1,0:T(8,128)(2,1)S(1)} %get-tuple-element.40), channel_id=1, source_target_pairs={{0,6},{1,7},{2,4},{3,5},{4,2},{5,3},{6,0},{7,1},{8,14},{9,15},{10,... | collective-permute-start | bytes 442376 | tf_op jit(solution)/shard_map/ppermute | solution.py:441
  35.9 2.0 %collective-permute-start.8 = (bf16[144,512]{1,0:T(8,128)(2,1)S(1)}, bf16[144,512]{1,0:T(8,128)(2,1)S(1)}, u32[]{:S(2)}, u32[]{:S(2)}) collective-permute-start(bf16[144,512]{1,0:T(8,128)(2,1)S(1)} %get-tuple-element.40), channel_id=1, source_target_pairs={{0,4},{1,5},{2,6},{3,7},{4,0},{5,1},{6,2},{7,3},{8,12},{9,13},{10,... | collective-permute-start | bytes 442376 | tf_op jit(solution)/shard_map/ppermute | solution.py:441
  37.8 0.5 collective-permute-start.13
  38.3 0.7 %collective-permute-done.12.refs_12_ = bf16[256,128]{1,0:T(8,128)(2,1)S(1)} collective-permute-done((bf16[256,128]{1,0:T(8,128)(2,1)S(1)}, bf16[256,128]{1,0:T(8,128)(2,1)S(1)}, u32[]{:S(2)}, u32[]{:S(2)}) %collective-permute-start.12) | collective-permute-done | bytes 65568 | tf_op jit(solution)/shard_map/ppermute | solution.py:441
  39.1 0.2 collective-permute-start.15
  39.3 0.4 collective-permute-start.2
  39.6 2.5 %collective-permute-done.3.refs_2_ = bf16[176,512]{1,0:T(8,128)(2,1)S(1)} collective-permute-done((bf16[176,512]{1,0:T(8,128)(2,1)S(1)}, bf16[176,512]{1,0:T(8,128)(2,1)S(1)}, u32[]{:S(2)}, u32[]{:S(2)}) %collective-permute-start.3) | collective-permute-done | bytes 180256 | tf_op jit(solution)/shard_map/ppermute | solution.py:441
  42.1 0.0 collective-permute-start.4
  42.1 0.0 collective-permute-done.15.refs_15_
  42.1 0.5 collective-permute-start.14
  42.6 0.0 collective-permute-done.10.refs_6_
  42.6 0.1 collective-permute-start.11
  42.7 0.0 collective-permute-done.8.refs_4_
  42.7 0.4 collective-permute-start.9
  43.1 0.6 %collective-permute-done.14.refs_14_ = bf16[576,128]{1,0:T(8,128)(2,1)S(1)} collective-permute-done((bf16[576,128]{1,0:T(8,128)(2,1)S(1)}, bf16[576,128]{1,0:T(8,128)(2,1)S(1)}, u32[]{:S(2)}, u32[]{:S(2)}) %collective-permute-start.14) | collective-permute-done | bytes 147488 | tf_op jit(solution)/shard_map/ppermute | solution.py:441
  43.7 0.0 collective-permute-done.2.refs_1_
  43.7 0.3 collective-permute-done.11.refs_7_
  44.0 0.2 collective-permute-done.9.refs_5_
  44.2 0.0 collective-permute-done.4.refs_3_
  44.2 2.0 %shard_map.132 = (bf16[320,128]{1,0:T(8,128)(2,1)}, f32[112,512]{1,0:T(8,128)S(1)}, bf16[112,512]{1,0:T(8,128)(2,1)S(1)}, bf16[112,512]{1,0:T(8,128)(2,1)S(1)}, bf16[112,512]{1,0:T(8,128)(2,1)S(1)}) custom-call(s32[28]{0:T(128)S(1)} %copy-done.6, bf16[176,512]{1,0:T(8,128)(2,1)S(1)} %get-tuple-element.35.refs_0_.grad_ref, ...), custom_call_target="tpu_custom_call" | custom-call | flops 100663296 | bytes 2408560 | tf_op jit(solution)/shard_map/pallas_call | solution.py:25
  46.2 0.0 collective-permute-start.16
  46.2 1.8 %collective-permute-start.17 = (bf16[112,512]{1,0:T(8,128)(2,1)S(1)}, bf16[112,512]{1,0:T(8,128)(2,1)S(1)}, u32[]{:S(2)}, u32[]{:S(2)}) collective-permute-start(bf16[112,512]{1,0:T(8,128)(2,1)S(1)} %get-tuple-element.48), channel_id=1, source_target_pairs={{0,16},{1,17},{2,18},{3,19},{4,20},{5,21},{6,22},{7,23},{8,24},{9,... | collective-permute-start | bytes 344072 | tf_op jit(solution)/shard_map/ppermute | solution.py:441
  48.0 2.6 %collective-permute-start.18 = (bf16[112,512]{1,0:T(8,128)(2,1)S(1)}, bf16[112,512]{1,0:T(8,128)(2,1)S(1)}, u32[]{:S(2)}, u32[]{:S(2)}) collective-permute-start(bf16[112,512]{1,0:T(8,128)(2,1)S(1)} %get-tuple-element.49), channel_id=1, source_target_pairs={{0,24},{1,25},{2,26},{3,27},{4,28},{5,29},{6,30},{7,31},{8,16},{9,... | collective-permute-start | bytes 344072 | tf_op jit(solution)/shard_map/ppermute | solution.py:441
  50.6 1.9 %shard_map.133 = bf16[256,512]{1,0:T(8,128)(2,1)} custom-call(s32[28]{0:T(128)S(1)} %copy-done.6, bf16[176,512]{1,0:T(8,128)(2,1)S(1)} %get-tuple-element.35.refs_0_.grad_ref, bf16[2,1024,512]{2,1,0:T(8,128)(2,1)S(1)} %copy-done), custom_call_target="tpu_custom_call" | custom-call | flops 67108864 | bytes 2277488 | tf_op jit(solution)/shard_map/pallas_call | solution.py:25
  52.5 0.8 %collective-permute-done.16.refs_1_ = bf16[112,512]{1,0:T(8,128)(2,1)S(1)} collective-permute-done((bf16[112,512]{1,0:T(8,128)(2,1)S(1)}, bf16[112,512]{1,0:T(8,128)(2,1)S(1)}, u32[]{:S(2)}, u32[]{:S(2)}) %collective-permute-start.16) | collective-permute-done | bytes 114720 | tf_op jit(solution)/shard_map/ppermute | solution.py:441
  53.3 4.8 %collective-permute-done.17.refs_2_ = bf16[112,512]{1,0:T(8,128)(2,1)S(1)} collective-permute-done((bf16[112,512]{1,0:T(8,128)(2,1)S(1)}, bf16[112,512]{1,0:T(8,128)(2,1)S(1)}, u32[]{:S(2)}, u32[]{:S(2)}) %collective-permute-start.17) | collective-permute-done | bytes 114720 | tf_op jit(solution)/shard_map/ppermute | solution.py:441
  58.1 0.0 collective-permute-done.18.refs_3_
  58.1 1.3 %shard_map.134 = (f32[2,32,512]{2,1,0:T(8,128)}, f32[2,32]{1,0:T(2,128)}, f32[64,320]{1,0:T(8,128)}) custom-call(s32[28]{0:T(128)S(1)} %copy-done.6, f32[112,512]{1,0:T(8,128)S(1)} %get-tuple-element.46.refs_0_, bf16[112,512]{1,0:T(8,128)(2,1)S(1)} %collective-permute-done.16.refs_1_, bf16[112,512]{1,0:T(8,128)(2,1)S(1)} %collective-permute-done.17.refs_2_, ...), custom_call_target="tpu_custom_call" | custom-call | bytes 573552 | tf_op jit(solution)/shard_map/pallas_call | solution.py:25
  (16 shorter events, 0.0 us)
Async XLA Ops:
  2.6 7.3 %collective-permute-start = (bf16[128,512]{1,0:T(8,128)(2,1)}, bf16[128,512]{1,0:T(8,128)(2,1)S(1)}, u32[]{:S(2)}, u32[]{:S(2)}) collective-permute-start(bf16[128,512]{1,0:T(8,128)(2,1)} %get-tuple-element.32), channel_id=1, source_target_pairs={{0,1},{1,0},{2,3},{3,2},{4,5},{5,4},{6,7},{7,6},{8,9},{9,8},{10,11... | collective-permute-start | bytes 393224 | tf_op jit(solution)/shard_map/ppermute | solution.py:441
  3.1 13.6 %all-to-all-start = ((s32[8,1,128]{2,1,0:T(1,128)}), s32[8,1,128]{2,1,0:T(1,128)S(1)}, u32[]{:S(2)}, u32[]{:S(2)}) async-start(s32[8,1,128]{2,1,0:T(1,128)} %bitcast.19), calls=%async_computation | async-start | bytes 8192 | tf_op jit(solution)/shard_map/all_to_all | solution.py:466
  10.9 5.9 %collective-permute-start.1 = (bf16[128,512]{1,0:T(8,128)(2,1)S(1)}, bf16[128,512]{1,0:T(8,128)(2,1)S(1)}, u32[]{:S(2)}, u32[]{:S(2)}) collective-permute-start(bf16[128,512]{1,0:T(8,128)(2,1)S(1)} %add_convert_fusion.mine_ref), channel_id=1, source_target_pairs={{0,2},{1,3},{2,0},{3,1},{4,6},{5,7},{6,4},{7,5},{8,10},{9,11},{10,... | collective-permute-start | bytes 393224 | tf_op jit(solution)/shard_map/ppermute | solution.py:441
  12.5 19.9 %copy-start = (bf16[2,1024,512]{2,1,0:T(8,128)(2,1)S(1)}, bf16[2,1024,512]{2,1,0:T(8,128)(2,1)}, u32[]{:S(2)}) copy-start(bf16[2,1024,512]{2,1,0:T(8,128)(2,1)} %weight_ref.3) | copy-start | bytes 6291460
  16.8 27.5 %copy-start.1 = (bf16[512,320]{0,1:T(8,128)(2,1)S(1)}, bf16[512,320]{0,1:T(8,128)(2,1)}, u32[]{:S(2)}) copy-start(bf16[512,320]{0,1:T(8,128)(2,1)} %param.16) | copy-start | bytes 983044
  16.8 27.5 %copy-start.3 = (bf16[128,320]{0,1:T(8,128)(2,1)S(1)}, bf16[128,320]{0,1:T(8,128)(2,1)}, u32[]{:S(2)}) copy-start(bf16[128,320]{0,1:T(8,128)(2,1)} %param.17) | copy-start | bytes 245764
  16.8 0.9 %copy-start.4 = (bf16[64,512]{1,0:T(8,128)(2,1)S(1)}, bf16[64,512]{1,0:T(8,128)(2,1)}, u32[]{:S(2)}) copy-start(bf16[64,512]{1,0:T(8,128)(2,1)} %get-tuple-element.33.sent_ref) | copy-start | bytes 196612
  17.7 20.1 %copy-start.5 = (bf16[256,128]{1,0:T(8,128)(2,1)S(1)}, bf16[256,128]{1,0:T(8,128)(2,1)}, u32[]{:S(2)}) copy-start(bf16[256,128]{1,0:T(8,128)(2,1)} %get-tuple-element.41.refs_8_) | copy-start | bytes 196612
  17.7 26.5 %copy-start.6 = (s32[28]{0:T(128)S(1)}, s32[28]{0:T(128)}, u32[]{:S(2)}) copy-start(s32[28]{0:T(128)} %get-tuple-element.30.me_ref) | copy-start | bytes 340
  19.0 13.4 %all-to-all-start.1 = ((bf16[8,16,512]{2,1,0:T(8,128)(2,1)}), bf16[8,16,512]{2,1,0:T(8,128)(2,1)S(1)}, u32[]{:S(2)}, u32[]{:S(2)}) async-start(bf16[8,16,512]{2,1,0:T(8,128)(2,1)} %shard_map.130), calls=%async_computation.1 | async-start | bytes 262144 | tf_op jit(solution)/shard_map/all_to_all | solution.py:514
  25.0 10.9 %collective-permute-start.6 = (bf16[576,128]{1,0:T(8,128)(2,1)}, bf16[576,128]{1,0:T(8,128)(2,1)S(1)}, u32[]{:S(2)}, u32[]{:S(2)}) collective-permute-start(bf16[576,128]{1,0:T(8,128)(2,1)} %get-tuple-element.38), channel_id=1, source_target_pairs={{0,4},{1,5},{2,6},{3,7},{4,0},{5,1},{6,2},{7,3},{8,12},{9,13},{10,... | collective-permute-start | bytes 442376 | tf_op jit(solution)/shard_map/ppermute | solution.py:441
  27.0 8.8 %collective-permute-start.5 = (bf16[256,128]{1,0:T(8,128)(2,1)}, bf16[256,128]{1,0:T(8,128)(2,1)S(1)}, u32[]{:S(2)}, u32[]{:S(2)}) collective-permute-start(bf16[256,128]{1,0:T(8,128)(2,1)} %get-tuple-element.37), channel_id=1, source_target_pairs={{0,2},{1,3},{2,0},{3,1},{4,6},{5,7},{6,4},{7,5},{8,10},{9,11},{10,... | collective-permute-start | bytes 196616 | tf_op jit(solution)/shard_map/ppermute | solution.py:441
  28.0 7.8 %collective-permute-start.7 = (bf16[256,128]{1,0:T(8,128)(2,1)}, bf16[256,128]{1,0:T(8,128)(2,1)S(1)}, u32[]{:S(2)}, u32[]{:S(2)}) collective-permute-start(bf16[256,128]{1,0:T(8,128)(2,1)} %get-tuple-element.39), channel_id=1, source_target_pairs={{0,6},{1,7},{2,4},{3,5},{4,2},{5,3},{6,0},{7,1},{8,14},{9,15},{10,... | collective-permute-start | bytes 196616 | tf_op jit(solution)/shard_map/ppermute | solution.py:441
  32.4 1.0 %copy-start.2 = (f32[232,512]{1,0:T(8,128)S(1)}, f32[232,512]{1,0:T(8,128)}, u32[]{:S(2)}) copy-start(f32[232,512]{1,0:T(8,128)} %get-tuple-element.34.state_ref) | copy-start | bytes 1425412
  34.2 7.9 %collective-permute-start.3 = (bf16[176,512]{1,0:T(8,128)(2,1)S(1)}, bf16[176,512]{1,0:T(8,128)(2,1)S(1)}, u32[]{:S(2)}, u32[]{:S(2)}) collective-permute-start(bf16[176,512]{1,0:T(8,128)(2,1)S(1)} %get-tuple-element.35.refs_0_.grad_ref), channel_id=1, source_target_pairs={{0,2},{1,3},{2,0},{3,1},{4,6},{5,7},{6,4},{7,5},{8,10},{9,11},{10,... | collective-permute-start | bytes 540680 | tf_op jit(solution)/shard_map/ppermute | solution.py:441
  35.2 7.5 %collective-permute-start.10 = (bf16[144,512]{1,0:T(8,128)(2,1)S(1)}, bf16[144,512]{1,0:T(8,128)(2,1)S(1)}, u32[]{:S(2)}, u32[]{:S(2)}) collective-permute-start(bf16[144,512]{1,0:T(8,128)(2,1)S(1)} %get-tuple-element.40), channel_id=1, source_target_pairs={{0,6},{1,7},{2,4},{3,5},{4,2},{5,3},{6,0},{7,1},{8,14},{9,15},{10,... | collective-permute-start | bytes 442376 | tf_op jit(solution)/shard_map/ppermute | solution.py:441
  35.9 6.9 %collective-permute-start.8 = (bf16[144,512]{1,0:T(8,128)(2,1)S(1)}, bf16[144,512]{1,0:T(8,128)(2,1)S(1)}, u32[]{:S(2)}, u32[]{:S(2)}) collective-permute-start(bf16[144,512]{1,0:T(8,128)(2,1)S(1)} %get-tuple-element.40), channel_id=1, source_target_pairs={{0,4},{1,5},{2,6},{3,7},{4,0},{5,1},{6,2},{7,3},{8,12},{9,13},{10,... | collective-permute-start | bytes 442376 | tf_op jit(solution)/shard_map/ppermute | solution.py:441
  37.8 1.3 %collective-permute-start.12 = (bf16[256,128]{1,0:T(8,128)(2,1)S(1)}, bf16[256,128]{1,0:T(8,128)(2,1)S(1)}, u32[]{:S(2)}, u32[]{:S(2)}) collective-permute-start(bf16[256,128]{1,0:T(8,128)(2,1)S(1)} %copy-done.5), channel_id=1, source_target_pairs={{0,1},{1,0},{2,3},{3,2},{4,5},{5,4},{6,7},{7,6},{8,9},{9,8},{10,11... | collective-permute-start | bytes 196616 | tf_op jit(solution)/shard_map/ppermute | solution.py:441
  37.8 1.4 %collective-permute-start.13 = (bf16[256,128]{1,0:T(8,128)(2,1)S(1)}, bf16[256,128]{1,0:T(8,128)(2,1)S(1)}, u32[]{:S(2)}, u32[]{:S(2)}) collective-permute-start(bf16[256,128]{1,0:T(8,128)(2,1)S(1)} %collective-permute-done.5.refs_9_), channel_id=1, source_target_pairs={{0,1},{1,0},{2,3},{3,2},{4,5},{5,4},{6,7},{7,6},{8,9},{9,8},{10,11... | collective-permute-start | bytes 196616 | tf_op jit(solution)/shard_map/ppermute | solution.py:441
  39.1 3.0 %collective-permute-start.15 = (bf16[256,128]{1,0:T(8,128)(2,1)S(1)}, bf16[256,128]{1,0:T(8,128)(2,1)S(1)}, u32[]{:S(2)}, u32[]{:S(2)}) collective-permute-start(bf16[256,128]{1,0:T(8,128)(2,1)S(1)} %collective-permute-done.7.refs_11_), channel_id=1, source_target_pairs={{0,1},{1,0},{2,3},{3,2},{4,5},{5,4},{6,7},{7,6},{8,9},{9,8},{10,11... | collective-permute-start | bytes 196616 | tf_op jit(solution)/shard_map/ppermute | solution.py:441
  39.3 4.5 %collective-permute-start.2 = (bf16[176,512]{1,0:T(8,128)(2,1)S(1)}, bf16[176,512]{1,0:T(8,128)(2,1)S(1)}, u32[]{:S(2)}, u32[]{:S(2)}) collective-permute-start(bf16[176,512]{1,0:T(8,128)(2,1)S(1)} %get-tuple-element.35.refs_0_.grad_ref), channel_id=1, source_target_pairs={{0,1},{1,0},{2,3},{3,2},{4,5},{5,4},{6,7},{7,6},{8,9},{9,8},{10,11... | collective-permute-start | bytes 540680 | tf_op jit(solution)/shard_map/ppermute | solution.py:441
  42.1 2.1 %collective-permute-start.4 = (bf16[176,512]{1,0:T(8,128)(2,1)S(1)}, bf16[176,512]{1,0:T(8,128)(2,1)S(1)}, u32[]{:S(2)}, u32[]{:S(2)}) collective-permute-start(bf16[176,512]{1,0:T(8,128)(2,1)S(1)} %collective-permute-done.3.refs_2_), channel_id=1, source_target_pairs={{0,1},{1,0},{2,3},{3,2},{4,5},{5,4},{6,7},{7,6},{8,9},{9,8},{10,11... | collective-permute-start | bytes 540680 | tf_op jit(solution)/shard_map/ppermute | solution.py:441
  42.1 1.6 %collective-permute-start.14 = (bf16[576,128]{1,0:T(8,128)(2,1)S(1)}, bf16[576,128]{1,0:T(8,128)(2,1)S(1)}, u32[]{:S(2)}, u32[]{:S(2)}) collective-permute-start(bf16[576,128]{1,0:T(8,128)(2,1)S(1)} %collective-permute-done.6.refs_10_), channel_id=1, source_target_pairs={{0,1},{1,0},{2,3},{3,2},{4,5},{5,4},{6,7},{7,6},{8,9},{9,8},{10,11... | collective-permute-start | bytes 442376 | tf_op jit(solution)/shard_map/ppermute | solution.py:441
  42.6 1.4 %collective-permute-start.11 = (bf16[144,512]{1,0:T(8,128)(2,1)S(1)}, bf16[144,512]{1,0:T(8,128)(2,1)S(1)}, u32[]{:S(2)}, u32[]{:S(2)}) collective-permute-start(bf16[144,512]{1,0:T(8,128)(2,1)S(1)} %collective-permute-done.10.refs_6_), channel_id=1, source_target_pairs={{0,1},{1,0},{2,3},{3,2},{4,5},{5,4},{6,7},{7,6},{8,9},{9,8},{10,11... | collective-permute-start | bytes 442376 | tf_op jit(solution)/shard_map/ppermute | solution.py:441
  42.7 1.5 %collective-permute-start.9 = (bf16[144,512]{1,0:T(8,128)(2,1)S(1)}, bf16[144,512]{1,0:T(8,128)(2,1)S(1)}, u32[]{:S(2)}, u32[]{:S(2)}) collective-permute-start(bf16[144,512]{1,0:T(8,128)(2,1)S(1)} %collective-permute-done.8.refs_4_), channel_id=1, source_target_pairs={{0,1},{1,0},{2,3},{3,2},{4,5},{5,4},{6,7},{7,6},{8,9},{9,8},{10,11... | collective-permute-start | bytes 442376 | tf_op jit(solution)/shard_map/ppermute | solution.py:441
  46.2 7.1 %collective-permute-start.16 = (bf16[112,512]{1,0:T(8,128)(2,1)S(1)}, bf16[112,512]{1,0:T(8,128)(2,1)S(1)}, u32[]{:S(2)}, u32[]{:S(2)}) collective-permute-start(bf16[112,512]{1,0:T(8,128)(2,1)S(1)} %get-tuple-element.47), channel_id=1, source_target_pairs={{0,8},{1,9},{2,10},{3,11},{4,12},{5,13},{6,14},{7,15},{8,0},{9,1},... | collective-permute-start | bytes 344072 | tf_op jit(solution)/shard_map/ppermute | solution.py:441
  46.2 11.8 %collective-permute-start.17 = (bf16[112,512]{1,0:T(8,128)(2,1)S(1)}, bf16[112,512]{1,0:T(8,128)(2,1)S(1)}, u32[]{:S(2)}, u32[]{:S(2)}) collective-permute-start(bf16[112,512]{1,0:T(8,128)(2,1)S(1)} %get-tuple-element.48), channel_id=1, source_target_pairs={{0,16},{1,17},{2,18},{3,19},{4,20},{5,21},{6,22},{7,23},{8,24},{9,... | collective-permute-start | bytes 344072 | tf_op jit(solution)/shard_map/ppermute | solution.py:441
  48.0 10.0 %collective-permute-start.18 = (bf16[112,512]{1,0:T(8,128)(2,1)S(1)}, bf16[112,512]{1,0:T(8,128)(2,1)S(1)}, u32[]{:S(2)}, u32[]{:S(2)}) collective-permute-start(bf16[112,512]{1,0:T(8,128)(2,1)S(1)} %get-tuple-element.49), channel_id=1, source_target_pairs={{0,24},{1,25},{2,26},{3,27},{4,28},{5,29},{6,30},{7,31},{8,16},{9,... | collective-permute-start | bytes 344072 | tf_op jit(solution)/shard_map/ppermute | solution.py:441

commit v10 on v9

--- a/solution.py
+++ b/solution.py
@@ -273,8 +273,9 @@
         pick = jnp.concatenate(picks, axis=0).T.astype(BF)
         shards.append(dot(pick, jnp.concatenate(sent, axis=0)))
     packed_ref[...] = dot_nt(weight_ref[...], shards[0].astype(BF)).astype(BF)
-    partial = dot_nt(shards[0].T.astype(BF), mine_ref[...])
-    theirs = dot_nt(shards[1].T.astype(BF), other)
+    turn = (((0,), (1,)), ((), ()))
+    partial = lax.dot_general(shards[0].astype(BF), mine_ref[...], turn, preferred_element_type=F32)
+    theirs = lax.dot_general(shards[1].astype(BF), other, turn, preferred_element_type=F32)
     each = channels // dp_count
     depth = -(-(n1 + n2) // 128) * 128
     lane = lax.broadcasted_iota(jnp.int32, (rows, depth), 1)
@@ -523,7 +524,7 @@
     by_mask = {0: grads}
     for mask in range(2, near, 2):
         leaving = grads if mask < mp_count else half_grads
-        if mask == 4:
+        if mask == mp_count:
             leaving, *in_sides[1 : near // 2] = lax.optimization_barrier(
                 (leaving, *in_sides[1 : near // 2])
             )

time: 59.7 us -> 59.7 us (level)
  no operation moved by 1% of the time
where the time goes in v10:
time: 59.7 us; the launch traced here: 59.3 us
  starting transfers between devices  28.5 us (48%)
  waiting for transfers between devices  13.8 us (23%)
  Pallas kernels  13.4 us (22%)
  local copies, waits for them, and re-layouts  1.93 us (3%)
  other arithmetic  0.95 us (2%)
  between operations  0.74 us (1%)
    ppermute x19, starting transfers between devices, swap(): lax.ppermute(x, everyone, [(i, i ^ mask) for i in range(dp_count * mp_cou...  15.7 us
    pallas_call x7, Pallas kernels, call(): pl.pallas_call(body, out_shape=out, in_specs=specs, out_specs=[pl.BlockSp...  13.4 us
    ppermute x19, waiting for transfers between devices, swap(): lax.ppermute(x, everyone, [(i, i ^ mask) for i in range(dp_count * mp_cou...  9.91 us
    all_to_all x1, starting transfers between devices, local(): lax.all_to_all(index, 'dp', split_axis=0, concat_axis=0, tiled=True)  6.82 us
    all_to_all x1, starting transfers between devices, local(): slots = lax.all_to_all(sent, 'dp', split_axis=0, concat_axis=0, tiled=True)  5.99 us
    all_to_all x1, waiting for transfers between devices, local(): slots = lax.all_to_all(sent, 'dp', split_axis=0, concat_axis=0, tiled=True)  3.93 us
    unnamed x14, local copies, waits for them, and re-layouts  1.93 us
  transfers between devices with their start and end apart: 21, of which 8 were waited for; matrix products, arithmetic and copies ran while one was open for 2% of the time, Pallas kernels for 12%

profile of v10, /device:TPU:0, one launch (start us, length us, event | category | flops | bytes accessed | tf_op | source)
XLA Modules:
  0.0 59.3 jit_solution(16236523856631555004)
XLA Ops:
  0.6 2.0 %shard_map.128 = (s32[28]{0:T(128)}, s32[8,128]{1,0:T(8,128)}, bf16[128,512]{1,0:T(8,128)(2,1)}) custom-call(bf16[320,512]{1,0:T(8,128)(2,1)} %bitcast.10, bf16[320,128]{1,0:T(8,128)(2,1)} %bitcast.13, s32[8]{0:T(128)} %lengths_hbm.1, s32[8]{0:T(128)} %dests_hbm.1, s32[8]{0:T(128)} %offsets_hbm.1), custom_call_target="tpu_custom_call" | custom-call | flops 41943040 | bytes 409696 | tf_op jit(solution)/shard_map/pallas_call | solution.py:25
  2.6 0.5 collective-permute-start
  3.1 6.8 %all-to-all-start = ((s32[8,1,128]{2,1,0:T(1,128)}), s32[8,1,128]{2,1,0:T(1,128)S(1)}, u32[]{:S(2)}, u32[]{:S(2)}) async-start(s32[8,1,128]{2,1,0:T(1,128)} %bitcast.19), calls=%async_computation | async-start | bytes 8192 | tf_op jit(solution)/shard_map/all_to_all | solution.py:467
  10.0 1.0 %add_convert_fusion.mine_ref = bf16[128,512]{1,0:T(8,128)(2,1)S(1)} fusion(bf16[128,512]{1,0:T(8,128)(2,1)S(1)} %collective-permute-done, bf16[128,512]{1,0:T(8,128)(2,1)} %get-tuple-element.32), kind=kLoop, calls=%fused_computation | loop fusion | flops 262144 | bytes 393216 | tf_op jit(solution)/shard_map/convert_element_type | solution.py:505
  10.9 1.6 %collective-permute-start.1 = (bf16[128,512]{1,0:T(8,128)(2,1)S(1)}, bf16[128,512]{1,0:T(8,128)(2,1)S(1)}, u32[]{:S(2)}, u32[]{:S(2)}) collective-permute-start(bf16[128,512]{1,0:T(8,128)(2,1)S(1)} %add_convert_fusion.mine_ref), channel_id=1, source_target_pairs={{0,2},{1,3},{2,0},{3,1},{4,6},{5,7},{6,4},{7,5},{8,10},{9,11},{10,... | collective-permute-start | bytes 393224 | tf_op jit(solution)/shard_map/ppermute | solution.py:442
  12.5 4.2 %shard_map.129 = (s32[28]{0:T(128)}, bf16[64,512]{1,0:T(8,128)(2,1)}, f32[232,512]{1,0:T(8,128)}, bf16[256,128]{1,0:T(8,128)(2,1)}, bf16[256,128]{1,0:T(8,128)(2...) custom-call(s32[28]{0:T(128)} %get-tuple-element.29.me_ref, bf16[256,512]{1,0:T(8,128)(2,1)} %bitcast.20, ...), custom_call_target="tpu_custom_call" | custom-call | flops 10000000000 | bytes 2449520 | tf_op jit(solution)/shard_map/pallas_call | solution.py:25
  16.8 0.0 copy-start.1
  16.8 0.0 copy-start.3
  16.8 0.0 all-to-all-done
  16.8 0.0 copy-start.4
  16.8 0.9 %copy-done.4 = bf16[64,512]{1,0:T(8,128)(2,1)S(1)} copy-done((bf16[64,512]{1,0:T(8,128)(2,1)S(1)}, bf16[64,512]{1,0:T(8,128)(2,1)}, u32[]{:S(2)}) %copy-start.4) | copy-done | bytes 65560
  17.7 1.3 %shard_map.130 = bf16[8,16,512]{2,1,0:T(8,128)(2,1)} custom-call(s32[8,128]{1,0:T(8,128)S(1)} %bitcast.16, bf16[128,512]{1,0:T(8,128)(2,1)S(1)} %add_convert_fusion.mine_ref, bf16[128,512]{1,0:T(8,128)(2,1)S(1)} %collective-permute-done.1.other_ref, bf16[64,512]{1,0:T(8,128)(2,1)S(1)} %copy-done.4), custom_call_target="tpu_custom_call" | custom-call | bytes 331776 | tf_op jit(solution)/shard_map/pallas_call | solution.py:25
  19.0 6.0 %all-to-all-start.1 = ((bf16[8,16,512]{2,1,0:T(8,128)(2,1)}), bf16[8,16,512]{2,1,0:T(8,128)(2,1)S(1)}, u32[]{:S(2)}, u32[]{:S(2)}) async-start(bf16[8,16,512]{2,1,0:T(8,128)(2,1)} %shard_map.130), calls=%async_computation.1 | async-start | bytes 262144 | tf_op jit(solution)/shard_map/all_to_all | solution.py:515
  25.0 2.0 %collective-permute-start.6 = (bf16[576,128]{1,0:T(8,128)(2,1)}, bf16[576,128]{1,0:T(8,128)(2,1)S(1)}, u32[]{:S(2)}, u32[]{:S(2)}) collective-permute-start(bf16[576,128]{1,0:T(8,128)(2,1)} %get-tuple-element.38), channel_id=1, source_target_pairs={{0,4},{1,5},{2,6},{3,7},{4,0},{5,1},{6,2},{7,3},{8,12},{9,13},{10,... | collective-permute-start | bytes 442376 | tf_op jit(solution)/shard_map/ppermute | solution.py:442
  27.0 1.0 %collective-permute-start.5 = (bf16[256,128]{1,0:T(8,128)(2,1)}, bf16[256,128]{1,0:T(8,128)(2,1)S(1)}, u32[]{:S(2)}, u32[]{:S(2)}) collective-permute-start(bf16[256,128]{1,0:T(8,128)(2,1)} %get-tuple-element.37), channel_id=1, source_target_pairs={{0,2},{1,3},{2,0},{3,1},{4,6},{5,7},{6,4},{7,5},{8,10},{9,11},{10,... | collective-permute-start | bytes 196616 | tf_op jit(solution)/shard_map/ppermute | solution.py:442
  28.0 0.5 collective-permute-start.7
  28.5 3.9 %all-to-all-done.1 = bf16[8,16,512]{2,1,0:T(8,128)(2,1)S(1)} async-done(((bf16[8,16,512]{2,1,0:T(8,128)(2,1)}), bf16[8,16,512]{2,1,0:T(8,128)(2,1)S(1)}, u32[]{:S(2)}, u32[]{:S(2)}) %all-to-all-start.1) | async-done | bytes 131104 | tf_op jit(solution)/shard_map/all_to_all | solution.py:515
  32.4 1.0 %copy-done.2 = f32[232,512]{1,0:T(8,128)S(1)} copy-done((f32[232,512]{1,0:T(8,128)S(1)}, f32[232,512]{1,0:T(8,128)}, u32[]{:S(2)}) %copy-start.2) | copy-done | bytes 475160
  33.5 0.7 %shard_map.131 = (bf16[176,512]{1,0:T(8,128)(2,1)S(1)}, bf16[144,512]{1,0:T(8,128)(2,1)S(1)}) custom-call(bf16[128,512]{1,0:T(8,128)(2,1)S(1)} %bitcast.12, s32[8,128]{1,0:T(8,128)S(1)} %bitcast.17, f32[232,512]{1,0:T(8,128)S(1)} %copy-done.2, bf16[2,1024,512]{2,1,0:T(8,128)(2,1)S(1)} %copy-done), custom_call_target="tpu_custom_call" | custom-call | flops 33554432 | bytes 2707456 | tf_op jit(solution)/shard_map/pallas_call | solution.py:25
  34.2 1.0 %collective-permute-start.3 = (bf16[176,512]{1,0:T(8,128)(2,1)S(1)}, bf16[176,512]{1,0:T(8,128)(2,1)S(1)}, u32[]{:S(2)}, u32[]{:S(2)}) collective-permute-start(bf16[176,512]{1,0:T(8,128)(2,1)S(1)} %get-tuple-element.35.refs_0_.grad_ref), channel_id=1, source_target_pairs={{0,2},{1,3},{2,0},{3,1},{4,6},{5,7},{6,4},{7,5},{8,10},{9,11},{10,... | collective-permute-start | bytes 540680 | tf_op jit(solution)/shard_map/ppermute | solution.py:442
  35.2 0.7 %collective-permute-start.10 = (bf16[144,512]{1,0:T(8,128)(2,1)S(1)}, bf16[144,512]{1,0:T(8,128)(2,1)S(1)}, u32[]{:S(2)}, u32[]{:S(2)}) collective-permute-start(bf16[144,512]{1,0:T(8,128)(2,1)S(1)} %get-tuple-element.40), channel_id=1, source_target_pairs={{0,6},{1,7},{2,4},{3,5},{4,2},{5,3},{6,0},{7,1},{8,14},{9,15},{10,... | collective-permute-start | bytes 442376 | tf_op jit(solution)/shard_map/ppermute | solution.py:442
  35.9 2.0 %collective-permute-start.8 = (bf16[144,512]{1,0:T(8,128)(2,1)S(1)}, bf16[144,512]{1,0:T(8,128)(2,1)S(1)}, u32[]{:S(2)}, u32[]{:S(2)}) collective-permute-start(bf16[144,512]{1,0:T(8,128)(2,1)S(1)} %get-tuple-element.40), channel_id=1, source_target_pairs={{0,4},{1,5},{2,6},{3,7},{4,0},{5,1},{6,2},{7,3},{8,12},{9,13},{10,... | collective-permute-start | bytes 442376 | tf_op jit(solution)/shard_map/ppermute | solution.py:442
  37.8 0.5 collective-permute-start.13
  38.3 0.7 %collective-permute-done.12.refs_12_ = bf16[256,128]{1,0:T(8,128)(2,1)S(1)} collective-permute-done((bf16[256,128]{1,0:T(8,128)(2,1)S(1)}, bf16[256,128]{1,0:T(8,128)(2,1)S(1)}, u32[]{:S(2)}, u32[]{:S(2)}) %collective-permute-start.12) | collective-permute-done | bytes 65568 | tf_op jit(solution)/shard_map/ppermute | solution.py:442
  39.1 0.2 collective-permute-start.15
  39.3 0.4 collective-permute-start.2
  39.6 2.5 %collective-permute-done.3.refs_2_ = bf16[176,512]{1,0:T(8,128)(2,1)S(1)} collective-permute-done((bf16[176,512]{1,0:T(8,128)(2,1)S(1)}, bf16[176,512]{1,0:T(8,128)(2,1)S(1)}, u32[]{:S(2)}, u32[]{:S(2)}) %collective-permute-start.3) | collective-permute-done | bytes 180256 | tf_op jit(solution)/shard_map/ppermute | solution.py:442
  42.1 0.0 collective-permute-start.4
  42.1 0.0 collective-permute-done.15.refs_15_
  42.1 0.5 collective-permute-start.14
  42.6 0.0 collective-permute-done.10.refs_6_
  42.6 0.1 collective-permute-start.11
  42.7 0.0 collective-permute-done.8.refs_4_
  42.7 0.4 collective-permute-start.9
  43.1 0.6 %collective-permute-done.14.refs_14_ = bf16[576,128]{1,0:T(8,128)(2,1)S(1)} collective-permute-done((bf16[576,128]{1,0:T(8,128)(2,1)S(1)}, bf16[576,128]{1,0:T(8,128)(2,1)S(1)}, u32[]{:S(2)}, u32[]{:S(2)}) %collective-permute-start.14) | collective-permute-done | bytes 147488 | tf_op jit(solution)/shard_map/ppermute | solution.py:442
  43.7 0.0 collective-permute-done.2.refs_1_
  43.7 0.3 collective-permute-done.11.refs_7_
  44.0 0.2 collective-permute-done.9.refs_5_
  44.2 0.0 collective-permute-done.4.refs_3_
  44.2 2.0 %shard_map.132 = (bf16[320,128]{1,0:T(8,128)(2,1)}, f32[112,512]{1,0:T(8,128)S(1)}, bf16[112,512]{1,0:T(8,128)(2,1)S(1)}, bf16[112,512]{1,0:T(8,128)(2,1)S(1)}, bf16[112,512]{1,0:T(8,128)(2,1)S(1)}) custom-call(s32[28]{0:T(128)S(1)} %copy-done.6, bf16[176,512]{1,0:T(8,128)(2,1)S(1)} %get-tuple-element.35.refs_0_.grad_ref, ...), custom_call_target="tpu_custom_call" | custom-call | flops 100663296 | bytes 2408560 | tf_op jit(solution)/shard_map/pallas_call | solution.py:25
  46.2 0.0 collective-permute-start.16
  46.2 1.8 %collective-permute-start.17 = (bf16[112,512]{1,0:T(8,128)(2,1)S(1)}, bf16[112,512]{1,0:T(8,128)(2,1)S(1)}, u32[]{:S(2)}, u32[]{:S(2)}) collective-permute-start(bf16[112,512]{1,0:T(8,128)(2,1)S(1)} %get-tuple-element.48), channel_id=1, source_target_pairs={{0,16},{1,17},{2,18},{3,19},{4,20},{5,21},{6,22},{7,23},{8,24},{9,... | collective-permute-start | bytes 344072 | tf_op jit(solution)/shard_map/ppermute | solution.py:442
  48.0 2.6 %collective-permute-start.18 = (bf16[112,512]{1,0:T(8,128)(2,1)S(1)}, bf16[112,512]{1,0:T(8,128)(2,1)S(1)}, u32[]{:S(2)}, u32[]{:S(2)}) collective-permute-start(bf16[112,512]{1,0:T(8,128)(2,1)S(1)} %get-tuple-element.49), channel_id=1, source_target_pairs={{0,24},{1,25},{2,26},{3,27},{4,28},{5,29},{6,30},{7,31},{8,16},{9,... | collective-permute-start | bytes 344072 | tf_op jit(solution)/shard_map/ppermute | solution.py:442
  50.6 1.9 %shard_map.133 = bf16[256,512]{1,0:T(8,128)(2,1)} custom-call(s32[28]{0:T(128)S(1)} %copy-done.6, bf16[176,512]{1,0:T(8,128)(2,1)S(1)} %get-tuple-element.35.refs_0_.grad_ref, bf16[2,1024,512]{2,1,0:T(8,128)(2,1)S(1)} %copy-done), custom_call_target="tpu_custom_call" | custom-call | flops 67108864 | bytes 2277488 | tf_op jit(solution)/shard_map/pallas_call | solution.py:25
  52.5 0.8 %collective-permute-done.16.refs_1_ = bf16[112,512]{1,0:T(8,128)(2,1)S(1)} collective-permute-done((bf16[112,512]{1,0:T(8,128)(2,1)S(1)}, bf16[112,512]{1,0:T(8,128)(2,1)S(1)}, u32[]{:S(2)}, u32[]{:S(2)}) %collective-permute-start.16) | collective-permute-done | bytes 114720 | tf_op jit(solution)/shard_map/ppermute | solution.py:442
  53.3 4.8 %collective-permute-done.17.refs_2_ = bf16[112,512]{1,0:T(8,128)(2,1)S(1)} collective-permute-done((bf16[112,512]{1,0:T(8,128)(2,1)S(1)}, bf16[112,512]{1,0:T(8,128)(2,1)S(1)}, u32[]{:S(2)}, u32[]{:S(2)}) %collective-permute-start.17) | collective-permute-done | bytes 114720 | tf_op jit(solution)/shard_map/ppermute | solution.py:442
  58.1 0.0 collective-permute-done.18.refs_3_
  58.1 1.3 %shard_map.134 = (f32[2,32,512]{2,1,0:T(8,128)}, f32[2,32]{1,0:T(2,128)}, f32[64,320]{1,0:T(8,128)}) custom-call(s32[28]{0:T(128)S(1)} %copy-done.6, f32[112,512]{1,0:T(8,128)S(1)} %get-tuple-element.46.refs_0_, bf16[112,512]{1,0:T(8,128)(2,1)S(1)} %collective-permute-done.16.refs_1_, bf16[112,512]{1,0:T(8,128)(2,1)S(1)} %collective-permute-done.17.refs_2_, ...), custom_call_target="tpu_custom_call" | custom-call | bytes 573552 | tf_op jit(solution)/shard_map/pallas_call | solution.py:25
  (16 shorter events, 0.0 us)
Async XLA Ops:
  2.6 7.3 %collective-permute-start = (bf16[128,512]{1,0:T(8,128)(2,1)}, bf16[128,512]{1,0:T(8,128)(2,1)S(1)}, u32[]{:S(2)}, u32[]{:S(2)}) collective-permute-start(bf16[128,512]{1,0:T(8,128)(2,1)} %get-tuple-element.32), channel_id=1, source_target_pairs={{0,1},{1,0},{2,3},{3,2},{4,5},{5,4},{6,7},{7,6},{8,9},{9,8},{10,11... | collective-permute-start | bytes 393224 | tf_op jit(solution)/shard_map/ppermute | solution.py:442
  3.1 13.6 %all-to-all-start = ((s32[8,1,128]{2,1,0:T(1,128)}), s32[8,1,128]{2,1,0:T(1,128)S(1)}, u32[]{:S(2)}, u32[]{:S(2)}) async-start(s32[8,1,128]{2,1,0:T(1,128)} %bitcast.19), calls=%async_computation | async-start | bytes 8192 | tf_op jit(solution)/shard_map/all_to_all | solution.py:467
  10.9 5.9 %collective-permute-start.1 = (bf16[128,512]{1,0:T(8,128)(2,1)S(1)}, bf16[128,512]{1,0:T(8,128)(2,1)S(1)}, u32[]{:S(2)}, u32[]{:S(2)}) collective-permute-start(bf16[128,512]{1,0:T(8,128)(2,1)S(1)} %add_convert_fusion.mine_ref), channel_id=1, source_target_pairs={{0,2},{1,3},{2,0},{3,1},{4,6},{5,7},{6,4},{7,5},{8,10},{9,11},{10,... | collective-permute-start | bytes 393224 | tf_op jit(solution)/shard_map/ppermute | solution.py:442
  12.5 19.9 %copy-start = (bf16[2,1024,512]{2,1,0:T(8,128)(2,1)S(1)}, bf16[2,1024,512]{2,1,0:T(8,128)(2,1)}, u32[]{:S(2)}) copy-start(bf16[2,1024,512]{2,1,0:T(8,128)(2,1)} %weight_ref.3) | copy-start | bytes 6291460
  16.8 27.5 %copy-start.1 = (bf16[512,320]{0,1:T(8,128)(2,1)S(1)}, bf16[512,320]{0,1:T(8,128)(2,1)}, u32[]{:S(2)}) copy-start(bf16[512,320]{0,1:T(8,128)(2,1)} %param.16) | copy-start | bytes 983044
  16.8 27.5 %copy-start.3 = (bf16[128,320]{0,1:T(8,128)(2,1)S(1)}, bf16[128,320]{0,1:T(8,128)(2,1)}, u32[]{:S(2)}) copy-start(bf16[128,320]{0,1:T(8,128)(2,1)} %param.17) | copy-start | bytes 245764
  16.8 0.9 %copy-start.4 = (bf16[64,512]{1,0:T(8,128)(2,1)S(1)}, bf16[64,512]{1,0:T(8,128)(2,1)}, u32[]{:S(2)}) copy-start(bf16[64,512]{1,0:T(8,128)(2,1)} %get-tuple-element.33.sent_ref) | copy-start | bytes 196612
  17.7 20.1 %copy-start.5 = (bf16[256,128]{1,0:T(8,128)(2,1)S(1)}, bf16[256,128]{1,0:T(8,128)(2,1)}, u32[]{:S(2)}) copy-start(bf16[256,128]{1,0:T(8,128)(2,1)} %get-tuple-element.41.refs_8_) | copy-start | bytes 196612
  17.7 26.5 %copy-start.6 = (s32[28]{0:T(128)S(1)}, s32[28]{0:T(128)}, u32[]{:S(2)}) copy-start(s32[28]{0:T(128)} %get-tuple-element.30.me_ref) | copy-start | bytes 340
  19.0 13.4 %all-to-all-start.1 = ((bf16[8,16,512]{2,1,0:T(8,128)(2,1)}), bf16[8,16,512]{2,1,0:T(8,128)(2,1)S(1)}, u32[]{:S(2)}, u32[]{:S(2)}) async-start(bf16[8,16,512]{2,1,0:T(8,128)(2,1)} %shard_map.130), calls=%async_computation.1 | async-start | bytes 262144 | tf_op jit(solution)/shard_map/all_to_all | solution.py:515
  25.0 10.9 %collective-permute-start.6 = (bf16[576,128]{1,0:T(8,128)(2,1)}, bf16[576,128]{1,0:T(8,128)(2,1)S(1)}, u32[]{:S(2)}, u32[]{:S(2)}) collective-permute-start(bf16[576,128]{1,0:T(8,128)(2,1)} %get-tuple-element.38), channel_id=1, source_target_pairs={{0,4},{1,5},{2,6},{3,7},{4,0},{5,1},{6,2},{7,3},{8,12},{9,13},{10,... | collective-permute-start | bytes 442376 | tf_op jit(solution)/shard_map/ppermute | solution.py:442
  27.0 8.8 %collective-permute-start.5 = (bf16[256,128]{1,0:T(8,128)(2,1)}, bf16[256,128]{1,0:T(8,128)(2,1)S(1)}, u32[]{:S(2)}, u32[]{:S(2)}) collective-permute-start(bf16[256,128]{1,0:T(8,128)(2,1)} %get-tuple-element.37), channel_id=1, source_target_pairs={{0,2},{1,3},{2,0},{3,1},{4,6},{5,7},{6,4},{7,5},{8,10},{9,11},{10,... | collective-permute-start | bytes 196616 | tf_op jit(solution)/shard_map/ppermute | solution.py:442
  28.0 7.8 %collective-permute-start.7 = (bf16[256,128]{1,0:T(8,128)(2,1)}, bf16[256,128]{1,0:T(8,128)(2,1)S(1)}, u32[]{:S(2)}, u32[]{:S(2)}) collective-permute-start(bf16[256,128]{1,0:T(8,128)(2,1)} %get-tuple-element.39), channel_id=1, source_target_pairs={{0,6},{1,7},{2,4},{3,5},{4,2},{5,3},{6,0},{7,1},{8,14},{9,15},{10,... | collective-permute-start | bytes 196616 | tf_op jit(solution)/shard_map/ppermute | solution.py:442
  32.4 1.0 %copy-start.2 = (f32[232,512]{1,0:T(8,128)S(1)}, f32[232,512]{1,0:T(8,128)}, u32[]{:S(2)}) copy-start(f32[232,512]{1,0:T(8,128)} %get-tuple-element.34.state_ref) | copy-start | bytes 1425412
  34.2 7.9 %collective-permute-start.3 = (bf16[176,512]{1,0:T(8,128)(2,1)S(1)}, bf16[176,512]{1,0:T(8,128)(2,1)S(1)}, u32[]{:S(2)}, u32[]{:S(2)}) collective-permute-start(bf16[176,512]{1,0:T(8,128)(2,1)S(1)} %get-tuple-element.35.refs_0_.grad_ref), channel_id=1, source_target_pairs={{0,2},{1,3},{2,0},{3,1},{4,6},{5,7},{6,4},{7,5},{8,10},{9,11},{10,... | collective-permute-start | bytes 540680 | tf_op jit(solution)/shard_map/ppermute | solution.py:442
  35.2 7.5 %collective-permute-start.10 = (bf16[144,512]{1,0:T(8,128)(2,1)S(1)}, bf16[144,512]{1,0:T(8,128)(2,1)S(1)}, u32[]{:S(2)}, u32[]{:S(2)}) collective-permute-start(bf16[144,512]{1,0:T(8,128)(2,1)S(1)} %get-tuple-element.40), channel_id=1, source_target_pairs={{0,6},{1,7},{2,4},{3,5},{4,2},{5,3},{6,0},{7,1},{8,14},{9,15},{10,... | collective-permute-start | bytes 442376 | tf_op jit(solution)/shard_map/ppermute | solution.py:442
  35.9 6.9 %collective-permute-start.8 = (bf16[144,512]{1,0:T(8,128)(2,1)S(1)}, bf16[144,512]{1,0:T(8,128)(2,1)S(1)}, u32[]{:S(2)}, u32[]{:S(2)}) collective-permute-start(bf16[144,512]{1,0:T(8,128)(2,1)S(1)} %get-tuple-element.40), channel_id=1, source_target_pairs={{0,4},{1,5},{2,6},{3,7},{4,0},{5,1},{6,2},{7,3},{8,12},{9,13},{10,... | collective-permute-start | bytes 442376 | tf_op jit(solution)/shard_map/ppermute | solution.py:442
  37.8 1.3 %collective-permute-start.12 = (bf16[256,128]{1,0:T(8,128)(2,1)S(1)}, bf16[256,128]{1,0:T(8,128)(2,1)S(1)}, u32[]{:S(2)}, u32[]{:S(2)}) collective-permute-start(bf16[256,128]{1,0:T(8,128)(2,1)S(1)} %copy-done.5), channel_id=1, source_target_pairs={{0,1},{1,0},{2,3},{3,2},{4,5},{5,4},{6,7},{7,6},{8,9},{9,8},{10,11... | collective-permute-start | bytes 196616 | tf_op jit(solution)/shard_map/ppermute | solution.py:442
  37.8 1.4 %collective-permute-start.13 = (bf16[256,128]{1,0:T(8,128)(2,1)S(1)}, bf16[256,128]{1,0:T(8,128)(2,1)S(1)}, u32[]{:S(2)}, u32[]{:S(2)}) collective-permute-start(bf16[256,128]{1,0:T(8,128)(2,1)S(1)} %collective-permute-done.5.refs_9_), channel_id=1, source_target_pairs={{0,1},{1,0},{2,3},{3,2},{4,5},{5,4},{6,7},{7,6},{8,9},{9,8},{10,11... | collective-permute-start | bytes 196616 | tf_op jit(solution)/shard_map/ppermute | solution.py:442
  39.1 3.0 %collective-permute-start.15 = (bf16[256,128]{1,0:T(8,128)(2,1)S(1)}, bf16[256,128]{1,0:T(8,128)(2,1)S(1)}, u32[]{:S(2)}, u32[]{:S(2)}) collective-permute-start(bf16[256,128]{1,0:T(8,128)(2,1)S(1)} %collective-permute-done.7.refs_11_), channel_id=1, source_target_pairs={{0,1},{1,0},{2,3},{3,2},{4,5},{5,4},{6,7},{7,6},{8,9},{9,8},{10,11... | collective-permute-start | bytes 196616 | tf_op jit(solution)/shard_map/ppermute | solution.py:442
  39.3 4.5 %collective-permute-start.2 = (bf16[176,512]{1,0:T(8,128)(2,1)S(1)}, bf16[176,512]{1,0:T(8,128)(2,1)S(1)}, u32[]{:S(2)}, u32[]{:S(2)}) collective-permute-start(bf16[176,512]{1,0:T(8,128)(2,1)S(1)} %get-tuple-element.35.refs_0_.grad_ref), channel_id=1, source_target_pairs={{0,1},{1,0},{2,3},{3,2},{4,5},{5,4},{6,7},{7,6},{8,9},{9,8},{10,11... | collective-permute-start | bytes 540680 | tf_op jit(solution)/shard_map/ppermute | solution.py:442
  42.1 2.1 %collective-permute-start.4 = (bf16[176,512]{1,0:T(8,128)(2,1)S(1)}, bf16[176,512]{1,0:T(8,128)(2,1)S(1)}, u32[]{:S(2)}, u32[]{:S(2)}) collective-permute-start(bf16[176,512]{1,0:T(8,128)(2,1)S(1)} %collective-permute-done.3.refs_2_), channel_id=1, source_target_pairs={{0,1},{1,0},{2,3},{3,2},{4,5},{5,4},{6,7},{7,6},{8,9},{9,8},{10,11... | collective-permute-start | bytes 540680 | tf_op jit(solution)/shard_map/ppermute | solution.py:442
  42.1 1.6 %collective-permute-start.14 = (bf16[576,128]{1,0:T(8,128)(2,1)S(1)}, bf16[576,128]{1,0:T(8,128)(2,1)S(1)}, u32[]{:S(2)}, u32[]{:S(2)}) collective-permute-start(bf16[576,128]{1,0:T(8,128)(2,1)S(1)} %collective-permute-done.6.refs_10_), channel_id=1, source_target_pairs={{0,1},{1,0},{2,3},{3,2},{4,5},{5,4},{6,7},{7,6},{8,9},{9,8},{10,11... | collective-permute-start | bytes 442376 | tf_op jit(solution)/shard_map/ppermute | solution.py:442
  42.6 1.4 %collective-permute-start.11 = (bf16[144,512]{1,0:T(8,128)(2,1)S(1)}, bf16[144,512]{1,0:T(8,128)(2,1)S(1)}, u32[]{:S(2)}, u32[]{:S(2)}) collective-permute-start(bf16[144,512]{1,0:T(8,128)(2,1)S(1)} %collective-permute-done.10.refs_6_), channel_id=1, source_target_pairs={{0,1},{1,0},{2,3},{3,2},{4,5},{5,4},{6,7},{7,6},{8,9},{9,8},{10,11... | collective-permute-start | bytes 442376 | tf_op jit(solution)/shard_map/ppermute | solution.py:442
  42.7 1.5 %collective-permute-start.9 = (bf16[144,512]{1,0:T(8,128)(2,1)S(1)}, bf16[144,512]{1,0:T(8,128)(2,1)S(1)}, u32[]{:S(2)}, u32[]{:S(2)}) collective-permute-start(bf16[144,512]{1,0:T(8,128)(2,1)S(1)} %collective-permute-done.8.refs_4_), channel_id=1, source_target_pairs={{0,1},{1,0},{2,3},{3,2},{4,5},{5,4},{6,7},{7,6},{8,9},{9,8},{10,11... | collective-permute-start | bytes 442376 | tf_op jit(solution)/shard_map/ppermute | solution.py:442
  46.2 7.1 %collective-permute-start.16 = (bf16[112,512]{1,0:T(8,128)(2,1)S(1)}, bf16[112,512]{1,0:T(8,128)(2,1)S(1)}, u32[]{:S(2)}, u32[]{:S(2)}) collective-permute-start(bf16[112,512]{1,0:T(8,128)(2,1)S(1)} %get-tuple-element.47), channel_id=1, source_target_pairs={{0,8},{1,9},{2,10},{3,11},{4,12},{5,13},{6,14},{7,15},{8,0},{9,1},... | collective-permute-start | bytes 344072 | tf_op jit(solution)/shard_map/ppermute | solution.py:442
  46.2 11.8 %collective-permute-start.17 = (bf16[112,512]{1,0:T(8,128)(2,1)S(1)}, bf16[112,512]{1,0:T(8,128)(2,1)S(1)}, u32[]{:S(2)}, u32[]{:S(2)}) collective-permute-start(bf16[112,512]{1,0:T(8,128)(2,1)S(1)} %get-tuple-element.48), channel_id=1, source_target_pairs={{0,16},{1,17},{2,18},{3,19},{4,20},{5,21},{6,22},{7,23},{8,24},{9,... | collective-permute-start | bytes 344072 | tf_op jit(solution)/shard_map/ppermute | solution.py:442
  48.0 10.0 %collective-permute-start.18 = (bf16[112,512]{1,0:T(8,128)(2,1)S(1)}, bf16[112,512]{1,0:T(8,128)(2,1)S(1)}, u32[]{:S(2)}, u32[]{:S(2)}) collective-permute-start(bf16[112,512]{1,0:T(8,128)(2,1)S(1)} %get-tuple-element.49), channel_id=1, source_target_pairs={{0,24},{1,25},{2,26},{3,27},{4,28},{5,29},{6,30},{7,31},{8,16},{9,... | collective-permute-start | bytes 344072 | tf_op jit(solution)/shard_map/ppermute | solution.py:442

commit v11 on v10

--- a/solution.py
+++ b/solution.py
@@ -86,7 +86,7 @@
         pltpu.make_async_copy(source, target, copied.at[i])
         for i, (source, target) in enumerate(zip(sources, targets))
     ]
-    for copy in copies[::-1]:
+    for copy in copies:
         copy.start()
     for copy in copies[2:]:
         copy.wait()

time: 59.7 us -> 59.7 us (level)
  no operation moved by 1% of the time
where the time goes in v11:
time: 59.7 us; the launch traced here: 59.3 us
  starting transfers between devices  28.5 us (48%)
  waiting for transfers between devices  13.8 us (23%)
  Pallas kernels  13.4 us (22%)
  local copies, waits for them, and re-layouts  1.93 us (3%)
  other arithmetic  0.95 us (2%)
  between operations  0.74 us (1%)
    ppermute x19, starting transfers between devices, swap(): lax.ppermute(x, everyone, [(i, i ^ mask) for i in range(dp_count * mp_cou...  15.7 us
    pallas_call x7, Pallas kernels, call(): pl.pallas_call(body, out_shape=out, in_specs=specs, out_specs=[pl.BlockSp...  13.4 us
    ppermute x19, waiting for transfers between devices, swap(): lax.ppermute(x, everyone, [(i, i ^ mask) for i in range(dp_count * mp_cou...  9.91 us
    all_to_all x1, starting transfers between devices, local(): lax.all_to_all(index, 'dp', split_axis=0, concat_axis=0, tiled=True)  6.82 us
    all_to_all x1, starting transfers between devices, local(): slots = lax.all_to_all(sent, 'dp', split_axis=0, concat_axis=0, tiled=True)  5.99 us
    all_to_all x1, waiting for transfers between devices, local(): slots = lax.all_to_all(sent, 'dp', split_axis=0, concat_axis=0, tiled=True)  3.93 us
    unnamed x14, local copies, waits for them, and re-layouts  1.93 us
  transfers between devices with their start and end apart: 21, of which 8 were waited for; matrix products, arithmetic and copies ran while one was open for 2% of the time, Pallas kernels for 12%

profile of v11, /device:TPU:0, one launch (start us, length us, event | category | flops | bytes accessed | tf_op | source)
XLA Modules:
  0.0 59.3 jit_solution(14806332039571054842)
XLA Ops:
  0.6 1.9 %shard_map.128 = (s32[28]{0:T(128)}, s32[8,128]{1,0:T(8,128)}, bf16[128,512]{1,0:T(8,128)(2,1)}) custom-call(bf16[320,512]{1,0:T(8,128)(2,1)} %bitcast.10, bf16[320,128]{1,0:T(8,128)(2,1)} %bitcast.13, s32[8]{0:T(128)} %lengths_hbm.1, s32[8]{0:T(128)} %dests_hbm.1, s32[8]{0:T(128)} %offsets_hbm.1), custom_call_target="tpu_custom_call" | custom-call | flops 41943040 | bytes 409696 | tf_op jit(solution)/shard_map/pallas_call | solution.py:25
  2.6 0.5 collective-permute-start
  3.1 6.8 %all-to-all-start = ((s32[8,1,128]{2,1,0:T(1,128)}), s32[8,1,128]{2,1,0:T(1,128)S(1)}, u32[]{:S(2)}, u32[]{:S(2)}) async-start(s32[8,1,128]{2,1,0:T(1,128)} %bitcast.19), calls=%async_computation | async-start | bytes 8192 | tf_op jit(solution)/shard_map/all_to_all | solution.py:467
  9.9 0.0 collective-permute-done
  9.9 1.0 %add_convert_fusion.mine_ref = bf16[128,512]{1,0:T(8,128)(2,1)S(1)} fusion(bf16[128,512]{1,0:T(8,128)(2,1)S(1)} %collective-permute-done, bf16[128,512]{1,0:T(8,128)(2,1)} %get-tuple-element.32), kind=kLoop, calls=%fused_computation | loop fusion | flops 262144 | bytes 393216 | tf_op jit(solution)/shard_map/convert_element_type | solution.py:505
  10.9 1.6 %collective-permute-start.1 = (bf16[128,512]{1,0:T(8,128)(2,1)S(1)}, bf16[128,512]{1,0:T(8,128)(2,1)S(1)}, u32[]{:S(2)}, u32[]{:S(2)}) collective-permute-start(bf16[128,512]{1,0:T(8,128)(2,1)S(1)} %add_convert_fusion.mine_ref), channel_id=1, source_target_pairs={{0,2},{1,3},{2,0},{3,1},{4,6},{5,7},{6,4},{7,5},{8,10},{9,11},{10,... | collective-permute-start | bytes 393224 | tf_op jit(solution)/shard_map/ppermute | solution.py:442
  12.5 4.2 %shard_map.129 = (s32[28]{0:T(128)}, bf16[64,512]{1,0:T(8,128)(2,1)}, f32[232,512]{1,0:T(8,128)}, bf16[256,128]{1,0:T(8,128)(2,1)}, bf16[256,128]{1,0:T(8,128)(2...) custom-call(s32[28]{0:T(128)} %get-tuple-element.29.me_ref, bf16[256,512]{1,0:T(8,128)(2,1)} %bitcast.20, ...), custom_call_target="tpu_custom_call" | custom-call | flops 10000000000 | bytes 2449520 | tf_op jit(solution)/shard_map/pallas_call | solution.py:25
  16.7 0.0 copy-start.1
  16.7 0.0 copy-start.3
  16.7 0.0 all-to-all-done
  16.7 0.0 collective-permute-done.1.other_ref
  16.8 0.0 copy-start.4
  16.8 0.9 %copy-done.4 = bf16[64,512]{1,0:T(8,128)(2,1)S(1)} copy-done((bf16[64,512]{1,0:T(8,128)(2,1)S(1)}, bf16[64,512]{1,0:T(8,128)(2,1)}, u32[]{:S(2)}) %copy-start.4) | copy-done | bytes 65560
  17.6 1.3 %shard_map.130 = bf16[8,16,512]{2,1,0:T(8,128)(2,1)} custom-call(s32[8,128]{1,0:T(8,128)S(1)} %bitcast.16, bf16[128,512]{1,0:T(8,128)(2,1)S(1)} %add_convert_fusion.mine_ref, bf16[128,512]{1,0:T(8,128)(2,1)S(1)} %collective-permute-done.1.other_ref, bf16[64,512]{1,0:T(8,128)(2,1)S(1)} %copy-done.4), custom_call_target="tpu_custom_call" | custom-call | bytes 331776 | tf_op jit(solution)/shard_map/pallas_call | solution.py:25
  19.0 6.0 %all-to-all-start.1 = ((bf16[8,16,512]{2,1,0:T(8,128)(2,1)}), bf16[8,16,512]{2,1,0:T(8,128)(2,1)S(1)}, u32[]{:S(2)}, u32[]{:S(2)}) async-start(bf16[8,16,512]{2,1,0:T(8,128)(2,1)} %shard_map.130), calls=%async_computation.1 | async-start | bytes 262144 | tf_op jit(solution)/shard_map/all_to_all | solution.py:515
  24.9 2.0 %collective-permute-start.6 = (bf16[576,128]{1,0:T(8,128)(2,1)}, bf16[576,128]{1,0:T(8,128)(2,1)S(1)}, u32[]{:S(2)}, u32[]{:S(2)}) collective-permute-start(bf16[576,128]{1,0:T(8,128)(2,1)} %get-tuple-element.38), channel_id=1, source_target_pairs={{0,4},{1,5},{2,6},{3,7},{4,0},{5,1},{6,2},{7,3},{8,12},{9,13},{10,... | collective-permute-start | bytes 442376 | tf_op jit(solution)/shard_map/ppermute | solution.py:442
  27.0 1.0 %collective-permute-start.5 = (bf16[256,128]{1,0:T(8,128)(2,1)}, bf16[256,128]{1,0:T(8,128)(2,1)S(1)}, u32[]{:S(2)}, u32[]{:S(2)}) collective-permute-start(bf16[256,128]{1,0:T(8,128)(2,1)} %get-tuple-element.37), channel_id=1, source_target_pairs={{0,2},{1,3},{2,0},{3,1},{4,6},{5,7},{6,4},{7,5},{8,10},{9,11},{10,... | collective-permute-start | bytes 196616 | tf_op jit(solution)/shard_map/ppermute | solution.py:442
  28.0 0.5 collective-permute-start.7
  28.5 3.9 %all-to-all-done.1 = bf16[8,16,512]{2,1,0:T(8,128)(2,1)S(1)} async-done(((bf16[8,16,512]{2,1,0:T(8,128)(2,1)}), bf16[8,16,512]{2,1,0:T(8,128)(2,1)S(1)}, u32[]{:S(2)}, u32[]{:S(2)}) %all-to-all-start.1) | async-done | bytes 131104 | tf_op jit(solution)/shard_map/all_to_all | solution.py:515
  32.4 1.0 %copy-done.2 = f32[232,512]{1,0:T(8,128)S(1)} copy-done((f32[232,512]{1,0:T(8,128)S(1)}, f32[232,512]{1,0:T(8,128)}, u32[]{:S(2)}) %copy-start.2) | copy-done | bytes 475160
  33.4 0.7 %shard_map.131 = (bf16[176,512]{1,0:T(8,128)(2,1)S(1)}, bf16[144,512]{1,0:T(8,128)(2,1)S(1)}) custom-call(bf16[128,512]{1,0:T(8,128)(2,1)S(1)} %bitcast.12, s32[8,128]{1,0:T(8,128)S(1)} %bitcast.17, f32[232,512]{1,0:T(8,128)S(1)} %copy-done.2, bf16[2,1024,512]{2,1,0:T(8,128)(2,1)S(1)} %copy-done), custom_call_target="tpu_custom_call" | custom-call | flops 33554432 | bytes 2707456 | tf_op jit(solution)/shard_map/pallas_call | solution.py:25
  34.2 1.0 %collective-permute-start.3 = (bf16[176,512]{1,0:T(8,128)(2,1)S(1)}, bf16[176,512]{1,0:T(8,128)(2,1)S(1)}, u32[]{:S(2)}, u32[]{:S(2)}) collective-permute-start(bf16[176,512]{1,0:T(8,128)(2,1)S(1)} %get-tuple-element.35.refs_0_.grad_ref), channel_id=1, source_target_pairs={{0,2},{1,3},{2,0},{3,1},{4,6},{5,7},{6,4},{7,5},{8,10},{9,11},{10,... | collective-permute-start | bytes 540680 | tf_op jit(solution)/shard_map/ppermute | solution.py:442
  35.1 0.7 %collective-permute-start.10 = (bf16[144,512]{1,0:T(8,128)(2,1)S(1)}, bf16[144,512]{1,0:T(8,128)(2,1)S(1)}, u32[]{:S(2)}, u32[]{:S(2)}) collective-permute-start(bf16[144,512]{1,0:T(8,128)(2,1)S(1)} %get-tuple-element.40), channel_id=1, source_target_pairs={{0,6},{1,7},{2,4},{3,5},{4,2},{5,3},{6,0},{7,1},{8,14},{9,15},{10,... | collective-permute-start | bytes 442376 | tf_op jit(solution)/shard_map/ppermute | solution.py:442
  35.8 0.0 collective-permute-done.5.refs_9_
  35.8 0.0 collective-permute-done.7.refs_11_
  35.8 0.0 collective-permute-done.6.refs_10_
  35.8 2.0 %collective-permute-start.8 = (bf16[144,512]{1,0:T(8,128)(2,1)S(1)}, bf16[144,512]{1,0:T(8,128)(2,1)S(1)}, u32[]{:S(2)}, u32[]{:S(2)}) collective-permute-start(bf16[144,512]{1,0:T(8,128)(2,1)S(1)} %get-tuple-element.40), channel_id=1, source_target_pairs={{0,4},{1,5},{2,6},{3,7},{4,0},{5,1},{6,2},{7,3},{8,12},{9,13},{10,... | collective-permute-start | bytes 442376 | tf_op jit(solution)/shard_map/ppermute | solution.py:442
  37.8 0.5 collective-permute-start.13
  38.3 0.7 %collective-permute-done.12.refs_12_ = bf16[256,128]{1,0:T(8,128)(2,1)S(1)} collective-permute-done((bf16[256,128]{1,0:T(8,128)(2,1)S(1)}, bf16[256,128]{1,0:T(8,128)(2,1)S(1)}, u32[]{:S(2)}, u32[]{:S(2)}) %collective-permute-start.12) | collective-permute-done | bytes 65568 | tf_op jit(solution)/shard_map/ppermute | solution.py:442
  39.0 0.2 collective-permute-start.15
  39.2 0.0 collective-permute-done.13.refs_13_
  39.2 0.4 collective-permute-start.2
  39.6 2.5 %collective-permute-done.3.refs_2_ = bf16[176,512]{1,0:T(8,128)(2,1)S(1)} collective-permute-done((bf16[176,512]{1,0:T(8,128)(2,1)S(1)}, bf16[176,512]{1,0:T(8,128)(2,1)S(1)}, u32[]{:S(2)}, u32[]{:S(2)}) %collective-permute-start.3) | collective-permute-done | bytes 180256 | tf_op jit(solution)/shard_map/ppermute | solution.py:442
  42.1 0.5 collective-permute-start.14
  42.6 0.1 collective-permute-start.11
  42.7 0.4 collective-permute-start.9
  43.1 0.6 %collective-permute-done.14.refs_14_ = bf16[576,128]{1,0:T(8,128)(2,1)S(1)} collective-permute-done((bf16[576,128]{1,0:T(8,128)(2,1)S(1)}, bf16[576,128]{1,0:T(8,128)(2,1)S(1)}, u32[]{:S(2)}, u32[]{:S(2)}) %collective-permute-start.14) | collective-permute-done | bytes 147488 | tf_op jit(solution)/shard_map/ppermute | solution.py:442
  43.7 0.3 collective-permute-done.11.refs_7_
  44.0 0.2 collective-permute-done.9.refs_5_
  44.2 2.0 %shard_map.132 = (bf16[320,128]{1,0:T(8,128)(2,1)}, f32[112,512]{1,0:T(8,128)S(1)}, bf16[112,512]{1,0:T(8,128)(2,1)S(1)}, bf16[112,512]{1,0:T(8,128)(2,1)S(1)}, bf16[112,512]{1,0:T(8,128)(2,1)S(1)}) custom-call(s32[28]{0:T(128)S(1)} %copy-done.6, bf16[176,512]{1,0:T(8,128)(2,1)S(1)} %get-tuple-element.35.refs_0_.grad_ref, ...), custom_call_target="tpu_custom_call" | custom-call | flops 100663296 | bytes 2408560 | tf_op jit(solution)/shard_map/pallas_call | solution.py:25
  46.2 0.0 collective-permute-start.16
  46.2 1.8 %collective-permute-start.17 = (bf16[112,512]{1,0:T(8,128)(2,1)S(1)}, bf16[112,512]{1,0:T(8,128)(2,1)S(1)}, u32[]{:S(2)}, u32[]{:S(2)}) collective-permute-start(bf16[112,512]{1,0:T(8,128)(2,1)S(1)} %get-tuple-element.48), channel_id=1, source_target_pairs={{0,16},{1,17},{2,18},{3,19},{4,20},{5,21},{6,22},{7,23},{8,24},{9,... | collective-permute-start | bytes 344072 | tf_op jit(solution)/shard_map/ppermute | solution.py:442
  48.0 2.6 %collective-permute-start.18 = (bf16[112,512]{1,0:T(8,128)(2,1)S(1)}, bf16[112,512]{1,0:T(8,128)(2,1)S(1)}, u32[]{:S(2)}, u32[]{:S(2)}) collective-permute-start(bf16[112,512]{1,0:T(8,128)(2,1)S(1)} %get-tuple-element.49), channel_id=1, source_target_pairs={{0,24},{1,25},{2,26},{3,27},{4,28},{5,29},{6,30},{7,31},{8,16},{9,... | collective-permute-start | bytes 344072 | tf_op jit(solution)/shard_map/ppermute | solution.py:442
  50.6 1.9 %shard_map.133 = bf16[256,512]{1,0:T(8,128)(2,1)} custom-call(s32[28]{0:T(128)S(1)} %copy-done.6, bf16[176,512]{1,0:T(8,128)(2,1)S(1)} %get-tuple-element.35.refs_0_.grad_ref, bf16[2,1024,512]{2,1,0:T(8,128)(2,1)S(1)} %copy-done), custom_call_target="tpu_custom_call" | custom-call | flops 67108864 | bytes 2277488 | tf_op jit(solution)/shard_map/pallas_call | solution.py:25
  52.5 0.8 %collective-permute-done.16.refs_1_ = bf16[112,512]{1,0:T(8,128)(2,1)S(1)} collective-permute-done((bf16[112,512]{1,0:T(8,128)(2,1)S(1)}, bf16[112,512]{1,0:T(8,128)(2,1)S(1)}, u32[]{:S(2)}, u32[]{:S(2)}) %collective-permute-start.16) | collective-permute-done | bytes 114720 | tf_op jit(solution)/shard_map/ppermute | solution.py:442
  53.2 4.8 %collective-permute-done.17.refs_2_ = bf16[112,512]{1,0:T(8,128)(2,1)S(1)} collective-permute-done((bf16[112,512]{1,0:T(8,128)(2,1)S(1)}, bf16[112,512]{1,0:T(8,128)(2,1)S(1)}, u32[]{:S(2)}, u32[]{:S(2)}) %collective-permute-start.17) | collective-permute-done | bytes 114720 | tf_op jit(solution)/shard_map/ppermute | solution.py:442
  58.0 0.0 collective-permute-done.18.refs_3_
  58.0 1.3 %shard_map.134 = (f32[2,32,512]{2,1,0:T(8,128)}, f32[2,32]{1,0:T(2,128)}, f32[64,320]{1,0:T(8,128)}) custom-call(s32[28]{0:T(128)S(1)} %copy-done.6, f32[112,512]{1,0:T(8,128)S(1)} %get-tuple-element.46.refs_0_, bf16[112,512]{1,0:T(8,128)(2,1)S(1)} %collective-permute-done.16.refs_1_, bf16[112,512]{1,0:T(8,128)(2,1)S(1)} %collective-permute-done.17.refs_2_, ...), custom_call_target="tpu_custom_call" | custom-call | bytes 573552 | tf_op jit(solution)/shard_map/pallas_call | solution.py:25
  (16 shorter events, 0.0 us)
Async XLA Ops:
  2.6 7.3 %collective-permute-start = (bf16[128,512]{1,0:T(8,128)(2,1)}, bf16[128,512]{1,0:T(8,128)(2,1)S(1)}, u32[]{:S(2)}, u32[]{:S(2)}) collective-permute-start(bf16[128,512]{1,0:T(8,128)(2,1)} %get-tuple-element.32), channel_id=1, source_target_pairs={{0,1},{1,0},{2,3},{3,2},{4,5},{5,4},{6,7},{7,6},{8,9},{9,8},{10,11... | collective-permute-start | bytes 393224 | tf_op jit(solution)/shard_map/ppermute | solution.py:442
  3.1 13.6 %all-to-all-start = ((s32[8,1,128]{2,1,0:T(1,128)}), s32[8,1,128]{2,1,0:T(1,128)S(1)}, u32[]{:S(2)}, u32[]{:S(2)}) async-start(s32[8,1,128]{2,1,0:T(1,128)} %bitcast.19), calls=%async_computation | async-start | bytes 8192 | tf_op jit(solution)/shard_map/all_to_all | solution.py:467
  10.9 5.9 %collective-permute-start.1 = (bf16[128,512]{1,0:T(8,128)(2,1)S(1)}, bf16[128,512]{1,0:T(8,128)(2,1)S(1)}, u32[]{:S(2)}, u32[]{:S(2)}) collective-permute-start(bf16[128,512]{1,0:T(8,128)(2,1)S(1)} %add_convert_fusion.mine_ref), channel_id=1, source_target_pairs={{0,2},{1,3},{2,0},{3,1},{4,6},{5,7},{6,4},{7,5},{8,10},{9,11},{10,... | collective-permute-start | bytes 393224 | tf_op jit(solution)/shard_map/ppermute | solution.py:442
  12.5 19.9 %copy-start = (bf16[2,1024,512]{2,1,0:T(8,128)(2,1)S(1)}, bf16[2,1024,512]{2,1,0:T(8,128)(2,1)}, u32[]{:S(2)}) copy-start(bf16[2,1024,512]{2,1,0:T(8,128)(2,1)} %weight_ref.3) | copy-start | bytes 6291460
  16.7 27.5 %copy-start.1 = (bf16[512,320]{0,1:T(8,128)(2,1)S(1)}, bf16[512,320]{0,1:T(8,128)(2,1)}, u32[]{:S(2)}) copy-start(bf16[512,320]{0,1:T(8,128)(2,1)} %param.16) | copy-start | bytes 983044
  16.7 27.5 %copy-start.3 = (bf16[128,320]{0,1:T(8,128)(2,1)S(1)}, bf16[128,320]{0,1:T(8,128)(2,1)}, u32[]{:S(2)}) copy-start(bf16[128,320]{0,1:T(8,128)(2,1)} %param.17) | copy-start | bytes 245764
  16.8 0.9 %copy-start.4 = (bf16[64,512]{1,0:T(8,128)(2,1)S(1)}, bf16[64,512]{1,0:T(8,128)(2,1)}, u32[]{:S(2)}) copy-start(bf16[64,512]{1,0:T(8,128)(2,1)} %get-tuple-element.33.sent_ref) | copy-start | bytes 196612
  17.6 20.1 %copy-start.5 = (bf16[256,128]{1,0:T(8,128)(2,1)S(1)}, bf16[256,128]{1,0:T(8,128)(2,1)}, u32[]{:S(2)}) copy-start(bf16[256,128]{1,0:T(8,128)(2,1)} %get-tuple-element.41.refs_8_) | copy-start | bytes 196612
  17.6 26.5 %copy-start.6 = (s32[28]{0:T(128)S(1)}, s32[28]{0:T(128)}, u32[]{:S(2)}) copy-start(s32[28]{0:T(128)} %get-tuple-element.30.me_ref) | copy-start | bytes 340
  19.0 13.4 %all-to-all-start.1 = ((bf16[8,16,512]{2,1,0:T(8,128)(2,1)}), bf16[8,16,512]{2,1,0:T(8,128)(2,1)S(1)}, u32[]{:S(2)}, u32[]{:S(2)}) async-start(bf16[8,16,512]{2,1,0:T(8,128)(2,1)} %shard_map.130), calls=%async_computation.1 | async-start | bytes 262144 | tf_op jit(solution)/shard_map/all_to_all | solution.py:515
  24.9 10.9 %collective-permute-start.6 = (bf16[576,128]{1,0:T(8,128)(2,1)}, bf16[576,128]{1,0:T(8,128)(2,1)S(1)}, u32[]{:S(2)}, u32[]{:S(2)}) collective-permute-start(bf16[576,128]{1,0:T(8,128)(2,1)} %get-tuple-element.38), channel_id=1, source_target_pairs={{0,4},{1,5},{2,6},{3,7},{4,0},{5,1},{6,2},{7,3},{8,12},{9,13},{10,... | collective-permute-start | bytes 442376 | tf_op jit(solution)/shard_map/ppermute | solution.py:442
  27.0 8.8 %collective-permute-start.5 = (bf16[256,128]{1,0:T(8,128)(2,1)}, bf16[256,128]{1,0:T(8,128)(2,1)S(1)}, u32[]{:S(2)}, u32[]{:S(2)}) collective-permute-start(bf16[256,128]{1,0:T(8,128)(2,1)} %get-tuple-element.37), channel_id=1, source_target_pairs={{0,2},{1,3},{2,0},{3,1},{4,6},{5,7},{6,4},{7,5},{8,10},{9,11},{10,... | collective-permute-start | bytes 196616 | tf_op jit(solution)/shard_map/ppermute | solution.py:442
  28.0 7.8 %collective-permute-start.7 = (bf16[256,128]{1,0:T(8,128)(2,1)}, bf16[256,128]{1,0:T(8,128)(2,1)S(1)}, u32[]{:S(2)}, u32[]{:S(2)}) collective-permute-start(bf16[256,128]{1,0:T(8,128)(2,1)} %get-tuple-element.39), channel_id=1, source_target_pairs={{0,6},{1,7},{2,4},{3,5},{4,2},{5,3},{6,0},{7,1},{8,14},{9,15},{10,... | collective-permute-start | bytes 196616 | tf_op jit(solution)/shard_map/ppermute | solution.py:442
  32.4 1.0 %copy-start.2 = (f32[232,512]{1,0:T(8,128)S(1)}, f32[232,512]{1,0:T(8,128)}, u32[]{:S(2)}) copy-start(f32[232,512]{1,0:T(8,128)} %get-tuple-element.34.state_ref) | copy-start | bytes 1425412
  34.2 7.9 %collective-permute-start.3 = (bf16[176,512]{1,0:T(8,128)(2,1)S(1)}, bf16[176,512]{1,0:T(8,128)(2,1)S(1)}, u32[]{:S(2)}, u32[]{:S(2)}) collective-permute-start(bf16[176,512]{1,0:T(8,128)(2,1)S(1)} %get-tuple-element.35.refs_0_.grad_ref), channel_id=1, source_target_pairs={{0,2},{1,3},{2,0},{3,1},{4,6},{5,7},{6,4},{7,5},{8,10},{9,11},{10,... | collective-permute-start | bytes 540680 | tf_op jit(solution)/shard_map/ppermute | solution.py:442
  35.1 7.5 %collective-permute-start.10 = (bf16[144,512]{1,0:T(8,128)(2,1)S(1)}, bf16[144,512]{1,0:T(8,128)(2,1)S(1)}, u32[]{:S(2)}, u32[]{:S(2)}) collective-permute-start(bf16[144,512]{1,0:T(8,128)(2,1)S(1)} %get-tuple-element.40), channel_id=1, source_target_pairs={{0,6},{1,7},{2,4},{3,5},{4,2},{5,3},{6,0},{7,1},{8,14},{9,15},{10,... | collective-permute-start | bytes 442376 | tf_op jit(solution)/shard_map/ppermute | solution.py:442
  35.8 6.9 %collective-permute-start.8 = (bf16[144,512]{1,0:T(8,128)(2,1)S(1)}, bf16[144,512]{1,0:T(8,128)(2,1)S(1)}, u32[]{:S(2)}, u32[]{:S(2)}) collective-permute-start(bf16[144,512]{1,0:T(8,128)(2,1)S(1)} %get-tuple-element.40), channel_id=1, source_target_pairs={{0,4},{1,5},{2,6},{3,7},{4,0},{5,1},{6,2},{7,3},{8,12},{9,13},{10,... | collective-permute-start | bytes 442376 | tf_op jit(solution)/shard_map/ppermute | solution.py:442
  37.8 1.3 %collective-permute-start.12 = (bf16[256,128]{1,0:T(8,128)(2,1)S(1)}, bf16[256,128]{1,0:T(8,128)(2,1)S(1)}, u32[]{:S(2)}, u32[]{:S(2)}) collective-permute-start(bf16[256,128]{1,0:T(8,128)(2,1)S(1)} %copy-done.5), channel_id=1, source_target_pairs={{0,1},{1,0},{2,3},{3,2},{4,5},{5,4},{6,7},{7,6},{8,9},{9,8},{10,11... | collective-permute-start | bytes 196616 | tf_op jit(solution)/shard_map/ppermute | solution.py:442
  37.8 1.4 %collective-permute-start.13 = (bf16[256,128]{1,0:T(8,128)(2,1)S(1)}, bf16[256,128]{1,0:T(8,128)(2,1)S(1)}, u32[]{:S(2)}, u32[]{:S(2)}) collective-permute-start(bf16[256,128]{1,0:T(8,128)(2,1)S(1)} %collective-permute-done.5.refs_9_), channel_id=1, source_target_pairs={{0,1},{1,0},{2,3},{3,2},{4,5},{5,4},{6,7},{7,6},{8,9},{9,8},{10,11... | collective-permute-start | bytes 196616 | tf_op jit(solution)/shard_map/ppermute | solution.py:442
  39.0 3.0 %collective-permute-start.15 = (bf16[256,128]{1,0:T(8,128)(2,1)S(1)}, bf16[256,128]{1,0:T(8,128)(2,1)S(1)}, u32[]{:S(2)}, u32[]{:S(2)}) collective-permute-start(bf16[256,128]{1,0:T(8,128)(2,1)S(1)} %collective-permute-done.7.refs_11_), channel_id=1, source_target_pairs={{0,1},{1,0},{2,3},{3,2},{4,5},{5,4},{6,7},{7,6},{8,9},{9,8},{10,11... | collective-permute-start | bytes 196616 | tf_op jit(solution)/shard_map/ppermute | solution.py:442
  39.2 4.5 %collective-permute-start.2 = (bf16[176,512]{1,0:T(8,128)(2,1)S(1)}, bf16[176,512]{1,0:T(8,128)(2,1)S(1)}, u32[]{:S(2)}, u32[]{:S(2)}) collective-permute-start(bf16[176,512]{1,0:T(8,128)(2,1)S(1)} %get-tuple-element.35.refs_0_.grad_ref), channel_id=1, source_target_pairs={{0,1},{1,0},{2,3},{3,2},{4,5},{5,4},{6,7},{7,6},{8,9},{9,8},{10,11... | collective-permute-start | bytes 540680 | tf_op jit(solution)/shard_map/ppermute | solution.py:442
  42.1 2.1 %collective-permute-start.4 = (bf16[176,512]{1,0:T(8,128)(2,1)S(1)}, bf16[176,512]{1,0:T(8,128)(2,1)S(1)}, u32[]{:S(2)}, u32[]{:S(2)}) collective-permute-start(bf16[176,512]{1,0:T(8,128)(2,1)S(1)} %collective-permute-done.3.refs_2_), channel_id=1, source_target_pairs={{0,1},{1,0},{2,3},{3,2},{4,5},{5,4},{6,7},{7,6},{8,9},{9,8},{10,11... | collective-permute-start | bytes 540680 | tf_op jit(solution)/shard_map/ppermute | solution.py:442
  42.1 1.6 %collective-permute-start.14 = (bf16[576,128]{1,0:T(8,128)(2,1)S(1)}, bf16[576,128]{1,0:T(8,128)(2,1)S(1)}, u32[]{:S(2)}, u32[]{:S(2)}) collective-permute-start(bf16[576,128]{1,0:T(8,128)(2,1)S(1)} %collective-permute-done.6.refs_10_), channel_id=1, source_target_pairs={{0,1},{1,0},{2,3},{3,2},{4,5},{5,4},{6,7},{7,6},{8,9},{9,8},{10,11... | collective-permute-start | bytes 442376 | tf_op jit(solution)/shard_map/ppermute | solution.py:442
  42.6 1.4 %collective-permute-start.11 = (bf16[144,512]{1,0:T(8,128)(2,1)S(1)}, bf16[144,512]{1,0:T(8,128)(2,1)S(1)}, u32[]{:S(2)}, u32[]{:S(2)}) collective-permute-start(bf16[144,512]{1,0:T(8,128)(2,1)S(1)} %collective-permute-done.10.refs_6_), channel_id=1, source_target_pairs={{0,1},{1,0},{2,3},{3,2},{4,5},{5,4},{6,7},{7,6},{8,9},{9,8},{10,11... | collective-permute-start | bytes 442376 | tf_op jit(solution)/shard_map/ppermute | solution.py:442
  42.7 1.5 %collective-permute-start.9 = (bf16[144,512]{1,0:T(8,128)(2,1)S(1)}, bf16[144,512]{1,0:T(8,128)(2,1)S(1)}, u32[]{:S(2)}, u32[]{:S(2)}) collective-permute-start(bf16[144,512]{1,0:T(8,128)(2,1)S(1)} %collective-permute-done.8.refs_4_), channel_id=1, source_target_pairs={{0,1},{1,0},{2,3},{3,2},{4,5},{5,4},{6,7},{7,6},{8,9},{9,8},{10,11... | collective-permute-start | bytes 442376 | tf_op jit(solution)/shard_map/ppermute | solution.py:442
  46.2 7.1 %collective-permute-start.16 = (bf16[112,512]{1,0:T(8,128)(2,1)S(1)}, bf16[112,512]{1,0:T(8,128)(2,1)S(1)}, u32[]{:S(2)}, u32[]{:S(2)}) collective-permute-start(bf16[112,512]{1,0:T(8,128)(2,1)S(1)} %get-tuple-element.47), channel_id=1, source_target_pairs={{0,8},{1,9},{2,10},{3,11},{4,12},{5,13},{6,14},{7,15},{8,0},{9,1},... | collective-permute-start | bytes 344072 | tf_op jit(solution)/shard_map/ppermute | solution.py:442
  46.2 11.8 %collective-permute-start.17 = (bf16[112,512]{1,0:T(8,128)(2,1)S(1)}, bf16[112,512]{1,0:T(8,128)(2,1)S(1)}, u32[]{:S(2)}, u32[]{:S(2)}) collective-permute-start(bf16[112,512]{1,0:T(8,128)(2,1)S(1)} %get-tuple-element.48), channel_id=1, source_target_pairs={{0,16},{1,17},{2,18},{3,19},{4,20},{5,21},{6,22},{7,23},{8,24},{9,... | collective-permute-start | bytes 344072 | tf_op jit(solution)/shard_map/ppermute | solution.py:442
  48.0 10.0 %collective-permute-start.18 = (bf16[112,512]{1,0:T(8,128)(2,1)S(1)}, bf16[112,512]{1,0:T(8,128)(2,1)S(1)}, u32[]{:S(2)}, u32[]{:S(2)}) collective-permute-start(bf16[112,512]{1,0:T(8,128)(2,1)S(1)} %get-tuple-element.49), channel_id=1, source_target_pairs={{0,24},{1,25},{2,26},{3,27},{4,28},{5,29},{6,30},{7,31},{8,16},{9,... | collective-permute-start | bytes 344072 | tf_op jit(solution)/shard_map/ppermute | solution.py:442
